TPU v7x, 128 devices: a whole 4x4x4 slice. The times are simulated.
128 devices in a mesh: seq: 16 (over z, y), grp: 8 (over x, core).
Axes of the slice: x: 4, y: 4, z: 4, core: 2. Of those that a mesh axis runs over, the one named last changes fastest.
Arguments:
- x_group: bfloat16 [4096, 2304], P('seq'), may hold values from -6 to 6
- decode_input: bfloat16 [3, 128, 2304], P(None, 'seq'), may hold values from -6 to 6
- prompt_len: int32 [128], P('seq'), may hold values from 1 to 768, as said below
- latent_pages: bfloat16 [16, 16, 6, 64, 576], P('seq'), may hold values from -6 to 6
- slot_target: int32 [16, 16, 6], P(None, 'seq'), may hold values from 0 to 95, as said below
- page_counts: int32 [16, 16], P(None, 'seq'), may hold values from 0 to 6, as said below
- kda_state: float32 [128, 32, 128, 128], P(None, 'grp', 'seq'), may hold values from -4 to 4
- query_proj: bfloat16 [2304, 6144], P(None, 'grp'), may hold values from -1 to 1
- latent_proj: bfloat16 [2304, 576], replicated, may hold values from -1 to 1
- key_expand: bfloat16 [512, 4096], P(None, 'grp'), may hold values from -1 to 1
- value_expand: bfloat16 [512, 4096], P(None, 'grp'), may hold values from -0.25 to 0.25
- mla_output: bfloat16 [4096, 2304], P('grp'), may hold values from -0.09375 to 0.09375
- kda_inputs: bfloat16 [2304, 3, 4096], P(None, None, 'grp'), may hold values from -0.125 to 0.125
- kda_beta: bfloat16 [2304, 32], P(None, 'grp'), may hold values from -0.125 to 0.125
- decay_down: bfloat16 [2304, 128], replicated, may hold values from -0.125 to 0.125
- decay_up: bfloat16 [128, 4096], P(None, 'grp'), may hold values from -0.5 to 0.5
- gate_down: bfloat16 [2304, 128], replicated, may hold values from -0.125 to 0.125
- gate_up: bfloat16 [128, 4096], P(None, 'grp'), may hold values from -0.5 to 0.5
- decay_log: float32 [32], P('grp'), may hold values from -2.5 to 0.5
- kda_output: bfloat16 [4096, 2304], P('grp'), may hold values from -0.09375 to 0.09375
Outputs:
- prefill_out: bfloat16 [4096, 2304], P('seq', 'grp')
- decode_out: bfloat16 [3, 128, 2304], P(None, 'seq', 'grp')
Inputs may be any that keep to these rules, and one draw needn't show every extreme that they name: A request has ceil(prompt_len / 64) pages, at most 12; on one owner drawn from the seed all 8 requests have 12 pages. `slot_target`: entry k < page_counts[s, d] holds local request * 12 + page of owner d; every page of every request is held in exactly one slot; entries past the count are 0. `page_counts`: slots are filled from slot 0; the count 6 is reached on some pair in every draw.
All inputs are finite; a program needn't handle non-finite values.
Results may differ from a plain program's by a relative error of at most 0.02.
Values may be sent and summed in bfloat16 or wider, within the bound.
No kernel may reach another device: no remote copies, remote signals or barrier semaphores. Data moves between devices by JAX's collectives and lax.ppermute only.
A program may use at most 192 MiB of HBM per device.

v0:
```python
import jax
import jax.numpy as jnp
from jax import lax
from jax.sharding import PartitionSpec as P

LAT = 512
ROPE = 64
NOPE = 128
VH = 128
DK = 128
DV = 128
PAGE = 64
MAXP = 12


epsilon = 1e-06
masked_score = -1e30


def norm_rows(values):
    return values * lax.rsqrt(jnp.mean(values * values, axis=-1, keepdims=True) + epsilon)


def unit_rows(values):
    return values * lax.rsqrt(jnp.sum(values * values, axis=-1, keepdims=True) + epsilon)


def rotate(values, position):
    halfway = values.shape[-1] // 2
    frequency = jnp.exp(-jnp.log(10000.0) * jnp.arange(halfway, dtype=jnp.float32) / halfway)
    angles = position.astype(jnp.float32)[..., None] * frequency
    leading = values[..., :halfway]
    trailing = values[..., halfway:]
    return jnp.concatenate(
        [
            leading * jnp.cos(angles) - trailing * jnp.sin(angles),
            leading * jnp.sin(angles) + trailing * jnp.cos(angles),
        ],
        axis=-1,
    )


def make_latent(normed, latent_proj, position):
    projected = jnp.dot(normed, latent_proj, preferred_element_type=jnp.float32)
    return jnp.concatenate(
        [norm_rows(projected[:, :LAT]), rotate(projected[:, LAT:], position)], axis=-1
    ).astype(jnp.bfloat16)


def make_query(normed, query_proj, position):
    head_count = query_proj.shape[1] // (NOPE + ROPE)
    projected = jnp.dot(normed, query_proj, preferred_element_type=jnp.float32).reshape(
        normed.shape[0], head_count, NOPE + ROPE
    )
    return (
        projected[..., :NOPE].astype(jnp.bfloat16),
        rotate(projected[..., NOPE:], position[:, None]).astype(jnp.bfloat16),
    )


def absorb(q_nope, q_rope, key_expand):
    head_count = q_nope.shape[1]
    latent_query = jnp.einsum(
        "rhn,chn->rhc",
        q_nope,
        key_expand.reshape(LAT, head_count, NOPE),
        preferred_element_type=jnp.float32,
    )
    return jnp.concatenate([latent_query.astype(jnp.bfloat16), q_rope], axis=-1)


def partial_attend(queries, key_rows, live_mask):
    scores = jnp.einsum("rhc,kc->rhk", queries, key_rows, preferred_element_type=jnp.float32) * (
        NOPE + ROPE
    ) ** (-0.5)
    scores = jnp.where(live_mask[:, None, :], scores, masked_score)
    highest = jnp.max(scores, axis=-1)
    weights = jnp.where(live_mask[:, None, :], jnp.exp(scores - highest[..., None]), 0.0)
    totals = jnp.sum(weights, axis=-1)
    summed = jnp.einsum(
        "rhk,kc->rhc",
        weights.astype(jnp.bfloat16),
        key_rows[:, :LAT],
        preferred_element_type=jnp.float32,
    )
    return (highest, totals, summed)


def cache_mask(target, counts, lengths, offset, width):
    slot_live = jnp.arange(target.shape[1])[None, :] < counts[:, None]
    request = target // MAXP
    token_pos = (target % MAXP)[..., None] * PAGE + offset + jnp.arange(width)[None, None, :]
    owners = jnp.arange(lengths.shape[0])[:, None, None, None]
    live = (
        slot_live[None, :, :, None]
        & (request[None, :, :, None] == owners)
        & (token_pos[None] < lengths[:, None, None, None])
    )
    return live.reshape(lengths.shape[0], -1)


def shards(
    x_group,
    decode_input,
    prompt_len,
    latent_pages,
    slot_target,
    page_counts,
    kda_state,
    query_proj,
    latent_proj,
    key_expand,
    value_expand,
    mla_output,
    kda_inputs,
    kda_beta,
    decay_down,
    decay_up,
    gate_down,
    gate_up,
    decay_log,
    kda_output,
):
    seq_index = lax.axis_index("seq")
    grp_index = lax.axis_index("grp")
    head_local = key_expand.shape[1] // NOPE
    kh_local = decay_log.shape[0]
    model_width = x_group.shape[1]
    share_width = model_width // lax.axis_size("grp")
    column_start = grp_index * share_width
    states = lax.all_to_all(
        kda_state.astype(jnp.bfloat16), "seq", split_axis=0, concat_axis=2, tiled=True
    ).astype(kda_state.dtype)
    target = slot_target[:, 0, :]
    counts = page_counts[:, 0]
    sub_width = PAGE
    offset = 0
    arrived = lax.all_to_all(latent_pages, "seq", split_axis=1, concat_axis=0, tiled=True)
    cache_rows = arrived.reshape(-1, LAT + ROPE)
    cache_live = cache_mask(target, counts, prompt_len, offset, sub_width)
    rows_in = x_group.astype(jnp.float32)
    normed = norm_rows(rows_in).astype(jnp.bfloat16)
    group_rows = x_group.shape[0]
    position = seq_index * group_rows + jnp.arange(group_rows)
    q_nope, q_rope = make_query(normed, query_proj, position)
    own_latent = make_latent(normed, latent_proj, position)
    shard_rows = lax.all_gather(own_latent, "seq", axis=0, tiled=True)
    peak_old = jnp.full((group_rows, head_local), masked_score, jnp.float32)
    row_count = shard_rows.shape[0]
    k_nope = (
        jnp.dot(shard_rows[:, :LAT], key_expand, preferred_element_type=jnp.float32)
        .astype(jnp.bfloat16)
        .reshape(row_count, head_local, NOPE)
    )
    values = (
        jnp.dot(shard_rows[:, :LAT], value_expand, preferred_element_type=jnp.float32)
        .astype(jnp.bfloat16)
        .reshape(row_count, head_local, VH)
    )
    scores = jnp.einsum("qhn,khn->qhk", q_nope, k_nope, preferred_element_type=jnp.float32)
    scores = (
        scores
        + jnp.einsum("qhr,kr->qhk", q_rope, shard_rows[:, LAT:], preferred_element_type=jnp.float32)
    ) * (NOPE + ROPE) ** (-0.5)
    key_pos = jnp.arange(row_count)
    live = key_pos[None, None, :] <= position[:, None, None]
    scores = jnp.where(live, scores, masked_score)
    new_peak = jnp.maximum(peak_old, jnp.max(scores, axis=-1))
    weights = jnp.where(live, jnp.exp(scores - new_peak[..., None]), 0.0)
    totals_new = jnp.sum(weights, axis=-1)
    summed_new = jnp.einsum(
        "qhk,khv->qhv", weights.astype(jnp.bfloat16), values, preferred_element_type=jnp.float32
    )
    heads_out = (
        (summed_new / totals_new[..., None])
        .astype(jnp.bfloat16)
        .reshape(group_rows, head_local * VH)
    )
    prefill_part = jnp.dot(heads_out, mla_output, preferred_element_type=jnp.float32)
    attended = lax.psum_scatter(
        prefill_part.astype(jnp.bfloat16), "grp", scatter_dimension=1, tiled=True
    ).astype(jnp.float32)
    prefill_out = (
        lax.dynamic_slice_in_dim(rows_in, column_start, share_width, 1) + attended
    ).astype(jnp.bfloat16)
    steps_total = decode_input.shape[0]
    req_local = decode_input.shape[1]
    dec_rows = decode_input.astype(jnp.float32)
    dec_normed = norm_rows(dec_rows).astype(jnp.bfloat16)
    fresh_list = []
    results = []
    for step_index in range(steps_total):
        place = prompt_len + step_index
        q_nope_now, q_rope_now = make_query(dec_normed[step_index], query_proj, place)
        latent_query = absorb(q_nope_now, q_rope_now, key_expand)
        fresh_list.append(make_latent(dec_normed[step_index], latent_proj, place))
        fresh_keys = jnp.concatenate(fresh_list, axis=0)
        fresh_live = (jnp.arange(fresh_keys.shape[0]) % req_local)[None, :] == jnp.arange(
            req_local
        )[:, None]
        all_keys = jnp.concatenate([cache_rows, fresh_keys], axis=0)
        live_now = jnp.concatenate([cache_live, fresh_live], axis=1)
        peak_now, totals_now, summed_now = partial_attend(latent_query, all_keys, live_now)
        latent_out = (summed_now / totals_now[..., None]).astype(jnp.bfloat16)
        head_values = jnp.einsum(
            "rhc,chv->rhv",
            latent_out,
            value_expand.reshape(LAT, head_local, VH),
            preferred_element_type=jnp.float32,
        ).astype(jnp.bfloat16)
        mla_part = jnp.dot(
            head_values.reshape(req_local, head_local * VH),
            mla_output,
            preferred_element_type=jnp.float32,
        )
        mla_total = lax.psum(mla_part.astype(jnp.bfloat16), "grp").astype(jnp.float32)
        hidden = dec_rows[step_index] + mla_total
        kda_in = norm_rows(hidden).astype(jnp.bfloat16)
        hidden_share = lax.dynamic_slice_in_dim(hidden, column_start, share_width, 1)
        projected = jnp.dot(
            kda_in, kda_inputs.reshape(model_width, -1), preferred_element_type=jnp.float32
        ).reshape(req_local, 3, kh_local, DK)
        queries_kda = unit_rows(projected[:, 0]) * DK ** (-0.5)
        keys_kda = unit_rows(projected[:, 1])
        values_kda = projected[:, 2]
        write_rate = jax.nn.sigmoid(jnp.dot(kda_in, kda_beta, preferred_element_type=jnp.float32))
        decay_low = jnp.dot(kda_in, decay_down, preferred_element_type=jnp.float32).astype(
            jnp.bfloat16
        )
        decays = jnp.exp(
            -jnp.exp(decay_log)[None, :, None]
            * jax.nn.softplus(
                jnp.dot(decay_low, decay_up, preferred_element_type=jnp.float32).reshape(
                    req_local, kh_local, DK
                )
            )
        )
        gate_low = jnp.dot(kda_in, gate_down, preferred_element_type=jnp.float32).astype(
            jnp.bfloat16
        )
        out_gate = jax.nn.sigmoid(
            jnp.dot(gate_low, gate_up, preferred_element_type=jnp.float32).reshape(
                req_local, kh_local, DV
            )
        )
        states = states * decays[:, :, None, :]
        errors = values_kda - jnp.sum(states * keys_kda[:, :, None, :], axis=-1)
        states = states + write_rate[..., None, None] * errors[..., None] * keys_kda[:, :, None, :]
        readout = jnp.sum(states * queries_kda[:, :, None, :], axis=-1)
        blended = (
            (norm_rows(readout) * out_gate).astype(jnp.bfloat16).reshape(req_local, kh_local * DV)
        )
        kda_part = jnp.dot(blended, kda_output, preferred_element_type=jnp.float32)
        kda_share = lax.psum_scatter(
            kda_part.astype(jnp.bfloat16), "grp", scatter_dimension=1, tiled=True
        ).astype(jnp.float32)
        results.append((hidden_share + kda_share).astype(jnp.bfloat16))
    return (prefill_out, jnp.stack(results))


def solution(mesh):
    in_specs = (
        P("seq", None),
        P(None, "seq", None),
        P("seq"),
        P("seq", None, None, None, None),
        P(None, "seq", None),
        P(None, "seq"),
        P(None, "grp", "seq", None),
        P(None, "grp"),
        P(),
        P(None, "grp"),
        P(None, "grp"),
        P("grp", None),
        P(None, None, "grp"),
        P(None, "grp"),
        P(),
        P(None, "grp"),
        P(),
        P(None, "grp"),
        P("grp"),
        P("grp", None),
    )
    out_specs = (P("seq", "grp"), P(None, "seq", "grp"))
    return jax.shard_map(shards, mesh=mesh, in_specs=in_specs, out_specs=out_specs, check_vma=False)
```

profile of v0, /device:TPU:0, one launch (start us, length us, event | category | flops | bytes accessed | tf_op | source)
XLA Modules:
  0.0 462.2 jit_solution(6711538454815315076)
XLA Ops:
  8.0 8.5 %all-to-all-start = ((bf16[1,16,6,64,576]{4,3,2,0,1:T(8,128)(2,1)}), bf16[1,16,6,64,576]{4,3,2,0,1:T(8,128)(2,1)}, u32[]{:S(2)}, u32[]{:S(2)}) async-start(bf16[1,16,6,64,576]{4,3,2,0,1:T(8,128)(2,1)} %bitcast.379), calls=%async_computation.1 | async-start | bytes 15728640 | tf_op jit(solution)/shard_map/all_to_all | solution.py:138
  21.9 2.4 copy.217
  24.3 1.6 multiply_reduce_fusion
  25.9 2.1 fusion.86
  29.4 5.9 %copy.228 = bf16[2304,768]{0,1:T(8,128)(2,1)} copy(bf16[2304,768]{1,0:T(8,128)(2,1)} %param.27) | data formatting | bytes 7077888 | tf_op args[7]
  36.8 1.2 convert_element_type.249
  38.0 3.2 fusion.149
  41.2 3.1 fusion.145
  48.6 84.3 %all-to-all-done = bf16[1,16,6,64,576]{4,3,2,0,1:T(8,128)(2,1)} async-done(((bf16[1,16,6,64,576]{4,3,2,0,1:T(8,128)(2,1)}), bf16[1,16,6,64,576]{4,3,2,0,1:T(8,128)(2,1)}, u32[]{:S(2)}, u32[]{:S(2)}) %all-to-all-start) | async-done | bytes 7077920 | tf_op jit(solution)/shard_map/all_to_all | solution.py:138
  132.9 5.6 %all-to-all-start.1 = ((bf16[128,4,8,128]{3,2,1,0:T(8,128)(2,1)}), bf16[128,4,8,128]{3,2,1,0:T(8,128)(2,1)}, u32[]{:S(2)}, u32[]{:S(2)}) async-start(bf16[128,4,8,128]{3,2,1,0:T(8,128)(2,1)} %convert_element_type.249), calls=%async_computation.2 | async-start | bytes 2097152 | tf_op jit(solution)/shard_map/all_to_all | solution.py:131
  138.7 10.2 %copy.231 = bf16[6144,576]{0,1:T(8,128)(2,1)} copy(bf16[6144,576]{1,0:T(8,128)(2,1)} %bitcast.18) | data formatting | bytes 14155776 | tf_op jit(solution)/shard_map/reshape | solution.py:139
  148.9 11.2 %concatenate.65 = bf16[6160,576]{0,1:T(8,128)(2,1)} concatenate(bf16[6144,576]{0,1:T(8,128)(2,1)} %copy.231, bf16[8,576]{0,1:T(8,128)(2,1)S(1)} %copy.232, bf16[8,576]{0,1:T(8,128)(2,1)S(1)} %copy.249), dimensions={0} | concatenate | bytes 14192640 | tf_op jit(solution)/shard_map/concatenate | solution.py:201
  160.1 4.4 fusion.16
  165.6 11.3 %concatenate.69 = bf16[6168,576]{0,1:T(8,128)(2,1)} concatenate(bf16[6144,576]{0,1:T(8,128)(2,1)} %copy.231, bf16[8,576]{0,1:T(8,128)(2,1)S(1)} %copy.232, bf16[8,576]{0,1:T(8,128)(2,1)S(1)} %copy.249, bf16[8,576]{0,1:T(8,128)(2,1)S(1)} %copy.266), dimensions={0} | concatenate | bytes 14211072 | tf_op jit(solution)/shard_map/concatenate | solution.py:201
  176.9 4.4 fusion.15
  182.5 5.2 %fusion.64 = bf16[8,512]{1,0:T(8,128)(2,1)S(1)} fusion(bf16[6160,576]{0,1:T(8,128)(2,1)} %concatenate.65, bf16[8,4,6160]{2,0,1:T(8,128)(2,1)} %get-tuple-element.83, f32[8,4]{0,1:T(4,128)S(1)} %get-tuple-element.82, bf16[512,512]{1,0:T(8,128)(2,1)S(1)} %copy-done.55), kind=kOutput, calls=%fused_computation.100 | convolution fusion | flops 206082048 | bytes 7356544 | tf_op jit(solution)/shard_map/rhc,chv->rhv/dot_general | solution.py:205
  188.7 5.1 %fusion.65 = bf16[8,512]{1,0:T(8,128)(2,1)S(1)} fusion(bf16[6168,576]{0,1:T(8,128)(2,1)} %concatenate.69, bf16[8,4,6168]{2,0,1:T(8,128)(2,1)} %get-tuple-element.79, f32[8,4]{0,1:T(4,128)S(1)} %get-tuple-element.78, bf16[512,512]{1,0:T(8,128)(2,1)S(1)} %copy-done.55), kind=kOutput, calls=%fused_computation.101 | convolution fusion | flops 206344192 | bytes 7356544 | tf_op jit(solution)/shard_map/rhc,chv->rhv/dot_general | solution.py:205
  194.8 4.9 %fusion.17 = f32[8,4,6152]{2,0,1:T(8,128)S(1)} fusion(bf16[8,576]{0,1:T(8,128)(2,1)S(1)} %copy.232, bf16[6144,576]{0,1:T(8,128)(2,1)} %copy.231, pred[8,6152]{1,0:T(8,128)(4,1)S(1)} %pad_add_fusion, bf16[8,4,32]{2,0,1:T(8,128)(2,1)S(1)} %copy-done.42, bf16[8,4,32]{2,0,1:T(8,128)(2,1)S(1)} %copy-done.41, bf16[8,4,512]{2,0,1:T(8,128)(2,1)S(1)} %copy-done.40), kind=kOutput, calls=%fused_computation.23 | convolution fusion | flops 241465856 | bytes 7960640 | tf_op jit(solution)/shard_map/rhc,kc->rhk/dot_general | solution.py:73
  200.7 4.4 fusion.63
  207.2 3.9 fusion.85
  211.1 10.1 %copy.237 = bf16[2304,3,512]{0,2,1:T(8,128)(2,1)} copy(bf16[2304,3,512]{2,0,1:T(8,128)(2,1)} %param.32) | data formatting | bytes 14155776 | tf_op args[12]
  221.3 1.8 iota_compare_fusion
  223.7 43.0 %all-reduce.3.cloned.1.call-done = (bf16[8,2304]{1,0:T(8,128)(2,1)}, bf16[8,2304]{1,0:T(8,128)(2,1)}, bf16[8,2304]{1,0:T(8,128)(2,1)}) async-done(((bf16[8,2304]{1,0:T(8,128)(2,1)}, bf16[8,2304]{1,0:T(8,128)(2,1)}, bf16[8,2304]{1,0:T(8,128)(2,1)}), (bf16[8,2304]{1,0:T(8,128)(2,1)}, bf16[8,2304]{1,0:T(8,128)(2,1)}, bf16[8,2304]{1,0:T(8,128)(2,1)})) %all-reduce.3.cloned.1.call-update) | async-done | bytes 110608 | tf_op jit(solution)/shard_map/psum | solution.py:216
  268.4 5.0 %fusion.141 = f32[8,3,4,128]{3,0,2,1:T(8,128)S(1)} fusion(bf16[3,4,128,2304]{3,2,1,0:T(8,128)(2,1)} %bitcast.372, bf16[8,2304]{1,0:T(8,128)(2,1)S(1)} %multiply_convert_fusion.6), kind=kOutput, calls=%fused_computation.209 | convolution fusion | flops 56623104 | bytes 7163904 | tf_op jit(solution)/shard_map/dot_general | solution.py:220
  274.1 4.9 %fusion.143 = f32[8,3,4,128]{3,0,2,1:T(8,128)S(1)} fusion(bf16[3,4,128,2304]{3,2,1,0:T(8,128)(2,1)} %bitcast.373, bf16[8,2304]{1,0:T(8,128)(2,1)S(1)} %multiply_convert_fusion.7), kind=kOutput, calls=%fused_computation.211 | convolution fusion | flops 56623104 | bytes 7163904 | tf_op jit(solution)/shard_map/dot_general | solution.py:220
  281.2 4.9 %fusion.139 = f32[8,3,4,128]{3,0,2,1:T(8,128)S(1)} fusion(bf16[3,4,128,2304]{3,2,1,0:T(8,128)(2,1)} %bitcast.374, bf16[8,2304]{1,0:T(8,128)(2,1)S(1)} %multiply_convert_fusion.5), kind=kOutput, calls=%fused_computation.207 | convolution fusion | flops 56623104 | bytes 7163904 | tf_op jit(solution)/shard_map/dot_general | solution.py:220
  287.3 1.9 fusion.40
  289.5 2.5 multiply_reduce_fusion.4
  292.2 4.3 multiply_reduce_fusion.3
  298.1 1.8 copy.258
  299.8 1.3 slice.250
  301.2 1.6 squeeze.61
  305.2 1.2 fusion.114
  306.4 5.2 %multiply_reduce_fusion.5 = (f32[8,4,16,8]{3,1,0,2:T(4,128)S(1)}, f32[8,4,16,8]{3,1,0,2:T(4,128)}) fusion(bf16[16,8,4,8,128]{4,3,2,1,0:T(8,128)(2,1)} %bitcast.75, f32[8,4,128]{2,1,0:T(4,128)S(1)} %copy.240, f32[8,4,16,8]{3,1,0,2:T(4,128)S(1)} %fusion.116, f32[8,4,128]{2,1,0:T(4,128)S(1)} %copy.238, f32[8,4,128]{2,1,0:T(4,128)S(1)} %copy.235, ...), kind=kLoop, calls=%fused_computation.66 | loop fusion | flops 7331840 | bytes 1261568 | tf_op jit(solution)/shard_map/reduce_sum | solution.py:249
  313.1 1.8 copy.242
  317.4 1.4 convolution_convert_fusion.5
  330.2 4.6 convolution_convert_fusion
  334.8 8.1 %fusion.113 = f32[4,4096,256]{2,1,0:T(8,128)} fusion(bf16[4096,4,128]{0,2,1:T(8,128)(2,1)S(1)} %bitcast.378, f32[256,4,192]{0,2,1:T(8,128)S(1)} %bitcast.384), kind=kOutput, calls=%fused_computation.151 | convolution fusion | flops 1073741824 | bytes 21233664 | tf_op jit(solution)/shard_map/qhn,khn->qhk/dot_general | solution.py:160
  343.0 11.0 %fusion.207 = (f32[256,4]{0,1:T(4,128)S(1)}, f32[256,4,4096]{0,2,1:T(8,128)}) fusion(bf16[4096,576]{0,1:T(8,128)(2,1)} %all-gather.2.cloned.1.call-done, bf16[256,4,32]{0,2,1:T(8,128)(2,1)S(1)} %copy-done.32, bf16[256,4,32]{0,2,1:T(8,128)(2,1)S(1)} %copy-done.31, f32[4,4096,256]{2,1,0:T(8,128)} %fusion.113, pred[256,4096]{0,1:T(8,128)(4,1)S(1)} %copy-done.6), kind=kOutput, calls=%fused_computation.361 | convolution fusion | flops 553909248 | bytes 35262464 | tf_op jit(solution)/shard_map/qhr,kr->qhk/dot_general | solution.py:163
  354.0 8.9 %fusion.5 = f32[256,4]{0,1:T(4,128)S(1)} fusion(f32[256,4,4096]{0,2,1:T(8,128)} %get-tuple-element.77, f32[256,4]{0,1:T(4,128)S(1)} %broadcast_maximum_fusion, pred[256,4096]{0,1:T(8,128)(4,1)S(1)} %copy-done.6), kind=kLoop, calls=%fused_computation.7 | loop fusion | flops 12581888 | bytes 17833984 | tf_op jit(solution)/shard_map/reduce_sum | solution.py:170
  362.8 4.6 convolution_convert_fusion.1
  367.4 7.7 %fusion.90 = bf16[256,4,128]{0,2,1:T(8,128)(2,1)S(1)} fusion(bf16[4096,4,128]{0,2,1:T(8,128)(2,1)S(1)} %bitcast.390, f32[256,4,4096]{0,2,1:T(8,128)} %get-tuple-element.77, f32[256,4]{0,1:T(4,128)S(1)} %broadcast_maximum_fusion, pred[256,4096]{0,1:T(8,128)(4,1)S(1)} %copy-done.6, f32[256,4]{0,1:T(4,128)S(1)} %fusion.5), kind=kOutput, calls=%fused_computation.129 | convolution fusion | flops 1086586880 | bytes 22290432 | tf_op jit(solution)/shard_map/qhk,khv->qhv/dot_general | solution.py:171
  375.2 2.1 convolution_convert_fusion.2
  377.3 2.9 convert_element_type.228
  381.1 6.5 %reduce-scatter.13.cloned.1.call-done = bf16[288,8]{1,0:T(8,128)(2,1)} async-done(((bf16[2304,8]{1,0:T(8,128)(2,1)}), bf16[288,8]{1,0:T(8,128)(2,1)}) %reduce-scatter.13.cloned.1.call-update) | async-done | bytes 4624
  388.5 31.4 %reduce-scatter.17.cloned.1.call-done = bf16[288,8]{1,0:T(8,128)(2,1)} async-done(((bf16[2304,8]{1,0:T(8,128)(2,1)}), bf16[288,8]{1,0:T(8,128)(2,1)}) %reduce-scatter.17.cloned.1.call-update) | async-done | bytes 4624
  423.1 30.1 %reduce-scatter.11.cloned.1.call-done = bf16[256,288]{0,1:T(8,128)(2,1)} async-done(((bf16[256,2304]{0,1:T(8,128)(2,1)}), bf16[256,288]{0,1:T(8,128)(2,1)}) %reduce-scatter.11.cloned.1.call-update) | async-done | bytes 147472 | tf_op jit(solution)/shard_map/reduce_scatter | solution.py:180
  453.2 1.7 add_convert_fusion
  (274 shorter events, 50.8 us)
Async XLA Ops:
  8.0 8.7 %copy-start = (bf16[2304,576]{0,1:T(8,128)(2,1)S(1)}, bf16[2304,576]{0,1:T(8,128)(2,1)}, u32[]{:S(2)}) copy-start(bf16[2304,576]{0,1:T(8,128)(2,1)} %param.28) | copy-start | bytes 7962628
  8.0 8.5 %copy-start.19 = (bf16[3,8,2304]{2,1,0:T(8,128)(2,1)S(1)}, bf16[3,8,2304]{2,1,0:T(8,128)(2,1)}, u32[]{:S(2)}) copy-start(bf16[3,8,2304]{2,1,0:T(8,128)(2,1)} %param.21) | copy-start | bytes 331780
  8.0 124.8 %all-to-all-start = ((bf16[1,16,6,64,576]{4,3,2,0,1:T(8,128)(2,1)}), bf16[1,16,6,64,576]{4,3,2,0,1:T(8,128)(2,1)}, u32[]{:S(2)}, u32[]{:S(2)}) async-start(bf16[1,16,6,64,576]{4,3,2,0,1:T(8,128)(2,1)} %bitcast.379), calls=%async_computation.1 | async-start | bytes 15728640 | tf_op jit(solution)/shard_map/all_to_all | solution.py:138
  19.2 9.5 %copy-start.45 = (f32[32]{0:T(128)}, f32[32]{0:T(128)S(1)}, u32[]{:S(2)}) copy-start(f32[32]{0:T(128)S(1)} %multiply_exponential_fusion) | copy-start | bytes 388
  29.4 7.3 %copy-start.14 = (f32[128,4,8,128]{3,2,1,0:T(8,128)S(1)}, f32[128,4,8,128]{3,2,1,0:T(8,128)}, u32[]{:S(2)}) copy-start(f32[128,4,8,128]{3,2,1,0:T(8,128)} %param.26) | copy-start | bytes 6291460
  38.0 6.5 %copy-start.2 = (bf16[2304,768]{0,1:T(8,128)(2,1)S(1)}, bf16[2304,768]{0,1:T(8,128)(2,1)}, u32[]{:S(2)}) copy-start(bf16[2304,768]{0,1:T(8,128)(2,1)} %copy.228) | copy-start | bytes 10616836
  41.2 5.8 %copy-start.9 = (bf16[512,512]{1,0:T(8,128)(2,1)S(1)}, bf16[512,512]{1,0:T(8,128)(2,1)}, u32[]{:S(2)}) copy-start(bf16[512,512]{1,0:T(8,128)(2,1)} %param.29) | copy-start | bytes 1572868
  132.9 154.4 %all-to-all-start.1 = ((bf16[128,4,8,128]{3,2,1,0:T(8,128)(2,1)}), bf16[128,4,8,128]{3,2,1,0:T(8,128)(2,1)}, u32[]{:S(2)}, u32[]{:S(2)}) async-start(bf16[128,4,8,128]{3,2,1,0:T(8,128)(2,1)} %convert_element_type.249), calls=%async_computation.2 | async-start | bytes 2097152 | tf_op jit(solution)/shard_map/all_to_all | solution.py:131
  138.5 128.3 %all-reduce.3.cloned.1.call-start = ((), (), s32[]{:S(2)}) async-start(), calls=%async_computation.11 | async-start | bytes 221184 | tf_op jit(solution)/shard_map/psum | solution.py:216
  176.9 5.5 %copy-start.55 = (bf16[512,512]{1,0:T(8,128)(2,1)S(1)}, bf16[512,512]{1,0:T(8,128)(2,1)}, u32[]{:S(2)}) copy-start(bf16[512,512]{1,0:T(8,128)(2,1)} %param.30) | copy-start | bytes 1572868
  188.7 6.1 %copy-start.40 = (bf16[8,4,512]{2,0,1:T(8,128)(2,1)S(1)}, bf16[8,4,512]{2,0,1:T(8,128)(2,1)}, u32[]{:S(2)}) copy-start(bf16[8,4,512]{2,0,1:T(8,128)(2,1)} %fusion.45) | copy-start | bytes 98308
  188.7 6.1 %copy-start.41 = (bf16[8,4,32]{2,0,1:T(8,128)(2,1)S(1)}, bf16[8,4,32]{2,0,1:T(8,128)(2,1)}, u32[]{:S(2)}) copy-start(bf16[8,4,32]{2,0,1:T(8,128)(2,1)} %get-tuple-element.37) | copy-start | bytes 6148
  188.7 6.1 %copy-start.42 = (bf16[8,4,32]{2,0,1:T(8,128)(2,1)S(1)}, bf16[8,4,32]{2,0,1:T(8,128)(2,1)}, u32[]{:S(2)}) copy-start(bf16[8,4,32]{2,0,1:T(8,128)(2,1)} %get-tuple-element.38) | copy-start | bytes 6148
  200.7 5.6 %copy-start.38 = (bf16[256,32]{0,1:T(8,128)(2,1)S(1)}, bf16[256,32]{0,1:T(8,128)(2,1)}, u32[]{:S(2)}) copy-start(bf16[256,32]{0,1:T(8,128)(2,1)} %get-tuple-element.51) | copy-start | bytes 49156
  200.7 5.6 %copy-start.39 = (bf16[256,32]{0,1:T(8,128)(2,1)S(1)}, bf16[256,32]{0,1:T(8,128)(2,1)}, u32[]{:S(2)}) copy-start(bf16[256,32]{0,1:T(8,128)(2,1)} %get-tuple-element.52) | copy-start | bytes 49156
  200.7 6.4 %copy-start.20 = (bf16[3,8,2304]{2,1,0:T(8,128)(2,1)S(1)}, bf16[3,8,2304]{2,1,0:T(8,128)(2,1)}, u32[]{:S(2)}) copy-start(bf16[3,8,2304]{2,1,0:T(8,128)(2,1)} %param.21) | copy-start | bytes 331780
  206.2 123.9 %all-gather.2.cloned.1.call-start = ((), (), s32[]{:S(2)}) async-start(), calls=%async_computation.6 | async-start | bytes 5013504 | tf_op jit(solution)/shard_map/all_gather | solution.py:147
  207.1 173.1 %reduce-scatter.15.cloned.1.call-start = ((), (), s32[]{:S(2)}) async-start(), calls=%async_computation.9 | async-start | bytes 663552
  211.0 12.0 %copy-start.15 = (f32[256,768]{0,1:T(8,128)}, f32[256,768]{0,1:T(8,128)S(1)}, u32[]{:S(2)}) copy-start(f32[256,768]{0,1:T(8,128)S(1)} %fusion.85) | copy-start | bytes 2359300
  211.1 10.2 %copy-start.58 = (f32[4]{0:T(128)S(1)}, f32[4]{0:T(128)}, u32[]{:S(2)}) copy-start(f32[4]{0:T(128)} %param.38) | copy-start | bytes 52
  211.1 12.0 %copy-start.35 = (f32[256,32]{0,1:T(8,128)S(1)}, f32[256,32]{0,1:T(8,128)}, u32[]{:S(2)}) copy-start(f32[256,32]{0,1:T(8,128)} %get-tuple-element.49) | copy-start | bytes 98308
  211.1 12.0 %copy-start.36 = (f32[256,32]{0,1:T(8,128)S(1)}, f32[256,32]{0,1:T(8,128)}, u32[]{:S(2)}) copy-start(f32[256,32]{0,1:T(8,128)} %get-tuple-element.50) | copy-start | bytes 98308
  267.8 6.3 %copy-start.27 = (f32[8,2304]{1,0:T(8,128)}, f32[8,2304]{1,0:T(8,128)S(1)}, u32[]{:S(2)}) copy-start(f32[8,2304]{1,0:T(8,128)S(1)} %get-tuple-element.28) | copy-start | bytes 221188
  267.8 13.3 %copy-start.28 = (f32[8,2304]{1,0:T(8,128)}, f32[8,2304]{1,0:T(8,128)S(1)}, u32[]{:S(2)}) copy-start(f32[8,2304]{1,0:T(8,128)S(1)} %get-tuple-element.26) | copy-start | bytes 221188
  268.4 5.2 %copy-start.18 = (bf16[128,512]{1,0:T(8,128)(2,1)S(1)}, bf16[128,512]{1,0:T(8,128)(2,1)}, u32[]{:S(2)}) copy-start(bf16[128,512]{1,0:T(8,128)(2,1)} %param.35) | copy-start | bytes 393220
  273.6 18.5 %copy-start.29 = (f32[8,4,128]{2,1,0:T(4,128)}, f32[8,4,128]{2,1,0:T(4,128)S(1)}, u32[]{:S(2)}) copy-start(f32[8,4,128]{2,1,0:T(4,128)S(1)} %copy.254) | copy-start | bytes 49156
  274.0 18.1 %copy-start.30 = (f32[8,4,128]{2,1,0:T(4,128)}, f32[8,4,128]{2,1,0:T(4,128)S(1)}, u32[]{:S(2)}) copy-start(f32[8,4,128]{2,1,0:T(4,128)S(1)} %copy.252) | copy-start | bytes 49156
  274.1 6.3 %copy-start.21 = (bf16[8,2304]{1,0:T(8,128)(2,1)}, bf16[8,2304]{1,0:T(8,128)(2,1)S(1)}, u32[]{:S(2)}) copy-start(bf16[8,2304]{1,0:T(8,128)(2,1)S(1)} %multiply_convert_fusion.7) | copy-start | bytes 110596
  274.1 6.3 %copy-start.57 = (bf16[2304,4]{0,1:T(4,128)(2,1)S(1)}, bf16[2304,4]{0,1:T(4,128)(2,1)}, u32[]{:S(2)}) copy-start(bf16[2304,4]{0,1:T(4,128)(2,1)} %param.33) | copy-start | bytes 55300
  281.2 5.8 %copy-start.23 = (bf16[8,2304]{1,0:T(8,128)(2,1)}, bf16[8,2304]{1,0:T(8,128)(2,1)S(1)}, u32[]{:S(2)}) copy-start(bf16[8,2304]{1,0:T(8,128)(2,1)S(1)} %multiply_convert_fusion.5) | copy-start | bytes 110596
  286.1 6.1 %copy-start.25 = (f32[8,3,4,128]{3,0,2,1:T(8,128)}, f32[8,3,4,128]{3,0,2,1:T(8,128)S(1)}, u32[]{:S(2)}) copy-start(f32[8,3,4,128]{3,0,2,1:T(8,128)S(1)} %fusion.139) | copy-start | bytes 147460
  286.9 5.2 %copy-start.33 = (f32[8,4,128]{2,1,0:T(4,128)}, f32[8,4,128]{2,1,0:T(4,128)S(1)}, u32[]{:S(2)}) copy-start(f32[8,4,128]{2,1,0:T(4,128)S(1)} %copy.271) | copy-start | bytes 49156
  296.5 20.7 %copy-start.7 = (bf16[2304,128]{1,0:T(8,128)(2,1)S(1)}, bf16[2304,128]{1,0:T(8,128)(2,1)}, u32[]{:S(2)}) copy-start(bf16[2304,128]{1,0:T(8,128)(2,1)} %param.36) | copy-start | bytes 1769476
  296.5 20.8 %copy-start.5 = (bf16[512,2304]{1,0:T(8,128)(2,1)S(1)}, bf16[512,2304]{1,0:T(8,128)(2,1)}, u32[]{:S(2)}) copy-start(bf16[512,2304]{1,0:T(8,128)(2,1)} %param.39) | copy-start | bytes 7077892
  311.6 10.5 %copy-start.11 = (f32[8,4,16,8]{3,1,0,2:T(4,128)S(1)}, f32[8,4,16,8]{3,1,0,2:T(4,128)}, u32[]{:S(2)}) copy-start(f32[8,4,16,8]{3,1,0,2:T(4,128)} %get-tuple-element.5) | copy-start | bytes 49156
  311.6 12.5 %copy-start.22 = (bf16[8,2304]{1,0:T(8,128)(2,1)S(1)}, bf16[8,2304]{1,0:T(8,128)(2,1)}, u32[]{:S(2)}) copy-start(bf16[8,2304]{1,0:T(8,128)(2,1)} %copy-done.21) | copy-start | bytes 110596
  311.6 12.7 %copy-start.24 = (bf16[8,2304]{1,0:T(8,128)(2,1)S(1)}, bf16[8,2304]{1,0:T(8,128)(2,1)}, u32[]{:S(2)}) copy-start(bf16[8,2304]{1,0:T(8,128)(2,1)} %copy-done.23) | copy-start | bytes 110596
  314.9 9.8 %copy-start.17 = (bf16[128,512]{1,0:T(8,128)(2,1)S(1)}, bf16[128,512]{1,0:T(8,128)(2,1)}, u32[]{:S(2)}) copy-start(bf16[128,512]{1,0:T(8,128)(2,1)} %param.37) | copy-start | bytes 393220
  324.5 5.6 %copy-start.10 = (bf16[512,512]{1,0:T(8,128)(2,1)S(1)}, bf16[512,512]{1,0:T(8,128)(2,1)}, u32[]{:S(2)}) copy-start(bf16[512,512]{1,0:T(8,128)(2,1)} %param.29) | copy-start | bytes 1572868
  324.5 63.0 %reduce-scatter.13.cloned.1.call-start = ((), (), s32[]{:S(2)}) async-start(), calls=%async_computation.8 | async-start | bytes 663552
  328.4 91.5 %reduce-scatter.17.cloned.1.call-start = ((), (), s32[]{:S(2)}) async-start(), calls=%async_computation.10 | async-start | bytes 663552
  330.1 123.1 %reduce-scatter.11.cloned.1.call-start = ((), (), s32[]{:S(2)}) async-start(), calls=%async_computation.7 | async-start | bytes 1327104 | tf_op jit(solution)/shard_map/reduce_scatter | solution.py:180
  334.8 8.1 %copy-start.6 = (pred[256,4096]{0,1:T(8,128)(4,1)S(1)}, pred[256,4096]{0,1:T(8,128)(4,1)}, u32[]{:S(2)}) copy-start(pred[256,4096]{0,1:T(8,128)(4,1)} %iota_compare_fusion) | copy-start | bytes 3145732
  334.8 8.1 %copy-start.31 = (bf16[256,4,32]{0,2,1:T(8,128)(2,1)S(1)}, bf16[256,4,32]{0,2,1:T(8,128)(2,1)}, u32[]{:S(2)}) copy-start(bf16[256,4,32]{0,2,1:T(8,128)(2,1)} %get-tuple-element.21) | copy-start | bytes 196612
  334.8 8.1 %copy-start.32 = (bf16[256,4,32]{0,2,1:T(8,128)(2,1)S(1)}, bf16[256,4,32]{0,2,1:T(8,128)(2,1)}, u32[]{:S(2)}) copy-start(bf16[256,4,32]{0,2,1:T(8,128)(2,1)} %get-tuple-element.22) | copy-start | bytes 196612
  354.0 8.9 %copy-start.56 = (bf16[512,512]{1,0:T(8,128)(2,1)S(1)}, bf16[512,512]{1,0:T(8,128)(2,1)}, u32[]{:S(2)}) copy-start(bf16[512,512]{1,0:T(8,128)(2,1)} %param.30) | copy-start | bytes 1572868
  367.4 7.7 %copy-start.4 = (bf16[512,2304]{1,0:T(8,128)(2,1)S(1)}, bf16[512,2304]{1,0:T(8,128)(2,1)}, u32[]{:S(2)}) copy-start(bf16[512,2304]{1,0:T(8,128)(2,1)} %param.31) | copy-start | bytes 7077892
  375.2 79.7 %copy-start.1 = (bf16[2304,576]{0,1:T(8,128)(2,1)S(1)}, bf16[2304,576]{0,1:T(8,128)(2,1)}, u32[]{:S(2)}) copy-start(bf16[2304,576]{0,1:T(8,128)(2,1)} %param.28) | copy-start | bytes 7962628
  (19 other events, 64.6 us)
Sparse Core Ops, SparseCore 0:
  206.4 60.3 all-reduce.2
  324.6 30.4 reduce-scatter.14
  357.7 29.8 reduce-scatter.12
  389.9 29.9 reduce-scatter.16
  422.3 30.8 reduce-scatter.10
Sparse Core Ops, SparseCore 1:
  209.0 61.2 all-gather.1
where the time goes:
time: 470 us; the launch traced here: 462 us
  waiting for transfers between devices  195 us (41%)
  matrix products  107 us (23%)
  local copies, waits for them, and re-layouts  76.8 us (16%)
  other arithmetic  52.3 us (11%)
  between operations  16.4 us (3%)
  starting transfers between devices  14.7 us (3%)
    all_to_all x1, waiting for transfers between devices, shards(): lax.all_to_all(latent_pages, 'seq', split_axis=1, concat_axis=0, tiled=True)  84.3 us
    psum x1, waiting for transfers between devices, shards(): lax.psum(mla_part.astype(jnp.bfloat16), 'grp').astype(jnp.float32)  43 us
    unnamed x9, waiting for transfers between devices  37.9 us
    reduce_scatter x1, waiting for transfers between devices, shards(): lax.psum_scatter(prefill_part.astype(jnp.bfloat16), 'grp', scatter_dimens...  30.1 us
    unnamed x127, local copies, waits for them, and re-layouts  26.7 us
    concatenate x2, local copies, waits for them, and re-layouts, shards(): all_keys = jnp.concatenate([cache_rows, fresh_keys], axis=0)  22.5 us
    dot_general x3, matrix products, shards(): jnp.dot(kda_in, kda_inputs.reshape(model_width, -1), preferred_element_ty...  14.9 us
    dot_general x3, matrix products, shards(): jnp.einsum('rhc,chv->rhv', latent_out, value_expand.reshape(LAT, head_loc...  14.7 us
  transfers between devices with their start and end apart: 8, of which 5 were waited for; matrix products, arithmetic and copies ran while one was open for 50% of the time, Pallas kernels for 0%

commit v1 on v0

v1 whole, which is shorter than its diff:
```python
import functools

import jax
import jax.numpy as jnp
from jax import lax
from jax.experimental import pallas as pl
from jax.experimental.pallas import tpu as pltpu
from jax.sharding import PartitionSpec as P

LAT = 512
ROPE = 64
NOPE = 128
VH = 128
DK = 128
DV = 128
PAGE = 64
MAXP = 12
WIDE = LAT + ROPE
SENT = LAT + 128

epsilon = 1e-06
masked_score = -1e30
scale = (NOPE + ROPE) ** (-0.5)
log2e = 1.4426950408889634

f32 = jnp.float32
bf16 = jnp.bfloat16
MIB = 1024 * 1024


def params(mib):
    return pltpu.CompilerParams(vmem_limit_bytes=mib * MIB)


def dot_nt(a, b):
    return lax.dot_general(a, b, (((1,), (1,)), ((), ())), preferred_element_type=f32)


def dot_nn(a, b):
    return lax.dot_general(a, b, (((1,), (0,)), ((), ())), preferred_element_type=f32)


def norm_rows(values):
    return values * lax.rsqrt(jnp.mean(values * values, axis=-1, keepdims=True) + epsilon)


def unit_rows(values):
    return values * lax.rsqrt(jnp.sum(values * values, axis=-1, keepdims=True) + epsilon)


def turn(values, cos, sin):
    half = ROPE // 2
    swapped = jnp.concatenate([values[:, half:], values[:, :half]], axis=-1)
    return values * cos + swapped * sin


def rope_tables(position):
    half = ROPE // 2
    frequency = jnp.exp(-jnp.log(10000.0) * jnp.arange(half, dtype=f32) / half)
    angles = position.astype(f32)[:, None] * frequency
    cos, sin = jnp.cos(angles), jnp.sin(angles)
    return jnp.concatenate([cos, cos], axis=-1), jnp.concatenate([-sin, sin], axis=-1)


def latent_kernel(x_ref, dec_ref, proj_ref, cos_ref, sin_ref, normed_ref, lat_ref, fresh_ref):
    rows = x_ref.shape[0]
    normed = jnp.concatenate(
        [norm_rows(x_ref[...].astype(f32)), norm_rows(dec_ref[...].astype(f32))], axis=0
    ).astype(bf16)
    normed_ref[...] = normed
    projected = dot_nt(normed, proj_ref[...])
    latent = jnp.concatenate(
        [norm_rows(projected[:, :LAT]), turn(projected[:, LAT:], cos_ref[...], sin_ref[...])],
        axis=-1,
    )
    lat_ref[...] = latent[:rows].astype(bf16)
    fresh = latent[rows:]
    extra = jnp.zeros((fresh_ref.shape[0] - fresh.shape[0], WIDE), f32)
    fresh_ref[...] = jnp.concatenate([fresh, extra], axis=0).astype(bf16)


def make_latents(x, dec, proj_t, cos, sin):
    rows, width = x.shape
    total = rows + dec.shape[0]
    return pl.pallas_call(
        latent_kernel,
        out_shape=(
            jax.ShapeDtypeStruct((total, width), bf16),
            jax.ShapeDtypeStruct((rows, WIDE), bf16),
            jax.ShapeDtypeStruct((32, WIDE), bf16),
        ),
        compiler_params=params(40),
    )(x, dec, proj_t, cos, sin)


def query_kernel(heads, rows, normed_ref, proj_ref, cos_ref, sin_ref, expand_ref, qp_ref, qd_ref, acc):
    step = pl.program_id(0)

    @pl.when(step == 0)
    def _():
        acc[...] = jnp.zeros_like(acc)

    acc[...] += dot_nn(normed_ref[...], proj_ref[...])

    @pl.when(step == pl.num_programs(0) - 1)
    def _():
        cos, sin = cos_ref[...], sin_ref[...]
        decode = []
        for head in range(heads):
            at = head * (NOPE + ROPE)
            nope = acc[:, at : at + NOPE]
            turned = turn(acc[:, at + NOPE : at + NOPE + ROPE], cos, sin)
            qp_ref[head] = jnp.concatenate([nope[:rows], turned[:rows]], axis=-1).astype(bf16)
            absorbed = dot_nt(
                nope[rows:].astype(bf16), expand_ref[:, head * NOPE : (head + 1) * NOPE]
            )
            decode.append(jnp.concatenate([absorbed, turned[rows:]], axis=-1))
        qd_ref[...] = jnp.concatenate(decode, axis=0).astype(bf16)


def make_queries(normed, rows, query_proj, cos, sin, key_expand):
    total, width = normed.shape
    heads = key_expand.shape[1] // NOPE
    parts = 3
    depth = width // parts
    columns = query_proj.shape[1]
    whole = lambda shape: pl.BlockSpec(shape, lambda i: (0,) * len(shape))
    return pl.pallas_call(
        functools.partial(query_kernel, heads, rows),
        grid=(parts,),
        in_specs=[
            pl.BlockSpec((total, depth), lambda i: (0, i)),
            pl.BlockSpec((depth, columns), lambda i: (i, 0)),
            whole(cos.shape),
            whole(sin.shape),
            whole(key_expand.shape),
        ],
        out_specs=(
            whole((heads, rows, NOPE + ROPE)),
            whole((heads * (total - rows), WIDE)),
        ),
        out_shape=(
            jax.ShapeDtypeStruct((heads, rows, NOPE + ROPE), bf16),
            jax.ShapeDtypeStruct((heads * (total - rows), WIDE), bf16),
        ),
        scratch_shapes=[pltpu.VMEM((total, columns), f32)],
        compiler_params=params(40),
    )(normed, query_proj, cos, sin, key_expand)


def flash_kernel(
    heads,
    block,
    place_ref,
    q_ref,
    lat_ref,
    ke_ref,
    vet_ref,
    out_ref,
    sum_ref,
    peak,
    total,
    acc,
):
    step = pl.program_id(0)
    rows = q_ref.shape[1]
    first = place_ref[0]

    @pl.when(step == 0)
    def _():
        peak[...] = jnp.full_like(peak, masked_score)
        total[...] = jnp.zeros_like(total)
        acc[...] = jnp.zeros_like(acc)

    def work(masked):
        lat = lat_ref[...]
        keys = dot_nn(lat[:, :LAT], ke_ref[...]).astype(bf16)
        values = dot_nt(vet_ref[...], lat[:, :LAT]).astype(bf16)
        if masked:
            key_pos = step * block + lax.broadcasted_iota(jnp.int32, (block, rows), 0)
            live = key_pos <= first + lax.broadcasted_iota(jnp.int32, (block, rows), 1)
        for head in range(heads):
            whole_keys = jnp.concatenate(
                [keys[:, head * NOPE : (head + 1) * NOPE], lat[:, LAT:]], axis=-1
            )
            scores = dot_nt(whole_keys, q_ref[head]) * (scale * log2e)
            if masked:
                scores = jnp.where(live, scores, masked_score)
            old = peak[head]
            new = jnp.maximum(old, jnp.max(scores, axis=0, keepdims=True))
            fade = jnp.exp2(old - new)
            weights = jnp.exp2(scores - new)
            peak[head] = new
            total[head] = total[head] * fade + jnp.sum(weights, axis=0, keepdims=True)
            acc[head] = acc[head] * fade + dot_nn(
                values[head * VH : (head + 1) * VH], weights.astype(bf16)
            )

    @pl.when((step + 1) * block <= first + 1)
    def _():
        work(False)

    @pl.when(((step + 1) * block > first + 1) & (step * block < first + rows))
    def _():
        work(True)

    @pl.when(step == pl.num_programs(0) - 1)
    def _():
        mixed = jnp.concatenate([(acc[h] / total[h]).T for h in range(heads)], axis=-1)
        summed = dot_nn(mixed.astype(bf16), out_ref[...])
        sum_ref[...] = summed.T.astype(bf16)


def prefill_attend(place, q, lat_all, key_expand, value_expand_t, mla_output):
    heads, rows, _ = q.shape
    keys = lat_all.shape[0]
    block = min(512, keys)
    width = mla_output.shape[1]
    whole = lambda shape: pl.BlockSpec(shape, lambda i, s: (0,) * len(shape))
    return pl.pallas_call(
        functools.partial(flash_kernel, heads, block),
        grid_spec=pltpu.PrefetchScalarGridSpec(
            num_scalar_prefetch=1,
            grid=(keys // block,),
            in_specs=[
                whole(q.shape),
                pl.BlockSpec((block, WIDE), lambda i, s: (i, 0)),
                whole(key_expand.shape),
                whole(value_expand_t.shape),
                whole(mla_output.shape),
            ],
            out_specs=whole((width, rows)),
            scratch_shapes=[
                pltpu.VMEM((heads, 1, rows), f32),
                pltpu.VMEM((heads, 1, rows), f32),
                pltpu.VMEM((heads, VH, rows), f32),
            ],
        ),
        out_shape=jax.ShapeDtypeStruct((width, rows), bf16),
        compiler_params=params(56),
    )(place, q, lat_all, key_expand, value_expand_t, mla_output)


def pages_kernel(group, requests, first_ref, q_ref, keys_ref, fresh_ref, owner_ref, sent_ref):
    rows = q_ref.shape[0]
    q = q_ref[...]
    keys = keys_ref[...]
    fresh = fresh_ref[...]
    within = lax.rem(lax.broadcasted_iota(jnp.int32, (rows, 1), 0), group)
    request = lax.rem(within, requests)
    step = within // requests
    live_old = owner_ref[...] == request
    column = lax.broadcasted_iota(jnp.int32, (1, fresh.shape[0]), 1)
    fresh_request = lax.rem(column, requests)
    fresh_step = column // requests + first_ref[0] * group
    live_new = (fresh_request == request) & (fresh_step <= step)
    old = jnp.where(live_old, dot_nt(q, keys) * scale, masked_score)
    new = jnp.where(live_new, dot_nt(q, fresh) * scale, masked_score)
    highest = jnp.maximum(
        jnp.max(old, axis=-1, keepdims=True), jnp.max(new, axis=-1, keepdims=True)
    )
    w_old = jnp.where(live_old, jnp.exp(old - highest), 0.0)
    w_new = jnp.where(live_new, jnp.exp(new - highest), 0.0)
    total = jnp.sum(w_old, axis=-1, keepdims=True) + jnp.sum(w_new, axis=-1, keepdims=True)
    some = total > 0.0
    safe = jnp.where(some, total, 1.0)
    mixed = dot_nn(w_old.astype(bf16), keys[:, :LAT]) + dot_nn(w_new.astype(bf16), fresh[:, :LAT])
    mixed = mixed / safe
    level = jnp.where(some, highest + jnp.log(safe), masked_score)
    high = level.astype(bf16).astype(f32)
    middle = (level - high).astype(bf16).astype(f32)
    low = level - high - middle
    lane = lax.broadcasted_iota(jnp.int32, (rows, SENT - LAT), 1)
    tail = jnp.where(lane == 0, high, jnp.where(lane == 1, middle, jnp.where(lane == 2, low, 0.0)))
    sent_ref[...] = jnp.concatenate([mixed, tail], axis=-1).astype(bf16)


def pages_attend(first, q_all, keys, fresh, owner, group, requests):
    rows = q_all.shape[0]
    parts = 4
    block = rows // parts
    whole = lambda shape: pl.BlockSpec(shape, lambda i, s: (0,) * len(shape))
    return pl.pallas_call(
        functools.partial(pages_kernel, group, requests),
        grid_spec=pltpu.PrefetchScalarGridSpec(
            num_scalar_prefetch=1,
            grid=(parts,),
            in_specs=[
                pl.BlockSpec((block, WIDE), lambda i, s: (i, 0)),
                whole(keys.shape),
                whole(fresh.shape),
                whole(owner.shape),
            ],
            out_specs=pl.BlockSpec((block, SENT), lambda i, s: (i, 0)),
        ),
        out_shape=jax.ShapeDtypeStruct((rows, SENT), bf16),
        compiler_params=params(40),
    )(first, q_all, keys, fresh, owner)


def combine_kernel(heads, parts_ref, ve_ref, out_ref, sum_ref):
    tails = parts_ref[:, :, LAT:].astype(f32)
    lane = lax.broadcasted_iota(jnp.int32, tails.shape, 2)
    level = jnp.sum(jnp.where(lane < 3, tails, 0.0), axis=-1, keepdims=True)
    weights = jnp.exp(level - jnp.max(level, axis=0, keepdims=True))
    total = jnp.sum(weights, axis=0)
    mixed = jnp.sum(parts_ref[:, :, :LAT].astype(f32) * weights, axis=0) / total
    count = mixed.shape[0] // heads
    head_values = [
        dot_nn(
            mixed[h * count : (h + 1) * count].astype(bf16), ve_ref[:, h * VH : (h + 1) * VH]
        )
        for h in range(heads)
    ]
    joined = jnp.concatenate(head_values, axis=-1).astype(bf16)
    sum_ref[...] = dot_nn(joined, out_ref[...]).astype(bf16)


def combine(parts, value_expand, mla_output):
    heads = value_expand.shape[1] // VH
    return pl.pallas_call(
        functools.partial(combine_kernel, heads),
        out_shape=jax.ShapeDtypeStruct((parts.shape[1] // heads, mla_output.shape[1]), bf16),
        compiler_params=params(40),
    )(parts, value_expand, mla_output)


def kda_kernel(
    heads,
    requests,
    parts_ref,
    dec_ref,
    inputs_ref,
    beta_ref,
    decay_down_ref,
    decay_up_ref,
    gate_down_ref,
    gate_up_ref,
    rate_ref,
    states_ref,
    output_ref,
    hidden_ref,
    sum_ref,
    kin,
    projected,
):
    part = pl.program_id(0)
    shares, rows, share = hidden_ref.shape

    @pl.when(part == 0)
    def _():
        hidden = dec_ref[...].astype(f32) + jnp.sum(parts_ref[...].astype(f32), axis=0)
        for g in range(shares):
            hidden_ref[g] = hidden[:, g * share : (g + 1) * share]
        kin[...] = norm_rows(hidden).astype(bf16)

    projected[part] = dot_nn(kin[...], inputs_ref[0])

    @pl.when(part == pl.num_programs(0) - 1)
    def _():
        read_in = kin[...]
        beta = jax.nn.sigmoid(dot_nt(read_in, beta_ref[...]))
        decay_low = dot_nn(read_in, decay_down_ref[...]).astype(bf16)
        decays = jnp.exp(
            -rate_ref[...] * jax.nn.softplus(dot_nn(decay_low, decay_up_ref[...]))
        )
        gate_low = dot_nn(read_in, gate_down_ref[...]).astype(bf16)
        gates = jax.nn.sigmoid(dot_nn(gate_low, gate_up_ref[...]))
        steps = rows // requests
        at = lambda values, t: values[t * requests : (t + 1) * requests]
        along = lambda a, b: jnp.sum(a * b, axis=-1, keepdims=True)
        blended = []
        for head in range(heads):
            lanes = slice(head * DK, (head + 1) * DK)
            q = unit_rows(projected[0, :, lanes]) * DK ** (-0.5)
            k = unit_rows(projected[1, :, lanes])
            v = projected[2, :, lanes]
            a = decays[:, lanes]
            b = beta[:, head : head + 1]
            vectors = []
            held = None
            for t in range(steps):
                held = at(a, t) if held is None else held * at(a, t)
                vectors += [held * at(k, t), held * at(q, t)]
            vectors = jnp.concatenate(vectors, axis=0)
            high = vectors.astype(bf16)
            both = jnp.concatenate([high.astype(f32), vectors - high.astype(f32)], axis=0)
            owner = lax.rem(lax.broadcasted_iota(jnp.int32, (both.shape[0], 1), 0), requests)
            spread = jnp.concatenate(
                [jnp.where(owner == r, both, 0.0) for r in range(requests)], axis=-1
            ).astype(bf16)
            held_states = jnp.concatenate(
                [
                    states_ref[:, r, head].astype(f32).reshape(DV, DK)
                    for r in range(requests)
                ],
                axis=-1,
            ).astype(bf16)
            met = dot_nt(spread, held_states)
            met = met[: vectors.shape[0]] + met[vectors.shape[0] :]
            carried = []
            reads = []
            for t in range(steps):
                seen = at(met, 2 * t)
                read = at(met, 2 * t + 1)
                carried = [(u, w * at(a, t)) for u, w in carried]
                for u, w in carried:
                    seen = seen + u * along(w, at(k, t))
                u = at(b, t) * (at(v, t) - seen)
                carried.append((u, at(k, t)))
                for u, w in carried:
                    read = read + u * along(w, at(q, t))
                reads.append(read)
            read = jnp.concatenate(reads, axis=0)
            blended.append(norm_rows(read) * gates[:, lanes])
        mixed = jnp.concatenate(blended, axis=-1).astype(bf16)
        summed = dot_nn(mixed, output_ref[...])
        for g in range(shares):
            sum_ref[g] = summed[:, g * share : (g + 1) * share].astype(bf16)


def kda(parts, dec, inputs, beta_t, decay_down, decay_up, gate_down, gate_up, rate, states, output):
    shares, rows, width = parts.shape
    heads = beta_t.shape[0]
    requests = states.shape[1]
    columns = inputs.shape[2]
    whole = lambda a: pl.BlockSpec(a.shape, lambda i: (0,) * len(a.shape))
    share_spec = pl.BlockSpec((shares, rows, width // shares), lambda i: (0, 0, 0))
    return pl.pallas_call(
        functools.partial(kda_kernel, heads, requests),
        grid=(3,),
        in_specs=[
            whole(parts),
            whole(dec),
            pl.BlockSpec((1, width, columns), lambda i: (i, 0, 0)),
            whole(beta_t),
            whole(decay_down),
            whole(decay_up),
            whole(gate_down),
            whole(gate_up),
            whole(rate),
            whole(states),
            whole(output),
        ],
        out_specs=(share_spec, share_spec),
        out_shape=(
            jax.ShapeDtypeStruct((shares, rows, width // shares), f32),
            jax.ShapeDtypeStruct((shares, rows, width // shares), bf16),
        ),
        scratch_shapes=[pltpu.VMEM((rows, width), bf16), pltpu.VMEM((3, rows, columns), f32)],
        compiler_params=params(48),
    )(parts, dec, inputs, beta_t, decay_down, decay_up, gate_down, gate_up, rate, states, output)


def shards(
    x_group,
    decode_input,
    prompt_len,
    latent_pages,
    slot_target,
    page_counts,
    kda_state,
    query_proj,
    latent_proj,
    key_expand,
    value_expand,
    mla_output,
    kda_inputs,
    kda_beta,
    decay_down,
    decay_up,
    gate_down,
    gate_up,
    decay_log,
    kda_output,
):
    seq_index = lax.axis_index("seq")
    grp_index = lax.axis_index("grp")
    seq_size = lax.axis_size("seq")
    grp_size = lax.axis_size("grp")
    rows, width = x_group.shape
    steps, requests, _ = decode_input.shape
    decode_rows = steps * requests
    share = width // grp_size
    first_row = seq_index * rows
    place = jnp.concatenate(
        [first_row + jnp.arange(rows)]
        + [prompt_len + t for t in range(steps)]
    )
    cos, sin = rope_tables(place)
    dec = decode_input.reshape(decode_rows, width)

    normed, own_latent, fresh = make_latents(x_group, dec, latent_proj.T, cos, sin)
    lat_all = lax.all_gather(own_latent, "seq", axis=0, tiled=True)

    tokens = PAGE // grp_size
    own_tokens = lax.dynamic_slice_in_dim(latent_pages[0], grp_index * tokens, tokens, 2)
    arrived = lax.all_to_all(own_tokens, "seq", split_axis=0, concat_axis=0, tiled=True)
    slots = arrived.shape[1]
    page_keys = arrived.reshape(seq_size * slots * tokens, WIDE)
    target = slot_target[:, 0, :]
    owner = target // MAXP
    lengths = jnp.sum(
        jnp.where(owner[..., None] == jnp.arange(requests), prompt_len, 0), axis=-1
    )
    held = jnp.arange(slots)[None, :] < page_counts
    token_pos = (
        ((target % MAXP) * PAGE + grp_index * tokens)[..., None] + jnp.arange(tokens)
    )
    key_owner = jnp.where(
        held[..., None] & (token_pos < lengths[..., None]), owner[..., None], -1
    ).reshape(1, -1)

    states = lax.all_to_all(
        kda_state.astype(bf16), "seq", split_axis=0, concat_axis=0, tiled=True
    ).reshape((seq_size, requests) + kda_state.shape[1:])

    q_prefill, q_decode = make_queries(normed, rows, query_proj, cos, sin, key_expand)
    q_all = lax.all_gather(q_decode, "grp", axis=0, tiled=True)
    partial = pages_attend(
        grp_index.astype(jnp.int32).reshape(1), q_all, page_keys, fresh, key_owner, decode_rows, requests
    )
    partial = lax.all_to_all(
        partial.reshape(grp_size, -1, SENT), "grp", split_axis=0, concat_axis=0, tiled=True
    )
    mla_part = combine(partial, value_expand, mla_output)
    mla_parts = lax.all_gather(mla_part, "grp", axis=0, tiled=False)
    hidden, kda_part = kda(
        mla_parts,
        dec,
        kda_inputs.transpose(1, 0, 2),
        kda_beta.T,
        decay_down,
        decay_up,
        gate_down,
        gate_up,
        jnp.repeat(jnp.exp(decay_log), DK)[None, :],
        states,
        kda_output,
    )
    kda_parts = lax.all_to_all(kda_part, "grp", split_axis=0, concat_axis=0, tiled=True)
    hidden_share = lax.dynamic_index_in_dim(hidden, grp_index, 0, keepdims=False)
    decode_out = (hidden_share + jnp.sum(kda_parts.astype(f32), axis=0)).astype(bf16)

    prefill_part = prefill_attend(
        first_row.astype(jnp.int32).reshape(1),
        q_prefill,
        lat_all,
        key_expand,
        value_expand.T,
        mla_output,
    )
    prefill_parts = lax.all_to_all(
        prefill_part.reshape(grp_size, share, rows), "grp", split_axis=0, concat_axis=0, tiled=True
    )
    own_columns = lax.dynamic_slice_in_dim(x_group, grp_index * share, share, 1).T
    prefill_out = (
        own_columns.astype(f32) + jnp.sum(prefill_parts.astype(f32), axis=0)
    ).astype(bf16).T
    return (prefill_out, decode_out.reshape(steps, requests, share))


def solution(mesh):
    in_specs = (
        P("seq", None),
        P(None, "seq", None),
        P("seq"),
        P("seq", None, None, None, None),
        P(None, "seq", None),
        P(None, "seq"),
        P(None, "grp", "seq", None),
        P(None, "grp"),
        P(),
        P(None, "grp"),
        P(None, "grp"),
        P("grp", None),
        P(None, None, "grp"),
        P(None, "grp"),
        P(),
        P(None, "grp"),
        P(),
        P(None, "grp"),
        P("grp"),
        P("grp", None),
    )
    out_specs = (P("seq", "grp"), P(None, "seq", "grp"))
    return jax.shard_map(shards, mesh=mesh, in_specs=in_specs, out_specs=out_specs, check_vma=False)
```

time: 470 us -> 166 us (0.35)
  the two profiles are of different devices: /device:TPU:0 before, /device:TPU:112 now
where the time goes in v1:
time: 166 us; the launch traced here: 165 us
  Pallas kernels  43.4 us (26%)
  waiting for transfers between devices  27.7 us (17%)
  blocking collectives  27.5 us (17%)
  starting transfers between devices  26.1 us (16%)
  local copies, waits for them, and re-layouts  18.9 us (11%)
  between operations  14.2 us (9%)
  other arithmetic  7.35 us (4%)
    pallas_call x1, Pallas kernels, prefill_attend(): pl.pallas_call(functools.partial(flash_kernel, heads, block), grid_spec=p...  23.6 us
    all_to_all x1, waiting for transfers between devices, shards(): lax.all_to_all(prefill_part.reshape(grp_size, share, rows), 'grp', split_...  15.5 us
    unnamed x44, local copies, waits for them, and re-layouts  15.2 us
    all_gather x1, blocking collectives, shards(): q_all = lax.all_gather(q_decode, 'grp', axis=0, tiled=True)  13.9 us
    all_gather x1, blocking collectives, shards(): mla_parts = lax.all_gather(mla_part, 'grp', axis=0, tiled=False)  13.6 us
    all_to_all x1, waiting for transfers between devices, shards(): lax.all_to_all(partial.reshape(grp_size, -1, SENT), 'grp', split_axis=0,...  12.2 us
    pallas_call x1, Pallas kernels, kda(): pl.pallas_call(functools.partial(kda_kernel, heads, requests), grid=(3,),...  7.67 us
    all_to_all x1, starting transfers between devices, shards(): lax.all_to_all(kda_state.astype(bf16), 'seq', split_axis=0, concat_axis=0...  7.22 us
  transfers between devices with their start and end apart: 6, of which 2 were waited for; matrix products, arithmetic and copies ran while one was open for 6% of the time, Pallas kernels for 25%

profile of v1, /device:TPU:112, one launch (start us, length us, event | category | flops | bytes accessed | tf_op | source)
XLA Modules:
  0.0 165.1 jit_solution(3763398886279675725)
XLA Ops:
  7.2 0.0 all-gather.3.cloned.1.call-start
  7.2 0.7 broadcast_add_fusion.1
  7.9 0.7 add_convert_fusion
  8.6 0.6 fusion.3
  9.2 0.1 pad_maximum_fusion
  9.4 1.7 %copy-done.4 = bf16[2304,576]{0,1:T(8,128)(2,1)S(1)} copy-done((bf16[2304,576]{0,1:T(8,128)(2,1)S(1)}, bf16[2304,576]{0,1:T(8,128)(2,1)}, u32[]{:S(2)}) %copy-start.4) | copy-done | bytes 2654232
  11.1 1.3 copy-done.8
  12.4 0.9 copy-done.12
  13.3 2.6 %shard_map.206 = (bf16[280,2304]{1,0:T(8,128)(2,1)S(1)}, bf16[256,576]{1,0:T(8,128)(2,1)}, bf16[32,576]{1,0:T(8,128)(2,1)S(1)}) custom-call(bf16[256,2304]{1,0:T(8,128)(2,1)S(1)} %copy-done.8, bf16[24,2304]{1,0:T(8,128)(2,1)S(1)} %bitcast.60, bf16[576,2304]{1,0:T(8,128)(2,1)S(1)} %bitcast.59, f32[280,64]{1,0:T(8,128)S(1)} %get-tuple-element.23.cos_ref, ...), custom_call_target="tpu_custom_call" | custom-call | tf_op jit(solution)/shard_map/pallas_call | solution.py:85
  15.9 0.0 all-gather.3.cloned.1.call-update
  15.9 2.3 %dynamic-slice_bitcast_fusion = bf16[16,6,8,576]{3,2,1,0:T(8,128)(2,1)} fusion(bf16[1,16,6,64,576]{4,3,2,1,0:T(8,128)(2,1)} %param.23, s32[]{:T(128)S(6)} %select_n.49), kind=kLoop, calls=%fused_computation.1 | loop fusion | bytes 1769476 | tf_op jit(solution)/shard_map/dynamic_slice | solution.py:497
  18.2 6.9 %all-to-all-start.1 = ((bf16[16,6,8,576]{3,2,1,0:T(8,128)(2,1)}), bf16[16,6,8,576]{3,2,1,0:T(8,128)(2,1)S(1)}, u32[]{:S(2)}, u32[]{:S(2)}) async-start(bf16[16,6,8,576]{3,2,1,0:T(8,128)(2,1)} %dynamic-slice_bitcast_fusion), calls=%async_computation.1 | async-start | bytes 1966080 | tf_op jit(solution)/shard_map/all_to_all | solution.py:498
  25.2 0.1 copy.35
  25.3 0.1 copy.32
  25.3 0.4 select_reduce_fusion
  25.8 0.1 iota_compare_fusion.1
  25.8 0.1 fusion.2
  26.0 0.1 select_n.54.owner_ref
  26.1 2.1 %copy-done.3 = bf16[2304,768]{1,0:T(8,128)(2,1)S(1)} copy-done((bf16[2304,768]{1,0:T(8,128)(2,1)S(1)}, bf16[2304,768]{1,0:T(8,128)(2,1)}, u32[]{:S(2)}) %copy-start.3) | copy-done | bytes 3538968
  28.2 2.5 %shard_map.207 = (bf16[4,256,192]{2,1,0:T(8,128)(2,1)S(1)}, bf16[96,576]{1,0:T(8,128)(2,1)S(1)}) custom-call(bf16[280,2304]{1,0:T(8,128)(2,1)S(1)} %get-tuple-element.9.normed_ref, bf16[2304,768]{1,0:T(8,128)(2,1)S(1)} %copy-done.3, f32[280,64]{1,0:T(8,128)S(1)} %get-tuple-element.23.cos_ref, f32[280,64]{1,0:T(8,128)S(1)} %get-tuple-element.24.sin_ref, ...), custom_call_target="tpu_custom_call" | custom-call | tf_op jit(solution)/shard_map/pallas_call | solution.py:128
  30.7 0.8 copy-done.11
  31.5 13.9 %all_gather.13.q_ref = bf16[768,576]{1,0:T(8,128)(2,1)S(1)} all-gather(bf16[96,576]{1,0:T(8,128)(2,1)S(1)} %get-tuple-element.12), channel_id=1, replica_groups=mesh['seq'=16,'grp'=8] {'grp'}, dimensions={0}, use_global_device_ids=true | all-gather | bytes 995328 | tf_op jit(solution)/shard_map/all_gather | solution.py:519
  45.5 6.3 %shard_map.209 = bf16[768,640]{1,0:T(8,128)(2,1)} custom-call(s32[1]{0:T(128)} %bitcast.6.first_ref, bf16[768,576]{1,0:T(8,128)(2,1)S(1)} %all_gather.13.q_ref, bf16[768,576]{1,0:T(8,128)(2,1)S(1)} %bitcast.57, bf16[32,576]{1,0:T(8,128)(2,1)S(1)} %get-tuple-element.13.fresh_ref, s32[1,768]{1,0:T(1,128)S(1)} %select_n.54.owner_ref), custom_call_target="tpu_custom_call" | custom-call | tf_op jit(solution)/shard_map/pallas_call | solution.py:283
  51.7 3.8 %all-to-all-start.2 = ((bf16[8,96,640]{2,1,0:T(8,128)(2,1)}), bf16[8,96,640]{2,1,0:T(8,128)(2,1)S(1)}, u32[]{:S(2)}, u32[]{:S(2)}) async-start(bf16[8,96,640]{2,1,0:T(8,128)(2,1)} %bitcast.13), calls=%async_computation.2 | async-start | bytes 1966080 | tf_op jit(solution)/shard_map/all_to_all | solution.py:523
  55.6 3.1 %convert_element_type.32 = bf16[128,4,8,128]{3,2,1,0:T(8,128)(2,1)} convert(f32[128,4,8,128]{3,2,1,0:T(8,128)} %param.26) | non-fusion elementwise | flops 524288 | bytes 3145728 | tf_op jit(solution)/shard_map/convert_element_type | solution.py:515
  58.6 12.2 %all-to-all-done.2.parts_ref = bf16[8,96,640]{2,1,0:T(8,128)(2,1)S(1)} async-done(((bf16[8,96,640]{2,1,0:T(8,128)(2,1)}), bf16[8,96,640]{2,1,0:T(8,128)(2,1)S(1)}, u32[]{:S(2)}, u32[]{:S(2)}) %all-to-all-start.2) | async-done | bytes 983072 | tf_op jit(solution)/shard_map/all_to_all | solution.py:523
  70.8 0.9 copy-done.1
  71.8 7.2 %all-to-all-start.3 = ((bf16[128,4,8,128]{3,2,1,0:T(8,128)(2,1)}), bf16[128,4,8,128]{3,2,1,0:T(8,128)(2,1)S(1)}, u32[]{:S(2)}, u32[]{:S(2)}) async-start(bf16[128,4,8,128]{3,2,1,0:T(8,128)(2,1)} %convert_element_type.32), calls=%async_computation.3 | async-start | bytes 2097152 | tf_op jit(solution)/shard_map/all_to_all | solution.py:514
  79.0 1.2 copy-done.2
  80.2 1.0 copy-done.5
  81.3 0.8 shard_map.210
  82.1 13.6 %all-gather = bf16[192,2304]{1,0:T(8,128)(2,1)S(1)} all-gather(bf16[24,2304]{1,0:T(8,128)(2,1)S(1)} %shard_map.210), channel_id=2, replica_groups=mesh['seq'=16,'grp'=8] {'grp'}, dimensions={0}, use_global_device_ids=true | all-gather | bytes 995328 | tf_op jit(solution)/shard_map/all_gather | solution.py:527
  95.7 0.1 broadcast_in_dim.34
  95.8 1.1 copy-done.9
  96.8 1.1 copy-done.10
  97.9 0.9 copy-done.14
  98.8 0.9 copy-done.15
  99.7 7.7 %shard_map.211 = (f32[8,24,288]{2,1,0:T(8,128)S(1)}, bf16[8,24,288]{2,1,0:T(8,128)(2,1)}) custom-call(bf16[8,24,2304]{2,1,0:T(8,128)(2,1)S(1)} %bitcast.58, bf16[24,2304]{1,0:T(8,128)(2,1)S(1)} %bitcast.61, bf16[3,2304,512]{2,1,0:T(8,128)(2,1)} %bitcast.64, bf16[4,2304]{1,0:T(4,128)(2,1)S(1)} %bitcast.62, bf16[2304,128]{1,0:T(8,128)(2,1)S(1)} %copy-done.9, ...), custom_call_target="tpu_custom_call" | custom-call | tf_op jit(solution)/shard_map/pallas_call | solution.py:429
  107.4 3.6 %all-to-all-start.4 = ((bf16[8,24,288]{2,1,0:T(8,128)(2,1)}), bf16[8,24,288]{2,1,0:T(8,128)(2,1)S(1)}, u32[]{:S(2)}, u32[]{:S(2)}) async-start(bf16[8,24,288]{2,1,0:T(8,128)(2,1)} %get-tuple-element.15), calls=%async_computation.4 | async-start | bytes 294912 | tf_op jit(solution)/shard_map/all_to_all | solution.py:541
  110.9 1.0 copy.30
  112.0 23.6 %shard_map.208 = bf16[2304,256]{1,0:T(8,128)(2,1)} custom-call(s32[1]{0:T(128)} %bitcast.place_ref, bf16[4,256,192]{2,1,0:T(8,128)(2,1)} %copy-done.11, bf16[4096,576]{1,0:T(8,128)(2,1)} %all-gather.3.cloned.1.call-done.lat_ref, bf16[512,512]{1,0:T(8,128)(2,1)} %ke_ref.1, bf16[512,512]{1,0:T(8,128)(2,1)} %bitcast.66, bf16[512,2304]{1,0:T(8,128)(2,1)} %out_ref.3), custom_call_target="tpu_custom_call" | custom-call | tf_op jit(solution)/shard_map/pallas_call | solution.py:220
  135.5 4.5 %all-to-all-start = ((bf16[8,288,256]{2,1,0:T(8,128)(2,1)}), bf16[8,288,256]{2,1,0:T(8,128)(2,1)S(1)}, u32[]{:S(2)}, u32[]{:S(2)}) async-start(bf16[8,288,256]{2,1,0:T(8,128)(2,1)} %bitcast.65), calls=%async_computation | async-start | bytes 2359296 | tf_op jit(solution)/shard_map/all_to_all | solution.py:553
  140.1 1.1 constant_dynamic-slice_fusion
  141.1 0.1 copy.36
  141.3 0.6 fusion.4
  141.9 15.5 %all-to-all-done = bf16[8,288,256]{2,1,0:T(8,128)(2,1)S(1)} async-done(((bf16[8,288,256]{2,1,0:T(8,128)(2,1)}), bf16[8,288,256]{2,1,0:T(8,128)(2,1)S(1)}, u32[]{:S(2)}, u32[]{:S(2)}) %all-to-all-start) | async-done | bytes 1179680 | tf_op jit(solution)/shard_map/all_to_all | solution.py:553
  157.4 0.2 convert_reduce_fusion
  157.6 0.7 fusion
  (39 shorter events, 0.1 us)
Async XLA Ops:
  7.2 104.8 %all-gather.3.cloned.1.call-start = ((), (), s32[]{:S(2)}) async-start(), calls=%async_computation.5 | async-start | bytes 5570560 | tf_op jit(solution)/shard_map/all_gather | solution.py:494
  9.4 1.8 %copy-start.4 = (bf16[2304,576]{0,1:T(8,128)(2,1)S(1)}, bf16[2304,576]{0,1:T(8,128)(2,1)}, u32[]{:S(2)}) copy-start(bf16[2304,576]{0,1:T(8,128)(2,1)} %param.28) | copy-start | bytes 7962628
  11.1 1.3 copy-start.8
  12.4 0.9 copy-start.12
  15.9 9.3 %copy-start.17 = (s32[16,1,6]{0,1,2:T(1,128)S(1)}, s32[16,1,6]{0,1,2:T(1,128)}, u32[]{:S(2)}) copy-start(s32[16,1,6]{0,1,2:T(1,128)} %param.24) | copy-start | bytes 1156
  15.9 9.5 %copy-start.18 = (s32[8]{0:T(128)S(1)}, s32[8]{0:T(128)}, u32[]{:S(2)}) copy-start(s32[8]{0:T(128)} %param.22) | copy-start | bytes 100
  15.9 9.9 %copy-start.19 = (s32[16,1]{0,1:T(1,128)S(1)}, s32[16,1]{0,1:T(1,128)}, u32[]{:S(2)}) copy-start(s32[16,1]{0,1:T(1,128)} %param.25) | copy-start | bytes 196
  15.9 10.2 %copy-start.7 = (bf16[512,512]{1,0:T(8,128)(2,1)S(1)}, bf16[512,512]{1,0:T(8,128)(2,1)}, u32[]{:S(2)}) copy-start(bf16[512,512]{1,0:T(8,128)(2,1)} %ke_ref.1) | copy-start | bytes 1572868
  18.2 27.2 %all-to-all-start.1 = ((bf16[16,6,8,576]{3,2,1,0:T(8,128)(2,1)}), bf16[16,6,8,576]{3,2,1,0:T(8,128)(2,1)S(1)}, u32[]{:S(2)}, u32[]{:S(2)}) async-start(bf16[16,6,8,576]{3,2,1,0:T(8,128)(2,1)} %dynamic-slice_bitcast_fusion), calls=%async_computation.1 | async-start | bytes 1966080 | tf_op jit(solution)/shard_map/all_to_all | solution.py:498
  26.1 2.2 %copy-start.3 = (bf16[2304,768]{1,0:T(8,128)(2,1)S(1)}, bf16[2304,768]{1,0:T(8,128)(2,1)}, u32[]{:S(2)}) copy-start(bf16[2304,768]{1,0:T(8,128)(2,1)} %proj_ref.1) | copy-start | bytes 10616836
  30.7 0.8 copy-start.11
  51.7 19.1 %all-to-all-start.2 = ((bf16[8,96,640]{2,1,0:T(8,128)(2,1)}), bf16[8,96,640]{2,1,0:T(8,128)(2,1)S(1)}, u32[]{:S(2)}, u32[]{:S(2)}) async-start(bf16[8,96,640]{2,1,0:T(8,128)(2,1)} %bitcast.13), calls=%async_computation.2 | async-start | bytes 1966080 | tf_op jit(solution)/shard_map/all_to_all | solution.py:523
  55.5 23.4 %copy-start.20 = (f32[4]{0:T(128)S(1)}, f32[4]{0:T(128)}, u32[]{:S(2)}) copy-start(f32[4]{0:T(128)} %param.38) | copy-start | bytes 52
  55.5 23.5 %copy-start = (bf16[512,2304]{1,0:T(8,128)(2,1)S(1)}, bf16[512,2304]{1,0:T(8,128)(2,1)}, u32[]{:S(2)}) copy-start(bf16[512,2304]{1,0:T(8,128)(2,1)} %out_ref.3) | copy-start | bytes 7077892
  70.8 0.9 copy-start.1
  71.8 23.9 %all-to-all-start.3 = ((bf16[128,4,8,128]{3,2,1,0:T(8,128)(2,1)}), bf16[128,4,8,128]{3,2,1,0:T(8,128)(2,1)S(1)}, u32[]{:S(2)}, u32[]{:S(2)}) async-start(bf16[128,4,8,128]{3,2,1,0:T(8,128)(2,1)} %convert_element_type.32), calls=%async_computation.3 | async-start | bytes 2097152 | tf_op jit(solution)/shard_map/all_to_all | solution.py:514
  79.0 1.2 copy-start.2
  80.2 1.0 copy-start.5
  81.3 14.5 %copy-start.13 = (bf16[3,8,2304]{2,1,0:T(8,128)(2,1)S(1)}, bf16[3,8,2304]{2,1,0:T(8,128)(2,1)}, u32[]{:S(2)}) copy-start(bf16[3,8,2304]{2,1,0:T(8,128)(2,1)} %param.21) | copy-start | bytes 331780
  81.3 14.5 %copy-start.16 = (bf16[2304,4]{0,1:T(4,128)(2,1)S(1)}, bf16[2304,4]{0,1:T(4,128)(2,1)}, u32[]{:S(2)}) copy-start(bf16[2304,4]{0,1:T(4,128)(2,1)} %param.33) | copy-start | bytes 55300
  95.7 1.1 copy-start.9
  96.8 1.1 copy-start.10
  97.9 0.9 copy-start.14
  98.8 0.9 copy-start.15
  99.7 11.2 %copy-start.6 = (bf16[512,512]{1,0:T(8,128)(2,1)S(1)}, bf16[512,512]{1,0:T(8,128)(2,1)}, u32[]{:S(2)}) copy-start(bf16[512,512]{1,0:T(8,128)(2,1)} %ve_ref.1) | copy-start | bytes 1572868
  107.4 28.2 %all-to-all-start.4 = ((bf16[8,24,288]{2,1,0:T(8,128)(2,1)}), bf16[8,24,288]{2,1,0:T(8,128)(2,1)S(1)}, u32[]{:S(2)}, u32[]{:S(2)}) async-start(bf16[8,24,288]{2,1,0:T(8,128)(2,1)} %get-tuple-element.15), calls=%async_computation.4 | async-start | bytes 294912 | tf_op jit(solution)/shard_map/all_to_all | solution.py:541
  135.5 21.9 %all-to-all-start = ((bf16[8,288,256]{2,1,0:T(8,128)(2,1)}), bf16[8,288,256]{2,1,0:T(8,128)(2,1)S(1)}, u32[]{:S(2)}, u32[]{:S(2)}) async-start(bf16[8,288,256]{2,1,0:T(8,128)(2,1)} %bitcast.65), calls=%async_computation | async-start | bytes 2359296 | tf_op jit(solution)/shard_map/all_to_all | solution.py:553
Sparse Core Ops, SparseCore 0:
  16.0 62.7 all-gather.2

commit v2 on v1

v2 whole, which is shorter than its diff:
```python
import functools

import jax
import jax.numpy as jnp
import numpy as np
from jax import lax
from jax.experimental import pallas as pl
from jax.experimental.pallas import tpu as pltpu
from jax.sharding import PartitionSpec as P

LAT = 512
ROPE = 64
NOPE = 128
VH = 128
DK = 128
DV = 128
PAGE = 64
MAXP = 12
WIDE = LAT + ROPE
SENT = LAT + 128

epsilon = 1e-06
masked_score = -1e30
scale = (NOPE + ROPE) ** (-0.5)
log2e = 1.4426950408889634

f32 = jnp.float32
bf16 = jnp.bfloat16
MIB = 1024 * 1024


def params(mib):
    return pltpu.CompilerParams(vmem_limit_bytes=mib * MIB)


def dot_nt(a, b):
    return lax.dot_general(a, b, (((1,), (1,)), ((), ())), preferred_element_type=f32)


def dot_nn(a, b):
    return lax.dot_general(a, b, (((1,), (0,)), ((), ())), preferred_element_type=f32)


def norm_rows(values):
    return values * lax.rsqrt(jnp.mean(values * values, axis=-1, keepdims=True) + epsilon)


def unit_rows(values):
    return values * lax.rsqrt(jnp.sum(values * values, axis=-1, keepdims=True) + epsilon)


def turn(values, cos, sin):
    half = ROPE // 2
    swapped = jnp.concatenate([values[:, half:], values[:, :half]], axis=-1)
    return values * cos + swapped * sin


def rope_tables(positions):
    half = ROPE // 2
    frequency = np.exp(-np.log(10000.0) * np.arange(half) / half)
    angles = np.asarray(positions, np.float64)[:, None] * frequency
    cos, sin = np.cos(angles), np.sin(angles)
    both = np.stack([np.concatenate([cos, cos], -1), np.concatenate([-sin, sin], -1)])
    return jnp.asarray(both, f32)


def front_kernel(
    place_ref,
    lengths_ref,
    fine_ref,
    coarse_ref,
    x_hbm,
    dec_hbm,
    lat_proj_hbm,
    query_proj_hbm,
    expand_hbm,
    pages_hbm,
    lat_ref,
    fresh_ref,
    qp_ref,
    qd_ref,
    own_hbm,
    x_ref,
    dec_ref,
    lat_proj_ref,
    query_proj_ref,
    expand_ref,
    normed,
    turns,
    sems,
):
    seq, grp = place_ref[0], place_ref[1]
    rows, width = x_ref.shape
    count = dec_ref.shape[0]
    half_rows = lat_ref.shape[0]
    core = lax.rem(grp, 2)
    _, slots, tokens, _ = own_hbm.shape
    heads = qp_ref.shape[0]
    requests = lengths_ref.shape[0]
    chunks = 3
    depth = width // chunks
    loads = [
        pltpu.make_async_copy(x_hbm, x_ref, sems.at[0]),
        pltpu.make_async_copy(dec_hbm, dec_ref, sems.at[1]),
        pltpu.make_async_copy(lat_proj_hbm, lat_proj_ref, sems.at[2]),
        pltpu.make_async_copy(expand_hbm, expand_ref, sems.at[3]),
    ]
    loads += [
        pltpu.make_async_copy(
            query_proj_hbm.at[pl.ds(i * depth, depth)],
            query_proj_ref.at[pl.ds(i * depth, depth)],
            sems.at[4 + i],
        )
        for i in range(chunks)
    ]
    pages = pltpu.make_async_copy(
        pages_hbm.at[:, pl.ds(core * slots, slots), pl.ds((grp // 2) * tokens, tokens), :],
        own_hbm,
        sems.at[4 + chunks],
    )
    for load in loads:
        load.start()
    pages.start()
    for r in range(requests):
        for t in range(count // requests):
            at = rows + t * requests + r
            row = lengths_ref[r] + t
            turns[0, at : at + 1] = fine_ref[0, pl.ds(row, 1)]
            turns[1, at : at + 1] = fine_ref[1, pl.ds(row, 1)]
    turns[:, rows + count :] = jnp.zeros((2, turns.shape[1] - rows - count, ROPE), f32)
    base_cos, base_sin = coarse_ref[0, pl.ds(seq, 1)], coarse_ref[1, pl.ds(seq, 1)]
    fine_cos, fine_sin = fine_ref[0, :rows], fine_ref[1, :rows]
    turns[0, :rows] = base_cos * fine_cos - base_sin * fine_sin
    turns[1, :rows] = base_sin * fine_cos + base_cos * fine_sin
    loads[0].wait()
    normed[:rows] = norm_rows(x_ref[...].astype(f32)).astype(bf16)
    loads[1].wait()
    tail = normed.shape[0] - rows - count
    normed[rows:] = jnp.concatenate(
        [norm_rows(dec_ref[...].astype(f32)), jnp.zeros((tail, width), f32)], axis=0
    ).astype(bf16)
    loads[2].wait()

    def latents(inputs, cos, sin):
        projected = dot_nt(inputs, lat_proj_ref[...])
        return jnp.concatenate(
            [norm_rows(projected[:, :LAT]), turn(projected[:, LAT:], cos, sin)], axis=-1
        ).astype(bf16)

    own = pl.ds(pl.multiple_of(core * half_rows, half_rows), half_rows)
    lat_ref[...] = latents(normed[own], turns[0, own], turns[1, own])
    fresh_ref[...] = latents(normed[rows:], turns[0, rows:], turns[1, rows:])
    total = None
    for i in range(chunks):
        loads[4 + i].wait()
        lanes = slice(i * depth, (i + 1) * depth)
        term = dot_nn(normed[:, lanes], query_proj_ref[lanes])
        total = term if total is None else total + term
    loads[3].wait()
    fold = scale * log2e
    decode = []
    cos, sin = turns[0], turns[1]
    for head in range(heads):
        at = head * (NOPE + ROPE)
        nope = total[:, at : at + NOPE]
        turned = turn(total[:, at + NOPE : at + NOPE + ROPE], cos, sin)
        qp_ref[head] = (
            jnp.concatenate([nope[:rows], turned[:rows]], axis=-1) * fold
        ).astype(bf16)
        absorbed = dot_nt(
            nope[rows:].astype(bf16), expand_ref[:, head * NOPE : (head + 1) * NOPE]
        )
        decode.append(jnp.concatenate([absorbed, turned[rows:]], axis=-1)[:count])
    qd_ref[...] = (jnp.concatenate(decode, axis=0) * fold).astype(bf16)
    pages.wait()


def front(place, lengths, x, dec, lat_proj_t, query_proj, key_expand, pages, seq_size, grp_size):
    rows, width = x.shape
    count = dec.shape[0]
    heads = key_expand.shape[1] // NOPE
    padded = count + 8
    requests = lengths.shape[0]
    fine = rope_tables(range(max(rows, MAXP * PAGE + count // requests)))
    coarse = rope_tables([rows * i for i in range(seq_size)])
    slots, tokens = pages.shape[1] // 2, PAGE // (grp_size // 2)
    smem = pl.BlockSpec(memory_space=pltpu.SMEM)
    vmem = pl.BlockSpec(memory_space=pltpu.VMEM)
    hbm = pl.BlockSpec(memory_space=pltpu.HBM)
    return pl.pallas_call(
        front_kernel,
        in_specs=[smem, smem, vmem, vmem] + [hbm] * 6,
        out_specs=(vmem, vmem, vmem, vmem, hbm),
        out_shape=(
            jax.ShapeDtypeStruct((rows // 2, WIDE), bf16),
            jax.ShapeDtypeStruct((padded, WIDE), bf16),
            jax.ShapeDtypeStruct((heads, rows, NOPE + ROPE), bf16),
            jax.ShapeDtypeStruct((heads * count, WIDE), bf16),
            jax.ShapeDtypeStruct((pages.shape[0], slots, tokens, WIDE), bf16),
        ),
        scratch_shapes=[
            pltpu.VMEM(x.shape, bf16),
            pltpu.VMEM(dec.shape, bf16),
            pltpu.VMEM(lat_proj_t.shape, bf16),
            pltpu.VMEM(query_proj.shape, bf16),
            pltpu.VMEM(key_expand.shape, bf16),
            pltpu.VMEM((rows + padded, width), bf16),
            pltpu.VMEM((2, rows + padded, ROPE), f32),
            pltpu.SemaphoreType.DMA((8,)),
        ],
        compiler_params=params(40),
    )(place, lengths, fine, coarse, x, dec, lat_proj_t, query_proj, key_expand, pages)


def pack_shares(summed, sum_ref):
    shares = sum_ref.shape[0]
    rows, width = summed.shape
    share = width // shares
    for g in range(shares):
        part = summed[:, g * share : (g + 1) * share]
        sum_ref[g, :rows] = part[:, :128].astype(bf16)
        sum_ref[g, rows : 2 * rows] = part[:, 128:256].astype(bf16)
        rest = part[:, 256:]
        count = 128 // rest.shape[1]
        piece = rows // count
        sum_ref[g, 2 * rows :] = jnp.concatenate(
            [rest[i * piece : (i + 1) * piece] for i in range(count)], axis=1
        ).astype(bf16)


def flash_kernel(
    heads, place_ref, q_ref, mine_ref, other_ref, ke_ref, vet_ref, out_hbm, sum_ref,
    peak, acc, out_ref, sem,
):
    step = pl.program_id(0)
    rows = q_ref.shape[1]
    half = rows // 2
    first, core = place_ref[0] * rows, lax.rem(place_ref[1], 2)
    side = mine_ref.shape[0]
    block = 2 * side
    load = pltpu.make_async_copy(out_hbm, out_ref, sem)

    @pl.when(step == 0)
    def _():
        load.start()
        peak[...] = jnp.full_like(peak, masked_score)
        acc[...] = jnp.zeros_like(acc)

    def work(masked):
        lat = jnp.concatenate([mine_ref[...], other_ref[...]], axis=0)
        low, rope = lat[:, :LAT], lat[:, LAT:]
        ones = jnp.ones((16, block), bf16)
        keys = dot_nn(low, ke_ref[...]).astype(bf16)
        values = dot_nt(vet_ref[...], low).astype(bf16)
        scores = []
        for head in range(heads):
            whole_keys = jnp.concatenate(
                [keys[:, head * NOPE : (head + 1) * NOPE], rope], axis=-1
            )
            scores.append(dot_nt(whole_keys, q_ref[head]))
        if masked:
            row = lax.broadcasted_iota(jnp.int32, (block, rows), 0)
            from_other = row >= side
            row = jnp.where(from_other, row - side, row)
            which = jnp.where(from_other, 1 - core, core)
            key_pos = step * block + (row // half) * rows + which * half + lax.rem(row, half)
            live = key_pos <= first + lax.broadcasted_iota(jnp.int32, (block, rows), 1)
            scores = [jnp.where(live, s, masked_score) for s in scores]
        for head in range(heads):
            old = peak[head]
            new = jnp.maximum(old, jnp.max(scores[head], axis=0, keepdims=True))
            fade = jnp.exp2(old - new)
            weights = jnp.exp2(scores[head] - new).astype(bf16)
            peak[head] = new
            carried = jnp.concatenate([values[head * VH : (head + 1) * VH], ones], axis=0)
            acc[head] = acc[head] * fade + dot_nn(carried, weights)

    @pl.when((step + 1) * block <= first + 1)
    def _():
        work(False)

    @pl.when(((step + 1) * block > first + 1) & (step * block < first + rows))
    def _():
        work(True)

    @pl.when(step == pl.num_programs(0) - 1)
    def _():
        mixed = jnp.concatenate(
            [(acc[h, :VH] / acc[h, VH : VH + 1]).T for h in range(heads)], axis=-1
        ).astype(bf16)
        load.wait()
        pack_shares(dot_nn(mixed, out_ref[...]), sum_ref)


def prefill_attend(place, q, mine, other, key_expand, value_expand_t, mla_output, shares):
    heads, rows, _ = q.shape
    keys = mine.shape[0]
    side = min(512, keys)
    width = mla_output.shape[1]
    dense = rows * width // shares // 128
    whole = lambda shape: pl.BlockSpec(shape, lambda i, s: (0,) * len(shape))
    return pl.pallas_call(
        functools.partial(flash_kernel, heads),
        grid_spec=pltpu.PrefetchScalarGridSpec(
            num_scalar_prefetch=1,
            grid=(keys // side,),
            in_specs=[
                whole(q.shape),
                pl.BlockSpec((side, WIDE), lambda i, s: (i, 0)),
                pl.BlockSpec((side, WIDE), lambda i, s: (i, 0)),
                whole(key_expand.shape),
                whole(value_expand_t.shape),
                pl.BlockSpec(memory_space=pltpu.HBM),
            ],
            out_specs=whole((shares, dense, 128)),
            scratch_shapes=[
                pltpu.VMEM((heads, 1, rows), f32),
                pltpu.VMEM((heads, VH + 16, rows), f32),
                pltpu.VMEM(mla_output.shape, bf16),
                pltpu.SemaphoreType.DMA,
            ],
        ),
        out_shape=jax.ShapeDtypeStruct((shares, dense, 128), bf16),
        compiler_params=params(56),
    )(place, q, mine, other, key_expand, value_expand_t, mla_output)


def gather_share_kernel(parts_ref, x_ref, out_ref):
    rows, share = x_ref.shape
    x = x_ref[...].astype(f32)
    total = jnp.sum(parts_ref[...].astype(f32), axis=0)
    left = total[:rows] + x[:, :128]
    right = total[rows : 2 * rows] + x[:, 128:256]
    rest = total[2 * rows :]
    wide = share - 256
    rest = jnp.concatenate(
        [rest[:, i * wide : (i + 1) * wide] for i in range(128 // wide)], axis=0
    )
    rest = rest + x[:, 256:]
    out_ref[...] = jnp.concatenate([left.T, right.T, rest.T], axis=0).astype(bf16)


def gather_share(parts, x):
    rows, share = x.shape
    return pl.pallas_call(
        gather_share_kernel,
        out_shape=jax.ShapeDtypeStruct((share, rows), bf16),
        compiler_params=params(32),
    )(parts, x)


def pages_kernel(group, requests, first_ref, q_ref, keys_ref, fresh_ref, owner_ref, sent_ref):
    rows = q_ref.shape[0]
    parts = 4
    block = rows // parts
    keys = keys_ref[...]
    fresh = fresh_ref[...]
    within = lax.rem(lax.broadcasted_iota(jnp.int32, (block, 1), 0), group)
    request = lax.rem(within, requests)
    step = within // requests
    live_old = owner_ref[...] == request
    column = lax.broadcasted_iota(jnp.int32, (1, fresh.shape[0]), 1)
    fresh_step = column // requests + first_ref[1] * group
    live_new = (lax.rem(column, requests) == request) & (fresh_step <= step)
    lane = lax.broadcasted_iota(jnp.int32, (block, SENT - LAT), 1)
    scores = []
    for i in range(parts):
        q = q_ref[i * block : (i + 1) * block]
        scores.append(
            (
                jnp.where(live_old, dot_nt(q, keys), masked_score),
                jnp.where(live_new, dot_nt(q, fresh), masked_score),
            )
        )
    for i in range(parts):
        old, new = scores[i]
        highest = jnp.maximum(
            jnp.max(old, axis=-1, keepdims=True), jnp.max(new, axis=-1, keepdims=True)
        )
        highest = jnp.maximum(highest, 0.1 * masked_score)
        w_old = jnp.exp2(old - highest)
        w_new = jnp.exp2(new - highest)
        total = jnp.sum(w_old, axis=-1, keepdims=True) + jnp.sum(w_new, axis=-1, keepdims=True)
        some = total > 0.0
        safe = jnp.where(some, total, 1.0)
        mixed = dot_nn(w_old.astype(bf16), keys[:, :LAT]) + dot_nn(
            w_new.astype(bf16), fresh[:, :LAT]
        )
        mixed = mixed / safe
        level = jnp.where(some, highest + jnp.log2(safe), masked_score)
        high = level.astype(bf16).astype(f32)
        middle = (level - high).astype(bf16).astype(f32)
        low = level - high - middle
        tail = jnp.where(
            lane == 0, high, jnp.where(lane == 1, middle, jnp.where(lane == 2, low, 0.0))
        )
        sent_ref[i * block : (i + 1) * block] = jnp.concatenate([mixed, tail], axis=-1).astype(
            bf16
        )


def pages_attend(place, q_all, keys, fresh, owner, group, requests):
    smem = pl.BlockSpec(memory_space=pltpu.SMEM)
    vmem = pl.BlockSpec(memory_space=pltpu.VMEM)
    return pl.pallas_call(
        functools.partial(pages_kernel, group, requests),
        in_specs=[smem, vmem, vmem, vmem, vmem],
        out_specs=vmem,
        out_shape=jax.ShapeDtypeStruct((q_all.shape[0], SENT), bf16),
        compiler_params=params(40),
    )(place, q_all, keys, fresh, owner)


def combine_kernel(heads, parts_ref, ve_ref, out_ref, sum_ref):
    tails = parts_ref[:, :, LAT:].astype(f32)
    lane = lax.broadcasted_iota(jnp.int32, tails.shape, 2)
    level = jnp.sum(jnp.where(lane < 3, tails, 0.0), axis=-1, keepdims=True)
    weights = jnp.exp2(level - jnp.max(level, axis=0, keepdims=True))
    total = jnp.sum(weights, axis=0)
    mixed = jnp.sum(parts_ref[:, :, :LAT].astype(f32) * weights, axis=0) / total
    count = mixed.shape[0] // heads
    head_values = [
        dot_nn(
            mixed[h * count : (h + 1) * count].astype(bf16), ve_ref[:, h * VH : (h + 1) * VH]
        )
        for h in range(heads)
    ]
    joined = jnp.concatenate(head_values, axis=-1).astype(bf16)
    sum_ref[...] = dot_nn(joined, out_ref[...]).astype(bf16)


def combine(parts, value_expand, mla_output):
    heads = value_expand.shape[1] // VH
    return pl.pallas_call(
        functools.partial(combine_kernel, heads),
        out_shape=jax.ShapeDtypeStruct((parts.shape[1] // heads, mla_output.shape[1]), bf16),
        compiler_params=params(40),
    )(parts, value_expand, mla_output)


def kda_kernel(
    heads,
    requests,
    parts_ref,
    dec_ref,
    inputs_ref,
    beta_ref,
    decay_down_ref,
    decay_up_ref,
    gate_down_ref,
    gate_up_ref,
    rate_ref,
    states_ref,
    output_ref,
    hidden_ref,
    sum_ref,
    kin,
    projected,
):
    part = pl.program_id(0)
    shares, rows, share = hidden_ref.shape

    @pl.when(part == 0)
    def _():
        hidden = dec_ref[...].astype(f32) + jnp.sum(parts_ref[...].astype(f32), axis=0)
        for g in range(shares):
            hidden_ref[g] = hidden[:, g * share : (g + 1) * share]
        kin[...] = norm_rows(hidden).astype(bf16)

    projected[part] = dot_nn(kin[...], inputs_ref[0])

    @pl.when(part == pl.num_programs(0) - 1)
    def _():
        read_in = kin[...]
        beta = jax.nn.sigmoid(dot_nt(read_in, beta_ref[...]))
        decay_low = dot_nn(read_in, decay_down_ref[...]).astype(bf16)
        decays = jnp.exp(
            -rate_ref[...] * jax.nn.softplus(dot_nn(decay_low, decay_up_ref[...]))
        )
        gate_low = dot_nn(read_in, gate_down_ref[...]).astype(bf16)
        gates = jax.nn.sigmoid(dot_nn(gate_low, gate_up_ref[...]))
        steps = rows // requests
        at = lambda values, t: values[t * requests : (t + 1) * requests]
        along = lambda a, b: jnp.sum(a * b, axis=-1, keepdims=True)
        blended = []
        for head in range(heads):
            lanes = slice(head * DK, (head + 1) * DK)
            q = unit_rows(projected[0, :, lanes]) * DK ** (-0.5)
            k = unit_rows(projected[1, :, lanes])
            v = projected[2, :, lanes]
            a = decays[:, lanes]
            b = beta[:, head : head + 1]
            vectors = []
            held = None
            for t in range(steps):
                held = at(a, t) if held is None else held * at(a, t)
                vectors += [held * at(k, t), held * at(q, t)]
            vectors = jnp.concatenate(vectors, axis=0)
            high = vectors.astype(bf16)
            both = jnp.concatenate([high.astype(f32), vectors - high.astype(f32)], axis=0)
            owner = lax.rem(lax.broadcasted_iota(jnp.int32, (both.shape[0], 1), 0), requests)
            spread = jnp.concatenate(
                [jnp.where(owner == r, both, 0.0) for r in range(requests)], axis=-1
            ).astype(bf16)
            held_states = jnp.concatenate(
                [
                    states_ref[:, r, head].astype(f32).reshape(DV, DK)
                    for r in range(requests)
                ],
                axis=-1,
            ).astype(bf16)
            met = dot_nt(spread, held_states)
            met = met[: vectors.shape[0]] + met[vectors.shape[0] :]
            carried = []
            reads = []
            for t in range(steps):
                seen = at(met, 2 * t)
                read = at(met, 2 * t + 1)
                carried = [(u, w * at(a, t)) for u, w in carried]
                for u, w in carried:
                    seen = seen + u * along(w, at(k, t))
                u = at(b, t) * (at(v, t) - seen)
                carried.append((u, at(k, t)))
                for u, w in carried:
                    read = read + u * along(w, at(q, t))
                reads.append(read)
            read = jnp.concatenate(reads, axis=0)
            blended.append(norm_rows(read) * gates[:, lanes])
        mixed = jnp.concatenate(blended, axis=-1).astype(bf16)
        summed = dot_nn(mixed, output_ref[...])
        for g in range(shares):
            sum_ref[g] = summed[:, g * share : (g + 1) * share].astype(bf16)


def kda(parts, dec, inputs, beta_t, decay_down, decay_up, gate_down, gate_up, rate, states, output):
    shares, rows, width = parts.shape
    heads = beta_t.shape[0]
    requests = states.shape[1]
    columns = inputs.shape[2]
    whole = lambda a: pl.BlockSpec(a.shape, lambda i: (0,) * len(a.shape))
    share_spec = pl.BlockSpec((shares, rows, width // shares), lambda i: (0, 0, 0))
    return pl.pallas_call(
        functools.partial(kda_kernel, heads, requests),
        grid=(3,),
        in_specs=[
            whole(parts),
            whole(dec),
            pl.BlockSpec((1, width, columns), lambda i: (i, 0, 0)),
            whole(beta_t),
            whole(decay_down),
            whole(decay_up),
            whole(gate_down),
            whole(gate_up),
            whole(rate),
            whole(states),
            whole(output),
        ],
        out_specs=(share_spec, share_spec),
        out_shape=(
            jax.ShapeDtypeStruct((shares, rows, width // shares), f32),
            jax.ShapeDtypeStruct((shares, rows, width // shares), bf16),
        ),
        scratch_shapes=[pltpu.VMEM((rows, width), bf16), pltpu.VMEM((3, rows, columns), f32)],
        compiler_params=params(48),
    )(parts, dec, inputs, beta_t, decay_down, decay_up, gate_down, gate_up, rate, states, output)


def shards(
    x_group,
    decode_input,
    prompt_len,
    latent_pages,
    slot_target,
    page_counts,
    kda_state,
    query_proj,
    latent_proj,
    key_expand,
    value_expand,
    mla_output,
    kda_inputs,
    kda_beta,
    decay_down,
    decay_up,
    gate_down,
    gate_up,
    decay_log,
    kda_output,
):
    seq_index = lax.axis_index("seq")
    grp_index = lax.axis_index("grp")
    seq_size = lax.axis_size("seq")
    grp_size = lax.axis_size("grp")
    rows, width = x_group.shape
    steps, requests, _ = decode_input.shape
    decode_rows = steps * requests
    share = width // grp_size
    dec = decode_input.reshape(decode_rows, width)
    place = jnp.stack([seq_index, grp_index]).astype(jnp.int32)

    own_latent, fresh, q_prefill, q_decode, own_tokens = front(
        place,
        prompt_len,
        x_group,
        dec,
        latent_proj.T,
        query_proj,
        key_expand,
        latent_pages[0],
        seq_size,
        grp_size,
    )
    mine = lax.all_gather(own_latent, "seq", axis=0, tiled=True)
    other = lax.ppermute(mine, "grp", [(g, g ^ 1) for g in range(grp_size)])

    arrived = lax.all_to_all(own_tokens, "seq", split_axis=0, concat_axis=0, tiled=True)
    _, slots, tokens, _ = own_tokens.shape
    page_keys = arrived.reshape(seq_size * slots * tokens, WIDE)
    core = grp_index % 2
    target = lax.dynamic_slice_in_dim(slot_target[:, 0, :], core * slots, slots, 1)
    owner = target // MAXP
    lengths = jnp.sum(
        jnp.where(owner[..., None] == jnp.arange(requests), prompt_len, 0), axis=-1
    )
    held = core * slots + jnp.arange(slots)[None, :] < page_counts
    token_pos = (
        ((target % MAXP) * PAGE + (grp_index // 2) * tokens)[..., None] + jnp.arange(tokens)
    )
    key_owner = jnp.where(
        held[..., None] & (token_pos < lengths[..., None]), owner[..., None], -1
    ).reshape(1, -1)

    states = lax.all_to_all(
        kda_state.astype(bf16), "seq", split_axis=0, concat_axis=0, tiled=True
    ).reshape((seq_size, requests) + kda_state.shape[1:])

    q_all = lax.all_gather(q_decode, "grp", axis=0, tiled=True)
    partial = pages_attend(place, q_all, page_keys, fresh, key_owner, decode_rows, requests)
    partial = lax.all_to_all(
        partial.reshape(grp_size, -1, SENT), "grp", split_axis=0, concat_axis=0, tiled=True
    )
    mla_part = combine(partial, value_expand, mla_output)
    mla_parts = lax.all_gather(mla_part, "grp", axis=0, tiled=False)
    hidden, kda_part = kda(
        mla_parts,
        dec,
        kda_inputs.transpose(1, 0, 2),
        kda_beta.T,
        decay_down,
        decay_up,
        gate_down,
        gate_up,
        jnp.repeat(jnp.exp(decay_log), DK)[None, :],
        states,
        kda_output,
    )
    kda_parts = lax.all_to_all(kda_part, "grp", split_axis=0, concat_axis=0, tiled=True)
    hidden_share = lax.dynamic_index_in_dim(hidden, grp_index, 0, keepdims=False)
    decode_out = (hidden_share + jnp.sum(kda_parts.astype(f32), axis=0)).astype(bf16)

    prefill_part = prefill_attend(
        place, q_prefill, mine, other, key_expand, value_expand.T, mla_output, grp_size
    )
    prefill_parts = lax.all_to_all(
        prefill_part, "grp", split_axis=0, concat_axis=0, tiled=True
    )
    own_columns = lax.dynamic_slice_in_dim(x_group, grp_index * share, share, 1)
    prefill_out = gather_share(prefill_parts, own_columns).T
    return (prefill_out, decode_out.reshape(steps, requests, share))


def solution(mesh):
    in_specs = (
        P("seq", None),
        P(None, "seq", None),
        P("seq"),
        P("seq", None, None, None, None),
        P(None, "seq", None),
        P(None, "seq"),
        P(None, "grp", "seq", None),
        P(None, "grp"),
        P(),
        P(None, "grp"),
        P(None, "grp"),
        P("grp", None),
        P(None, None, "grp"),
        P(None, "grp"),
        P(),
        P(None, "grp"),
        P(),
        P(None, "grp"),
        P("grp"),
        P("grp", None),
    )
    out_specs = (P("seq", "grp"), P(None, "seq", "grp"))
    return jax.shard_map(shards, mesh=mesh, in_specs=in_specs, out_specs=out_specs, check_vma=False)
```

time: 166 us -> 236 us (1.42)
  the two profiles are of different devices: /device:TPU:112 before, /device:TPU:96 now
where the time goes in v2:
time: 236 us; the launch traced here: 235 us
  waiting for transfers between devices  72.9 us (31%)
  Pallas kernels  62.6 us (27%)
  local copies, waits for them, and re-layouts  28.8 us (12%)
  blocking collectives  27.6 us (12%)
  starting transfers between devices  24.9 us (11%)
  between operations  14.2 us (6%)
  other arithmetic  4.05 us (2%)
    all_gather x1, waiting for transfers between devices, shards(): mine = lax.all_gather(own_latent, 'seq', axis=0, tiled=True)  44.9 us
    pallas_call x1, Pallas kernels, front(): pl.pallas_call(front_kernel, in_specs=[smem, smem, vmem, vmem] + [hbm] *...  33.5 us
    unnamed x51, local copies, waits for them, and re-layouts  18.5 us
    all_to_all x1, waiting for transfers between devices, shards(): lax.all_to_all(prefill_part, 'grp', split_axis=0, concat_axis=0, tiled=True)  15.6 us
    pallas_call x1, Pallas kernels, prefill_attend(): pl.pallas_call(functools.partial(flash_kernel, heads), grid_spec=pltpu.Pr...  15.4 us
    all_gather x1, blocking collectives, shards(): q_all = lax.all_gather(q_decode, 'grp', axis=0, tiled=True)  14.1 us
    all_gather x1, blocking collectives, shards(): mla_parts = lax.all_gather(mla_part, 'grp', axis=0, tiled=False)  13.6 us
    all_to_all x1, waiting for transfers between devices, shards(): lax.all_to_all(partial.reshape(grp_size, -1, SENT), 'grp', split_axis=0,...  12.2 us
  transfers between devices with their start and end apart: 7, of which 3 were waited for; matrix products, arithmetic and copies ran while one was open for 7% of the time, Pallas kernels for 12%

profile of v2, /device:TPU:96, one launch (start us, length us, event | category | flops | bytes accessed | tf_op | source)
XLA Modules:
  0.0 235.1 jit_solution(10922838548795679608)
XLA Ops:
  7.2 0.0 all-gather.3.cloned.1.call-start
  7.2 0.1 pad_add_fusion.place_ref.first_ref
  7.3 2.0 copy-done.3
  9.3 1.7 copy-done.4
  11.0 1.0 copy-done.7
  12.1 1.3 copy-done.8
  13.4 1.1 copy-done.9
  14.5 0.9 copy-done.13
  15.4 0.7 copy-done.18
  16.1 0.7 copy-done.20
  16.8 33.5 %shard_map.224 = (bf16[128,576]{1,0:T(8,128)(2,1)}, bf16[32,576]{1,0:T(8,128)(2,1)S(1)}, bf16[4,256,192]{2,1,0:T(8,128)(2,1)S(1)}, bf16[96,576]{1,0:T(8,128)(2,1)S(1)}, bf16[16,3,16,576]{3,2,1,0:T(8,128)(2,1)}) custom-call(s32[2]{0:T(128)S(1)} %pad_add_fusion.place_ref.first_ref, s32[8]{0:T(128)S(1)} %copy-done.20, f32[2,771,64]{2,1,0:T(8,128)S(1)} %copy-done.9, ...), custom_call_target="tpu_custom_call" | custom-call | tf_op jit(solution)/shard_map/pallas_call | solution.py:190
  50.3 0.8 copy-done.12
  51.2 7.2 %all-to-all-start.1 = ((bf16[16,3,16,576]{3,2,1,0:T(8,128)(2,1)}), bf16[16,3,16,576]{3,2,1,0:T(8,128)(2,1)S(1)}, u32[]{:S(2)}, u32[]{:S(2)}) async-start(bf16[16,3,16,576]{3,2,1,0:T(8,128)(2,1)} %get-tuple-element.12), calls=%async_computation.1 | async-start | bytes 1966080 | tf_op jit(solution)/shard_map/all_to_all | solution.py:616
  58.4 0.1 copy.43
  58.5 0.1 select_reduce_fusion
  58.6 0.1 copy.42
  58.7 0.1 copy.41
  58.8 0.1 broadcast_compare_fusion
  58.8 44.9 %all-gather.3.cloned.1.call-done.mine_ref = bf16[2048,576]{1,0:T(8,128)(2,1)} async-done(((bf16[128,576]{1,0:T(8,128)(2,1)}), bf16[2048,576]{1,0:T(8,128)(2,1)}) %all-gather.3.cloned.1.call-update) | async-done | bytes 2359312 | tf_op jit(solution)/shard_map/all_gather | solution.py:613
  103.8 4.4 %copy.38 = bf16[2048,576]{0,1:T(8,128)(2,1)} copy(bf16[2048,576]{1,0:T(8,128)(2,1)} %all-gather.3.cloned.1.call-done.mine_ref) | data formatting | bytes 4718592 | tf_op jit(solution)/shard_map/all_gather | solution.py:613
  108.2 0.1 fusion.2
  108.3 0.1 select_n.66.owner_ref
  108.4 14.1 %all_gather.13.q_ref = bf16[768,576]{1,0:T(8,128)(2,1)S(1)} all-gather(bf16[96,576]{1,0:T(8,128)(2,1)S(1)} %get-tuple-element.11), channel_id=1, replica_groups=mesh['seq'=16,'grp'=8] {'grp'}, dimensions={0}, use_global_device_ids=true | all-gather | bytes 995328 | tf_op jit(solution)/shard_map/all_gather | solution.py:637
  122.5 4.3 %shard_map.227 = bf16[768,640]{1,0:T(8,128)(2,1)} custom-call(s32[2]{0:T(128)S(1)} %pad_add_fusion.place_ref.first_ref, bf16[768,576]{1,0:T(8,128)(2,1)S(1)} %all_gather.13.q_ref, bf16[768,576]{1,0:T(8,128)(2,1)S(1)} %bitcast.40, bf16[32,576]{1,0:T(8,128)(2,1)S(1)} %get-tuple-element.13.fresh_ref, s32[1,768]{1,0:T(1,128)S(1)} %select_n.66.owner_ref), custom_call_target="tpu_custom_call" | custom-call | tf_op jit(solution)/shard_map/pallas_call | solution.py:405
  126.8 3.9 %all-to-all-start.2 = ((bf16[8,96,640]{2,1,0:T(8,128)(2,1)}), bf16[8,96,640]{2,1,0:T(8,128)(2,1)S(1)}, u32[]{:S(2)}, u32[]{:S(2)}) async-start(bf16[8,96,640]{2,1,0:T(8,128)(2,1)} %bitcast.9), calls=%async_computation.2 | async-start | bytes 1966080 | tf_op jit(solution)/shard_map/all_to_all | solution.py:639
  130.8 3.0 %convert_element_type.10 = bf16[128,4,8,128]{3,2,1,0:T(8,128)(2,1)} convert(f32[128,4,8,128]{3,2,1,0:T(8,128)} %param.28) | non-fusion elementwise | flops 524288 | bytes 3145728 | tf_op jit(solution)/shard_map/convert_element_type | solution.py:634
  133.8 12.2 %all-to-all-done.2.parts_ref = bf16[8,96,640]{2,1,0:T(8,128)(2,1)S(1)} async-done(((bf16[8,96,640]{2,1,0:T(8,128)(2,1)}), bf16[8,96,640]{2,1,0:T(8,128)(2,1)S(1)}, u32[]{:S(2)}, u32[]{:S(2)}) %all-to-all-start.2) | async-done | bytes 983072 | tf_op jit(solution)/shard_map/all_to_all | solution.py:639
  146.0 0.9 copy-done.1
  147.0 5.7 %all-to-all-start.3 = ((bf16[128,4,8,128]{3,2,1,0:T(8,128)(2,1)}), bf16[128,4,8,128]{3,2,1,0:T(8,128)(2,1)S(1)}, u32[]{:S(2)}, u32[]{:S(2)}) async-start(bf16[128,4,8,128]{3,2,1,0:T(8,128)(2,1)} %convert_element_type.10), calls=%async_computation.3 | async-start | bytes 2097152 | tf_op jit(solution)/shard_map/all_to_all | solution.py:633
  152.7 1.2 copy-done.2
  153.9 1.0 copy-done.5
  154.9 0.8 shard_map.228
  155.8 13.6 %all-gather = bf16[192,2304]{1,0:T(8,128)(2,1)S(1)} all-gather(bf16[24,2304]{1,0:T(8,128)(2,1)S(1)} %shard_map.228), channel_id=2, replica_groups=mesh['seq'=16,'grp'=8] {'grp'}, dimensions={0}, use_global_device_ids=true | all-gather | bytes 995328 | tf_op jit(solution)/shard_map/all_gather | solution.py:643
  169.3 0.1 broadcast_in_dim.35
  169.4 1.1 copy-done.10
  170.5 1.1 copy-done.11
  171.5 0.9 copy-done.15
  172.4 0.9 copy-done.16
  173.3 7.7 %shard_map.229 = (f32[8,24,288]{2,1,0:T(8,128)S(1)}, bf16[8,24,288]{2,1,0:T(8,128)(2,1)}) custom-call(bf16[8,24,2304]{2,1,0:T(8,128)(2,1)S(1)} %bitcast.41, bf16[24,2304]{1,0:T(8,128)(2,1)S(1)} %bitcast.44, bf16[3,2304,512]{2,1,0:T(8,128)(2,1)} %bitcast.48, bf16[4,2304]{1,0:T(4,128)(2,1)S(1)} %bitcast.45, bf16[2304,128]{1,0:T(8,128)(2,1)S(1)} %copy-done.10, ...), custom_call_target="tpu_custom_call" | custom-call | tf_op jit(solution)/shard_map/pallas_call | solution.py:542
  181.0 3.6 %all-to-all-start.4 = ((bf16[8,24,288]{2,1,0:T(8,128)(2,1)}), bf16[8,24,288]{2,1,0:T(8,128)(2,1)S(1)}, u32[]{:S(2)}, u32[]{:S(2)}) async-start(bf16[8,24,288]{2,1,0:T(8,128)(2,1)} %get-tuple-element.15), calls=%async_computation.4 | async-start | bytes 294912 | tf_op jit(solution)/shard_map/all_to_all | solution.py:657
  184.6 1.1 copy.39
  185.6 4.4 %copy.40.other_ref = bf16[2048,576]{1,0:T(8,128)(2,1)} copy(bf16[2048,576]{0,1:T(8,128)(2,1)} %collective-permute-done) | data formatting | bytes 4718592 | tf_op jit(solution)/shard_map/ppermute | solution.py:614
  190.0 15.4 %shard_map.225 = bf16[8,576,128]{2,1,0:T(8,128)(2,1)} custom-call(s32[2]{0:T(128)} %copy-done.19, bf16[4,256,192]{2,1,0:T(8,128)(2,1)} %copy-done.12, bf16[2048,576]{1,0:T(8,128)(2,1)} %all-gather.3.cloned.1.call-done.mine_ref, bf16[2048,576]{1,0:T(8,128)(2,1)} %copy.40.other_ref, bf16[512,512]{1,0:T(8,128)(2,1)} %ke_ref.1, bf16[512,512]{1,0:T(8,128)(2,1)} %bitcast.49, ...), custom_call_target="tpu_custom_call" | custom-call | tf_op jit(solution)/shard_map/pallas_call | solution.py:302
  205.4 4.5 %all-to-all-start = ((bf16[8,576,128]{2,1,0:T(8,128)(2,1)}), bf16[8,576,128]{2,1,0:T(8,128)(2,1)S(1)}, u32[]{:S(2)}, u32[]{:S(2)}) async-start(bf16[8,576,128]{2,1,0:T(8,128)(2,1)} %shard_map.225), calls=%async_computation | async-start | bytes 2359296 | tf_op jit(solution)/shard_map/all_to_all | solution.py:664
  210.0 1.1 constant_dynamic-slice_fusion.1.x_ref
  211.1 0.6 fusion
  211.7 15.6 %all-to-all-done.parts_ref = bf16[8,576,128]{2,1,0:T(8,128)(2,1)S(1)} async-done(((bf16[8,576,128]{2,1,0:T(8,128)(2,1)}), bf16[8,576,128]{2,1,0:T(8,128)(2,1)S(1)}, u32[]{:S(2)}, u32[]{:S(2)}) %all-to-all-start) | async-done | bytes 1179680 | tf_op jit(solution)/shard_map/all_to_all | solution.py:664
  227.3 0.9 shard_map.226
  (46 shorter events, 0.2 us)
Async XLA Ops:
  7.2 96.6 %all-gather.3.cloned.1.call-start = ((), (), s32[]{:S(2)}) async-start(), calls=%async_computation.5 | async-start | bytes 2785280 | tf_op jit(solution)/shard_map/all_gather | solution.py:613
  7.3 115.2 %copy-start.19 = (s32[2]{0:T(128)}, s32[2]{0:T(128)S(1)}, u32[]{:S(2)}) copy-start(s32[2]{0:T(128)S(1)} %pad_add_fusion.place_ref.first_ref) | copy-start | bytes 28
  7.3 2.0 copy-start.3
  9.3 1.7 copy-start.4
  11.0 1.0 copy-start.7
  12.1 1.3 copy-start.8
  13.4 1.1 copy-start.9
  14.5 0.9 copy-start.13
  15.4 0.7 copy-start.18
  16.1 0.7 copy-start.20
  16.8 41.6 %copy-start.22 = (s32[16,1,6]{0,1,2:T(1,128)S(1)}, s32[16,1,6]{0,1,2:T(1,128)}, u32[]{:S(2)}) copy-start(s32[16,1,6]{0,1,2:T(1,128)} %param.26) | copy-start | bytes 1156
  16.8 41.7 %copy-start.21 = (s32[8]{0:T(128)S(1)}, s32[8]{0:T(128)}, u32[]{:S(2)}) copy-start(s32[8]{0:T(128)} %lengths_ref.1) | copy-start | bytes 100
  16.8 42.0 %copy-start.23 = (s32[16,1]{0,1:T(1,128)S(1)}, s32[16,1]{0,1:T(1,128)}, u32[]{:S(2)}) copy-start(s32[16,1]{0,1:T(1,128)} %param.27) | copy-start | bytes 196
  50.3 0.8 copy-start.12
  51.2 71.4 %all-to-all-start.1 = ((bf16[16,3,16,576]{3,2,1,0:T(8,128)(2,1)}), bf16[16,3,16,576]{3,2,1,0:T(8,128)(2,1)S(1)}, u32[]{:S(2)}, u32[]{:S(2)}) async-start(bf16[16,3,16,576]{3,2,1,0:T(8,128)(2,1)} %get-tuple-element.12), calls=%async_computation.1 | async-start | bytes 1966080 | tf_op jit(solution)/shard_map/all_to_all | solution.py:616
  108.2 77.4 %collective-permute-start = (bf16[2048,576]{0,1:T(8,128)(2,1)}, bf16[2048,576]{0,1:T(8,128)(2,1)}, u32[]{:S(2)}, u32[]{:S(2)}) collective-permute-start(bf16[2048,576]{0,1:T(8,128)(2,1)} %copy.38), channel_id=1, source_target_pairs={{0,1},{1,0},{2,3},{3,2},{4,5},{5,4},{6,7},{7,6},{8,9},{9,8},{10,11... | collective-permute-start | bytes 7077896 | tf_op jit(solution)/shard_map/ppermute | solution.py:614
  126.8 19.2 %all-to-all-start.2 = ((bf16[8,96,640]{2,1,0:T(8,128)(2,1)}), bf16[8,96,640]{2,1,0:T(8,128)(2,1)S(1)}, u32[]{:S(2)}, u32[]{:S(2)}) async-start(bf16[8,96,640]{2,1,0:T(8,128)(2,1)} %bitcast.9), calls=%async_computation.2 | async-start | bytes 1966080 | tf_op jit(solution)/shard_map/all_to_all | solution.py:639
  130.7 21.9 %copy-start.24 = (f32[4]{0:T(128)S(1)}, f32[4]{0:T(128)}, u32[]{:S(2)}) copy-start(f32[4]{0:T(128)} %param.40) | copy-start | bytes 52
  130.7 21.9 %copy-start = (bf16[512,2304]{1,0:T(8,128)(2,1)S(1)}, bf16[512,2304]{1,0:T(8,128)(2,1)}, u32[]{:S(2)}) copy-start(bf16[512,2304]{1,0:T(8,128)(2,1)} %out_ref.1) | copy-start | bytes 7077892
  146.0 1.0 copy-start.1
  147.0 22.4 %all-to-all-start.3 = ((bf16[128,4,8,128]{3,2,1,0:T(8,128)(2,1)}), bf16[128,4,8,128]{3,2,1,0:T(8,128)(2,1)S(1)}, u32[]{:S(2)}, u32[]{:S(2)}) async-start(bf16[128,4,8,128]{3,2,1,0:T(8,128)(2,1)} %convert_element_type.10), calls=%async_computation.3 | async-start | bytes 2097152 | tf_op jit(solution)/shard_map/all_to_all | solution.py:633
  152.7 1.2 copy-start.2
  153.9 1.0 copy-start.5
  154.9 14.5 %copy-start.14 = (bf16[3,8,2304]{2,1,0:T(8,128)(2,1)S(1)}, bf16[3,8,2304]{2,1,0:T(8,128)(2,1)}, u32[]{:S(2)}) copy-start(bf16[3,8,2304]{2,1,0:T(8,128)(2,1)} %param.23) | copy-start | bytes 331780
  154.9 14.5 %copy-start.17 = (bf16[2304,4]{0,1:T(4,128)(2,1)S(1)}, bf16[2304,4]{0,1:T(4,128)(2,1)}, u32[]{:S(2)}) copy-start(bf16[2304,4]{0,1:T(4,128)(2,1)} %param.35) | copy-start | bytes 55300
  169.4 1.1 copy-start.10
  170.5 1.1 copy-start.11
  171.5 0.9 copy-start.15
  172.4 0.9 copy-start.16
  173.3 11.2 %copy-start.6 = (bf16[512,512]{1,0:T(8,128)(2,1)S(1)}, bf16[512,512]{1,0:T(8,128)(2,1)}, u32[]{:S(2)}) copy-start(bf16[512,512]{1,0:T(8,128)(2,1)} %ve_ref.1) | copy-start | bytes 1572868
  181.0 24.4 %all-to-all-start.4 = ((bf16[8,24,288]{2,1,0:T(8,128)(2,1)}), bf16[8,24,288]{2,1,0:T(8,128)(2,1)S(1)}, u32[]{:S(2)}, u32[]{:S(2)}) async-start(bf16[8,24,288]{2,1,0:T(8,128)(2,1)} %get-tuple-element.15), calls=%async_computation.4 | async-start | bytes 294912 | tf_op jit(solution)/shard_map/all_to_all | solution.py:657
  205.4 21.9 %all-to-all-start = ((bf16[8,576,128]{2,1,0:T(8,128)(2,1)}), bf16[8,576,128]{2,1,0:T(8,128)(2,1)S(1)}, u32[]{:S(2)}, u32[]{:S(2)}) async-start(bf16[8,576,128]{2,1,0:T(8,128)(2,1)} %shard_map.225), calls=%async_computation | async-start | bytes 2359296 | tf_op jit(solution)/shard_map/all_to_all | solution.py:664
Sparse Core Ops, SparseCore 0:
  51.3 52.4 all-gather.2

commit v3 on v2

--- a/solution.py
+++ b/solution.py
@@ -29,7 +29,7 @@
 MIB = 1024 * 1024
 
 
-def params(mib):
+def params(mib=58):
     return pltpu.CompilerParams(vmem_limit_bytes=mib * MIB)
 
 
@@ -64,8 +64,56 @@
     return jnp.asarray(both, f32)
 
 
+def slice_kernel(pages_hbm, own_hbm, held, in_sems, out_sems):
+    grp = lax.axis_index("grp")
+    owners, slots, tokens, _ = own_hbm.shape
+    parts = in_sems.shape[0]
+    each = owners // parts
+    first = lax.rem(grp, 2) * slots
+    row = pl.multiple_of((grp // 2) * tokens, tokens)
+    loads = [
+        pltpu.make_async_copy(
+            pages_hbm.at[pl.ds(i * each, each), pl.ds(first, slots), pl.ds(row, tokens), :],
+            held.at[pl.ds(i * each, each)],
+            in_sems.at[i],
+        )
+        for i in range(parts)
+    ]
+    stores = [
+        pltpu.make_async_copy(
+            held.at[pl.ds(i * each, each)], own_hbm.at[pl.ds(i * each, each)], out_sems.at[i]
+        )
+        for i in range(parts)
+    ]
+    for load in loads:
+        load.start()
+    for load, store in zip(loads, stores):
+        load.wait()
+        store.start()
+    for store in stores:
+        store.wait()
+
+
+def slice_pages(pages, grp_size):
+    owners, cap, page, wide = pages.shape
+    shape = (owners, cap // 2, page // (grp_size // 2), wide)
+    parts = 4
+    hbm = pl.BlockSpec(memory_space=pltpu.HBM)
+    return pl.pallas_call(
+        slice_kernel,
+        in_specs=[hbm],
+        out_specs=hbm,
+        out_shape=jax.ShapeDtypeStruct(shape, bf16),
+        scratch_shapes=[
+            pltpu.VMEM(shape, bf16),
+            pltpu.SemaphoreType.DMA((parts,)),
+            pltpu.SemaphoreType.DMA((parts,)),
+        ],
+        compiler_params=params(),
+    )(pages)
+
+
 def front_kernel(
-    place_ref,
     lengths_ref,
     fine_ref,
     coarse_ref,
@@ -74,12 +122,10 @@
     lat_proj_hbm,
     query_proj_hbm,
     expand_hbm,
-    pages_hbm,
-    lat_ref,
+    lat_hbm,
     fresh_ref,
     qp_ref,
     qd_ref,
-    own_hbm,
     x_ref,
     dec_ref,
     lat_proj_ref,
@@ -87,14 +133,15 @@
     expand_ref,
     normed,
     turns,
+    lat_ref,
     sems,
+    out_sems,
 ):
-    seq, grp = place_ref[0], place_ref[1]
+    seq, grp = lax.axis_index("seq"), lax.axis_index("grp")
     rows, width = x_ref.shape
     count = dec_ref.shape[0]
     half_rows = lat_ref.shape[0]
     core = lax.rem(grp, 2)
-    _, slots, tokens, _ = own_hbm.shape
     heads = qp_ref.shape[0]
     requests = lengths_ref.shape[0]
     chunks = 3
@@ -113,14 +160,8 @@
         )
         for i in range(chunks)
     ]
-    pages = pltpu.make_async_copy(
-        pages_hbm.at[:, pl.ds(core * slots, slots), pl.ds((grp // 2) * tokens, tokens), :],
-        own_hbm,
-        sems.at[4 + chunks],
-    )
     for load in loads:
         load.start()
-    pages.start()
     for r in range(requests):
         for t in range(count // requests):
             at = rows + t * requests + r
@@ -148,7 +189,16 @@
         ).astype(bf16)
 
     own = pl.ds(pl.multiple_of(core * half_rows, half_rows), half_rows)
-    lat_ref[...] = latents(normed[own], turns[0, own], turns[1, own])
+    gap = jnp.zeros((half_rows, SENT - WIDE), bf16)
+    lat_ref[...] = jnp.concatenate(
+        [latents(normed[own], turns[0, own], turns[1, own]), gap], axis=-1
+    )
+    stores = [
+        pltpu.make_async_copy(lat_ref, lat_hbm.at[i], out_sems.at[i])
+        for i in range(lat_hbm.shape[0])
+    ]
+    for store in stores:
+        store.start()
     fresh_ref[...] = latents(normed[rows:], turns[0, rows:], turns[1, rows:])
     total = None
     for i in range(chunks):
@@ -170,12 +220,14 @@
         absorbed = dot_nt(
             nope[rows:].astype(bf16), expand_ref[:, head * NOPE : (head + 1) * NOPE]
         )
-        decode.append(jnp.concatenate([absorbed, turned[rows:]], axis=-1)[:count])
+        blank = jnp.zeros((absorbed.shape[0], SENT - WIDE), f32)
+        decode.append(jnp.concatenate([absorbed, turned[rows:], blank], axis=-1)[:count])
     qd_ref[...] = (jnp.concatenate(decode, axis=0) * fold).astype(bf16)
-    pages.wait()
-
-
-def front(place, lengths, x, dec, lat_proj_t, query_proj, key_expand, pages, seq_size, grp_size):
+    for store in stores:
+        store.wait()
+
+
+def front(lengths, x, dec, lat_proj_t, query_proj, key_expand, seq_size):
     rows, width = x.shape
     count = dec.shape[0]
     heads = key_expand.shape[1] // NOPE
@@ -183,20 +235,18 @@
     requests = lengths.shape[0]
     fine = rope_tables(range(max(rows, MAXP * PAGE + count // requests)))
     coarse = rope_tables([rows * i for i in range(seq_size)])
-    slots, tokens = pages.shape[1] // 2, PAGE // (grp_size // 2)
     smem = pl.BlockSpec(memory_space=pltpu.SMEM)
     vmem = pl.BlockSpec(memory_space=pltpu.VMEM)
     hbm = pl.BlockSpec(memory_space=pltpu.HBM)
     return pl.pallas_call(
         front_kernel,
-        in_specs=[smem, smem, vmem, vmem] + [hbm] * 6,
-        out_specs=(vmem, vmem, vmem, vmem, hbm),
+        in_specs=[smem, vmem, vmem] + [hbm] * 5,
+        out_specs=(hbm, vmem, vmem, vmem),
         out_shape=(
-            jax.ShapeDtypeStruct((rows // 2, WIDE), bf16),
+            jax.ShapeDtypeStruct((seq_size, rows // 2, SENT), bf16),
             jax.ShapeDtypeStruct((padded, WIDE), bf16),
             jax.ShapeDtypeStruct((heads, rows, NOPE + ROPE), bf16),
-            jax.ShapeDtypeStruct((heads * count, WIDE), bf16),
-            jax.ShapeDtypeStruct((pages.shape[0], slots, tokens, WIDE), bf16),
+            jax.ShapeDtypeStruct((heads * count, SENT), bf16),
         ),
         scratch_shapes=[
             pltpu.VMEM(x.shape, bf16),
@@ -206,10 +256,12 @@
             pltpu.VMEM(key_expand.shape, bf16),
             pltpu.VMEM((rows + padded, width), bf16),
             pltpu.VMEM((2, rows + padded, ROPE), f32),
-            pltpu.SemaphoreType.DMA((8,)),
+            pltpu.VMEM((rows // 2, SENT), bf16),
+            pltpu.SemaphoreType.DMA((7,)),
+            pltpu.SemaphoreType.DMA((seq_size,)),
         ],
-        compiler_params=params(40),
-    )(place, lengths, fine, coarse, x, dec, lat_proj_t, query_proj, key_expand, pages)
+        compiler_params=params(),
+    )(lengths, fine, coarse, x, dec, lat_proj_t, query_proj, key_expand)
 
 
 def pack_shares(summed, sum_ref):
@@ -229,13 +281,13 @@
 
 
 def flash_kernel(
-    heads, place_ref, q_ref, mine_ref, other_ref, ke_ref, vet_ref, out_hbm, sum_ref,
-    peak, acc, out_ref, sem,
+    heads, q_ref, mine_ref, other_ref, ke_ref, ve_ref, out_hbm, sum_ref,
+    peak, acc, vet_ref, out_ref, sem,
 ):
     step = pl.program_id(0)
     rows = q_ref.shape[1]
     half = rows // 2
-    first, core = place_ref[0] * rows, lax.rem(place_ref[1], 2)
+    first, core = lax.axis_index("seq") * rows, lax.rem(lax.axis_index("grp"), 2)
     side = mine_ref.shape[0]
     block = 2 * side
     load = pltpu.make_async_copy(out_hbm, out_ref, sem)
@@ -243,12 +295,13 @@
     @pl.when(step == 0)
     def _():
         load.start()
+        vet_ref[...] = ve_ref[...].astype(f32).T.astype(bf16)
         peak[...] = jnp.full_like(peak, masked_score)
         acc[...] = jnp.zeros_like(acc)
 
     def work(masked):
         lat = jnp.concatenate([mine_ref[...], other_ref[...]], axis=0)
-        low, rope = lat[:, :LAT], lat[:, LAT:]
+        low, rope = lat[:, :LAT], lat[:, LAT:WIDE]
         ones = jnp.ones((16, block), bf16)
         keys = dot_nn(low, ke_ref[...]).astype(bf16)
         values = dot_nt(vet_ref[...], low).astype(bf16)
@@ -292,37 +345,35 @@
         pack_shares(dot_nn(mixed, out_ref[...]), sum_ref)
 
 
-def prefill_attend(place, q, mine, other, key_expand, value_expand_t, mla_output, shares):
+def prefill_attend(q, mine, other, key_expand, value_expand, mla_output, shares):
     heads, rows, _ = q.shape
     keys = mine.shape[0]
     side = min(512, keys)
     width = mla_output.shape[1]
     dense = rows * width // shares // 128
-    whole = lambda shape: pl.BlockSpec(shape, lambda i, s: (0,) * len(shape))
+    whole = lambda shape: pl.BlockSpec(shape, lambda i: (0,) * len(shape))
     return pl.pallas_call(
         functools.partial(flash_kernel, heads),
-        grid_spec=pltpu.PrefetchScalarGridSpec(
-            num_scalar_prefetch=1,
-            grid=(keys // side,),
-            in_specs=[
-                whole(q.shape),
-                pl.BlockSpec((side, WIDE), lambda i, s: (i, 0)),
-                pl.BlockSpec((side, WIDE), lambda i, s: (i, 0)),
-                whole(key_expand.shape),
-                whole(value_expand_t.shape),
-                pl.BlockSpec(memory_space=pltpu.HBM),
-            ],
-            out_specs=whole((shares, dense, 128)),
-            scratch_shapes=[
-                pltpu.VMEM((heads, 1, rows), f32),
-                pltpu.VMEM((heads, VH + 16, rows), f32),
-                pltpu.VMEM(mla_output.shape, bf16),
-                pltpu.SemaphoreType.DMA,
-            ],
-        ),
+        grid=(keys // side,),
+        in_specs=[
+            whole(q.shape),
+            pl.BlockSpec((side, SENT), lambda i: (i, 0)),
+            pl.BlockSpec((side, SENT), lambda i: (i, 0)),
+            whole(key_expand.shape),
+            whole(value_expand.shape),
+            pl.BlockSpec(memory_space=pltpu.HBM),
+        ],
+        out_specs=whole((shares, dense, 128)),
+        scratch_shapes=[
+            pltpu.VMEM((heads, 1, rows), f32),
+            pltpu.VMEM((heads, VH + 16, rows), f32),
+            pltpu.VMEM((value_expand.shape[1], value_expand.shape[0]), bf16),
+            pltpu.VMEM(mla_output.shape, bf16),
+            pltpu.SemaphoreType.DMA,
+        ],
         out_shape=jax.ShapeDtypeStruct((shares, dense, 128), bf16),
-        compiler_params=params(56),
-    )(place, q, mine, other, key_expand, value_expand_t, mla_output)
+        compiler_params=params(),
+    )(q, mine, other, key_expand, value_expand, mla_output)
 
 
 def gather_share_kernel(parts_ref, x_ref, out_ref):
@@ -345,14 +396,40 @@
     return pl.pallas_call(
         gather_share_kernel,
         out_shape=jax.ShapeDtypeStruct((share, rows), bf16),
-        compiler_params=params(32),
+        compiler_params=params(),
     )(parts, x)
 
 
-def pages_kernel(group, requests, first_ref, q_ref, keys_ref, fresh_ref, owner_ref, sent_ref):
-    rows = q_ref.shape[0]
-    parts = 4
-    block = rows // parts
+def split_level(level, rows):
+    lane = lax.broadcasted_iota(jnp.int32, (rows, SENT - LAT), 1)
+    high = level.astype(bf16).astype(f32)
+    middle = (level - high).astype(bf16).astype(f32)
+    low = level - high - middle
+    return jnp.where(
+        lane == 0, high, jnp.where(lane == 1, middle, jnp.where(lane == 2, low, 0.0))
+    )
+
+
+def join_level(part):
+    tail = part[:, LAT:].astype(f32)
+    lane = lax.broadcasted_iota(jnp.int32, tail.shape, 1)
+    return jnp.sum(jnp.where(lane < 3, tail, 0.0), axis=-1, keepdims=True)
+
+
+def merge_parts(parts):
+    levels = [join_level(p) for p in parts]
+    highest = functools.reduce(jnp.maximum, levels)
+    weights = [jnp.exp2(v - highest) for v in levels]
+    total = sum(weights)
+    mixed = sum(p[:, :LAT].astype(f32) * w for p, w in zip(parts, weights)) / total
+    return mixed, highest + jnp.log2(total)
+
+
+def pages_kernel(group, requests, count, *refs):
+    q_refs = refs[: 2 * count]
+    keys_ref, fresh_ref, owner_ref, keep_ref, send_ref = refs[2 * count :]
+    each = q_refs[0].shape[0]
+    block = 2 * each
     keys = keys_ref[...]
     fresh = fresh_ref[...]
     within = lax.rem(lax.broadcasted_iota(jnp.int32, (block, 1), 0), group)
@@ -360,20 +437,18 @@
     step = within // requests
     live_old = owner_ref[...] == request
     column = lax.broadcasted_iota(jnp.int32, (1, fresh.shape[0]), 1)
-    fresh_step = column // requests + first_ref[1] * group
+    fresh_step = column // requests + lax.axis_index("grp") * group
     live_new = (lax.rem(column, requests) == request) & (fresh_step <= step)
-    lane = lax.broadcasted_iota(jnp.int32, (block, SENT - LAT), 1)
     scores = []
-    for i in range(parts):
-        q = q_ref[i * block : (i + 1) * block]
+    for i in range(0, 2 * count, 2):
+        q = jnp.concatenate([q_refs[i][:, :WIDE], q_refs[i + 1][:, :WIDE]], axis=0)
         scores.append(
             (
                 jnp.where(live_old, dot_nt(q, keys), masked_score),
                 jnp.where(live_new, dot_nt(q, fresh), masked_score),
             )
         )
-    for i in range(parts):
-        old, new = scores[i]
+    for i, (old, new) in enumerate(scores):
         highest = jnp.maximum(
             jnp.max(old, axis=-1, keepdims=True), jnp.max(new, axis=-1, keepdims=True)
         )
@@ -386,43 +461,49 @@
         mixed = dot_nn(w_old.astype(bf16), keys[:, :LAT]) + dot_nn(
             w_new.astype(bf16), fresh[:, :LAT]
         )
-        mixed = mixed / safe
         level = jnp.where(some, highest + jnp.log2(safe), masked_score)
-        high = level.astype(bf16).astype(f32)
-        middle = (level - high).astype(bf16).astype(f32)
-        low = level - high - middle
-        tail = jnp.where(
-            lane == 0, high, jnp.where(lane == 1, middle, jnp.where(lane == 2, low, 0.0))
-        )
-        sent_ref[i * block : (i + 1) * block] = jnp.concatenate([mixed, tail], axis=-1).astype(
-            bf16
-        )
-
-
-def pages_attend(place, q_all, keys, fresh, owner, group, requests):
-    smem = pl.BlockSpec(memory_space=pltpu.SMEM)
+        out_ref = keep_ref if 2 * i < count else send_ref
+        both = jnp.concatenate([mixed / safe, split_level(level, block)], axis=-1).astype(bf16)
+        out_ref[2 * i % count] = both[:each]
+        out_ref[2 * i % count + 1] = both[each:]
+
+
+def pages_attend(queries, keys, fresh, owner, group, requests):
+    count = len(queries) // 2
     vmem = pl.BlockSpec(memory_space=pltpu.VMEM)
+    shape = jax.ShapeDtypeStruct((count, queries[0].shape[0], SENT), bf16)
     return pl.pallas_call(
-        functools.partial(pages_kernel, group, requests),
-        in_specs=[smem, vmem, vmem, vmem, vmem],
-        out_specs=vmem,
-        out_shape=jax.ShapeDtypeStruct((q_all.shape[0], SENT), bf16),
-        compiler_params=params(40),
-    )(place, q_all, keys, fresh, owner)
-
-
-def combine_kernel(heads, parts_ref, ve_ref, out_ref, sum_ref):
-    tails = parts_ref[:, :, LAT:].astype(f32)
-    lane = lax.broadcasted_iota(jnp.int32, tails.shape, 2)
-    level = jnp.sum(jnp.where(lane < 3, tails, 0.0), axis=-1, keepdims=True)
-    weights = jnp.exp2(level - jnp.max(level, axis=0, keepdims=True))
-    total = jnp.sum(weights, axis=0)
-    mixed = jnp.sum(parts_ref[:, :, :LAT].astype(f32) * weights, axis=0) / total
-    count = mixed.shape[0] // heads
+        functools.partial(pages_kernel, group, requests, count),
+        in_specs=[vmem] * (2 * count + 3),
+        out_specs=(vmem, vmem),
+        out_shape=(shape, shape),
+        compiler_params=params(),
+    )(*queries, keys, fresh, owner)
+
+
+def merge_kernel(keep_ref, got_ref, *out_refs):
+    for i, out_ref in enumerate(out_refs):
+        mixed, level = merge_parts([keep_ref[i], got_ref[i]])
+        out_ref[...] = jnp.concatenate(
+            [mixed, split_level(level, mixed.shape[0])], axis=-1
+        ).astype(bf16)
+
+
+def merge_pair(keep, got):
+    shape = jax.ShapeDtypeStruct(keep.shape[1:], bf16)
+    return pl.pallas_call(
+        merge_kernel,
+        out_shape=(shape,) * keep.shape[0],
+        compiler_params=params(),
+    )(keep, got)
+
+
+def combine_kernel(heads, count, *refs):
+    ve_ref, out_ref, sum_ref = refs[count:]
+    mixed, _ = merge_parts([ref[...] for ref in refs[:count]])
+    each = mixed.shape[0] // heads
     head_values = [
-        dot_nn(
-            mixed[h * count : (h + 1) * count].astype(bf16), ve_ref[:, h * VH : (h + 1) * VH]
-        )
+        dot_nn(mixed[h * each : (h + 1) * each].astype(bf16), ve_ref[:, h * VH : (h + 1) * VH])
         for h in range(heads)
     ]
     joined = jnp.concatenate(head_values, axis=-1).astype(bf16)
@@ -432,16 +513,17 @@
 def combine(parts, value_expand, mla_output):
     heads = value_expand.shape[1] // VH
     return pl.pallas_call(
-        functools.partial(combine_kernel, heads),
-        out_shape=jax.ShapeDtypeStruct((parts.shape[1] // heads, mla_output.shape[1]), bf16),
-        compiler_params=params(40),
-    )(parts, value_expand, mla_output)
+        functools.partial(combine_kernel, heads, len(parts)),
+        out_shape=jax.ShapeDtypeStruct((parts[0].shape[0] // heads, mla_output.shape[1]), bf16),
+        compiler_params=params(20),
+    )(*parts, value_expand, mla_output)
 
 
 def kda_kernel(
     heads,
     requests,
-    parts_ref,
+    one_ref,
+    two_ref,
     dec_ref,
     inputs_ref,
     beta_ref,
@@ -453,18 +535,23 @@
     states_ref,
     output_ref,
     hidden_ref,
-    sum_ref,
+    keep_ref,
+    send_ref,
     kin,
     projected,
+    by_share,
+    summed_ref,
 ):
     part = pl.program_id(0)
-    shares, rows, share = hidden_ref.shape
+    shares, rows, share = by_share.shape
+    grp = lax.axis_index("grp")
 
     @pl.when(part == 0)
     def _():
-        hidden = dec_ref[...].astype(f32) + jnp.sum(parts_ref[...].astype(f32), axis=0)
+        hidden = dec_ref[...].astype(f32) + one_ref[...] + two_ref[...]
         for g in range(shares):
-            hidden_ref[g] = hidden[:, g * share : (g + 1) * share]
+            by_share[g] = hidden[:, g * share : (g + 1) * share]
+        hidden_ref[...] = by_share[grp]
         kin[...] = norm_rows(hidden).astype(bf16)
 
     projected[part] = dot_nn(kin[...], inputs_ref[0])
@@ -529,21 +616,29 @@
         mixed = jnp.concatenate(blended, axis=-1).astype(bf16)
         summed = dot_nn(mixed, output_ref[...])
         for g in range(shares):
-            sum_ref[g] = summed[:, g * share : (g + 1) * share].astype(bf16)
-
-
-def kda(parts, dec, inputs, beta_t, decay_down, decay_up, gate_down, gate_up, rate, states, output):
-    shares, rows, width = parts.shape
+            summed_ref[g] = summed[:, g * share : (g + 1) * share]
+        core = lax.rem(grp, 2)
+        for by in range(shares // 2):
+            pair = 2 * lax.rem(grp // 2 + by, shares // 2)
+            keep_ref[by] = summed_ref[pair + core]
+            send_ref[by] = summed_ref[pair + 1 - core].astype(bf16)
+
+
+def kda(shares, one, two, dec, inputs, beta_t, decay_down, decay_up, gate_down, gate_up, rate, states, output):
+    rows, width = dec.shape
     heads = beta_t.shape[0]
     requests = states.shape[1]
     columns = inputs.shape[2]
     whole = lambda a: pl.BlockSpec(a.shape, lambda i: (0,) * len(a.shape))
-    share_spec = pl.BlockSpec((shares, rows, width // shares), lambda i: (0, 0, 0))
+    share = width // shares
+    sides = shares // 2
+    held = lambda shape: pl.BlockSpec(shape, lambda i: (0,) * len(shape))
     return pl.pallas_call(
         functools.partial(kda_kernel, heads, requests),
         grid=(3,),
         in_specs=[
-            whole(parts),
+            whole(one),
+            whole(two),
             whole(dec),
             pl.BlockSpec((1, width, columns), lambda i: (i, 0, 0)),
             whole(beta_t),
@@ -555,14 +650,20 @@
             whole(states),
             whole(output),
         ],
-        out_specs=(share_spec, share_spec),
+        out_specs=(held((rows, share)), held((sides, rows, share)), held((sides, rows, share))),
         out_shape=(
-            jax.ShapeDtypeStruct((shares, rows, width // shares), f32),
-            jax.ShapeDtypeStruct((shares, rows, width // shares), bf16),
+            jax.ShapeDtypeStruct((rows, share), f32),
+            jax.ShapeDtypeStruct((sides, rows, share), f32),
+            jax.ShapeDtypeStruct((sides, rows, share), bf16),
         ),
-        scratch_shapes=[pltpu.VMEM((rows, width), bf16), pltpu.VMEM((3, rows, columns), f32)],
-        compiler_params=params(48),
-    )(parts, dec, inputs, beta_t, decay_down, decay_up, gate_down, gate_up, rate, states, output)
+        scratch_shapes=[
+            pltpu.VMEM((rows, width), bf16),
+            pltpu.VMEM((3, rows, columns), f32),
+            pltpu.VMEM((shares, rows, share), f32),
+            pltpu.VMEM((shares, rows, share), f32),
+        ],
+        compiler_params=params(),
+    )(one, two, dec, inputs, beta_t, decay_down, decay_up, gate_down, gate_up, rate, states, output)
 
 
 def shards(
@@ -596,24 +697,26 @@
     decode_rows = steps * requests
     share = width // grp_size
     dec = decode_input.reshape(decode_rows, width)
-    place = jnp.stack([seq_index, grp_index]).astype(jnp.int32)
-
-    own_latent, fresh, q_prefill, q_decode, own_tokens = front(
-        place,
-        prompt_len,
-        x_group,
-        dec,
-        latent_proj.T,
-        query_proj,
-        key_expand,
-        latent_pages[0],
-        seq_size,
-        grp_size,
-    )
-    mine = lax.all_gather(own_latent, "seq", axis=0, tiled=True)
-    other = lax.ppermute(mine, "grp", [(g, g ^ 1) for g in range(grp_size)])
+
+    own_tokens = slice_pages(latent_pages[0], grp_size)
+    x_rows, own_tokens = lax.optimization_barrier((x_group, own_tokens))
+    own_latent, fresh, q_prefill, q_decode = front(
+        prompt_len, x_rows, dec, latent_proj.T, query_proj, key_expand, seq_size
+    )
+    sides = grp_size // 2
+
+    def shift(value, by):
+        return lax.ppermute(
+            value, "grp", [(g, (g + 2 * by) % grp_size) for g in range(grp_size)]
+        )
+
+    def swap(value):
+        return lax.ppermute(value, "grp", [(g, g ^ 1) for g in range(grp_size)])
 
     arrived = lax.all_to_all(own_tokens, "seq", split_axis=0, concat_axis=0, tiled=True)
+    own_latent, arrived = lax.optimization_barrier((own_latent, arrived))
+    mine = lax.all_to_all(own_latent, "seq", split_axis=0, concat_axis=0, tiled=True)
+    mine = mine.reshape(-1, SENT)
     _, slots, tokens, _ = own_tokens.shape
     page_keys = arrived.reshape(seq_size * slots * tokens, WIDE)
     core = grp_index % 2
@@ -630,19 +733,40 @@
         held[..., None] & (token_pos < lengths[..., None]), owner[..., None], -1
     ).reshape(1, -1)
 
+    queries = [q_decode] + [shift(q_decode, by) for by in range(1, sides)]
+    queries += [swap(q) for q in queries]
+    keep, send = pages_attend(
+        queries, page_keys, fresh, key_owner, decode_rows, requests
+    )
+    merged = merge_pair(keep, swap(send))
+    state_rows, mine = lax.optimization_barrier((kda_state, mine))
     states = lax.all_to_all(
-        kda_state.astype(bf16), "seq", split_axis=0, concat_axis=0, tiled=True
+        state_rows.astype(bf16), "seq", split_axis=0, concat_axis=0, tiled=True
     ).reshape((seq_size, requests) + kda_state.shape[1:])
-
-    q_all = lax.all_gather(q_decode, "grp", axis=0, tiled=True)
-    partial = pages_attend(place, q_all, page_keys, fresh, key_owner, decode_rows, requests)
-    partial = lax.all_to_all(
-        partial.reshape(grp_size, -1, SENT), "grp", split_axis=0, concat_axis=0, tiled=True
-    )
+    partial = [merged[0]] + [shift(merged[by], -by) for by in range(1, sides)]
     mla_part = combine(partial, value_expand, mla_output)
-    mla_parts = lax.all_gather(mla_part, "grp", axis=0, tiled=False)
-    hidden, kda_part = kda(
-        mla_parts,
+    mine, mla_part = lax.optimization_barrier((mine, mla_part))
+    mla_half = mla_part.astype(f32)
+    for by in range(1, sides):
+        mla_half = mla_half + shift(mla_part, by).astype(f32)
+    mla_rest = swap(mla_half)
+
+    prefill_part = prefill_attend(
+        q_prefill, mine, swap(mine), key_expand, value_expand, mla_output, grp_size
+    )
+    mla_half, mla_rest, prefill_part = lax.optimization_barrier(
+        (mla_half, mla_rest, prefill_part)
+    )
+    prefill_parts = lax.all_to_all(
+        prefill_part, "grp", split_axis=0, concat_axis=0, tiled=True
+    )
+    own_columns = lax.dynamic_slice_in_dim(x_group, grp_index * share, share, 1)
+    prefill_out = gather_share(prefill_parts, own_columns).T
+
+    hidden_share, keep, send = kda(
+        grp_size,
+        mla_half,
+        mla_rest,
         dec,
         kda_inputs.transpose(1, 0, 2),
         kda_beta.T,
@@ -654,18 +778,12 @@
         states,
         kda_output,
     )
-    kda_parts = lax.all_to_all(kda_part, "grp", split_axis=0, concat_axis=0, tiled=True)
-    hidden_share = lax.dynamic_index_in_dim(hidden, grp_index, 0, keepdims=False)
-    decode_out = (hidden_share + jnp.sum(kda_parts.astype(f32), axis=0)).astype(bf16)
-
-    prefill_part = prefill_attend(
-        place, q_prefill, mine, other, key_expand, value_expand.T, mla_output, grp_size
-    )
-    prefill_parts = lax.all_to_all(
-        prefill_part, "grp", split_axis=0, concat_axis=0, tiled=True
-    )
-    own_columns = lax.dynamic_slice_in_dim(x_group, grp_index * share, share, 1)
-    prefill_out = gather_share(prefill_parts, own_columns).T
+    crossing = swap(send)
+    kda_total = keep[0] + crossing[0].astype(f32)
+    for by in range(1, sides):
+        pair = keep[by] + crossing[by].astype(f32)
+        kda_total = kda_total + shift(pair.astype(bf16), by).astype(f32)
+    decode_out = (hidden_share + kda_total).astype(bf16)
     return (prefill_out, decode_out.reshape(steps, requests, share))
 
 

time: 236 us -> 127 us (0.54)
  the two profiles are of different devices: /device:TPU:96 before, /device:TPU:0 now
where the time goes in v3:
time: 127 us
  starting transfers between devices  42.5 us (33%)
  Pallas kernels  38.3 us (30%)
  waiting for transfers between devices  32.4 us (26%)
  local copies, waits for them, and re-layouts  7.09 us (6%)
  other arithmetic  5.42 us (4%)
    ppermute x12, starting transfers between devices, shift(): lax.ppermute(value, 'grp', [(g, (g + 2 * by) % grp_size) for g in range(g...  21.7 us
    ppermute x12, waiting for transfers between devices, shift(): lax.ppermute(value, 'grp', [(g, (g + 2 * by) % grp_size) for g in range(g...  9.76 us
    all_to_all x1, waiting for transfers between devices, shards(): lax.all_to_all(state_rows.astype(bf16), 'seq', split_axis=0, concat_axis=...  8.88 us
    pallas_call x1, Pallas kernels, front(): pl.pallas_call(front_kernel, in_specs=[smem, vmem, vmem] + [hbm] * 5, out...  8.67 us
    pallas_call x1, Pallas kernels, prefill_attend(): pl.pallas_call(functools.partial(flash_kernel, heads), grid=(keys // side...  8.59 us
    pallas_call x1, Pallas kernels, kda(): pl.pallas_call(functools.partial(kda_kernel, heads, requests), grid=(3,),...  8.51 us
    all_to_all x1, waiting for transfers between devices, shards(): lax.all_to_all(own_tokens, 'seq', split_axis=0, concat_axis=0, tiled=True)  8.18 us
    all_to_all x1, starting transfers between devices, shards(): lax.all_to_all(own_tokens, 'seq', split_axis=0, concat_axis=0, tiled=True)  8.14 us
  transfers between devices with their start and end apart: 24, of which 13 were waited for; matrix products, arithmetic and copies ran while one was open for 7% of the time, Pallas kernels for 27%

profile of v3, /device:TPU:0, one launch (start us, length us, event | category | flops | bytes accessed | tf_op | source)
XLA Modules:
  0.0 126.6 jit_solution(1396323226535661728)
XLA Ops:
  0.6 2.1 %shard_map.224 = bf16[16,3,16,576]{3,2,1,0:T(8,128)(2,1)} custom-call(bf16[16,6,64,576]{3,2,1,0:T(8,128)(2,1)} %bitcast.49), custom_call_target="tpu_custom_call" | custom-call | tf_op jit(solution)/shard_map/pallas_call | solution.py:102
  2.7 8.1 %all-to-all-start = ((bf16[16,3,16,576]{3,2,1,0:T(8,128)(2,1)}), bf16[16,3,16,576]{3,2,1,0:T(8,128)(2,1)S(1)}, u32[]{:S(2)}, u32[]{:S(2)}) async-start(bf16[16,3,16,576]{3,2,1,0:T(8,128)(2,1)} %shard_map.224), calls=%async_computation | async-start | bytes 1966080 | tf_op jit(solution)/shard_map/all_to_all | solution.py:716
  10.9 8.7 %shard_map.225 = (bf16[16,128,640]{2,1,0:T(8,128)(2,1)}, bf16[32,576]{1,0:T(8,128)(2,1)}, bf16[4,256,192]{2,1,0:T(8,128)(2,1)}, bf16[96,640]{1,0:T(8,128)(2,1)}) custom-call(s32[8]{0:T(128)} %lengths_ref.1, f32[2,771,64]{2,1,0:T(8,128)} %constant.64.clone.fine_ref, f32[2,16,64]{2,1,0:T(8,128)} %constant.65.clone.coarse_ref, bf16[256,2304]{1,0:T(8,128)(2,1)} %x_hbm, ...), custom_call_target="tpu_custom_call" | custom-call | tf_op jit(solution)/shard_map/pallas_call | solution.py:241
  19.6 8.2 %all-to-all-done = bf16[16,3,16,576]{3,2,1,0:T(8,128)(2,1)S(1)} async-done(((bf16[16,3,16,576]{3,2,1,0:T(8,128)(2,1)}), bf16[16,3,16,576]{3,2,1,0:T(8,128)(2,1)S(1)}, u32[]{:S(2)}, u32[]{:S(2)}) %all-to-all-start) | async-done | bytes 884768 | tf_op jit(solution)/shard_map/all_to_all | solution.py:716
  27.8 0.9 copy-done.5
  28.7 4.5 %all-to-all-start.1 = ((bf16[16,128,640]{2,1,0:T(8,128)(2,1)}), bf16[16,128,640]{2,1,0:T(8,128)(2,1)}, u32[]{:S(2)}, u32[]{:S(2)}) async-start(bf16[16,128,640]{2,1,0:T(8,128)(2,1)} %get-tuple-element.29), calls=%async_computation.1 | async-start | bytes 5242880 | tf_op jit(solution)/shard_map/all_to_all | solution.py:718
  33.2 1.6 %collective-permute-start = (bf16[96,640]{1,0:T(8,128)(2,1)S(1)}, bf16[96,640]{1,0:T(8,128)(2,1)S(1)}, u32[]{:S(2)}, u32[]{:S(2)}) collective-permute-start(bf16[96,640]{1,0:T(8,128)(2,1)S(1)} %copy-done.9), channel_id=1, source_target_pairs={{0,2},{1,3},{2,4},{3,5},{4,6},{5,7},{6,0},{7,1},{8,10},{9,11},{10,... | collective-permute-start | bytes 368648 | tf_op jit(solution)/shard_map/ppermute | solution.py:709
  34.8 2.7 %collective-permute-start.1 = (bf16[96,640]{1,0:T(8,128)(2,1)S(1)}, bf16[96,640]{1,0:T(8,128)(2,1)S(1)}, u32[]{:S(2)}, u32[]{:S(2)}) collective-permute-start(bf16[96,640]{1,0:T(8,128)(2,1)S(1)} %copy-done.9), channel_id=1, source_target_pairs={{0,4},{1,5},{2,6},{3,7},{4,0},{5,1},{6,2},{7,3},{8,12},{9,13},{10,... | collective-permute-start | bytes 368648 | tf_op jit(solution)/shard_map/ppermute | solution.py:709
  37.5 1.4 %collective-permute-start.2 = (bf16[96,640]{1,0:T(8,128)(2,1)S(1)}, bf16[96,640]{1,0:T(8,128)(2,1)S(1)}, u32[]{:S(2)}, u32[]{:S(2)}) collective-permute-start(bf16[96,640]{1,0:T(8,128)(2,1)S(1)} %copy-done.9), channel_id=1, source_target_pairs={{0,6},{1,7},{2,0},{3,1},{4,2},{5,3},{6,4},{7,5},{8,14},{9,15},{10,... | collective-permute-start | bytes 368648 | tf_op jit(solution)/shard_map/ppermute | solution.py:709
  39.4 0.6 collective-permute-done.refs_1_
  40.0 1.7 %collective-permute-done.1.refs_2_ = bf16[96,640]{1,0:T(8,128)(2,1)S(1)} collective-permute-done((bf16[96,640]{1,0:T(8,128)(2,1)S(1)}, bf16[96,640]{1,0:T(8,128)(2,1)S(1)}, u32[]{:S(2)}, u32[]{:S(2)}) %collective-permute-start.1) | collective-permute-done | bytes 122912 | tf_op jit(solution)/shard_map/ppermute | solution.py:709
  41.7 0.7 collective-permute-done.2.refs_3_
  42.5 0.7 select_n.61.refs_10_
  43.2 0.6 collective-permute-done.6.refs_7_
  43.9 5.2 %shard_map.226 = (bf16[4,96,640]{2,1,0:T(8,128)(2,1)}, bf16[4,96,640]{2,1,0:T(8,128)(2,1)}) custom-call(bf16[96,640]{1,0:T(8,128)(2,1)} %get-tuple-element.31.refs_0_, bf16[96,640]{1,0:T(8,128)(2,1)} %copy-done.10, bf16[96,640]{1,0:T(8,128)(2,1)} %copy-done.11, bf16[96,640]{1,0:T(8,128)(2,1)} %copy-done.12, bf16[96,640]{1,0:T(8,128)(2,1)} %copy-done.13, ...), custom_call_target="tpu_custom_call" | custom-call | tf_op jit(solution)/shard_map/pallas_call | solution.py:475
  49.1 0.5 collective-permute-start.7
  49.6 1.7 %collective-permute-done.7.got_ref = bf16[4,96,640]{2,1,0:T(8,128)(2,1)S(1)} collective-permute-done((bf16[4,96,640]{2,1,0:T(8,128)(2,1)}, bf16[4,96,640]{2,1,0:T(8,128)(2,1)S(1)}, u32[]{:S(2)}, u32[]{:S(2)}) %collective-permute-start.7) | collective-permute-done | bytes 491552 | tf_op jit(solution)/shard_map/ppermute | solution.py:714
  51.3 0.8 copy-done.7
  52.1 2.2 %shard_map.227 = (bf16[96,640]{1,0:T(8,128)(2,1)}, bf16[96,640]{1,0:T(8,128)(2,1)}, bf16[96,640]{1,0:T(8,128)(2,1)}, bf16[96,640]{1,0:T(8,128)(2,1)}) custom-call(bf16[4,96,640]{2,1,0:T(8,128)(2,1)} %get-tuple-element.34.keep_ref, bf16[4,96,640]{2,1,0:T(8,128)(2,1)} %copy-done.7), custom_call_target="tpu_custom_call" | custom-call | tf_op jit(solution)/shard_map/pallas_call | solution.py:494
  54.3 1.2 collective-permute-start.10
  55.5 2.0 %collective-permute-start.8 = (bf16[96,640]{1,0:T(8,128)(2,1)}, bf16[96,640]{1,0:T(8,128)(2,1)S(1)}, u32[]{:S(2)}, u32[]{:S(2)}) collective-permute-start(bf16[96,640]{1,0:T(8,128)(2,1)} %get-tuple-element.37), channel_id=1, source_target_pairs={{0,6},{1,7},{2,0},{3,1},{4,2},{5,3},{6,4},{7,5},{8,14},{9,15},{10,... | collective-permute-start | bytes 368648 | tf_op jit(solution)/shard_map/ppermute | solution.py:709
  57.6 1.0 collective-permute-start.9
  58.6 2.7 %collective-permute-done.10.refs_3_ = bf16[96,640]{1,0:T(8,128)(2,1)S(1)} collective-permute-done((bf16[96,640]{1,0:T(8,128)(2,1)}, bf16[96,640]{1,0:T(8,128)(2,1)S(1)}, u32[]{:S(2)}, u32[]{:S(2)}) %collective-permute-start.10) | collective-permute-done | bytes 122912 | tf_op jit(solution)/shard_map/ppermute | solution.py:709
  61.3 2.0 %collective-permute-done.8.refs_1_ = bf16[96,640]{1,0:T(8,128)(2,1)S(1)} collective-permute-done((bf16[96,640]{1,0:T(8,128)(2,1)}, bf16[96,640]{1,0:T(8,128)(2,1)S(1)}, u32[]{:S(2)}, u32[]{:S(2)}) %collective-permute-start.8) | collective-permute-done | bytes 122912 | tf_op jit(solution)/shard_map/ppermute | solution.py:709
  63.4 1.5 %collective-permute-done.9.refs_2_ = bf16[96,640]{1,0:T(8,128)(2,1)S(1)} collective-permute-done((bf16[96,640]{1,0:T(8,128)(2,1)}, bf16[96,640]{1,0:T(8,128)(2,1)S(1)}, u32[]{:S(2)}, u32[]{:S(2)}) %collective-permute-start.9) | collective-permute-done | bytes 122912 | tf_op jit(solution)/shard_map/ppermute | solution.py:709
  64.8 0.9 copy-done.2
  65.7 0.7 shard_map.228
  66.5 2.2 %all-to-all-done.1 = bf16[16,128,640]{2,1,0:T(8,128)(2,1)} async-done(((bf16[16,128,640]{2,1,0:T(8,128)(2,1)}), bf16[16,128,640]{2,1,0:T(8,128)(2,1)}, u32[]{:S(2)}, u32[]{:S(2)}) %all-to-all-start.1) | async-done | bytes 2621472 | tf_op jit(solution)/shard_map/all_to_all | solution.py:718
  68.6 1.5 %collective-permute-start.11 = (bf16[24,2304]{1,0:T(8,128)(2,1)S(1)}, bf16[24,2304]{1,0:T(8,128)(2,1)S(1)}, u32[]{:S(2)}, u32[]{:S(2)}) collective-permute-start(bf16[24,2304]{1,0:T(8,128)(2,1)S(1)} %shard_map.228), channel_id=1, source_target_pairs={{0,2},{1,3},{2,4},{3,5},{4,6},{5,7},{6,0},{7,1},{8,10},{9,11},{10,... | collective-permute-start | bytes 331784 | tf_op jit(solution)/shard_map/ppermute | solution.py:709
  70.1 2.7 %collective-permute-start.12 = (bf16[24,2304]{1,0:T(8,128)(2,1)S(1)}, bf16[24,2304]{1,0:T(8,128)(2,1)S(1)}, u32[]{:S(2)}, u32[]{:S(2)}) collective-permute-start(bf16[24,2304]{1,0:T(8,128)(2,1)S(1)} %shard_map.228), channel_id=1, source_target_pairs={{0,4},{1,5},{2,6},{3,7},{4,0},{5,1},{6,2},{7,3},{8,12},{9,13},{10,... | collective-permute-start | bytes 331784 | tf_op jit(solution)/shard_map/ppermute | solution.py:709
  72.8 1.4 %collective-permute-start.13 = (bf16[24,2304]{1,0:T(8,128)(2,1)S(1)}, bf16[24,2304]{1,0:T(8,128)(2,1)S(1)}, u32[]{:S(2)}, u32[]{:S(2)}) collective-permute-start(bf16[24,2304]{1,0:T(8,128)(2,1)S(1)} %shard_map.228), channel_id=1, source_target_pairs={{0,6},{1,7},{2,0},{3,1},{4,2},{5,3},{6,4},{7,5},{8,14},{9,15},{10,... | collective-permute-start | bytes 331784 | tf_op jit(solution)/shard_map/ppermute | solution.py:709
  74.3 2.8 %convert_element_type.65 = bf16[128,4,8,128]{3,2,1,0:T(8,128)(2,1)} convert(f32[128,4,8,128]{3,2,1,0:T(8,128)} %param.28) | non-fusion elementwise | flops 524288 | bytes 3145728 | tf_op jit(solution)/shard_map/convert_element_type | solution.py:744
  77.1 3.7 %all-to-all-start.3 = ((bf16[128,4,8,128]{3,2,1,0:T(8,128)(2,1)}), bf16[128,4,8,128]{3,2,1,0:T(8,128)(2,1)S(1)}, u32[]{:S(2)}, u32[]{:S(2)}) async-start(bf16[128,4,8,128]{3,2,1,0:T(8,128)(2,1)} %convert_element_type.65), calls=%async_computation.3 | async-start | bytes 2097152 | tf_op jit(solution)/shard_map/all_to_all | solution.py:743
  81.0 8.6 %shard_map.229 = bf16[8,576,128]{2,1,0:T(8,128)(2,1)} custom-call(bf16[4,256,192]{2,1,0:T(8,128)(2,1)} %get-tuple-element.41.q_ref, bf16[2048,640]{1,0:T(8,128)(2,1)} %bitcast.3.mine_ref, bf16[2048,640]{1,0:T(8,128)(2,1)} %collective-permute-done.15.other_ref, bf16[512,512]{1,0:T(8,128)(2,1)} %ke_ref.1, bf16[512,512]{1,0:T(8,128)(2,1)} %ve_ref.1, ...), custom_call_target="tpu_custom_call" | custom-call | tf_op jit(solution)/shard_map/pallas_call | solution.py:355
  89.6 8.9 %all-to-all-done.3 = bf16[128,4,8,128]{3,2,1,0:T(8,128)(2,1)S(1)} async-done(((bf16[128,4,8,128]{3,2,1,0:T(8,128)(2,1)}), bf16[128,4,8,128]{3,2,1,0:T(8,128)(2,1)S(1)}, u32[]{:S(2)}, u32[]{:S(2)}) %all-to-all-start.3) | async-done | bytes 1048608 | tf_op jit(solution)/shard_map/all_to_all | solution.py:743
  98.5 3.6 %all-to-all-start.2 = ((bf16[8,576,128]{2,1,0:T(8,128)(2,1)}), bf16[8,576,128]{2,1,0:T(8,128)(2,1)S(1)}, u32[]{:S(2)}, u32[]{:S(2)}) async-start(bf16[8,576,128]{2,1,0:T(8,128)(2,1)} %shard_map.229), calls=%async_computation.2 | async-start | bytes 2359296 | tf_op jit(solution)/shard_map/all_to_all | solution.py:760
  102.1 0.6 broadcast_in_dim.35
  102.7 8.5 %shard_map.231 = (f32[24,288]{1,0:T(8,128)}, f32[4,24,288]{2,1,0:T(8,128)}, bf16[4,24,288]{2,1,0:T(8,128)(2,1)}) custom-call(f32[24,2304]{1,0:T(8,128)} %copy-done.6, f32[24,2304]{1,0:T(8,128)} %copy-done.8, bf16[24,2304]{1,0:T(8,128)(2,1)} %bitcast.55, bf16[3,2304,512]{2,1,0:T(8,128)(2,1)} %bitcast.50, bf16[4,2304]{1,0:T(4,128)(2,1)} %bitcast.57, ...), custom_call_target="tpu_custom_call" | custom-call | tf_op jit(solution)/shard_map/pallas_call | solution.py:636
  111.6 1.1 collective-permute-done.16
  112.7 0.8 fusion.6
  113.6 1.9 %collective-permute-start.17 = (bf16[24,288]{1,0:T(8,128)(2,1)S(1)}, bf16[24,288]{1,0:T(8,128)(2,1)S(1)}, u32[]{:S(2)}, u32[]{:S(2)}) collective-permute-start(bf16[24,288]{1,0:T(8,128)(2,1)S(1)} %get-tuple-element.50), channel_id=1, source_target_pairs={{0,2},{1,3},{2,4},{3,5},{4,6},{5,7},{6,0},{7,1},{8,10},{9,11},{10,... | collective-permute-start | bytes 41480 | tf_op jit(solution)/shard_map/ppermute | solution.py:709
  115.5 2.7 %collective-permute-start.18 = (bf16[24,288]{1,0:T(8,128)(2,1)S(1)}, bf16[24,288]{1,0:T(8,128)(2,1)S(1)}, u32[]{:S(2)}, u32[]{:S(2)}) collective-permute-start(bf16[24,288]{1,0:T(8,128)(2,1)S(1)} %get-tuple-element.52), channel_id=1, source_target_pairs={{0,4},{1,5},{2,6},{3,7},{4,0},{5,1},{6,2},{7,3},{8,12},{9,13},{10,... | collective-permute-start | bytes 41480 | tf_op jit(solution)/shard_map/ppermute | solution.py:709
  118.2 1.4 %collective-permute-start.19 = (bf16[24,288]{1,0:T(8,128)(2,1)S(1)}, bf16[24,288]{1,0:T(8,128)(2,1)S(1)}, u32[]{:S(2)}, u32[]{:S(2)}) collective-permute-start(bf16[24,288]{1,0:T(8,128)(2,1)S(1)} %get-tuple-element.51), channel_id=1, source_target_pairs={{0,6},{1,7},{2,0},{3,1},{4,2},{5,3},{6,4},{7,5},{8,14},{9,15},{10,... | collective-permute-start | bytes 41480 | tf_op jit(solution)/shard_map/ppermute | solution.py:709
  119.7 1.8 %constant_dynamic-slice_fusion.x_ref = bf16[256,288]{1,0:T(8,128)(2,1)} fusion(bf16[256,2304]{1,0:T(8,128)(2,1)} %x_hbm, s32[]{:T(128)S(6)} %select_n.62), kind=kLoop, calls=%fused_computation.31 | loop fusion | bytes 294916 | tf_op jit(solution)/shard_map/dynamic_slice | solution.py:763
  121.4 0.6 collective-permute-done.19
  122.0 1.4 %fusion.9 = bf16[3,8,288]{2,1,0:T(8,128)(2,1)} fusion(f32[24,288]{1,0:T(8,128)} %get-tuple-element.47, bf16[24,288]{1,0:T(8,128)(2,1)S(1)} %collective-permute-done.19, bf16[24,288]{1,0:T(8,128)(2,1)S(1)} %collective-permute-done.18, bf16[24,288]{1,0:T(8,128)(2,1)S(1)} %collective-permute-done.17, f32[4,24,288]{2,1,0:T(8,128)} %get-tuple-element.48, ...), kind=kLoop, calls=%fused_computation.15 | loop fusion | flops 69120 | bytes 124416 | tf_op jit(solution)/shard_map/reshape | solution.py:787
  123.4 1.1 copy-done.3
  124.5 2.2 %shard_map.230 = bf16[288,256]{1,0:T(8,128)(2,1)} custom-call(bf16[8,576,128]{2,1,0:T(8,128)(2,1)} %copy-done.3, bf16[256,288]{1,0:T(8,128)(2,1)} %constant_dynamic-slice_fusion.x_ref), custom_call_target="tpu_custom_call" | custom-call | tf_op jit(solution)/shard_map/pallas_call | solution.py:396
  (62 shorter events, 1.2 us)
Async XLA Ops:
  2.7 25.0 %all-to-all-start = ((bf16[16,3,16,576]{3,2,1,0:T(8,128)(2,1)}), bf16[16,3,16,576]{3,2,1,0:T(8,128)(2,1)S(1)}, u32[]{:S(2)}, u32[]{:S(2)}) async-start(bf16[16,3,16,576]{3,2,1,0:T(8,128)(2,1)} %shard_map.224), calls=%async_computation | async-start | bytes 1966080 | tf_op jit(solution)/shard_map/all_to_all | solution.py:716
  27.7 1.0 copy-start.5
  27.7 5.4 %copy-start.9 = (bf16[96,640]{1,0:T(8,128)(2,1)S(1)}, bf16[96,640]{1,0:T(8,128)(2,1)}, u32[]{:S(2)}) copy-start(bf16[96,640]{1,0:T(8,128)(2,1)} %get-tuple-element.31.refs_0_) | copy-start | bytes 368644
  27.7 11.2 %copy-start.14 = (s32[16,1,6]{0,1,2:T(1,128)S(1)}, s32[16,1,6]{0,1,2:T(1,128)}, u32[]{:S(2)}) copy-start(s32[16,1,6]{0,1,2:T(1,128)} %param.26) | copy-start | bytes 1156
  27.8 11.3 %copy-start.15 = (s32[8]{0:T(128)S(1)}, s32[8]{0:T(128)}, u32[]{:S(2)}) copy-start(s32[8]{0:T(128)} %lengths_ref.1) | copy-start | bytes 100
  27.8 11.6 %copy-start.16 = (s32[16,1]{0,1:T(1,128)S(1)}, s32[16,1]{0,1:T(1,128)}, u32[]{:S(2)}) copy-start(s32[16,1]{0,1:T(1,128)} %param.27) | copy-start | bytes 196
  28.7 39.9 %all-to-all-start.1 = ((bf16[16,128,640]{2,1,0:T(8,128)(2,1)}), bf16[16,128,640]{2,1,0:T(8,128)(2,1)}, u32[]{:S(2)}, u32[]{:S(2)}) async-start(bf16[16,128,640]{2,1,0:T(8,128)(2,1)} %get-tuple-element.29), calls=%async_computation.1 | async-start | bytes 5242880 | tf_op jit(solution)/shard_map/all_to_all | solution.py:718
  33.2 31.7 %copy-start = (bf16[512,2304]{1,0:T(8,128)(2,1)S(1)}, bf16[512,2304]{1,0:T(8,128)(2,1)}, u32[]{:S(2)}) copy-start(bf16[512,2304]{1,0:T(8,128)(2,1)} %out_hbm.1) | copy-start | bytes 7077892
  33.2 31.7 %copy-start.1 = (bf16[512,512]{1,0:T(8,128)(2,1)S(1)}, bf16[512,512]{1,0:T(8,128)(2,1)}, u32[]{:S(2)}) copy-start(bf16[512,512]{1,0:T(8,128)(2,1)} %ve_ref.1) | copy-start | bytes 1572868
  33.2 6.8 %collective-permute-start = (bf16[96,640]{1,0:T(8,128)(2,1)S(1)}, bf16[96,640]{1,0:T(8,128)(2,1)S(1)}, u32[]{:S(2)}, u32[]{:S(2)}) collective-permute-start(bf16[96,640]{1,0:T(8,128)(2,1)S(1)} %copy-done.9), channel_id=1, source_target_pairs={{0,2},{1,3},{2,4},{3,5},{4,6},{5,7},{6,0},{7,1},{8,10},{9,11},{10,... | collective-permute-start | bytes 368648 | tf_op jit(solution)/shard_map/ppermute | solution.py:709
  34.8 6.9 %collective-permute-start.1 = (bf16[96,640]{1,0:T(8,128)(2,1)S(1)}, bf16[96,640]{1,0:T(8,128)(2,1)S(1)}, u32[]{:S(2)}, u32[]{:S(2)}) collective-permute-start(bf16[96,640]{1,0:T(8,128)(2,1)S(1)} %copy-done.9), channel_id=1, source_target_pairs={{0,4},{1,5},{2,6},{3,7},{4,0},{5,1},{6,2},{7,3},{8,12},{9,13},{10,... | collective-permute-start | bytes 368648 | tf_op jit(solution)/shard_map/ppermute | solution.py:709
  37.5 4.9 %collective-permute-start.2 = (bf16[96,640]{1,0:T(8,128)(2,1)S(1)}, bf16[96,640]{1,0:T(8,128)(2,1)S(1)}, u32[]{:S(2)}, u32[]{:S(2)}) collective-permute-start(bf16[96,640]{1,0:T(8,128)(2,1)S(1)} %copy-done.9), channel_id=1, source_target_pairs={{0,6},{1,7},{2,0},{3,1},{4,2},{5,3},{6,4},{7,5},{8,14},{9,15},{10,... | collective-permute-start | bytes 368648 | tf_op jit(solution)/shard_map/ppermute | solution.py:709
  38.9 4.3 %collective-permute-start.3 = (bf16[96,640]{1,0:T(8,128)(2,1)S(1)}, bf16[96,640]{1,0:T(8,128)(2,1)S(1)}, u32[]{:S(2)}, u32[]{:S(2)}) collective-permute-start(bf16[96,640]{1,0:T(8,128)(2,1)S(1)} %copy-done.9), channel_id=1, source_target_pairs={{0,1},{1,0},{2,3},{3,2},{4,5},{5,4},{6,7},{7,6},{8,9},{9,8},{10,11... | collective-permute-start | bytes 368648 | tf_op jit(solution)/shard_map/ppermute | solution.py:714
  40.0 3.9 %copy-start.10 = (bf16[96,640]{1,0:T(8,128)(2,1)}, bf16[96,640]{1,0:T(8,128)(2,1)S(1)}, u32[]{:S(2)}) copy-start(bf16[96,640]{1,0:T(8,128)(2,1)S(1)} %collective-permute-done.refs_1_) | copy-start | bytes 368644
  40.0 3.2 %collective-permute-start.4 = (bf16[96,640]{1,0:T(8,128)(2,1)S(1)}, bf16[96,640]{1,0:T(8,128)(2,1)}, u32[]{:S(2)}, u32[]{:S(2)}) collective-permute-start(bf16[96,640]{1,0:T(8,128)(2,1)S(1)} %collective-permute-done.refs_1_), channel_id=1, source_target_pairs={{0,1},{1,0},{2,3},{3,2},{4,5},{5,4},{6,7},{7,6},{8,9},{9,8},{10,11... | collective-permute-start | bytes 368648 | tf_op jit(solution)/shard_map/ppermute | solution.py:714
  41.7 2.2 %copy-start.11 = (bf16[96,640]{1,0:T(8,128)(2,1)}, bf16[96,640]{1,0:T(8,128)(2,1)S(1)}, u32[]{:S(2)}) copy-start(bf16[96,640]{1,0:T(8,128)(2,1)S(1)} %collective-permute-done.1.refs_2_) | copy-start | bytes 368644
  41.7 1.5 %collective-permute-start.5 = (bf16[96,640]{1,0:T(8,128)(2,1)S(1)}, bf16[96,640]{1,0:T(8,128)(2,1)}, u32[]{:S(2)}, u32[]{:S(2)}) collective-permute-start(bf16[96,640]{1,0:T(8,128)(2,1)S(1)} %collective-permute-done.1.refs_2_), channel_id=1, source_target_pairs={{0,1},{1,0},{2,3},{3,2},{4,5},{5,4},{6,7},{7,6},{8,9},{9,8},{10,11... | collective-permute-start | bytes 368648 | tf_op jit(solution)/shard_map/ppermute | solution.py:714
  42.4 1.5 %copy-start.12 = (bf16[96,640]{1,0:T(8,128)(2,1)}, bf16[96,640]{1,0:T(8,128)(2,1)S(1)}, u32[]{:S(2)}) copy-start(bf16[96,640]{1,0:T(8,128)(2,1)S(1)} %collective-permute-done.2.refs_3_) | copy-start | bytes 368644
  42.4 1.5 %collective-permute-start.6 = (bf16[96,640]{1,0:T(8,128)(2,1)S(1)}, bf16[96,640]{1,0:T(8,128)(2,1)}, u32[]{:S(2)}, u32[]{:S(2)}) collective-permute-start(bf16[96,640]{1,0:T(8,128)(2,1)S(1)} %collective-permute-done.2.refs_3_), channel_id=1, source_target_pairs={{0,1},{1,0},{2,3},{3,2},{4,5},{5,4},{6,7},{7,6},{8,9},{9,8},{10,11... | collective-permute-start | bytes 368648 | tf_op jit(solution)/shard_map/ppermute | solution.py:714
  43.2 0.7 copy-start.13
  49.1 2.2 %collective-permute-start.7 = (bf16[4,96,640]{2,1,0:T(8,128)(2,1)}, bf16[4,96,640]{2,1,0:T(8,128)(2,1)S(1)}, u32[]{:S(2)}, u32[]{:S(2)}) collective-permute-start(bf16[4,96,640]{2,1,0:T(8,128)(2,1)} %get-tuple-element.35), channel_id=1, source_target_pairs={{0,1},{1,0},{2,3},{3,2},{4,5},{5,4},{6,7},{7,6},{8,9},{9,8},{10,11... | collective-permute-start | bytes 1474568 | tf_op jit(solution)/shard_map/ppermute | solution.py:714
  51.3 0.8 copy-start.7
  54.3 7.0 %collective-permute-start.10 = (bf16[96,640]{1,0:T(8,128)(2,1)}, bf16[96,640]{1,0:T(8,128)(2,1)S(1)}, u32[]{:S(2)}, u32[]{:S(2)}) collective-permute-start(bf16[96,640]{1,0:T(8,128)(2,1)} %get-tuple-element.39), channel_id=1, source_target_pairs={{0,2},{1,3},{2,4},{3,5},{4,6},{5,7},{6,0},{7,1},{8,10},{9,11},{10,... | collective-permute-start | bytes 368648 | tf_op jit(solution)/shard_map/ppermute | solution.py:709
  55.5 7.8 %collective-permute-start.8 = (bf16[96,640]{1,0:T(8,128)(2,1)}, bf16[96,640]{1,0:T(8,128)(2,1)S(1)}, u32[]{:S(2)}, u32[]{:S(2)}) collective-permute-start(bf16[96,640]{1,0:T(8,128)(2,1)} %get-tuple-element.37), channel_id=1, source_target_pairs={{0,6},{1,7},{2,0},{3,1},{4,2},{5,3},{6,4},{7,5},{8,14},{9,15},{10,... | collective-permute-start | bytes 368648 | tf_op jit(solution)/shard_map/ppermute | solution.py:709
  57.6 7.3 %collective-permute-start.9 = (bf16[96,640]{1,0:T(8,128)(2,1)}, bf16[96,640]{1,0:T(8,128)(2,1)S(1)}, u32[]{:S(2)}, u32[]{:S(2)}) collective-permute-start(bf16[96,640]{1,0:T(8,128)(2,1)} %get-tuple-element.38), channel_id=1, source_target_pairs={{0,4},{1,5},{2,6},{3,7},{4,0},{5,1},{6,2},{7,3},{8,12},{9,13},{10,... | collective-permute-start | bytes 368648 | tf_op jit(solution)/shard_map/ppermute | solution.py:709
  64.8 0.9 copy-start.2
  68.6 12.3 %collective-permute-start.15 = (bf16[2048,640]{1,0:T(8,128)(2,1)}, bf16[2048,640]{1,0:T(8,128)(2,1)}, u32[]{:S(2)}, u32[]{:S(2)}) collective-permute-start(bf16[2048,640]{1,0:T(8,128)(2,1)} %bitcast.3.mine_ref), channel_id=1, source_target_pairs={{0,1},{1,0},{2,3},{3,2},{4,5},{5,4},{6,7},{7,6},{8,9},{9,8},{10,11... | collective-permute-start | bytes 7864328 | tf_op jit(solution)/shard_map/ppermute | solution.py:714
  68.6 12.1 %collective-permute-start.11 = (bf16[24,2304]{1,0:T(8,128)(2,1)S(1)}, bf16[24,2304]{1,0:T(8,128)(2,1)S(1)}, u32[]{:S(2)}, u32[]{:S(2)}) collective-permute-start(bf16[24,2304]{1,0:T(8,128)(2,1)S(1)} %shard_map.228), channel_id=1, source_target_pairs={{0,2},{1,3},{2,4},{3,5},{4,6},{5,7},{6,0},{7,1},{8,10},{9,11},{10,... | collective-permute-start | bytes 331784 | tf_op jit(solution)/shard_map/ppermute | solution.py:709
  70.1 10.6 %collective-permute-start.12 = (bf16[24,2304]{1,0:T(8,128)(2,1)S(1)}, bf16[24,2304]{1,0:T(8,128)(2,1)S(1)}, u32[]{:S(2)}, u32[]{:S(2)}) collective-permute-start(bf16[24,2304]{1,0:T(8,128)(2,1)S(1)} %shard_map.228), channel_id=1, source_target_pairs={{0,4},{1,5},{2,6},{3,7},{4,0},{5,1},{6,2},{7,3},{8,12},{9,13},{10,... | collective-permute-start | bytes 331784 | tf_op jit(solution)/shard_map/ppermute | solution.py:709
  72.8 7.9 %collective-permute-start.13 = (bf16[24,2304]{1,0:T(8,128)(2,1)S(1)}, bf16[24,2304]{1,0:T(8,128)(2,1)S(1)}, u32[]{:S(2)}, u32[]{:S(2)}) collective-permute-start(bf16[24,2304]{1,0:T(8,128)(2,1)S(1)} %shard_map.228), channel_id=1, source_target_pairs={{0,6},{1,7},{2,0},{3,1},{4,2},{5,3},{6,4},{7,5},{8,14},{9,15},{10,... | collective-permute-start | bytes 331784 | tf_op jit(solution)/shard_map/ppermute | solution.py:709
  77.1 21.4 %all-to-all-start.3 = ((bf16[128,4,8,128]{3,2,1,0:T(8,128)(2,1)}), bf16[128,4,8,128]{3,2,1,0:T(8,128)(2,1)S(1)}, u32[]{:S(2)}, u32[]{:S(2)}) async-start(bf16[128,4,8,128]{3,2,1,0:T(8,128)(2,1)} %convert_element_type.65), calls=%async_computation.3 | async-start | bytes 2097152 | tf_op jit(solution)/shard_map/all_to_all | solution.py:743
  80.8 8.7 %copy-start.6 = (f32[24,2304]{1,0:T(8,128)}, f32[24,2304]{1,0:T(8,128)S(1)}, u32[]{:S(2)}) copy-start(f32[24,2304]{1,0:T(8,128)S(1)} %convert_add_fusion.one_ref) | copy-start | bytes 663556
  80.8 8.7 %collective-permute-start.14 = (f32[24,2304]{1,0:T(8,128)S(1)}, f32[24,2304]{1,0:T(8,128)S(1)}, u32[]{:S(2)}, u32[]{:S(2)}) collective-permute-start(f32[24,2304]{1,0:T(8,128)S(1)} %convert_add_fusion.one_ref), channel_id=1, source_target_pairs={{0,1},{1,0},{2,3},{3,2},{4,5},{5,4},{6,7},{7,6},{8,9},{9,8},{10,11... | collective-permute-start | bytes 663560 | tf_op jit(solution)/shard_map/ppermute | solution.py:714
  80.9 21.1 %copy-start.17 = (f32[4]{0:T(128)S(1)}, f32[4]{0:T(128)}, u32[]{:S(2)}) copy-start(f32[4]{0:T(128)} %param.40) | copy-start | bytes 52
  89.6 13.1 %copy-start.8 = (f32[24,2304]{1,0:T(8,128)}, f32[24,2304]{1,0:T(8,128)S(1)}, u32[]{:S(2)}) copy-start(f32[24,2304]{1,0:T(8,128)S(1)} %collective-permute-done.14.two_ref) | copy-start | bytes 663556
  98.5 4.2 %copy-start.4 = (bf16[128,4,8,128]{3,2,1,0:T(8,128)(2,1)}, bf16[128,4,8,128]{3,2,1,0:T(8,128)(2,1)S(1)}, u32[]{:S(2)}) copy-start(bf16[128,4,8,128]{3,2,1,0:T(8,128)(2,1)S(1)} %all-to-all-done.3) | copy-start | bytes 3145732
  98.5 24.9 %all-to-all-start.2 = ((bf16[8,576,128]{2,1,0:T(8,128)(2,1)}), bf16[8,576,128]{2,1,0:T(8,128)(2,1)S(1)}, u32[]{:S(2)}, u32[]{:S(2)}) async-start(bf16[8,576,128]{2,1,0:T(8,128)(2,1)} %shard_map.229), calls=%async_computation.2 | async-start | bytes 2359296 | tf_op jit(solution)/shard_map/all_to_all | solution.py:760
  111.2 1.5 %collective-permute-start.16 = (bf16[4,24,288]{2,1,0:T(8,128)(2,1)}, bf16[4,24,288]{2,1,0:T(8,128)(2,1)S(1)}, u32[]{:S(2)}, u32[]{:S(2)}) collective-permute-start(bf16[4,24,288]{2,1,0:T(8,128)(2,1)} %get-tuple-element.49), channel_id=1, source_target_pairs={{0,1},{1,0},{2,3},{3,2},{4,5},{5,4},{6,7},{7,6},{8,9},{9,8},{10,11... | collective-permute-start | bytes 165896 | tf_op jit(solution)/shard_map/ppermute | solution.py:714
  113.6 7.9 %collective-permute-start.17 = (bf16[24,288]{1,0:T(8,128)(2,1)S(1)}, bf16[24,288]{1,0:T(8,128)(2,1)S(1)}, u32[]{:S(2)}, u32[]{:S(2)}) collective-permute-start(bf16[24,288]{1,0:T(8,128)(2,1)S(1)} %get-tuple-element.50), channel_id=1, source_target_pairs={{0,2},{1,3},{2,4},{3,5},{4,6},{5,7},{6,0},{7,1},{8,10},{9,11},{10,... | collective-permute-start | bytes 41480 | tf_op jit(solution)/shard_map/ppermute | solution.py:709
  115.5 5.9 %collective-permute-start.18 = (bf16[24,288]{1,0:T(8,128)(2,1)S(1)}, bf16[24,288]{1,0:T(8,128)(2,1)S(1)}, u32[]{:S(2)}, u32[]{:S(2)}) collective-permute-start(bf16[24,288]{1,0:T(8,128)(2,1)S(1)} %get-tuple-element.52), channel_id=1, source_target_pairs={{0,4},{1,5},{2,6},{3,7},{4,0},{5,1},{6,2},{7,3},{8,12},{9,13},{10,... | collective-permute-start | bytes 41480 | tf_op jit(solution)/shard_map/ppermute | solution.py:709
  118.2 3.8 %collective-permute-start.19 = (bf16[24,288]{1,0:T(8,128)(2,1)S(1)}, bf16[24,288]{1,0:T(8,128)(2,1)S(1)}, u32[]{:S(2)}, u32[]{:S(2)}) collective-permute-start(bf16[24,288]{1,0:T(8,128)(2,1)S(1)} %get-tuple-element.51), channel_id=1, source_target_pairs={{0,6},{1,7},{2,0},{3,1},{4,2},{5,3},{6,4},{7,5},{8,14},{9,15},{10,... | collective-permute-start | bytes 41480 | tf_op jit(solution)/shard_map/ppermute | solution.py:709
  123.4 1.1 copy-start.3

commit v4 on v3

--- a/solution.py
+++ b/solution.py
@@ -60,7 +60,7 @@
     frequency = np.exp(-np.log(10000.0) * np.arange(half) / half)
     angles = np.asarray(positions, np.float64)[:, None] * frequency
     cos, sin = np.cos(angles), np.sin(angles)
-    both = np.stack([np.concatenate([cos, cos], -1), np.concatenate([-sin, sin], -1)])
+    both = np.concatenate([cos, cos, -sin, sin], -1)
     return jnp.asarray(both, f32)
 
 
@@ -113,24 +113,43 @@
     )(pages)
 
 
+def pack_rope(values):
+    count = LAT // ROPE
+    piece = values.shape[0] // count
+    return jnp.concatenate(
+        [values[i * piece : (i + 1) * piece] for i in range(count)], axis=1
+    )
+
+
+def unpack_rope(packed):
+    return jnp.concatenate(
+        [packed[:, i * ROPE : (i + 1) * ROPE] for i in range(LAT // ROPE)], axis=0
+    )
+
+
 def front_kernel(
     lengths_ref,
-    fine_ref,
-    coarse_ref,
+    fine_hbm,
+    coarse_hbm,
     x_hbm,
     dec_hbm,
     lat_proj_hbm,
     query_proj_hbm,
     expand_hbm,
+    state_hbm,
     lat_hbm,
     fresh_ref,
     qp_ref,
     qd_ref,
+    state_out_ref,
+    fine_ref,
+    coarse_ref,
     x_ref,
     dec_ref,
     lat_proj_ref,
     query_proj_ref,
     expand_ref,
+    state_ref,
     normed,
     turns,
     lat_ref,
@@ -140,7 +159,7 @@
     seq, grp = lax.axis_index("seq"), lax.axis_index("grp")
     rows, width = x_ref.shape
     count = dec_ref.shape[0]
-    half_rows = lat_ref.shape[0]
+    half_rows = rows // 2
     core = lax.rem(grp, 2)
     heads = qp_ref.shape[0]
     requests = lengths_ref.shape[0]
@@ -160,46 +179,57 @@
         )
         for i in range(chunks)
     ]
-    for load in loads:
-        load.start()
-    for r in range(requests):
-        for t in range(count // requests):
-            at = rows + t * requests + r
-            row = lengths_ref[r] + t
-            turns[0, at : at + 1] = fine_ref[0, pl.ds(row, 1)]
-            turns[1, at : at + 1] = fine_ref[1, pl.ds(row, 1)]
-    turns[:, rows + count :] = jnp.zeros((2, turns.shape[1] - rows - count, ROPE), f32)
-    base_cos, base_sin = coarse_ref[0, pl.ds(seq, 1)], coarse_ref[1, pl.ds(seq, 1)]
-    fine_cos, fine_sin = fine_ref[0, :rows], fine_ref[1, :rows]
-    turns[0, :rows] = base_cos * fine_cos - base_sin * fine_sin
-    turns[1, :rows] = base_sin * fine_cos + base_cos * fine_sin
+    loads.append(pltpu.make_async_copy(state_hbm, state_ref, sems.at[4 + chunks]))
+    loads.append(pltpu.make_async_copy(fine_hbm, fine_ref, sems.at[5 + chunks]))
+    loads.append(pltpu.make_async_copy(coarse_hbm, coarse_ref, sems.at[6 + chunks]))
+    for i in (0, 1, 2, 5 + chunks, 6 + chunks):
+        loads[i].start()
     loads[0].wait()
+    for i in range(4, 4 + chunks):
+        loads[i].start()
+    loads[3].start()
     normed[:rows] = norm_rows(x_ref[...].astype(f32)).astype(bf16)
     loads[1].wait()
     tail = normed.shape[0] - rows - count
     normed[rows:] = jnp.concatenate(
         [norm_rows(dec_ref[...].astype(f32)), jnp.zeros((tail, width), f32)], axis=0
     ).astype(bf16)
+    loads[4 + chunks].start()
+    loads[5 + chunks].wait()
+    loads[6 + chunks].wait()
+    for r in range(requests):
+        for t in range(count // requests):
+            at = rows + t * requests + r
+            row = lengths_ref[r] + t
+            turns[at : at + 1] = fine_ref[pl.ds(row, 1)]
+    turns[rows + count :] = jnp.zeros((turns.shape[0] - rows - count, 2 * ROPE), f32)
+    base, near = coarse_ref[pl.ds(seq, 1)], fine_ref[:rows]
+    base_cos, base_sin = base[:, :ROPE], base[:, ROPE:]
+    near_cos, near_sin = near[:, :ROPE], near[:, ROPE:]
+    turns[:rows] = jnp.concatenate(
+        [base_cos * near_cos - base_sin * near_sin, base_sin * near_cos + base_cos * near_sin],
+        axis=-1,
+    )
     loads[2].wait()
 
-    def latents(inputs, cos, sin):
-        projected = dot_nt(inputs, lat_proj_ref[...])
-        return jnp.concatenate(
-            [norm_rows(projected[:, :LAT]), turn(projected[:, LAT:], cos, sin)], axis=-1
-        ).astype(bf16)
-
     own = pl.ds(pl.multiple_of(core * half_rows, half_rows), half_rows)
-    gap = jnp.zeros((half_rows, SENT - WIDE), bf16)
-    lat_ref[...] = jnp.concatenate(
-        [latents(normed[own], turns[0, own], turns[1, own]), gap], axis=-1
-    )
+    projected = dot_nt(
+        jnp.concatenate([normed[own], normed[rows:]], axis=0), lat_proj_ref[...]
+    )
+    around = jnp.concatenate([turns[own], turns[rows:]], axis=0)
+    cos, sin = around[:, :ROPE], around[:, ROPE:]
+    latent = jnp.concatenate(
+        [norm_rows(projected[:, :LAT]), turn(projected[:, LAT:], cos, sin)], axis=-1
+    )
+    lat_ref[:half_rows] = latent[:half_rows, :LAT].astype(bf16)
+    lat_ref[half_rows:] = pack_rope(latent[:half_rows, LAT:]).astype(bf16)
     stores = [
         pltpu.make_async_copy(lat_ref, lat_hbm.at[i], out_sems.at[i])
         for i in range(lat_hbm.shape[0])
     ]
     for store in stores:
         store.start()
-    fresh_ref[...] = latents(normed[rows:], turns[0, rows:], turns[1, rows:])
+    fresh_ref[...] = latent[half_rows:].astype(bf16)
     total = None
     for i in range(chunks):
         loads[4 + i].wait()
@@ -209,7 +239,7 @@
     loads[3].wait()
     fold = scale * log2e
     decode = []
-    cos, sin = turns[0], turns[1]
+    cos, sin = turns[:, :ROPE], turns[:, ROPE:]
     for head in range(heads):
         at = head * (NOPE + ROPE)
         nope = total[:, at : at + NOPE]
@@ -223,45 +253,52 @@
         blank = jnp.zeros((absorbed.shape[0], SENT - WIDE), f32)
         decode.append(jnp.concatenate([absorbed, turned[rows:], blank], axis=-1)[:count])
     qd_ref[...] = (jnp.concatenate(decode, axis=0) * fold).astype(bf16)
+    loads[4 + chunks].wait()
+    state_out_ref[...] = state_ref[...].astype(bf16)
     for store in stores:
         store.wait()
 
 
-def front(lengths, x, dec, lat_proj_t, query_proj, key_expand, seq_size):
+def front(lengths, x, dec, lat_proj_t, query_proj, key_expand, states, seq_size):
     rows, width = x.shape
     count = dec.shape[0]
     heads = key_expand.shape[1] // NOPE
     padded = count + 8
     requests = lengths.shape[0]
-    fine = rope_tables(range(max(rows, MAXP * PAGE + count // requests)))
+    reach = max(rows, MAXP * PAGE + count // requests)
+    fine = rope_tables(range(-(-reach // 8) * 8))
     coarse = rope_tables([rows * i for i in range(seq_size)])
     smem = pl.BlockSpec(memory_space=pltpu.SMEM)
     vmem = pl.BlockSpec(memory_space=pltpu.VMEM)
     hbm = pl.BlockSpec(memory_space=pltpu.HBM)
     return pl.pallas_call(
         front_kernel,
-        in_specs=[smem, vmem, vmem] + [hbm] * 5,
-        out_specs=(hbm, vmem, vmem, vmem),
+        in_specs=[smem] + [hbm] * 8,
+        out_specs=(hbm, vmem, vmem, vmem, vmem),
         out_shape=(
-            jax.ShapeDtypeStruct((seq_size, rows // 2, SENT), bf16),
+            jax.ShapeDtypeStruct((seq_size, rows // 2 + rows * ROPE // (2 * LAT), LAT), bf16),
             jax.ShapeDtypeStruct((padded, WIDE), bf16),
             jax.ShapeDtypeStruct((heads, rows, NOPE + ROPE), bf16),
             jax.ShapeDtypeStruct((heads * count, SENT), bf16),
+            jax.ShapeDtypeStruct(states.shape, bf16),
         ),
         scratch_shapes=[
+            pltpu.VMEM(fine.shape, f32),
+            pltpu.VMEM(coarse.shape, f32),
             pltpu.VMEM(x.shape, bf16),
             pltpu.VMEM(dec.shape, bf16),
             pltpu.VMEM(lat_proj_t.shape, bf16),
             pltpu.VMEM(query_proj.shape, bf16),
             pltpu.VMEM(key_expand.shape, bf16),
+            pltpu.VMEM(states.shape, f32),
             pltpu.VMEM((rows + padded, width), bf16),
-            pltpu.VMEM((2, rows + padded, ROPE), f32),
-            pltpu.VMEM((rows // 2, SENT), bf16),
-            pltpu.SemaphoreType.DMA((7,)),
+            pltpu.VMEM((rows + padded, 2 * ROPE), f32),
+            pltpu.VMEM((rows // 2 + rows * ROPE // (2 * LAT), LAT), bf16),
+            pltpu.SemaphoreType.DMA((10,)),
             pltpu.SemaphoreType.DMA((seq_size,)),
         ],
         compiler_params=params(),
-    )(lengths, fine, coarse, x, dec, lat_proj_t, query_proj, key_expand)
+    )(lengths, fine, coarse, x, dec, lat_proj_t, query_proj, key_expand, states)
 
 
 def pack_shares(summed, sum_ref):
@@ -288,7 +325,7 @@
     rows = q_ref.shape[1]
     half = rows // 2
     first, core = lax.axis_index("seq") * rows, lax.rem(lax.axis_index("grp"), 2)
-    side = mine_ref.shape[0]
+    side = mine_ref.shape[0] * half
     block = 2 * side
     load = pltpu.make_async_copy(out_hbm, out_ref, sem)
 
@@ -300,8 +337,9 @@
         acc[...] = jnp.zeros_like(acc)
 
     def work(masked):
-        lat = jnp.concatenate([mine_ref[...], other_ref[...]], axis=0)
-        low, rope = lat[:, :LAT], lat[:, LAT:WIDE]
+        sources = [(ref, i) for ref in (mine_ref, other_ref) for i in range(ref.shape[0])]
+        low = jnp.concatenate([ref[i, :half] for ref, i in sources], axis=0)
+        rope = jnp.concatenate([unpack_rope(ref[i, half:]) for ref, i in sources], axis=0)
         ones = jnp.ones((16, block), bf16)
         keys = dot_nn(low, ke_ref[...]).astype(bf16)
         values = dot_nt(vet_ref[...], low).astype(bf16)
@@ -347,18 +385,18 @@
 
 def prefill_attend(q, mine, other, key_expand, value_expand, mla_output, shares):
     heads, rows, _ = q.shape
-    keys = mine.shape[0]
-    side = min(512, keys)
+    sources, packed, _ = mine.shape
+    side = max(1, min(sources, 1024 // rows))
     width = mla_output.shape[1]
     dense = rows * width // shares // 128
     whole = lambda shape: pl.BlockSpec(shape, lambda i: (0,) * len(shape))
     return pl.pallas_call(
         functools.partial(flash_kernel, heads),
-        grid=(keys // side,),
+        grid=(sources // side,),
         in_specs=[
             whole(q.shape),
-            pl.BlockSpec((side, SENT), lambda i: (i, 0)),
-            pl.BlockSpec((side, SENT), lambda i: (i, 0)),
+            pl.BlockSpec((side, packed, LAT), lambda i: (i, 0, 0)),
+            pl.BlockSpec((side, packed, LAT), lambda i: (i, 0, 0)),
             whole(key_expand.shape),
             whole(value_expand.shape),
             pl.BlockSpec(memory_space=pltpu.HBM),
@@ -396,7 +434,7 @@
     return pl.pallas_call(
         gather_share_kernel,
         out_shape=jax.ShapeDtypeStruct((share, rows), bf16),
-        compiler_params=params(),
+        compiler_params=params(20),
     )(parts, x)
 
 
@@ -477,7 +515,7 @@
         in_specs=[vmem] * (2 * count + 3),
         out_specs=(vmem, vmem),
         out_shape=(shape, shape),
-        compiler_params=params(),
+        compiler_params=params(24),
     )(*queries, keys, fresh, owner)
 
 
@@ -494,7 +532,7 @@
     return pl.pallas_call(
         merge_kernel,
         out_shape=(shape,) * keep.shape[0],
-        compiler_params=params(),
+        compiler_params=params(24),
     )(keep, got)
 
 
@@ -522,148 +560,169 @@
 def kda_kernel(
     heads,
     requests,
+    rate_ref,
+    one_hbm,
+    two_hbm,
+    dec_hbm,
+    inputs_hbm,
+    beta_hbm,
+    decay_down_hbm,
+    gate_down_hbm,
+    decay_up_hbm,
+    gate_up_hbm,
+    states_hbm,
+    output_hbm,
+    hidden_ref,
+    keep_ref,
+    send_ref,
     one_ref,
     two_ref,
     dec_ref,
     inputs_ref,
     beta_ref,
     decay_down_ref,
+    gate_down_ref,
     decay_up_ref,
-    gate_down_ref,
     gate_up_ref,
-    rate_ref,
     states_ref,
     output_ref,
-    hidden_ref,
-    keep_ref,
-    send_ref,
-    kin,
-    projected,
     by_share,
     summed_ref,
+    sems,
 ):
-    part = pl.program_id(0)
     shares, rows, share = by_share.shape
     grp = lax.axis_index("grp")
-
-    @pl.when(part == 0)
-    def _():
-        hidden = dec_ref[...].astype(f32) + one_ref[...] + two_ref[...]
-        for g in range(shares):
-            by_share[g] = hidden[:, g * share : (g + 1) * share]
-        hidden_ref[...] = by_share[grp]
-        kin[...] = norm_rows(hidden).astype(bf16)
-
-    projected[part] = dot_nn(kin[...], inputs_ref[0])
-
-    @pl.when(part == pl.num_programs(0) - 1)
-    def _():
-        read_in = kin[...]
-        beta = jax.nn.sigmoid(dot_nt(read_in, beta_ref[...]))
-        decay_low = dot_nn(read_in, decay_down_ref[...]).astype(bf16)
-        decays = jnp.exp(
-            -rate_ref[...] * jax.nn.softplus(dot_nn(decay_low, decay_up_ref[...]))
-        )
-        gate_low = dot_nn(read_in, gate_down_ref[...]).astype(bf16)
-        gates = jax.nn.sigmoid(dot_nn(gate_low, gate_up_ref[...]))
-        steps = rows // requests
-        at = lambda values, t: values[t * requests : (t + 1) * requests]
-        along = lambda a, b: jnp.sum(a * b, axis=-1, keepdims=True)
-        blended = []
-        for head in range(heads):
-            lanes = slice(head * DK, (head + 1) * DK)
-            q = unit_rows(projected[0, :, lanes]) * DK ** (-0.5)
-            k = unit_rows(projected[1, :, lanes])
-            v = projected[2, :, lanes]
-            a = decays[:, lanes]
-            b = beta[:, head : head + 1]
-            vectors = []
-            held = None
-            for t in range(steps):
-                held = at(a, t) if held is None else held * at(a, t)
-                vectors += [held * at(k, t), held * at(q, t)]
-            vectors = jnp.concatenate(vectors, axis=0)
-            high = vectors.astype(bf16)
-            both = jnp.concatenate([high.astype(f32), vectors - high.astype(f32)], axis=0)
-            owner = lax.rem(lax.broadcasted_iota(jnp.int32, (both.shape[0], 1), 0), requests)
-            spread = jnp.concatenate(
-                [jnp.where(owner == r, both, 0.0) for r in range(requests)], axis=-1
-            ).astype(bf16)
-            held_states = jnp.concatenate(
-                [
-                    states_ref[:, r, head].astype(f32).reshape(DV, DK)
-                    for r in range(requests)
-                ],
-                axis=-1,
-            ).astype(bf16)
-            met = dot_nt(spread, held_states)
-            met = met[: vectors.shape[0]] + met[vectors.shape[0] :]
-            carried = []
-            reads = []
-            for t in range(steps):
-                seen = at(met, 2 * t)
-                read = at(met, 2 * t + 1)
-                carried = [(u, w * at(a, t)) for u, w in carried]
-                for u, w in carried:
-                    seen = seen + u * along(w, at(k, t))
-                u = at(b, t) * (at(v, t) - seen)
-                carried.append((u, at(k, t)))
-                for u, w in carried:
-                    read = read + u * along(w, at(q, t))
-                reads.append(read)
-            read = jnp.concatenate(reads, axis=0)
-            blended.append(norm_rows(read) * gates[:, lanes])
-        mixed = jnp.concatenate(blended, axis=-1).astype(bf16)
-        summed = dot_nn(mixed, output_ref[...])
-        for g in range(shares):
-            summed_ref[g] = summed[:, g * share : (g + 1) * share]
-        core = lax.rem(grp, 2)
-        for by in range(shares // 2):
-            pair = 2 * lax.rem(grp // 2 + by, shares // 2)
-            keep_ref[by] = summed_ref[pair + core]
-            send_ref[by] = summed_ref[pair + 1 - core].astype(bf16)
-
-
-def kda(shares, one, two, dec, inputs, beta_t, decay_down, decay_up, gate_down, gate_up, rate, states, output):
+    pairs = [
+        (one_hbm, one_ref),
+        (two_hbm, two_ref),
+        (dec_hbm, dec_ref),
+        (inputs_hbm.at[1], inputs_ref.at[1]),
+        (beta_hbm, beta_ref),
+        (decay_down_hbm, decay_down_ref),
+        (gate_down_hbm, gate_down_ref),
+        (decay_up_hbm, decay_up_ref),
+        (gate_up_hbm, gate_up_ref),
+        (inputs_hbm.at[0], inputs_ref.at[0]),
+        (states_hbm, states_ref),
+        (inputs_hbm.at[2], inputs_ref.at[2]),
+        (output_hbm, output_ref),
+    ]
+    loads = [pltpu.make_async_copy(a, b, sems.at[i]) for i, (a, b) in enumerate(pairs)]
+    for load in loads:
+        load.start()
+    for load in loads[:3]:
+        load.wait()
+    hidden = dec_ref[...].astype(f32) + one_ref[...] + two_ref[...]
+    for g in range(shares):
+        by_share[g] = hidden[:, g * share : (g + 1) * share]
+    hidden_ref[...] = by_share[grp]
+    kin = norm_rows(hidden).astype(bf16)
+    loads[3].wait()
+    all_keys = dot_nn(kin, inputs_ref[1])
+    for load in loads[4:9]:
+        load.wait()
+    beta = jax.nn.sigmoid(dot_nt(kin, beta_ref[...]))
+    decay_low = dot_nn(kin, decay_down_ref[...]).astype(bf16)
+    rises = jax.nn.softplus(dot_nn(decay_low, decay_up_ref[...]))
+    gate_low = dot_nn(kin, gate_down_ref[...]).astype(bf16)
+    gates = jax.nn.sigmoid(dot_nn(gate_low, gate_up_ref[...]))
+    loads[9].wait()
+    all_queries = dot_nn(kin, inputs_ref[0])
+    loads[10].wait()
+    held_states = [states_ref[:, r].astype(f32) for r in range(requests)]
+    steps = rows // requests
+    piece = held_states[0].shape[1] // heads
+    at = lambda values, t: values[t * requests : (t + 1) * requests]
+    along = lambda a, b: jnp.sum(a * b, axis=-1, keepdims=True)
+    ready = []
+    for head in range(heads):
+        lanes = slice(head * DK, (head + 1) * DK)
+        q = unit_rows(all_queries[:, lanes]) * DK ** (-0.5)
+        k = unit_rows(all_keys[:, lanes])
+        rate = jnp.exp(jnp.full((1, DK), rate_ref[head], f32))
+        a = jnp.exp(-rate * rises[:, lanes])
+        vectors = []
+        kept = None
+        for t in range(steps):
+            kept = at(a, t) if kept is None else kept * at(a, t)
+            vectors += [kept * at(k, t), kept * at(q, t)]
+        vectors = jnp.concatenate(vectors, axis=0)
+        high = vectors.astype(bf16).astype(f32)
+        both = jnp.concatenate([high, vectors - high], axis=0)
+        owner = lax.rem(lax.broadcasted_iota(jnp.int32, (both.shape[0], 1), 0), requests)
+        spread = jnp.concatenate(
+            [jnp.where(owner == r, both, 0.0) for r in range(requests)], axis=-1
+        ).astype(bf16)
+        facing = jnp.concatenate(
+            [
+                held_states[r][:, head * piece : (head + 1) * piece].reshape(DV, DK)
+                for r in range(requests)
+            ],
+            axis=-1,
+        ).astype(bf16)
+        met = dot_nt(spread, facing)
+        ready.append((q, k, a, met[: vectors.shape[0]] + met[vectors.shape[0] :]))
+    loads[11].wait()
+    all_values = dot_nn(kin, inputs_ref[2])
+    blended = []
+    for head in range(heads):
+        lanes = slice(head * DK, (head + 1) * DK)
+        q, k, a, met = ready[head]
+        v = all_values[:, lanes]
+        b = beta[:, head : head + 1]
+        carried = []
+        reads = []
+        for t in range(steps):
+            seen = at(met, 2 * t)
+            read = at(met, 2 * t + 1)
+            carried = [(u, w * at(a, t)) for u, w in carried]
+            for u, w in carried:
+                seen = seen + u * along(w, at(k, t))
+            u = at(b, t) * (at(v, t) - seen)
+            carried.append((u, at(k, t)))
+            for u, w in carried:
+                read = read + u * along(w, at(q, t))
+            reads.append(read)
+        read = jnp.concatenate(reads, axis=0)
+        blended.append(norm_rows(read) * gates[:, lanes])
+    mixed = jnp.concatenate(blended, axis=-1).astype(bf16)
+    loads[12].wait()
+    summed = dot_nn(mixed, output_ref[...])
+    for g in range(shares):
+        summed_ref[g] = summed[:, g * share : (g + 1) * share]
+    core = lax.rem(grp, 2)
+    for by in range(shares // 2):
+        pair = 2 * lax.rem(grp // 2 + by, shares // 2)
+        keep_ref[by] = summed_ref[pair + core]
+        send_ref[by] = summed_ref[pair + 1 - core].astype(bf16)
+
+
+def kda(shares, rate, *operands):
+    dec, beta_t, states = operands[2], operands[4], operands[9]
     rows, width = dec.shape
     heads = beta_t.shape[0]
     requests = states.shape[1]
-    columns = inputs.shape[2]
-    whole = lambda a: pl.BlockSpec(a.shape, lambda i: (0,) * len(a.shape))
     share = width // shares
     sides = shares // 2
-    held = lambda shape: pl.BlockSpec(shape, lambda i: (0,) * len(shape))
+    vmem = pl.BlockSpec(memory_space=pltpu.VMEM)
     return pl.pallas_call(
         functools.partial(kda_kernel, heads, requests),
-        grid=(3,),
-        in_specs=[
-            whole(one),
-            whole(two),
-            whole(dec),
-            pl.BlockSpec((1, width, columns), lambda i: (i, 0, 0)),
-            whole(beta_t),
-            whole(decay_down),
-            whole(decay_up),
-            whole(gate_down),
-            whole(gate_up),
-            whole(rate),
-            whole(states),
-            whole(output),
-        ],
-        out_specs=(held((rows, share)), held((sides, rows, share)), held((sides, rows, share))),
+        in_specs=[pl.BlockSpec(memory_space=pltpu.SMEM)]
+        + [pl.BlockSpec(memory_space=pltpu.HBM)] * len(operands),
+        out_specs=(vmem, vmem, vmem),
         out_shape=(
             jax.ShapeDtypeStruct((rows, share), f32),
             jax.ShapeDtypeStruct((sides, rows, share), f32),
             jax.ShapeDtypeStruct((sides, rows, share), bf16),
         ),
-        scratch_shapes=[
-            pltpu.VMEM((rows, width), bf16),
-            pltpu.VMEM((3, rows, columns), f32),
+        scratch_shapes=[pltpu.VMEM(a.shape, a.dtype) for a in operands]
+        + [
             pltpu.VMEM((shares, rows, share), f32),
             pltpu.VMEM((shares, rows, share), f32),
+            pltpu.SemaphoreType.DMA((len(operands) + 2,)),
         ],
         compiler_params=params(),
-    )(one, two, dec, inputs, beta_t, decay_down, decay_up, gate_down, gate_up, rate, states, output)
+    )(rate, *operands)
 
 
 def shards(
@@ -699,26 +758,7 @@
     dec = decode_input.reshape(decode_rows, width)
 
     own_tokens = slice_pages(latent_pages[0], grp_size)
-    x_rows, own_tokens = lax.optimization_barrier((x_group, own_tokens))
-    own_latent, fresh, q_prefill, q_decode = front(
-        prompt_len, x_rows, dec, latent_proj.T, query_proj, key_expand, seq_size
-    )
-    sides = grp_size // 2
-
-    def shift(value, by):
-        return lax.ppermute(
-            value, "grp", [(g, (g + 2 * by) % grp_size) for g in range(grp_size)]
-        )
-
-    def swap(value):
-        return lax.ppermute(value, "grp", [(g, g ^ 1) for g in range(grp_size)])
-
-    arrived = lax.all_to_all(own_tokens, "seq", split_axis=0, concat_axis=0, tiled=True)
-    own_latent, arrived = lax.optimization_barrier((own_latent, arrived))
-    mine = lax.all_to_all(own_latent, "seq", split_axis=0, concat_axis=0, tiled=True)
-    mine = mine.reshape(-1, SENT)
     _, slots, tokens, _ = own_tokens.shape
-    page_keys = arrived.reshape(seq_size * slots * tokens, WIDE)
     core = grp_index % 2
     target = lax.dynamic_slice_in_dim(slot_target[:, 0, :], core * slots, slots, 1)
     owner = target // MAXP
@@ -733,19 +773,44 @@
         held[..., None] & (token_pos < lengths[..., None]), owner[..., None], -1
     ).reshape(1, -1)
 
+    x_rows, _, key_owner = lax.optimization_barrier((x_group, own_tokens, key_owner))
+    own_latent, fresh, q_prefill, q_decode, state_rows = front(
+        prompt_len,
+        x_rows,
+        dec,
+        latent_proj.T,
+        query_proj,
+        key_expand,
+        kda_state.reshape(kda_state.shape[0], -1, DK),
+        seq_size,
+    )
+    sides = grp_size // 2
+
+    def shift(value, by):
+        return lax.ppermute(
+            value, "grp", [(g, (g + 2 * by) % grp_size) for g in range(grp_size)]
+        )
+
+    def swap(value):
+        return lax.ppermute(value, "grp", [(g, g ^ 1) for g in range(grp_size)])
+
+    arrived = lax.all_to_all(own_tokens, "seq", split_axis=0, concat_axis=0, tiled=True)
     queries = [q_decode] + [shift(q_decode, by) for by in range(1, sides)]
-    queries += [swap(q) for q in queries]
+    own_latent, _, _ = lax.optimization_barrier((own_latent, arrived, queries[1]))
+    mine = lax.all_to_all(own_latent, "seq", split_axis=0, concat_axis=0, tiled=True)
+    page_keys = arrived.reshape(-1, WIDE)
+    queries = queries + [swap(q) for q in queries]
     keep, send = pages_attend(
         queries, page_keys, fresh, key_owner, decode_rows, requests
     )
     merged = merge_pair(keep, swap(send))
-    state_rows, mine = lax.optimization_barrier((kda_state, mine))
+    state_rows, _ = lax.optimization_barrier((state_rows, mine))
     states = lax.all_to_all(
-        state_rows.astype(bf16), "seq", split_axis=0, concat_axis=0, tiled=True
-    ).reshape((seq_size, requests) + kda_state.shape[1:])
+        state_rows, "seq", split_axis=0, concat_axis=0, tiled=True
+    ).reshape((seq_size, requests) + state_rows.shape[1:])
     partial = [merged[0]] + [shift(merged[by], -by) for by in range(1, sides)]
     mla_part = combine(partial, value_expand, mla_output)
-    mine, mla_part = lax.optimization_barrier((mine, mla_part))
+    mine, _ = lax.optimization_barrier((mine, mla_part))
     mla_half = mla_part.astype(f32)
     for by in range(1, sides):
         mla_half = mla_half + shift(mla_part, by).astype(f32)
@@ -765,16 +830,16 @@
 
     hidden_share, keep, send = kda(
         grp_size,
+        decay_log,
         mla_half,
         mla_rest,
         dec,
         kda_inputs.transpose(1, 0, 2),
         kda_beta.T,
         decay_down,
+        gate_down,
         decay_up,
-        gate_down,
         gate_up,
-        jnp.repeat(jnp.exp(decay_log), DK)[None, :],
         states,
         kda_output,
     )

time: 127 us -> 117 us (0.921)
  Pallas kernels: 38.3 us -> 31.7 us
  local copies, waits for them, and re-layouts: 7.09 us -> 1.46 us
  waiting for transfers between devices: 32.4 us -> 36.7 us
  other arithmetic: 5.42 us -> 2.62 us
    ppermute x12, waiting for transfers between devices: 9.76 us -> 17.2 us  [shift(): lax.ppermute(value, 'grp', [(g, (g + 2 * by) % grp_size) for g in range(g...]
    all_to_all x1, waiting for transfers between devices: 8.18 us -> 1.13 us  [shards(): lax.all_to_all(own_tokens, 'seq', split_axis=0, concat_axis=0, tiled=True)]
    all_to_all x1, waiting for transfers between devices: 2.15 us -> 6.95 us  [shards(): lax.all_to_all(own_latent, 'seq', split_axis=0, concat_axis=0, tiled=True)]
    unnamed x36 -> x20, local copies, waits for them, and re-layouts: 3.75 us -> 0.05 us
    convert_element_type x1 -> x0, other arithmetic: 2.8 us -> none  [shards(): state_rows.astype(bf16)]
    ppermute x12, starting transfers between devices: 21.7 us -> 19.2 us  [shift(): lax.ppermute(value, 'grp', [(g, (g + 2 * by) % grp_size) for g in range(g...]
    pallas_call x3, Pallas kernels: 25.8 us -> 23.9 us  [the longest x1 8.48 us: prefill_attend(): pl.pallas_call(functools.partial(flash_kernel, heads), grid=(sources // s...]
    pallas_call x1, Pallas kernels: 2.24 us -> 0.38 us  [merge_pair(): pl.pallas_call(merge_kernel, out_shape=(shape,) * keep.shape[0], compiler...]
  transfers between devices with their start and end apart: 24 -> 24, of which waited for: 13 -> 17; matrix products, arithmetic and copies ran while one was open for 7% -> 3% of each run, Pallas kernels for 27% -> 25%
where the time goes in v4:
time: 117 us; the launch traced here: 116 us
  starting transfers between devices  42.4 us (36%)
  waiting for transfers between devices  36.7 us (31%)
  Pallas kernels  31.7 us (27%)
  other arithmetic  2.62 us (2%)
  local copies, waits for them, and re-layouts  1.46 us (1%)
    ppermute x12, starting transfers between devices, shift(): lax.ppermute(value, 'grp', [(g, (g + 2 * by) % grp_size) for g in range(g...  19.2 us
    ppermute x12, waiting for transfers between devices, shift(): lax.ppermute(value, 'grp', [(g, (g + 2 * by) % grp_size) for g in range(g...  17.2 us
    pallas_call x1, Pallas kernels, prefill_attend(): pl.pallas_call(functools.partial(flash_kernel, heads), grid=(sources // s...  8.48 us
    pallas_call x1, Pallas kernels, front(): pl.pallas_call(front_kernel, in_specs=[smem] + [hbm] * 8, out_specs=(hbm,...  8.47 us
    all_to_all x1, starting transfers between devices, shards(): lax.all_to_all(own_tokens, 'seq', split_axis=0, concat_axis=0, tiled=True)  8.14 us
    all_to_all x1, waiting for transfers between devices, shards(): lax.all_to_all(state_rows, 'seq', split_axis=0, concat_axis=0, tiled=True)  7.51 us
    all_to_all x1, waiting for transfers between devices, shards(): lax.all_to_all(own_latent, 'seq', split_axis=0, concat_axis=0, tiled=True)  6.95 us
    pallas_call x1, Pallas kernels, kda(): pl.pallas_call(functools.partial(kda_kernel, heads, requests), in_specs=[...  6.94 us
  transfers between devices with their start and end apart: 24, of which 17 were waited for; matrix products, arithmetic and copies ran while one was open for 3% of the time, Pallas kernels for 25%

profile of v4, /device:TPU:0, one launch (start us, length us, event | category | flops | bytes accessed | tf_op | source)
XLA Modules:
  0.0 115.8 jit_solution(14388444407442086011)
XLA Ops:
  0.7 2.1 %shard_map.224 = bf16[16,3,16,576]{3,2,1,0:T(8,128)(2,1)} custom-call(bf16[16,6,64,576]{3,2,1,0:T(8,128)(2,1)} %bitcast.49), custom_call_target="tpu_custom_call" | custom-call | tf_op jit(solution)/shard_map/pallas_call | solution.py:102
  2.7 8.1 %all-to-all-start = ((bf16[16,3,16,576]{3,2,1,0:T(8,128)(2,1)}), bf16[16,3,16,576]{3,2,1,0:T(8,128)(2,1)S(1)}, u32[]{:S(2)}, u32[]{:S(2)}) async-start(bf16[16,3,16,576]{3,2,1,0:T(8,128)(2,1)} %shard_map.224), calls=%async_computation | async-start | bytes 1966080 | tf_op jit(solution)/shard_map/all_to_all | solution.py:797
  11.7 8.5 %shard_map.225 = (bf16[16,144,512]{2,1,0:T(8,128)(2,1)}, bf16[32,576]{1,0:T(8,128)(2,1)}, bf16[4,256,192]{2,1,0:T(8,128)(2,1)}, bf16[96,640]{1,0:T(8,128)(2,1)}, bf16[128,32,128]{2,1,0:T(8,128)(2,1)}) custom-call(s32[8]{0:T(128)} %lengths_ref.1, f32[776,128]{1,0:T(8,128)} %constant.64.clone.fine_hbm, f32[16,128]{1,0:T(8,128)} %constant.65.clone.coarse_hbm, ...), custom_call_target="tpu_custom_call" | custom-call | tf_op jit(solution)/shard_map/pallas_call | solution.py:274
  20.1 1.6 %collective-permute-start = (bf16[96,640]{1,0:T(8,128)(2,1)}, bf16[96,640]{1,0:T(8,128)(2,1)}, u32[]{:S(2)}, u32[]{:S(2)}) collective-permute-start(bf16[96,640]{1,0:T(8,128)(2,1)} %get-tuple-element.25.refs_0_), channel_id=1, source_target_pairs={{0,2},{1,3},{2,4},{3,5},{4,6},{5,7},{6,0},{7,1},{8,10},{9,11},{10,... | collective-permute-start | bytes 368648 | tf_op jit(solution)/shard_map/ppermute | solution.py:790
  21.7 4.9 %collective-permute-done.refs_1_ = bf16[96,640]{1,0:T(8,128)(2,1)} collective-permute-done((bf16[96,640]{1,0:T(8,128)(2,1)}, bf16[96,640]{1,0:T(8,128)(2,1)}, u32[]{:S(2)}, u32[]{:S(2)}) %collective-permute-start) | collective-permute-done | bytes 122912 | tf_op jit(solution)/shard_map/ppermute | solution.py:790
  26.6 1.1 all-to-all-done
  27.8 6.2 %all-to-all-start.1 = ((bf16[16,144,512]{2,1,0:T(8,128)(2,1)}), bf16[16,144,512]{2,1,0:T(8,128)(2,1)}, u32[]{:S(2)}, u32[]{:S(2)}) async-start(bf16[16,144,512]{2,1,0:T(8,128)(2,1)} %get-tuple-element.36), calls=%async_computation.1 | async-start | bytes 4718592 | tf_op jit(solution)/shard_map/all_to_all | solution.py:800
  34.0 1.9 %collective-permute-start.1 = (bf16[96,640]{1,0:T(8,128)(2,1)S(1)}, bf16[96,640]{1,0:T(8,128)(2,1)S(1)}, u32[]{:S(2)}, u32[]{:S(2)}) collective-permute-start(bf16[96,640]{1,0:T(8,128)(2,1)S(1)} %copy-done.2), channel_id=1, source_target_pairs={{0,4},{1,5},{2,6},{3,7},{4,0},{5,1},{6,2},{7,3},{8,12},{9,13},{10,... | collective-permute-start | bytes 368648 | tf_op jit(solution)/shard_map/ppermute | solution.py:790
  35.9 1.1 collective-permute-start.2
  37.1 0.5 collective-permute-start.4
  37.6 2.9 %collective-permute-done.1.refs_2_ = bf16[96,640]{1,0:T(8,128)(2,1)S(1)} collective-permute-done((bf16[96,640]{1,0:T(8,128)(2,1)S(1)}, bf16[96,640]{1,0:T(8,128)(2,1)S(1)}, u32[]{:S(2)}, u32[]{:S(2)}) %collective-permute-start.1) | collective-permute-done | bytes 122912 | tf_op jit(solution)/shard_map/ppermute | solution.py:790
  40.5 0.3 collective-permute-done.2.refs_3_
  40.8 0.2 collective-permute-start.6
  41.0 0.8 collective-permute-done.5.refs_6_
  41.8 0.3 collective-permute-done.6.refs_7_
  42.2 3.7 %shard_map.226 = (bf16[4,96,640]{2,1,0:T(8,128)(2,1)S(1)}, bf16[4,96,640]{2,1,0:T(8,128)(2,1)S(1)}) custom-call(bf16[96,640]{1,0:T(8,128)(2,1)S(1)} %copy-done.2, bf16[96,640]{1,0:T(8,128)(2,1)} %collective-permute-done.refs_1_, bf16[96,640]{1,0:T(8,128)(2,1)S(1)} %collective-permute-done.1.refs_2_, bf16[96,640]{1,0:T(8,128)(2,1)S(1)} %collective-permute-done.2.refs_3_, ...), custom_call_target="tpu_custom_call" | custom-call | tf_op jit(solution)/shard_map/pallas_call | solution.py:513
  45.9 0.3 collective-permute-start.7
  46.2 1.7 %collective-permute-done.7.got_ref = bf16[4,96,640]{2,1,0:T(8,128)(2,1)S(1)} collective-permute-done((bf16[4,96,640]{2,1,0:T(8,128)(2,1)S(1)}, bf16[4,96,640]{2,1,0:T(8,128)(2,1)S(1)}, u32[]{:S(2)}, u32[]{:S(2)}) %collective-permute-start.7) | collective-permute-done | bytes 491552 | tf_op jit(solution)/shard_map/ppermute | solution.py:795
  47.8 0.4 shard_map.227
  48.2 1.3 %collective-permute-start.10 = (bf16[96,640]{1,0:T(8,128)(2,1)S(1)}, bf16[96,640]{1,0:T(8,128)(2,1)S(1)}, u32[]{:S(2)}, u32[]{:S(2)}) collective-permute-start(bf16[96,640]{1,0:T(8,128)(2,1)S(1)} %get-tuple-element.33), channel_id=1, source_target_pairs={{0,2},{1,3},{2,4},{3,5},{4,6},{5,7},{6,0},{7,1},{8,10},{9,11},{10,... | collective-permute-start | bytes 368648 | tf_op jit(solution)/shard_map/ppermute | solution.py:790
  49.6 2.0 %collective-permute-start.8 = (bf16[96,640]{1,0:T(8,128)(2,1)S(1)}, bf16[96,640]{1,0:T(8,128)(2,1)S(1)}, u32[]{:S(2)}, u32[]{:S(2)}) collective-permute-start(bf16[96,640]{1,0:T(8,128)(2,1)S(1)} %get-tuple-element.31), channel_id=1, source_target_pairs={{0,6},{1,7},{2,0},{3,1},{4,2},{5,3},{6,4},{7,5},{8,14},{9,15},{10,... | collective-permute-start | bytes 368648 | tf_op jit(solution)/shard_map/ppermute | solution.py:790
  51.5 0.8 collective-permute-start.9
  52.3 2.6 %collective-permute-done.10.refs_3_ = bf16[96,640]{1,0:T(8,128)(2,1)S(1)} collective-permute-done((bf16[96,640]{1,0:T(8,128)(2,1)S(1)}, bf16[96,640]{1,0:T(8,128)(2,1)S(1)}, u32[]{:S(2)}, u32[]{:S(2)}) %collective-permute-start.10) | collective-permute-done | bytes 122912 | tf_op jit(solution)/shard_map/ppermute | solution.py:790
  54.9 1.9 %collective-permute-done.8.refs_1_ = bf16[96,640]{1,0:T(8,128)(2,1)S(1)} collective-permute-done((bf16[96,640]{1,0:T(8,128)(2,1)S(1)}, bf16[96,640]{1,0:T(8,128)(2,1)S(1)}, u32[]{:S(2)}, u32[]{:S(2)}) %collective-permute-start.8) | collective-permute-done | bytes 122912 | tf_op jit(solution)/shard_map/ppermute | solution.py:790
  56.9 1.4 %collective-permute-done.9.refs_2_ = bf16[96,640]{1,0:T(8,128)(2,1)S(1)} collective-permute-done((bf16[96,640]{1,0:T(8,128)(2,1)S(1)}, bf16[96,640]{1,0:T(8,128)(2,1)S(1)}, u32[]{:S(2)}, u32[]{:S(2)}) %collective-permute-start.9) | collective-permute-done | bytes 122912 | tf_op jit(solution)/shard_map/ppermute | solution.py:790
  58.3 0.7 shard_map.228
  59.0 7.0 %all-to-all-done.1.mine_ref = bf16[16,144,512]{2,1,0:T(8,128)(2,1)} async-done(((bf16[16,144,512]{2,1,0:T(8,128)(2,1)}), bf16[16,144,512]{2,1,0:T(8,128)(2,1)}, u32[]{:S(2)}, u32[]{:S(2)}) %all-to-all-start.1) | async-done | bytes 2359328 | tf_op jit(solution)/shard_map/all_to_all | solution.py:800
  66.0 0.3 collective-permute-start.11
  66.3 2.7 %collective-permute-start.12 = (bf16[24,2304]{1,0:T(8,128)(2,1)S(1)}, bf16[24,2304]{1,0:T(8,128)(2,1)S(1)}, u32[]{:S(2)}, u32[]{:S(2)}) collective-permute-start(bf16[24,2304]{1,0:T(8,128)(2,1)S(1)} %shard_map.228), channel_id=1, source_target_pairs={{0,4},{1,5},{2,6},{3,7},{4,0},{5,1},{6,2},{7,3},{8,12},{9,13},{10,... | collective-permute-start | bytes 331784 | tf_op jit(solution)/shard_map/ppermute | solution.py:790
  69.0 1.4 %collective-permute-start.13 = (bf16[24,2304]{1,0:T(8,128)(2,1)S(1)}, bf16[24,2304]{1,0:T(8,128)(2,1)S(1)}, u32[]{:S(2)}, u32[]{:S(2)}) collective-permute-start(bf16[24,2304]{1,0:T(8,128)(2,1)S(1)} %shard_map.228), channel_id=1, source_target_pairs={{0,6},{1,7},{2,0},{3,1},{4,2},{5,3},{6,4},{7,5},{8,14},{9,15},{10,... | collective-permute-start | bytes 331784 | tf_op jit(solution)/shard_map/ppermute | solution.py:790
  70.4 3.7 %all-to-all-start.3 = ((bf16[128,32,128]{2,1,0:T(8,128)(2,1)}), bf16[128,32,128]{2,1,0:T(8,128)(2,1)S(1)}, u32[]{:S(2)}, u32[]{:S(2)}) async-start(bf16[128,32,128]{2,1,0:T(8,128)(2,1)} %get-tuple-element.42), calls=%async_computation.3 | async-start | bytes 2097152 | tf_op jit(solution)/shard_map/all_to_all | solution.py:808
  74.1 0.9 collective-permute-done.11
  75.0 0.6 collective-permute-done.13
  75.8 8.5 %shard_map.229 = bf16[8,576,128]{2,1,0:T(8,128)(2,1)} custom-call(bf16[4,256,192]{2,1,0:T(8,128)(2,1)} %get-tuple-element.34.q_ref, bf16[16,144,512]{2,1,0:T(8,128)(2,1)} %all-to-all-done.1.mine_ref, bf16[16,144,512]{2,1,0:T(8,128)(2,1)} %collective-permute-done.15.other_ref, bf16[512,512]{1,0:T(8,128)(2,1)} %ke_ref.1, bf16[512,512]{1,0:T(8,128)(2,1)} %ve_ref.1, ...), custom_call_target="tpu_custom_call" | custom-call | tf_op jit(solution)/shard_map/pallas_call | solution.py:393
  84.3 7.5 %all-to-all-done.3 = bf16[128,32,128]{2,1,0:T(8,128)(2,1)S(1)} async-done(((bf16[128,32,128]{2,1,0:T(8,128)(2,1)}), bf16[128,32,128]{2,1,0:T(8,128)(2,1)S(1)}, u32[]{:S(2)}, u32[]{:S(2)}) %all-to-all-start.3) | async-done | bytes 1048608 | tf_op jit(solution)/shard_map/all_to_all | solution.py:808
  91.8 3.6 %all-to-all-start.2 = ((bf16[8,576,128]{2,1,0:T(8,128)(2,1)}), bf16[8,576,128]{2,1,0:T(8,128)(2,1)S(1)}, u32[]{:S(2)}, u32[]{:S(2)}) async-start(bf16[8,576,128]{2,1,0:T(8,128)(2,1)} %shard_map.229), calls=%async_computation.2 | async-start | bytes 2359296 | tf_op jit(solution)/shard_map/all_to_all | solution.py:825
  95.4 6.9 %shard_map.231 = (f32[24,288]{1,0:T(8,128)}, f32[4,24,288]{2,1,0:T(8,128)}, bf16[4,24,288]{2,1,0:T(8,128)(2,1)}) custom-call(f32[4]{0:T(128)} %rate_ref.1, f32[24,2304]{1,0:T(8,128)} %copy-done.5, f32[24,2304]{1,0:T(8,128)} %copy-done.6, bf16[24,2304]{1,0:T(8,128)(2,1)} %bitcast.55, bf16[3,2304,512]{2,1,0:T(8,128)(2,1)} %bitcast.50, ...), custom_call_target="tpu_custom_call" | custom-call | tf_op jit(solution)/shard_map/pallas_call | solution.py:708
  102.4 0.5 collective-permute-start.16
  102.8 1.1 collective-permute-done.16
  103.9 0.8 fusion.6
  104.8 1.9 %collective-permute-start.17 = (bf16[24,288]{1,0:T(8,128)(2,1)S(1)}, bf16[24,288]{1,0:T(8,128)(2,1)S(1)}, u32[]{:S(2)}, u32[]{:S(2)}) collective-permute-start(bf16[24,288]{1,0:T(8,128)(2,1)S(1)} %get-tuple-element.46), channel_id=1, source_target_pairs={{0,2},{1,3},{2,4},{3,5},{4,6},{5,7},{6,0},{7,1},{8,10},{9,11},{10,... | collective-permute-start | bytes 41480 | tf_op jit(solution)/shard_map/ppermute | solution.py:790
  106.7 2.7 %collective-permute-start.18 = (bf16[24,288]{1,0:T(8,128)(2,1)S(1)}, bf16[24,288]{1,0:T(8,128)(2,1)S(1)}, u32[]{:S(2)}, u32[]{:S(2)}) collective-permute-start(bf16[24,288]{1,0:T(8,128)(2,1)S(1)} %get-tuple-element.48), channel_id=1, source_target_pairs={{0,4},{1,5},{2,6},{3,7},{4,0},{5,1},{6,2},{7,3},{8,12},{9,13},{10,... | collective-permute-start | bytes 41480 | tf_op jit(solution)/shard_map/ppermute | solution.py:790
  109.4 1.5 %collective-permute-start.19 = (bf16[24,288]{1,0:T(8,128)(2,1)S(1)}, bf16[24,288]{1,0:T(8,128)(2,1)S(1)}, u32[]{:S(2)}, u32[]{:S(2)}) collective-permute-start(bf16[24,288]{1,0:T(8,128)(2,1)S(1)} %get-tuple-element.47), channel_id=1, source_target_pairs={{0,6},{1,7},{2,0},{3,1},{4,2},{5,3},{6,4},{7,5},{8,14},{9,15},{10,... | collective-permute-start | bytes 41480 | tf_op jit(solution)/shard_map/ppermute | solution.py:790
  110.9 1.1 constant_dynamic-slice_fusion.x_ref
  111.9 1.3 %collective-permute-done.17 = bf16[24,288]{1,0:T(8,128)(2,1)S(1)} collective-permute-done((bf16[24,288]{1,0:T(8,128)(2,1)S(1)}, bf16[24,288]{1,0:T(8,128)(2,1)S(1)}, u32[]{:S(2)}, u32[]{:S(2)}) %collective-permute-start.17) | collective-permute-done | bytes 13856 | tf_op jit(solution)/shard_map/ppermute | solution.py:790
  113.2 0.3 collective-permute-done.18
  113.5 1.4 %fusion.9 = bf16[3,8,288]{2,1,0:T(8,128)(2,1)} fusion(f32[24,288]{1,0:T(8,128)} %get-tuple-element.43, bf16[24,288]{1,0:T(8,128)(2,1)S(1)} %collective-permute-done.19, bf16[24,288]{1,0:T(8,128)(2,1)S(1)} %collective-permute-done.18, bf16[24,288]{1,0:T(8,128)(2,1)S(1)} %collective-permute-done.17, f32[4,24,288]{2,1,0:T(8,128)} %get-tuple-element.44, ...), kind=kLoop, calls=%fused_computation.15 | loop fusion | flops 69120 | bytes 124416 | tf_op jit(solution)/shard_map/reshape | solution.py:852
  114.9 0.9 shard_map.230
  (43 shorter events, 0.9 us)
Async XLA Ops:
  0.6 10.3 %copy-start.7 = (s32[16,1,6]{0,1,2:T(1,128)S(1)}, s32[16,1,6]{0,1,2:T(1,128)}, u32[]{:S(2)}) copy-start(s32[16,1,6]{0,1,2:T(1,128)} %param.26) | copy-start | bytes 1156
  0.6 10.5 %copy-start.8 = (s32[8]{0:T(128)S(1)}, s32[8]{0:T(128)}, u32[]{:S(2)}) copy-start(s32[8]{0:T(128)} %lengths_ref.1) | copy-start | bytes 100
  0.7 10.7 %copy-start.9 = (s32[16,1]{0,1:T(1,128)S(1)}, s32[16,1]{0,1:T(1,128)}, u32[]{:S(2)}) copy-start(s32[16,1]{0,1:T(1,128)} %param.27) | copy-start | bytes 196
  2.7 25.0 %all-to-all-start = ((bf16[16,3,16,576]{3,2,1,0:T(8,128)(2,1)}), bf16[16,3,16,576]{3,2,1,0:T(8,128)(2,1)S(1)}, u32[]{:S(2)}, u32[]{:S(2)}) async-start(bf16[16,3,16,576]{3,2,1,0:T(8,128)(2,1)} %shard_map.224), calls=%async_computation | async-start | bytes 1966080 | tf_op jit(solution)/shard_map/all_to_all | solution.py:797
  20.1 6.5 %collective-permute-start = (bf16[96,640]{1,0:T(8,128)(2,1)}, bf16[96,640]{1,0:T(8,128)(2,1)}, u32[]{:S(2)}, u32[]{:S(2)}) collective-permute-start(bf16[96,640]{1,0:T(8,128)(2,1)} %get-tuple-element.25.refs_0_), channel_id=1, source_target_pairs={{0,2},{1,3},{2,4},{3,5},{4,6},{5,7},{6,0},{7,1},{8,10},{9,11},{10,... | collective-permute-start | bytes 368648 | tf_op jit(solution)/shard_map/ppermute | solution.py:790
  27.8 6.3 %copy-start.2 = (bf16[96,640]{1,0:T(8,128)(2,1)S(1)}, bf16[96,640]{1,0:T(8,128)(2,1)}, u32[]{:S(2)}) copy-start(bf16[96,640]{1,0:T(8,128)(2,1)} %get-tuple-element.25.refs_0_) | copy-start | bytes 368644
  27.8 14.4 %copy-start.3 = (bf16[32,576]{1,0:T(8,128)(2,1)S(1)}, bf16[32,576]{1,0:T(8,128)(2,1)}, u32[]{:S(2)}) copy-start(bf16[32,576]{1,0:T(8,128)(2,1)} %get-tuple-element.26.refs_9_) | copy-start | bytes 110596
  27.8 38.2 %all-to-all-start.1 = ((bf16[16,144,512]{2,1,0:T(8,128)(2,1)}), bf16[16,144,512]{2,1,0:T(8,128)(2,1)}, u32[]{:S(2)}, u32[]{:S(2)}) async-start(bf16[16,144,512]{2,1,0:T(8,128)(2,1)} %get-tuple-element.36), calls=%async_computation.1 | async-start | bytes 4718592 | tf_op jit(solution)/shard_map/all_to_all | solution.py:800
  34.0 24.3 %copy-start = (bf16[512,2304]{1,0:T(8,128)(2,1)S(1)}, bf16[512,2304]{1,0:T(8,128)(2,1)}, u32[]{:S(2)}) copy-start(bf16[512,2304]{1,0:T(8,128)(2,1)} %out_hbm.1) | copy-start | bytes 7077892
  34.0 24.3 %copy-start.1 = (bf16[512,512]{1,0:T(8,128)(2,1)S(1)}, bf16[512,512]{1,0:T(8,128)(2,1)}, u32[]{:S(2)}) copy-start(bf16[512,512]{1,0:T(8,128)(2,1)} %ve_ref.1) | copy-start | bytes 1572868
  34.0 6.5 %collective-permute-start.1 = (bf16[96,640]{1,0:T(8,128)(2,1)S(1)}, bf16[96,640]{1,0:T(8,128)(2,1)S(1)}, u32[]{:S(2)}, u32[]{:S(2)}) collective-permute-start(bf16[96,640]{1,0:T(8,128)(2,1)S(1)} %copy-done.2), channel_id=1, source_target_pairs={{0,4},{1,5},{2,6},{3,7},{4,0},{5,1},{6,2},{7,3},{8,12},{9,13},{10,... | collective-permute-start | bytes 368648 | tf_op jit(solution)/shard_map/ppermute | solution.py:790
  35.9 4.9 %collective-permute-start.2 = (bf16[96,640]{1,0:T(8,128)(2,1)S(1)}, bf16[96,640]{1,0:T(8,128)(2,1)S(1)}, u32[]{:S(2)}, u32[]{:S(2)}) collective-permute-start(bf16[96,640]{1,0:T(8,128)(2,1)S(1)} %copy-done.2), channel_id=1, source_target_pairs={{0,6},{1,7},{2,0},{3,1},{4,2},{5,3},{6,4},{7,5},{8,14},{9,15},{10,... | collective-permute-start | bytes 368648 | tf_op jit(solution)/shard_map/ppermute | solution.py:790
  37.1 4.0 %collective-permute-start.3 = (bf16[96,640]{1,0:T(8,128)(2,1)S(1)}, bf16[96,640]{1,0:T(8,128)(2,1)S(1)}, u32[]{:S(2)}, u32[]{:S(2)}) collective-permute-start(bf16[96,640]{1,0:T(8,128)(2,1)S(1)} %copy-done.2), channel_id=1, source_target_pairs={{0,1},{1,0},{2,3},{3,2},{4,5},{5,4},{6,7},{7,6},{8,9},{9,8},{10,11... | collective-permute-start | bytes 368648 | tf_op jit(solution)/shard_map/ppermute | solution.py:795
  37.1 4.0 %collective-permute-start.4 = (bf16[96,640]{1,0:T(8,128)(2,1)}, bf16[96,640]{1,0:T(8,128)(2,1)S(1)}, u32[]{:S(2)}, u32[]{:S(2)}) collective-permute-start(bf16[96,640]{1,0:T(8,128)(2,1)} %collective-permute-done.refs_1_), channel_id=1, source_target_pairs={{0,1},{1,0},{2,3},{3,2},{4,5},{5,4},{6,7},{7,6},{8,9},{9,8},{10,11... | collective-permute-start | bytes 368648 | tf_op jit(solution)/shard_map/ppermute | solution.py:795
  40.5 1.3 %collective-permute-start.5 = (bf16[96,640]{1,0:T(8,128)(2,1)S(1)}, bf16[96,640]{1,0:T(8,128)(2,1)S(1)}, u32[]{:S(2)}, u32[]{:S(2)}) collective-permute-start(bf16[96,640]{1,0:T(8,128)(2,1)S(1)} %collective-permute-done.1.refs_2_), channel_id=1, source_target_pairs={{0,1},{1,0},{2,3},{3,2},{4,5},{5,4},{6,7},{7,6},{8,9},{9,8},{10,11... | collective-permute-start | bytes 368648 | tf_op jit(solution)/shard_map/ppermute | solution.py:795
  40.8 1.3 %collective-permute-start.6 = (bf16[96,640]{1,0:T(8,128)(2,1)S(1)}, bf16[96,640]{1,0:T(8,128)(2,1)S(1)}, u32[]{:S(2)}, u32[]{:S(2)}) collective-permute-start(bf16[96,640]{1,0:T(8,128)(2,1)S(1)} %collective-permute-done.2.refs_3_), channel_id=1, source_target_pairs={{0,1},{1,0},{2,3},{3,2},{4,5},{5,4},{6,7},{7,6},{8,9},{9,8},{10,11... | collective-permute-start | bytes 368648 | tf_op jit(solution)/shard_map/ppermute | solution.py:795
  45.9 1.9 %collective-permute-start.7 = (bf16[4,96,640]{2,1,0:T(8,128)(2,1)S(1)}, bf16[4,96,640]{2,1,0:T(8,128)(2,1)S(1)}, u32[]{:S(2)}, u32[]{:S(2)}) collective-permute-start(bf16[4,96,640]{2,1,0:T(8,128)(2,1)S(1)} %get-tuple-element.29), channel_id=1, source_target_pairs={{0,1},{1,0},{2,3},{3,2},{4,5},{5,4},{6,7},{7,6},{8,9},{9,8},{10,11... | collective-permute-start | bytes 1474568 | tf_op jit(solution)/shard_map/ppermute | solution.py:795
  48.2 6.7 %collective-permute-start.10 = (bf16[96,640]{1,0:T(8,128)(2,1)S(1)}, bf16[96,640]{1,0:T(8,128)(2,1)S(1)}, u32[]{:S(2)}, u32[]{:S(2)}) collective-permute-start(bf16[96,640]{1,0:T(8,128)(2,1)S(1)} %get-tuple-element.33), channel_id=1, source_target_pairs={{0,2},{1,3},{2,4},{3,5},{4,6},{5,7},{6,0},{7,1},{8,10},{9,11},{10,... | collective-permute-start | bytes 368648 | tf_op jit(solution)/shard_map/ppermute | solution.py:790
  49.6 7.3 %collective-permute-start.8 = (bf16[96,640]{1,0:T(8,128)(2,1)S(1)}, bf16[96,640]{1,0:T(8,128)(2,1)S(1)}, u32[]{:S(2)}, u32[]{:S(2)}) collective-permute-start(bf16[96,640]{1,0:T(8,128)(2,1)S(1)} %get-tuple-element.31), channel_id=1, source_target_pairs={{0,6},{1,7},{2,0},{3,1},{4,2},{5,3},{6,4},{7,5},{8,14},{9,15},{10,... | collective-permute-start | bytes 368648 | tf_op jit(solution)/shard_map/ppermute | solution.py:790
  51.5 6.8 %collective-permute-start.9 = (bf16[96,640]{1,0:T(8,128)(2,1)S(1)}, bf16[96,640]{1,0:T(8,128)(2,1)S(1)}, u32[]{:S(2)}, u32[]{:S(2)}) collective-permute-start(bf16[96,640]{1,0:T(8,128)(2,1)S(1)} %get-tuple-element.32), channel_id=1, source_target_pairs={{0,4},{1,5},{2,6},{3,7},{4,0},{5,1},{6,2},{7,3},{8,12},{9,13},{10,... | collective-permute-start | bytes 368648 | tf_op jit(solution)/shard_map/ppermute | solution.py:790
  66.0 9.8 %collective-permute-start.15 = (bf16[16,144,512]{2,1,0:T(8,128)(2,1)}, bf16[16,144,512]{2,1,0:T(8,128)(2,1)}, u32[]{:S(2)}, u32[]{:S(2)}) collective-permute-start(bf16[16,144,512]{2,1,0:T(8,128)(2,1)} %all-to-all-done.1.mine_ref), channel_id=1, source_target_pairs={{0,1},{1,0},{2,3},{3,2},{4,5},{5,4},{6,7},{7,6},{8,9},{9,8},{10,11... | collective-permute-start | bytes 7077896 | tf_op jit(solution)/shard_map/ppermute | solution.py:795
  66.0 9.1 %collective-permute-start.11 = (bf16[24,2304]{1,0:T(8,128)(2,1)S(1)}, bf16[24,2304]{1,0:T(8,128)(2,1)S(1)}, u32[]{:S(2)}, u32[]{:S(2)}) collective-permute-start(bf16[24,2304]{1,0:T(8,128)(2,1)S(1)} %shard_map.228), channel_id=1, source_target_pairs={{0,2},{1,3},{2,4},{3,5},{4,6},{5,7},{6,0},{7,1},{8,10},{9,11},{10,... | collective-permute-start | bytes 331784 | tf_op jit(solution)/shard_map/ppermute | solution.py:790
  66.3 8.8 %collective-permute-start.12 = (bf16[24,2304]{1,0:T(8,128)(2,1)S(1)}, bf16[24,2304]{1,0:T(8,128)(2,1)S(1)}, u32[]{:S(2)}, u32[]{:S(2)}) collective-permute-start(bf16[24,2304]{1,0:T(8,128)(2,1)S(1)} %shard_map.228), channel_id=1, source_target_pairs={{0,4},{1,5},{2,6},{3,7},{4,0},{5,1},{6,2},{7,3},{8,12},{9,13},{10,... | collective-permute-start | bytes 331784 | tf_op jit(solution)/shard_map/ppermute | solution.py:790
  69.0 6.6 %collective-permute-start.13 = (bf16[24,2304]{1,0:T(8,128)(2,1)S(1)}, bf16[24,2304]{1,0:T(8,128)(2,1)S(1)}, u32[]{:S(2)}, u32[]{:S(2)}) collective-permute-start(bf16[24,2304]{1,0:T(8,128)(2,1)S(1)} %shard_map.228), channel_id=1, source_target_pairs={{0,6},{1,7},{2,0},{3,1},{4,2},{5,3},{6,4},{7,5},{8,14},{9,15},{10,... | collective-permute-start | bytes 331784 | tf_op jit(solution)/shard_map/ppermute | solution.py:790
  70.4 21.4 %all-to-all-start.3 = ((bf16[128,32,128]{2,1,0:T(8,128)(2,1)}), bf16[128,32,128]{2,1,0:T(8,128)(2,1)S(1)}, u32[]{:S(2)}, u32[]{:S(2)}) async-start(bf16[128,32,128]{2,1,0:T(8,128)(2,1)} %get-tuple-element.42), calls=%async_computation.3 | async-start | bytes 2097152 | tf_op jit(solution)/shard_map/all_to_all | solution.py:808
  75.7 8.6 %copy-start.5 = (f32[24,2304]{1,0:T(8,128)}, f32[24,2304]{1,0:T(8,128)S(1)}, u32[]{:S(2)}) copy-start(f32[24,2304]{1,0:T(8,128)S(1)} %convert_add_fusion.one_hbm) | copy-start | bytes 663556
  75.7 8.6 %collective-permute-start.14 = (f32[24,2304]{1,0:T(8,128)S(1)}, f32[24,2304]{1,0:T(8,128)S(1)}, u32[]{:S(2)}, u32[]{:S(2)}) collective-permute-start(f32[24,2304]{1,0:T(8,128)S(1)} %convert_add_fusion.one_hbm), channel_id=1, source_target_pairs={{0,1},{1,0},{2,3},{3,2},{4,5},{5,4},{6,7},{7,6},{8,9},{9,8},{10,11... | collective-permute-start | bytes 663560 | tf_op jit(solution)/shard_map/ppermute | solution.py:795
  84.3 11.1 %copy-start.6 = (f32[24,2304]{1,0:T(8,128)}, f32[24,2304]{1,0:T(8,128)S(1)}, u32[]{:S(2)}) copy-start(f32[24,2304]{1,0:T(8,128)S(1)} %collective-permute-done.14.two_hbm) | copy-start | bytes 663556
  91.8 3.6 %copy-start.4 = (bf16[128,32,128]{2,1,0:T(8,128)(2,1)}, bf16[128,32,128]{2,1,0:T(8,128)(2,1)S(1)}, u32[]{:S(2)}) copy-start(bf16[128,32,128]{2,1,0:T(8,128)(2,1)S(1)} %all-to-all-done.3) | copy-start | bytes 3145732
  91.8 23.1 %all-to-all-start.2 = ((bf16[8,576,128]{2,1,0:T(8,128)(2,1)}), bf16[8,576,128]{2,1,0:T(8,128)(2,1)S(1)}, u32[]{:S(2)}, u32[]{:S(2)}) async-start(bf16[8,576,128]{2,1,0:T(8,128)(2,1)} %shard_map.229), calls=%async_computation.2 | async-start | bytes 2359296 | tf_op jit(solution)/shard_map/all_to_all | solution.py:825
  102.4 1.6 %collective-permute-start.16 = (bf16[4,24,288]{2,1,0:T(8,128)(2,1)}, bf16[4,24,288]{2,1,0:T(8,128)(2,1)S(1)}, u32[]{:S(2)}, u32[]{:S(2)}) collective-permute-start(bf16[4,24,288]{2,1,0:T(8,128)(2,1)} %get-tuple-element.45), channel_id=1, source_target_pairs={{0,1},{1,0},{2,3},{3,2},{4,5},{5,4},{6,7},{7,6},{8,9},{9,8},{10,11... | collective-permute-start | bytes 165896 | tf_op jit(solution)/shard_map/ppermute | solution.py:795
  104.8 8.5 %collective-permute-start.17 = (bf16[24,288]{1,0:T(8,128)(2,1)S(1)}, bf16[24,288]{1,0:T(8,128)(2,1)S(1)}, u32[]{:S(2)}, u32[]{:S(2)}) collective-permute-start(bf16[24,288]{1,0:T(8,128)(2,1)S(1)} %get-tuple-element.46), channel_id=1, source_target_pairs={{0,2},{1,3},{2,4},{3,5},{4,6},{5,7},{6,0},{7,1},{8,10},{9,11},{10,... | collective-permute-start | bytes 41480 | tf_op jit(solution)/shard_map/ppermute | solution.py:790
  106.7 6.8 %collective-permute-start.18 = (bf16[24,288]{1,0:T(8,128)(2,1)S(1)}, bf16[24,288]{1,0:T(8,128)(2,1)S(1)}, u32[]{:S(2)}, u32[]{:S(2)}) collective-permute-start(bf16[24,288]{1,0:T(8,128)(2,1)S(1)} %get-tuple-element.48), channel_id=1, source_target_pairs={{0,4},{1,5},{2,6},{3,7},{4,0},{5,1},{6,2},{7,3},{8,12},{9,13},{10,... | collective-permute-start | bytes 41480 | tf_op jit(solution)/shard_map/ppermute | solution.py:790
  109.4 4.1 %collective-permute-start.19 = (bf16[24,288]{1,0:T(8,128)(2,1)S(1)}, bf16[24,288]{1,0:T(8,128)(2,1)S(1)}, u32[]{:S(2)}, u32[]{:S(2)}) collective-permute-start(bf16[24,288]{1,0:T(8,128)(2,1)S(1)} %get-tuple-element.47), channel_id=1, source_target_pairs={{0,6},{1,7},{2,0},{3,1},{4,2},{5,3},{6,4},{7,5},{8,14},{9,15},{10,... | collective-permute-start | bytes 41480 | tf_op jit(solution)/shard_map/ppermute | solution.py:790

commit v5 on v4

--- a/solution.py
+++ b/solution.py
@@ -127,7 +127,17 @@
     )
 
 
+def turned_tables(base, near):
+    base_cos, base_sin = base[:, :ROPE], base[:, ROPE:]
+    near_cos, near_sin = near[:, :ROPE], near[:, ROPE:]
+    return jnp.concatenate(
+        [base_cos * near_cos - base_sin * near_sin, base_sin * near_cos + base_cos * near_sin],
+        axis=-1,
+    )
+
+
 def front_kernel(
+    count,
     lengths_ref,
     fine_hbm,
     coarse_hbm,
@@ -136,12 +146,9 @@
     lat_proj_hbm,
     query_proj_hbm,
     expand_hbm,
-    state_hbm,
     lat_hbm,
     fresh_ref,
-    qp_ref,
     qd_ref,
-    state_out_ref,
     fine_ref,
     coarse_ref,
     x_ref,
@@ -149,7 +156,6 @@
     lat_proj_ref,
     query_proj_ref,
     expand_ref,
-    state_ref,
     normed,
     turns,
     lat_ref,
@@ -158,18 +164,144 @@
 ):
     seq, grp = lax.axis_index("seq"), lax.axis_index("grp")
     rows, width = x_ref.shape
-    count = dec_ref.shape[0]
-    half_rows = rows // 2
     core = lax.rem(grp, 2)
+    heads = expand_ref.shape[1] // NOPE
+    requests = lengths_ref.shape[0]
+    chunks = 3
+    depth = width // chunks
+    own = pl.ds(pl.multiple_of(core * rows, rows), rows)
+    first = [
+        pltpu.make_async_copy(x_hbm.at[own], x_ref, sems.at[0]),
+        pltpu.make_async_copy(dec_hbm, dec_ref, sems.at[1]),
+        pltpu.make_async_copy(lat_proj_hbm, lat_proj_ref, sems.at[2]),
+        pltpu.make_async_copy(fine_hbm, fine_ref, sems.at[3]),
+        pltpu.make_async_copy(coarse_hbm, coarse_ref, sems.at[4]),
+    ]
+    later = [
+        pltpu.make_async_copy(
+            query_proj_hbm.at[pl.ds(i * depth, depth)],
+            query_proj_ref.at[pl.ds(i * depth, depth)],
+            sems.at[5 + i],
+        )
+        for i in range(chunks)
+    ]
+    later.append(pltpu.make_async_copy(expand_hbm, expand_ref, sems.at[5 + chunks]))
+    for load in first + later:
+        load.start()
+    first[0].wait()
+    normed[:rows] = norm_rows(x_ref[...].astype(f32)).astype(bf16)
+    first[1].wait()
+    tail = normed.shape[0] - rows - count
+    normed[rows:] = jnp.concatenate(
+        [norm_rows(dec_ref[...].astype(f32)), jnp.zeros((tail, width), f32)], axis=0
+    ).astype(bf16)
+    first[3].wait()
+    first[4].wait()
+    for r in range(requests):
+        for t in range(count // requests):
+            at = rows + t * requests + r
+            turns[at : at + 1] = fine_ref[pl.ds(lengths_ref[r] + t, 1)]
+    turns[rows + count :] = jnp.zeros((tail, 2 * ROPE), f32)
+    turns[:rows] = turned_tables(coarse_ref[pl.ds(seq, 1)], fine_ref[own])
+    first[2].wait()
+    projected = dot_nt(normed[...], lat_proj_ref[...])
+    cos, sin = turns[:, :ROPE], turns[:, ROPE:]
+    latent = jnp.concatenate(
+        [norm_rows(projected[:, :LAT]), turn(projected[:, LAT:], cos, sin)], axis=-1
+    )
+    lat_ref[:rows] = latent[:rows, :LAT].astype(bf16)
+    lat_ref[rows:] = pack_rope(latent[:rows, LAT:]).astype(bf16)
+    stores = [
+        pltpu.make_async_copy(lat_ref, lat_hbm.at[i], out_sems.at[i])
+        for i in range(lat_hbm.shape[0])
+    ]
+    for store in stores:
+        store.start()
+    fresh_ref[...] = latent[rows:].astype(bf16)
+    total = None
+    for i in range(chunks):
+        later[i].wait()
+        lanes = slice(i * depth, (i + 1) * depth)
+        term = dot_nn(normed[rows:, lanes], query_proj_ref[lanes])
+        total = term if total is None else total + term
+    later[chunks].wait()
+    decode = []
+    for head in range(heads):
+        at = head * (NOPE + ROPE)
+        turned = turn(total[:, at + NOPE : at + NOPE + ROPE], cos[rows:], sin[rows:])
+        absorbed = dot_nt(
+            total[:, at : at + NOPE].astype(bf16),
+            expand_ref[:, head * NOPE : (head + 1) * NOPE],
+        )
+        blank = jnp.zeros((absorbed.shape[0], SENT - WIDE), f32)
+        decode.append(jnp.concatenate([absorbed, turned, blank], axis=-1)[:count])
+    qd_ref[...] = (jnp.concatenate(decode, axis=0) * (scale * log2e)).astype(bf16)
+    for store in stores:
+        store.wait()
+
+
+def front(lengths, fine, coarse, x, dec, lat_proj_t, query_proj, key_expand):
+    rows, width = x.shape
+    half = rows // 2
+    count = dec.shape[0]
+    heads = key_expand.shape[1] // NOPE
+    padded = count + 8
+    packed = half + half * ROPE // LAT
+    seq_size = coarse.shape[0]
+    smem = pl.BlockSpec(memory_space=pltpu.SMEM)
+    vmem = pl.BlockSpec(memory_space=pltpu.VMEM)
+    hbm = pl.BlockSpec(memory_space=pltpu.HBM)
+    return pl.pallas_call(
+        functools.partial(front_kernel, count),
+        in_specs=[smem] + [hbm] * 7,
+        out_specs=(hbm, vmem, vmem),
+        out_shape=(
+            jax.ShapeDtypeStruct((seq_size, packed, LAT), bf16),
+            jax.ShapeDtypeStruct((padded, WIDE), bf16),
+            jax.ShapeDtypeStruct((heads * count, SENT), bf16),
+        ),
+        scratch_shapes=[
+            pltpu.VMEM(fine.shape, f32),
+            pltpu.VMEM(coarse.shape, f32),
+            pltpu.VMEM((half, width), bf16),
+            pltpu.VMEM(dec.shape, bf16),
+            pltpu.VMEM(lat_proj_t.shape, bf16),
+            pltpu.VMEM(query_proj.shape, bf16),
+            pltpu.VMEM(key_expand.shape, bf16),
+            pltpu.VMEM((half + padded, width), bf16),
+            pltpu.VMEM((half + padded, 2 * ROPE), f32),
+            pltpu.VMEM((packed, LAT), bf16),
+            pltpu.SemaphoreType.DMA((9,)),
+            pltpu.SemaphoreType.DMA((seq_size,)),
+        ],
+        compiler_params=params(),
+    )(lengths, fine, coarse, x, dec, lat_proj_t, query_proj, key_expand)
+
+
+def prefill_query_kernel(
+    fine_hbm,
+    coarse_hbm,
+    x_hbm,
+    query_proj_hbm,
+    state_hbm,
+    qp_ref,
+    state_out_ref,
+    fine_ref,
+    coarse_ref,
+    x_ref,
+    query_proj_ref,
+    state_ref,
+    sems,
+):
+    rows, width = x_ref.shape
     heads = qp_ref.shape[0]
-    requests = lengths_ref.shape[0]
     chunks = 3
     depth = width // chunks
     loads = [
         pltpu.make_async_copy(x_hbm, x_ref, sems.at[0]),
-        pltpu.make_async_copy(dec_hbm, dec_ref, sems.at[1]),
-        pltpu.make_async_copy(lat_proj_hbm, lat_proj_ref, sems.at[2]),
-        pltpu.make_async_copy(expand_hbm, expand_ref, sems.at[3]),
+        pltpu.make_async_copy(fine_hbm.at[pl.ds(0, rows)], fine_ref, sems.at[1]),
+        pltpu.make_async_copy(coarse_hbm, coarse_ref, sems.at[2]),
+        pltpu.make_async_copy(state_hbm, state_ref, sems.at[3]),
     ]
     loads += [
         pltpu.make_async_copy(
@@ -179,126 +311,52 @@
         )
         for i in range(chunks)
     ]
-    loads.append(pltpu.make_async_copy(state_hbm, state_ref, sems.at[4 + chunks]))
-    loads.append(pltpu.make_async_copy(fine_hbm, fine_ref, sems.at[5 + chunks]))
-    loads.append(pltpu.make_async_copy(coarse_hbm, coarse_ref, sems.at[6 + chunks]))
-    for i in (0, 1, 2, 5 + chunks, 6 + chunks):
-        loads[i].start()
+    for load in loads:
+        load.start()
     loads[0].wait()
-    for i in range(4, 4 + chunks):
-        loads[i].start()
-    loads[3].start()
-    normed[:rows] = norm_rows(x_ref[...].astype(f32)).astype(bf16)
+    normed = norm_rows(x_ref[...].astype(f32)).astype(bf16)
     loads[1].wait()
-    tail = normed.shape[0] - rows - count
-    normed[rows:] = jnp.concatenate(
-        [norm_rows(dec_ref[...].astype(f32)), jnp.zeros((tail, width), f32)], axis=0
-    ).astype(bf16)
-    loads[4 + chunks].start()
-    loads[5 + chunks].wait()
-    loads[6 + chunks].wait()
-    for r in range(requests):
-        for t in range(count // requests):
-            at = rows + t * requests + r
-            row = lengths_ref[r] + t
-            turns[at : at + 1] = fine_ref[pl.ds(row, 1)]
-    turns[rows + count :] = jnp.zeros((turns.shape[0] - rows - count, 2 * ROPE), f32)
-    base, near = coarse_ref[pl.ds(seq, 1)], fine_ref[:rows]
-    base_cos, base_sin = base[:, :ROPE], base[:, ROPE:]
-    near_cos, near_sin = near[:, :ROPE], near[:, ROPE:]
-    turns[:rows] = jnp.concatenate(
-        [base_cos * near_cos - base_sin * near_sin, base_sin * near_cos + base_cos * near_sin],
-        axis=-1,
-    )
     loads[2].wait()
-
-    own = pl.ds(pl.multiple_of(core * half_rows, half_rows), half_rows)
-    projected = dot_nt(
-        jnp.concatenate([normed[own], normed[rows:]], axis=0), lat_proj_ref[...]
-    )
-    around = jnp.concatenate([turns[own], turns[rows:]], axis=0)
-    cos, sin = around[:, :ROPE], around[:, ROPE:]
-    latent = jnp.concatenate(
-        [norm_rows(projected[:, :LAT]), turn(projected[:, LAT:], cos, sin)], axis=-1
-    )
-    lat_ref[:half_rows] = latent[:half_rows, :LAT].astype(bf16)
-    lat_ref[half_rows:] = pack_rope(latent[:half_rows, LAT:]).astype(bf16)
-    stores = [
-        pltpu.make_async_copy(lat_ref, lat_hbm.at[i], out_sems.at[i])
-        for i in range(lat_hbm.shape[0])
-    ]
-    for store in stores:
-        store.start()
-    fresh_ref[...] = latent[half_rows:].astype(bf16)
+    turns = turned_tables(coarse_ref[pl.ds(lax.axis_index("seq"), 1)], fine_ref[...])
+    cos, sin = turns[:, :ROPE], turns[:, ROPE:]
+    loads[3].wait()
+    state_out_ref[...] = state_ref[...].astype(bf16)
     total = None
     for i in range(chunks):
         loads[4 + i].wait()
         lanes = slice(i * depth, (i + 1) * depth)
         term = dot_nn(normed[:, lanes], query_proj_ref[lanes])
         total = term if total is None else total + term
-    loads[3].wait()
-    fold = scale * log2e
-    decode = []
-    cos, sin = turns[:, :ROPE], turns[:, ROPE:]
     for head in range(heads):
         at = head * (NOPE + ROPE)
-        nope = total[:, at : at + NOPE]
         turned = turn(total[:, at + NOPE : at + NOPE + ROPE], cos, sin)
         qp_ref[head] = (
-            jnp.concatenate([nope[:rows], turned[:rows]], axis=-1) * fold
+            jnp.concatenate([total[:, at : at + NOPE], turned], axis=-1) * (scale * log2e)
         ).astype(bf16)
-        absorbed = dot_nt(
-            nope[rows:].astype(bf16), expand_ref[:, head * NOPE : (head + 1) * NOPE]
-        )
-        blank = jnp.zeros((absorbed.shape[0], SENT - WIDE), f32)
-        decode.append(jnp.concatenate([absorbed, turned[rows:], blank], axis=-1)[:count])
-    qd_ref[...] = (jnp.concatenate(decode, axis=0) * fold).astype(bf16)
-    loads[4 + chunks].wait()
-    state_out_ref[...] = state_ref[...].astype(bf16)
-    for store in stores:
-        store.wait()
-
-
-def front(lengths, x, dec, lat_proj_t, query_proj, key_expand, states, seq_size):
-    rows, width = x.shape
-    count = dec.shape[0]
-    heads = key_expand.shape[1] // NOPE
-    padded = count + 8
-    requests = lengths.shape[0]
-    reach = max(rows, MAXP * PAGE + count // requests)
-    fine = rope_tables(range(-(-reach // 8) * 8))
-    coarse = rope_tables([rows * i for i in range(seq_size)])
-    smem = pl.BlockSpec(memory_space=pltpu.SMEM)
+
+
+def prefill_queries(fine, coarse, x, query_proj, states):
+    rows = x.shape[0]
+    heads = query_proj.shape[1] // (NOPE + ROPE)
     vmem = pl.BlockSpec(memory_space=pltpu.VMEM)
-    hbm = pl.BlockSpec(memory_space=pltpu.HBM)
     return pl.pallas_call(
-        front_kernel,
-        in_specs=[smem] + [hbm] * 8,
-        out_specs=(hbm, vmem, vmem, vmem, vmem),
+        prefill_query_kernel,
+        in_specs=[pl.BlockSpec(memory_space=pltpu.HBM)] * 5,
+        out_specs=(vmem, vmem),
         out_shape=(
-            jax.ShapeDtypeStruct((seq_size, rows // 2 + rows * ROPE // (2 * LAT), LAT), bf16),
-            jax.ShapeDtypeStruct((padded, WIDE), bf16),
             jax.ShapeDtypeStruct((heads, rows, NOPE + ROPE), bf16),
-            jax.ShapeDtypeStruct((heads * count, SENT), bf16),
             jax.ShapeDtypeStruct(states.shape, bf16),
         ),
         scratch_shapes=[
-            pltpu.VMEM(fine.shape, f32),
+            pltpu.VMEM((rows, fine.shape[1]), f32),
             pltpu.VMEM(coarse.shape, f32),
             pltpu.VMEM(x.shape, bf16),
-            pltpu.VMEM(dec.shape, bf16),
-            pltpu.VMEM(lat_proj_t.shape, bf16),
             pltpu.VMEM(query_proj.shape, bf16),
-            pltpu.VMEM(key_expand.shape, bf16),
             pltpu.VMEM(states.shape, f32),
-            pltpu.VMEM((rows + padded, width), bf16),
-            pltpu.VMEM((rows + padded, 2 * ROPE), f32),
-            pltpu.VMEM((rows // 2 + rows * ROPE // (2 * LAT), LAT), bf16),
-            pltpu.SemaphoreType.DMA((10,)),
-            pltpu.SemaphoreType.DMA((seq_size,)),
+            pltpu.SemaphoreType.DMA((7,)),
         ],
         compiler_params=params(),
-    )(lengths, fine, coarse, x, dec, lat_proj_t, query_proj, key_expand, states)
+    )(fine, coarse, x, query_proj, states)
 
 
 def pack_shares(summed, sum_ref):
@@ -414,7 +472,9 @@
     )(q, mine, other, key_expand, value_expand, mla_output)
 
 
-def gather_share_kernel(parts_ref, x_ref, out_ref):
+def gather_share_kernel(parts_ref, x_ref, *refs):
+    sides, (out_ref, decode_ref) = refs[:-2], refs[-2:]
+    decode_ref[...] = sum(side[...].astype(f32) for side in sides).astype(bf16)
     rows, share = x_ref.shape
     x = x_ref[...].astype(f32)
     total = jnp.sum(parts_ref[...].astype(f32), axis=0)
@@ -429,13 +489,16 @@
     out_ref[...] = jnp.concatenate([left.T, right.T, rest.T], axis=0).astype(bf16)
 
 
-def gather_share(parts, x):
+def gather_share(parts, x, *sides):
     rows, share = x.shape
     return pl.pallas_call(
         gather_share_kernel,
-        out_shape=jax.ShapeDtypeStruct((share, rows), bf16),
+        out_shape=(
+            jax.ShapeDtypeStruct((share, rows), bf16),
+            jax.ShapeDtypeStruct(sides[0].shape, bf16),
+        ),
         compiler_params=params(20),
-    )(parts, x)
+    )(parts, x, *sides)
 
 
 def split_level(level, rows):
@@ -612,7 +675,9 @@
         load.start()
     for load in loads[:3]:
         load.wait()
-    hidden = dec_ref[...].astype(f32) + one_ref[...] + two_ref[...]
+    hidden = dec_ref[...].astype(f32) + (
+        one_ref[...].astype(f32) + two_ref[...].astype(f32)
+    )
     for g in range(shares):
         by_share[g] = hidden[:, g * share : (g + 1) * share]
     hidden_ref[...] = by_share[grp]
@@ -773,16 +838,12 @@
         held[..., None] & (token_pos < lengths[..., None]), owner[..., None], -1
     ).reshape(1, -1)
 
-    x_rows, _, key_owner = lax.optimization_barrier((x_group, own_tokens, key_owner))
-    own_latent, fresh, q_prefill, q_decode, state_rows = front(
-        prompt_len,
-        x_rows,
-        dec,
-        latent_proj.T,
-        query_proj,
-        key_expand,
-        kda_state.reshape(kda_state.shape[0], -1, DK),
-        seq_size,
+    x_rows, _ = lax.optimization_barrier((x_group, own_tokens))
+    reach = max(rows, MAXP * PAGE + steps)
+    fine = rope_tables(range(-(-reach // 8) * 8))
+    coarse = rope_tables([rows * i for i in range(seq_size)])
+    own_latent, fresh, q_decode = front(
+        prompt_len, fine, coarse, x_rows, dec, latent_proj.T, query_proj, key_expand
     )
     sides = grp_size // 2
 
@@ -796,7 +857,9 @@
 
     arrived = lax.all_to_all(own_tokens, "seq", split_axis=0, concat_axis=0, tiled=True)
     queries = [q_decode] + [shift(q_decode, by) for by in range(1, sides)]
-    own_latent, _, _ = lax.optimization_barrier((own_latent, arrived, queries[1]))
+    own_latent, _, _, key_owner = lax.optimization_barrier(
+        (own_latent, arrived, queries[1], key_owner)
+    )
     mine = lax.all_to_all(own_latent, "seq", split_axis=0, concat_axis=0, tiled=True)
     page_keys = arrived.reshape(-1, WIDE)
     queries = queries + [swap(q) for q in queries]
@@ -804,17 +867,26 @@
         queries, page_keys, fresh, key_owner, decode_rows, requests
     )
     merged = merge_pair(keep, swap(send))
+    x_again, _ = lax.optimization_barrier((x_group, merged[1]))
+    q_prefill, state_rows = prefill_queries(
+        fine, coarse, x_again, query_proj, kda_state.reshape(kda_state.shape[0], -1, DK)
+    )
+    partial = [merged[0]] + [shift(merged[by], -by) for by in range(1, sides)]
+    partial[0], _ = lax.optimization_barrier((partial[0], q_prefill))
+    mla_part = combine(partial, value_expand, mla_output)
+    add = lambda one, two: one.astype(f32) + two.astype(f32)
+    trade = lambda value, bits: lax.ppermute(
+        value, "grp", [(g, g ^ bits) for g in range(grp_size)]
+    )
+    mla_pair = add(mla_part, swap(mla_part)).astype(bf16)
+    mla_near = trade(mla_pair, 2)
+    mine, _ = lax.optimization_barrier((mine, mla_pair))
     state_rows, _ = lax.optimization_barrier((state_rows, mine))
     states = lax.all_to_all(
         state_rows, "seq", split_axis=0, concat_axis=0, tiled=True
     ).reshape((seq_size, requests) + state_rows.shape[1:])
-    partial = [merged[0]] + [shift(merged[by], -by) for by in range(1, sides)]
-    mla_part = combine(partial, value_expand, mla_output)
-    mine, _ = lax.optimization_barrier((mine, mla_part))
-    mla_half = mla_part.astype(f32)
-    for by in range(1, sides):
-        mla_half = mla_half + shift(mla_part, by).astype(f32)
-    mla_rest = swap(mla_half)
+    mla_half = add(mla_pair, mla_near).astype(bf16)
+    mla_rest = trade(mla_half, 6)
 
     prefill_part = prefill_attend(
         q_prefill, mine, swap(mine), key_expand, value_expand, mla_output, grp_size
@@ -826,7 +898,6 @@
         prefill_part, "grp", split_axis=0, concat_axis=0, tiled=True
     )
     own_columns = lax.dynamic_slice_in_dim(x_group, grp_index * share, share, 1)
-    prefill_out = gather_share(prefill_parts, own_columns).T
 
     hidden_share, keep, send = kda(
         grp_size,
@@ -844,12 +915,12 @@
         kda_output,
     )
     crossing = swap(send)
-    kda_total = keep[0] + crossing[0].astype(f32)
+    kda_sides = [keep[by] + crossing[by].astype(f32) for by in range(sides)]
+    kda_sides[0] = kda_sides[0] + hidden_share
     for by in range(1, sides):
-        pair = keep[by] + crossing[by].astype(f32)
-        kda_total = kda_total + shift(pair.astype(bf16), by).astype(f32)
-    decode_out = (hidden_share + kda_total).astype(bf16)
-    return (prefill_out, decode_out.reshape(steps, requests, share))
+        kda_sides[by] = shift(kda_sides[by].astype(bf16), by)
+    prefill_out, decode_out = gather_share(prefill_parts, own_columns, *kda_sides)
+    return (prefill_out.T, decode_out.reshape(steps, requests, share))
 
 
 def solution(mesh):

time: 117 us -> 113 us (0.966)
  waiting for transfers between devices: 36.7 us -> 30.1 us
  Pallas kernels: 31.7 us -> 34.6 us
    ppermute x12 -> x9, waiting for transfers between devices: 17.2 us -> 9.76 us  [shift(): lax.ppermute(value, 'grp', [(g, (g + 2 * by) % grp_size) for g in range(g...]
    all_to_all x1, waiting for transfers between devices: 7.51 us -> 3.06 us  [shards(): lax.all_to_all(state_rows, 'seq', split_axis=0, concat_axis=0, tiled=True)]
    ppermute x0 -> x2, starting transfers between devices: none -> 4.41 us  [shards(): lax.ppermute(value, 'grp', [(g, g ^ bits) for g in range(grp_size)])]
    ppermute x0 -> x2, waiting for transfers between devices: none -> 3.98 us  [shards(): lax.ppermute(value, 'grp', [(g, g ^ bits) for g in range(grp_size)])]
    pallas_call x2 -> x3, Pallas kernels: 9.38 us -> 13.3 us  [the longest x1 6.95 us: front(): pl.pallas_call(functools.partial(front_kernel, count), in_specs=[smem] +...]
    ppermute x12 -> x9, starting transfers between devices: 19.2 us -> 16 us  [shift(): lax.ppermute(value, 'grp', [(g, (g + 2 * by) % grp_size) for g in range(g...]
    all_to_all x1, waiting for transfers between devices: 1.13 us -> 3.49 us  [shards(): lax.all_to_all(own_tokens, 'seq', split_axis=0, concat_axis=0, tiled=True)]
    all_to_all x1, starting transfers between devices: 6.24 us -> 4.57 us  [shards(): lax.all_to_all(own_latent, 'seq', split_axis=0, concat_axis=0, tiled=True)]
  transfers between devices with their start and end apart: 24 -> 23, of which waited for: 17 -> 14; matrix products, arithmetic and copies ran while one was open for 3% -> 3% of each run, Pallas kernels for 25% -> 28%
where the time goes in v5:
time: 113 us; the launch traced here: 112 us
  starting transfers between devices  42.4 us (38%)
  Pallas kernels  34.6 us (31%)
  waiting for transfers between devices  30.1 us (27%)
  other arithmetic  2 us (2%)
  local copies, waits for them, and re-layouts  1.46 us (1%)
    ppermute x9, starting transfers between devices, shift(): lax.ppermute(value, 'grp', [(g, (g + 2 * by) % grp_size) for g in range(g...  16 us
    ppermute x9, waiting for transfers between devices, shift(): lax.ppermute(value, 'grp', [(g, (g + 2 * by) % grp_size) for g in range(g...  9.76 us
    pallas_call x1, Pallas kernels, prefill_attend(): pl.pallas_call(functools.partial(flash_kernel, heads), grid=(sources // s...  8.45 us
    all_to_all x1, starting transfers between devices, shards(): lax.all_to_all(own_tokens, 'seq', split_axis=0, concat_axis=0, tiled=True)  8.14 us
    pallas_call x1, Pallas kernels, front(): pl.pallas_call(functools.partial(front_kernel, count), in_specs=[smem] +...  6.95 us
    pallas_call x1, Pallas kernels, kda(): pl.pallas_call(functools.partial(kda_kernel, heads, requests), in_specs=[...  6.82 us
    pallas_call x1, Pallas kernels, prefill_queries(): pl.pallas_call(prefill_query_kernel, in_specs=[pl.BlockSpec(memory_space=...  5.47 us
    all_to_all x1, waiting for transfers between devices, shards(): lax.all_to_all(own_latent, 'seq', split_axis=0, concat_axis=0, tiled=True)  5.4 us
  transfers between devices with their start and end apart: 23, of which 14 were waited for; matrix products, arithmetic and copies ran while one was open for 3% of the time, Pallas kernels for 28%

profile of v5, /device:TPU:0, one launch (start us, length us, event | category | flops | bytes accessed | tf_op | source)
XLA Modules:
  0.0 111.5 jit_solution(1478624545052170164)
XLA Ops:
  0.6 2.1 %shard_map.224 = bf16[16,3,16,576]{3,2,1,0:T(8,128)(2,1)} custom-call(bf16[16,6,64,576]{3,2,1,0:T(8,128)(2,1)} %bitcast.38), custom_call_target="tpu_custom_call" | custom-call | tf_op jit(solution)/shard_map/pallas_call | solution.py:102
  2.7 8.1 %all-to-all-start = ((bf16[16,3,16,576]{3,2,1,0:T(8,128)(2,1)}), bf16[16,3,16,576]{3,2,1,0:T(8,128)(2,1)S(1)}, u32[]{:S(2)}, u32[]{:S(2)}) async-start(bf16[16,3,16,576]{3,2,1,0:T(8,128)(2,1)} %shard_map.224), calls=%async_computation | async-start | bytes 1966080 | tf_op jit(solution)/shard_map/all_to_all | solution.py:858
  10.9 7.0 %shard_map.225 = (bf16[16,144,512]{2,1,0:T(8,128)(2,1)}, bf16[32,576]{1,0:T(8,128)(2,1)}, bf16[96,640]{1,0:T(8,128)(2,1)}) custom-call(s32[8]{0:T(128)} %lengths_ref.1, f32[776,128]{1,0:T(8,128)} %constant.64.clone.fine_hbm, f32[16,128]{1,0:T(8,128)} %constant.65.clone.coarse_hbm, bf16[256,2304]{1,0:T(8,128)(2,1)} %x_hbm.1, bf16[24,2304]{1,0:T(8,128)(2,1)} %bitcast.43, ...), custom_call_target="tpu_custom_call" | custom-call | tf_op jit(solution)/shard_map/pallas_call | solution.py:254
  17.9 1.6 %collective-permute-start = (bf16[96,640]{1,0:T(8,128)(2,1)}, bf16[96,640]{1,0:T(8,128)(2,1)S(1)}, u32[]{:S(2)}, u32[]{:S(2)}) collective-permute-start(bf16[96,640]{1,0:T(8,128)(2,1)} %get-tuple-element.29.refs_0_), channel_id=1, source_target_pairs={{0,2},{1,3},{2,4},{3,5},{4,6},{5,7},{6,0},{7,1},{8,10},{9,11},{10,... | collective-permute-start | bytes 368648 | tf_op jit(solution)/shard_map/ppermute | solution.py:851
  19.5 0.1 copy.32
  19.6 0.1 select_reduce_fusion
  19.7 0.1 copy.31
  19.9 0.1 fusion.1
  20.1 0.1 select_n.61.refs_10_
  20.2 4.1 %collective-permute-done.refs_1_ = bf16[96,640]{1,0:T(8,128)(2,1)S(1)} collective-permute-done((bf16[96,640]{1,0:T(8,128)(2,1)}, bf16[96,640]{1,0:T(8,128)(2,1)S(1)}, u32[]{:S(2)}, u32[]{:S(2)}) %collective-permute-start) | collective-permute-done | bytes 122912 | tf_op jit(solution)/shard_map/ppermute | solution.py:851
  24.2 3.5 %all-to-all-done = bf16[16,3,16,576]{3,2,1,0:T(8,128)(2,1)S(1)} async-done(((bf16[16,3,16,576]{3,2,1,0:T(8,128)(2,1)}), bf16[16,3,16,576]{3,2,1,0:T(8,128)(2,1)S(1)}, u32[]{:S(2)}, u32[]{:S(2)}) %all-to-all-start) | async-done | bytes 884768 | tf_op jit(solution)/shard_map/all_to_all | solution.py:858
  27.7 4.6 %all-to-all-start.1 = ((bf16[16,144,512]{2,1,0:T(8,128)(2,1)}), bf16[16,144,512]{2,1,0:T(8,128)(2,1)}, u32[]{:S(2)}, u32[]{:S(2)}) async-start(bf16[16,144,512]{2,1,0:T(8,128)(2,1)} %get-tuple-element.42), calls=%async_computation.1 | async-start | bytes 4718592 | tf_op jit(solution)/shard_map/all_to_all | solution.py:863
  32.3 3.1 %collective-permute-start.1 = (bf16[96,640]{1,0:T(8,128)(2,1)S(1)}, bf16[96,640]{1,0:T(8,128)(2,1)S(1)}, u32[]{:S(2)}, u32[]{:S(2)}) collective-permute-start(bf16[96,640]{1,0:T(8,128)(2,1)S(1)} %copy-done.2), channel_id=1, source_target_pairs={{0,4},{1,5},{2,6},{3,7},{4,0},{5,1},{6,2},{7,3},{8,12},{9,13},{10,... | collective-permute-start | bytes 368648 | tf_op jit(solution)/shard_map/ppermute | solution.py:851
  35.4 1.1 %collective-permute-start.2 = (bf16[96,640]{1,0:T(8,128)(2,1)S(1)}, bf16[96,640]{1,0:T(8,128)(2,1)S(1)}, u32[]{:S(2)}, u32[]{:S(2)}) collective-permute-start(bf16[96,640]{1,0:T(8,128)(2,1)S(1)} %copy-done.2), channel_id=1, source_target_pairs={{0,6},{1,7},{2,0},{3,1},{4,2},{5,3},{6,4},{7,5},{8,14},{9,15},{10,... | collective-permute-start | bytes 368648 | tf_op jit(solution)/shard_map/ppermute | solution.py:851
  36.6 0.5 collective-permute-start.4
  37.1 1.7 %collective-permute-done.1.refs_2_ = bf16[96,640]{1,0:T(8,128)(2,1)S(1)} collective-permute-done((bf16[96,640]{1,0:T(8,128)(2,1)S(1)}, bf16[96,640]{1,0:T(8,128)(2,1)S(1)}, u32[]{:S(2)}, u32[]{:S(2)}) %collective-permute-start.1) | collective-permute-done | bytes 122912 | tf_op jit(solution)/shard_map/ppermute | solution.py:851
  38.8 1.5 %collective-permute-done.2.refs_3_ = bf16[96,640]{1,0:T(8,128)(2,1)S(1)} collective-permute-done((bf16[96,640]{1,0:T(8,128)(2,1)S(1)}, bf16[96,640]{1,0:T(8,128)(2,1)S(1)}, u32[]{:S(2)}, u32[]{:S(2)}) %collective-permute-start.2) | collective-permute-done | bytes 122912 | tf_op jit(solution)/shard_map/ppermute | solution.py:851
  40.3 1.3 %collective-permute-done.6.refs_7_ = bf16[96,640]{1,0:T(8,128)(2,1)S(1)} collective-permute-done((bf16[96,640]{1,0:T(8,128)(2,1)S(1)}, bf16[96,640]{1,0:T(8,128)(2,1)S(1)}, u32[]{:S(2)}, u32[]{:S(2)}) %collective-permute-start.6) | collective-permute-done | bytes 122912 | tf_op jit(solution)/shard_map/ppermute | solution.py:856
  41.6 2.8 %shard_map.226 = (bf16[4,96,640]{2,1,0:T(8,128)(2,1)S(1)}, bf16[4,96,640]{2,1,0:T(8,128)(2,1)S(1)}) custom-call(bf16[96,640]{1,0:T(8,128)(2,1)S(1)} %copy-done.2, bf16[96,640]{1,0:T(8,128)(2,1)S(1)} %collective-permute-done.refs_1_, bf16[96,640]{1,0:T(8,128)(2,1)S(1)} %collective-permute-done.1.refs_2_, bf16[96,640]{1,0:T(8,128)(2,1)S(1)} %collective-permute-done.2.refs_3_, ...), custom_call_target="tpu_custom_call" | custom-call | tf_op jit(solution)/shard_map/pallas_call | solution.py:576
  44.5 0.2 collective-permute-start.7
  44.7 1.7 %collective-permute-done.7.got_ref = bf16[4,96,640]{2,1,0:T(8,128)(2,1)S(1)} collective-permute-done((bf16[4,96,640]{2,1,0:T(8,128)(2,1)S(1)}, bf16[4,96,640]{2,1,0:T(8,128)(2,1)S(1)}, u32[]{:S(2)}, u32[]{:S(2)}) %collective-permute-start.7) | collective-permute-done | bytes 491552 | tf_op jit(solution)/shard_map/ppermute | solution.py:856
  46.4 0.4 shard_map.227
  46.8 1.4 %collective-permute-start.10 = (bf16[96,640]{1,0:T(8,128)(2,1)S(1)}, bf16[96,640]{1,0:T(8,128)(2,1)S(1)}, u32[]{:S(2)}, u32[]{:S(2)}) collective-permute-start(bf16[96,640]{1,0:T(8,128)(2,1)S(1)} %get-tuple-element.41), channel_id=1, source_target_pairs={{0,2},{1,3},{2,4},{3,5},{4,6},{5,7},{6,0},{7,1},{8,10},{9,11},{10,... | collective-permute-start | bytes 368648 | tf_op jit(solution)/shard_map/ppermute | solution.py:851
  48.2 1.9 %collective-permute-start.8 = (bf16[96,640]{1,0:T(8,128)(2,1)S(1)}, bf16[96,640]{1,0:T(8,128)(2,1)S(1)}, u32[]{:S(2)}, u32[]{:S(2)}) collective-permute-start(bf16[96,640]{1,0:T(8,128)(2,1)S(1)} %get-tuple-element.36), channel_id=1, source_target_pairs={{0,6},{1,7},{2,0},{3,1},{4,2},{5,3},{6,4},{7,5},{8,14},{9,15},{10,... | collective-permute-start | bytes 368648 | tf_op jit(solution)/shard_map/ppermute | solution.py:851
  50.1 0.8 collective-permute-start.9
  50.9 5.5 %shard_map.228 = (bf16[4,256,192]{2,1,0:T(8,128)(2,1)}, bf16[128,32,128]{2,1,0:T(8,128)(2,1)}) custom-call(f32[776,128]{1,0:T(8,128)} %constant.64.clone.fine_hbm, f32[16,128]{1,0:T(8,128)} %constant.65.clone.coarse_hbm, bf16[256,2304]{1,0:T(8,128)(2,1)} %x_hbm.1, bf16[2304,768]{1,0:T(8,128)(2,1)} %query_proj_hbm.3, f32[128,32,128]{2,1,0:T(8,128)} %bitcast.42), custom_call_target="tpu_custom_call" | custom-call | tf_op jit(solution)/shard_map/pallas_call | solution.py:342
  56.4 0.5 collective-permute-done.9.refs_2_
  56.9 0.7 shard_map.229
  57.7 1.3 %collective-permute-done.11 = bf16[24,2304]{1,0:T(8,128)(2,1)S(1)} collective-permute-done((bf16[24,2304]{1,0:T(8,128)(2,1)S(1)}, bf16[24,2304]{1,0:T(8,128)(2,1)S(1)}, u32[]{:S(2)}, u32[]{:S(2)}) %collective-permute-start.11) | collective-permute-done | bytes 110624 | tf_op jit(solution)/shard_map/ppermute | solution.py:856
  59.0 5.4 %all-to-all-done.1.mine_ref = bf16[16,144,512]{2,1,0:T(8,128)(2,1)} async-done(((bf16[16,144,512]{2,1,0:T(8,128)(2,1)}), bf16[16,144,512]{2,1,0:T(8,128)(2,1)}, u32[]{:S(2)}, u32[]{:S(2)}) %all-to-all-start.1) | async-done | bytes 2359328 | tf_op jit(solution)/shard_map/all_to_all | solution.py:863
  64.4 3.7 %all-to-all-start.3 = ((bf16[128,32,128]{2,1,0:T(8,128)(2,1)}), bf16[128,32,128]{2,1,0:T(8,128)(2,1)S(1)}, u32[]{:S(2)}, u32[]{:S(2)}) async-start(bf16[128,32,128]{2,1,0:T(8,128)(2,1)} %get-tuple-element.48), calls=%async_computation.3 | async-start | bytes 2097152 | tf_op jit(solution)/shard_map/all_to_all | solution.py:885
  68.1 1.6 %collective-permute-start.12 = (bf16[24,2304]{1,0:T(8,128)(2,1)S(1)}, bf16[24,2304]{1,0:T(8,128)(2,1)S(1)}, u32[]{:S(2)}, u32[]{:S(2)}) collective-permute-start(bf16[24,2304]{1,0:T(8,128)(2,1)S(1)} %add_convert_fusion.1), channel_id=1, source_target_pairs={{0,2},{1,3},{2,0},{3,1},{4,6},{5,7},{6,4},{7,5},{8,10},{9,11},{10,... | collective-permute-start | bytes 331784 | tf_op jit(solution)/shard_map/ppermute | solution.py:878
  69.7 4.0 %collective-permute-done.12 = bf16[24,2304]{1,0:T(8,128)(2,1)S(1)} collective-permute-done((bf16[24,2304]{1,0:T(8,128)(2,1)S(1)}, bf16[24,2304]{1,0:T(8,128)(2,1)S(1)}, u32[]{:S(2)}, u32[]{:S(2)}) %collective-permute-start.12) | collective-permute-done | bytes 110624 | tf_op jit(solution)/shard_map/ppermute | solution.py:878
  73.7 2.8 %collective-permute-start.13 = (bf16[24,2304]{1,0:T(8,128)(2,1)S(1)}, bf16[24,2304]{1,0:T(8,128)(2,1)S(1)}, u32[]{:S(2)}, u32[]{:S(2)}) collective-permute-start(bf16[24,2304]{1,0:T(8,128)(2,1)S(1)} %add_convert_fusion.one_hbm), channel_id=1, source_target_pairs={{0,6},{1,7},{2,4},{3,5},{4,2},{5,3},{6,0},{7,1},{8,14},{9,15},{10,... | collective-permute-start | bytes 331784 | tf_op jit(solution)/shard_map/ppermute | solution.py:878
  76.5 8.5 %shard_map.230 = bf16[8,576,128]{2,1,0:T(8,128)(2,1)} custom-call(bf16[4,256,192]{2,1,0:T(8,128)(2,1)} %get-tuple-element.38.q_ref, bf16[16,144,512]{2,1,0:T(8,128)(2,1)} %all-to-all-done.1.mine_ref, bf16[16,144,512]{2,1,0:T(8,128)(2,1)} %collective-permute-done.14.other_ref, bf16[512,512]{1,0:T(8,128)(2,1)} %ke_ref.1, bf16[512,512]{1,0:T(8,128)(2,1)} %ve_ref.1, ...), custom_call_target="tpu_custom_call" | custom-call | tf_op jit(solution)/shard_map/pallas_call | solution.py:451
  85.0 3.1 %all-to-all-done.3 = bf16[128,32,128]{2,1,0:T(8,128)(2,1)S(1)} async-done(((bf16[128,32,128]{2,1,0:T(8,128)(2,1)}), bf16[128,32,128]{2,1,0:T(8,128)(2,1)S(1)}, u32[]{:S(2)}, u32[]{:S(2)}) %all-to-all-start.3) | async-done | bytes 1048608 | tf_op jit(solution)/shard_map/all_to_all | solution.py:885
  88.1 4.3 %all-to-all-start.2 = ((bf16[8,576,128]{2,1,0:T(8,128)(2,1)}), bf16[8,576,128]{2,1,0:T(8,128)(2,1)S(1)}, u32[]{:S(2)}, u32[]{:S(2)}) async-start(bf16[8,576,128]{2,1,0:T(8,128)(2,1)} %shard_map.230), calls=%async_computation.2 | async-start | bytes 2359296 | tf_op jit(solution)/shard_map/all_to_all | solution.py:897
  92.4 6.8 %shard_map.231 = (f32[24,288]{1,0:T(8,128)}, f32[4,24,288]{2,1,0:T(8,128)}, bf16[4,24,288]{2,1,0:T(8,128)(2,1)}) custom-call(f32[4]{0:T(128)} %rate_ref.1, bf16[24,2304]{1,0:T(8,128)(2,1)} %copy-done.5, bf16[24,2304]{1,0:T(8,128)(2,1)} %copy-done.6, bf16[24,2304]{1,0:T(8,128)(2,1)} %bitcast.44, bf16[3,2304,512]{2,1,0:T(8,128)(2,1)} %bitcast.39, ...), custom_call_target="tpu_custom_call" | custom-call | tf_op jit(solution)/shard_map/pallas_call | solution.py:773
  99.2 0.6 collective-permute-start.15
  99.8 1.1 constant_dynamic-slice_fusion.x_ref
  100.9 0.8 fusion.4
  101.7 1.9 %collective-permute-start.16 = (bf16[24,288]{1,0:T(8,128)(2,1)S(1)}, bf16[24,288]{1,0:T(8,128)(2,1)S(1)}, u32[]{:S(2)}, u32[]{:S(2)}) collective-permute-start(bf16[24,288]{1,0:T(8,128)(2,1)S(1)} %get-tuple-element.56), channel_id=1, source_target_pairs={{0,2},{1,3},{2,4},{3,5},{4,6},{5,7},{6,0},{7,1},{8,10},{9,11},{10,... | collective-permute-start | bytes 41480 | tf_op jit(solution)/shard_map/ppermute | solution.py:851
  103.7 2.7 %collective-permute-start.17 = (bf16[24,288]{1,0:T(8,128)(2,1)S(1)}, bf16[24,288]{1,0:T(8,128)(2,1)S(1)}, u32[]{:S(2)}, u32[]{:S(2)}) collective-permute-start(bf16[24,288]{1,0:T(8,128)(2,1)S(1)} %get-tuple-element.55), channel_id=1, source_target_pairs={{0,4},{1,5},{2,6},{3,7},{4,0},{5,1},{6,2},{7,3},{8,12},{9,13},{10,... | collective-permute-start | bytes 41480 | tf_op jit(solution)/shard_map/ppermute | solution.py:851
  106.4 1.5 %collective-permute-start.18 = (bf16[24,288]{1,0:T(8,128)(2,1)S(1)}, bf16[24,288]{1,0:T(8,128)(2,1)S(1)}, u32[]{:S(2)}, u32[]{:S(2)}) collective-permute-start(bf16[24,288]{1,0:T(8,128)(2,1)S(1)} %get-tuple-element.54), channel_id=1, source_target_pairs={{0,6},{1,7},{2,0},{3,1},{4,2},{5,3},{6,4},{7,5},{8,14},{9,15},{10,... | collective-permute-start | bytes 41480 | tf_op jit(solution)/shard_map/ppermute | solution.py:851
  107.8 0.8 bitcast_add_fusion.refs_0_
  108.6 1.7 %collective-permute-done.16.refs_1_ = bf16[24,288]{1,0:T(8,128)(2,1)S(1)} collective-permute-done((bf16[24,288]{1,0:T(8,128)(2,1)S(1)}, bf16[24,288]{1,0:T(8,128)(2,1)S(1)}, u32[]{:S(2)}, u32[]{:S(2)}) %collective-permute-start.16) | collective-permute-done | bytes 13856 | tf_op jit(solution)/shard_map/ppermute | solution.py:851
  110.3 0.3 collective-permute-done.17.refs_2_
  110.6 0.9 shard_map.232
  (43 shorter events, 0.4 us)
Async XLA Ops:
  2.7 25.0 %all-to-all-start = ((bf16[16,3,16,576]{3,2,1,0:T(8,128)(2,1)}), bf16[16,3,16,576]{3,2,1,0:T(8,128)(2,1)S(1)}, u32[]{:S(2)}, u32[]{:S(2)}) async-start(bf16[16,3,16,576]{3,2,1,0:T(8,128)(2,1)} %shard_map.224), calls=%async_computation | async-start | bytes 1966080 | tf_op jit(solution)/shard_map/all_to_all | solution.py:858
  10.9 8.6 %copy-start.7 = (s32[16,1,6]{0,1,2:T(1,128)S(1)}, s32[16,1,6]{0,1,2:T(1,128)}, u32[]{:S(2)}) copy-start(s32[16,1,6]{0,1,2:T(1,128)} %param.26) | copy-start | bytes 1156
  10.9 8.7 %copy-start.8 = (s32[8]{0:T(128)S(1)}, s32[8]{0:T(128)}, u32[]{:S(2)}) copy-start(s32[8]{0:T(128)} %lengths_ref.1) | copy-start | bytes 100
  10.9 8.9 %copy-start.9 = (s32[16,1]{0,1:T(1,128)S(1)}, s32[16,1]{0,1:T(1,128)}, u32[]{:S(2)}) copy-start(s32[16,1]{0,1:T(1,128)} %param.27) | copy-start | bytes 196
  17.9 6.4 %collective-permute-start = (bf16[96,640]{1,0:T(8,128)(2,1)}, bf16[96,640]{1,0:T(8,128)(2,1)S(1)}, u32[]{:S(2)}, u32[]{:S(2)}) collective-permute-start(bf16[96,640]{1,0:T(8,128)(2,1)} %get-tuple-element.29.refs_0_), channel_id=1, source_target_pairs={{0,2},{1,3},{2,4},{3,5},{4,6},{5,7},{6,0},{7,1},{8,10},{9,11},{10,... | collective-permute-start | bytes 368648 | tf_op jit(solution)/shard_map/ppermute | solution.py:851
  27.7 4.6 %copy-start.2 = (bf16[96,640]{1,0:T(8,128)(2,1)S(1)}, bf16[96,640]{1,0:T(8,128)(2,1)}, u32[]{:S(2)}) copy-start(bf16[96,640]{1,0:T(8,128)(2,1)} %get-tuple-element.29.refs_0_) | copy-start | bytes 368644
  27.7 13.9 %copy-start.3 = (bf16[32,576]{1,0:T(8,128)(2,1)S(1)}, bf16[32,576]{1,0:T(8,128)(2,1)}, u32[]{:S(2)}) copy-start(bf16[32,576]{1,0:T(8,128)(2,1)} %get-tuple-element.30.refs_9_) | copy-start | bytes 110596
  27.7 36.7 %all-to-all-start.1 = ((bf16[16,144,512]{2,1,0:T(8,128)(2,1)}), bf16[16,144,512]{2,1,0:T(8,128)(2,1)}, u32[]{:S(2)}, u32[]{:S(2)}) async-start(bf16[16,144,512]{2,1,0:T(8,128)(2,1)} %get-tuple-element.42), calls=%async_computation.1 | async-start | bytes 4718592 | tf_op jit(solution)/shard_map/all_to_all | solution.py:863
  32.3 6.5 %collective-permute-start.1 = (bf16[96,640]{1,0:T(8,128)(2,1)S(1)}, bf16[96,640]{1,0:T(8,128)(2,1)S(1)}, u32[]{:S(2)}, u32[]{:S(2)}) collective-permute-start(bf16[96,640]{1,0:T(8,128)(2,1)S(1)} %copy-done.2), channel_id=1, source_target_pairs={{0,4},{1,5},{2,6},{3,7},{4,0},{5,1},{6,2},{7,3},{8,12},{9,13},{10,... | collective-permute-start | bytes 368648 | tf_op jit(solution)/shard_map/ppermute | solution.py:851
  35.4 4.9 %collective-permute-start.2 = (bf16[96,640]{1,0:T(8,128)(2,1)S(1)}, bf16[96,640]{1,0:T(8,128)(2,1)S(1)}, u32[]{:S(2)}, u32[]{:S(2)}) collective-permute-start(bf16[96,640]{1,0:T(8,128)(2,1)S(1)} %copy-done.2), channel_id=1, source_target_pairs={{0,6},{1,7},{2,0},{3,1},{4,2},{5,3},{6,4},{7,5},{8,14},{9,15},{10,... | collective-permute-start | bytes 368648 | tf_op jit(solution)/shard_map/ppermute | solution.py:851
  36.6 3.7 %collective-permute-start.3 = (bf16[96,640]{1,0:T(8,128)(2,1)S(1)}, bf16[96,640]{1,0:T(8,128)(2,1)S(1)}, u32[]{:S(2)}, u32[]{:S(2)}) collective-permute-start(bf16[96,640]{1,0:T(8,128)(2,1)S(1)} %copy-done.2), channel_id=1, source_target_pairs={{0,1},{1,0},{2,3},{3,2},{4,5},{5,4},{6,7},{7,6},{8,9},{9,8},{10,11... | collective-permute-start | bytes 368648 | tf_op jit(solution)/shard_map/ppermute | solution.py:856
  36.6 3.7 %collective-permute-start.4 = (bf16[96,640]{1,0:T(8,128)(2,1)S(1)}, bf16[96,640]{1,0:T(8,128)(2,1)S(1)}, u32[]{:S(2)}, u32[]{:S(2)}) collective-permute-start(bf16[96,640]{1,0:T(8,128)(2,1)S(1)} %collective-permute-done.refs_1_), channel_id=1, source_target_pairs={{0,1},{1,0},{2,3},{3,2},{4,5},{5,4},{6,7},{7,6},{8,9},{9,8},{10,11... | collective-permute-start | bytes 368648 | tf_op jit(solution)/shard_map/ppermute | solution.py:856
  38.8 1.5 %collective-permute-start.5 = (bf16[96,640]{1,0:T(8,128)(2,1)S(1)}, bf16[96,640]{1,0:T(8,128)(2,1)S(1)}, u32[]{:S(2)}, u32[]{:S(2)}) collective-permute-start(bf16[96,640]{1,0:T(8,128)(2,1)S(1)} %collective-permute-done.1.refs_2_), channel_id=1, source_target_pairs={{0,1},{1,0},{2,3},{3,2},{4,5},{5,4},{6,7},{7,6},{8,9},{9,8},{10,11... | collective-permute-start | bytes 368648 | tf_op jit(solution)/shard_map/ppermute | solution.py:856
  40.3 1.3 %collective-permute-start.6 = (bf16[96,640]{1,0:T(8,128)(2,1)S(1)}, bf16[96,640]{1,0:T(8,128)(2,1)S(1)}, u32[]{:S(2)}, u32[]{:S(2)}) collective-permute-start(bf16[96,640]{1,0:T(8,128)(2,1)S(1)} %collective-permute-done.2.refs_3_), channel_id=1, source_target_pairs={{0,1},{1,0},{2,3},{3,2},{4,5},{5,4},{6,7},{7,6},{8,9},{9,8},{10,11... | collective-permute-start | bytes 368648 | tf_op jit(solution)/shard_map/ppermute | solution.py:856
  44.5 1.9 %collective-permute-start.7 = (bf16[4,96,640]{2,1,0:T(8,128)(2,1)S(1)}, bf16[4,96,640]{2,1,0:T(8,128)(2,1)S(1)}, u32[]{:S(2)}, u32[]{:S(2)}) collective-permute-start(bf16[4,96,640]{2,1,0:T(8,128)(2,1)S(1)} %get-tuple-element.34), channel_id=1, source_target_pairs={{0,1},{1,0},{2,3},{3,2},{4,5},{5,4},{6,7},{7,6},{8,9},{9,8},{10,11... | collective-permute-start | bytes 1474568 | tf_op jit(solution)/shard_map/ppermute | solution.py:856
  46.8 9.6 %collective-permute-start.10 = (bf16[96,640]{1,0:T(8,128)(2,1)S(1)}, bf16[96,640]{1,0:T(8,128)(2,1)S(1)}, u32[]{:S(2)}, u32[]{:S(2)}) collective-permute-start(bf16[96,640]{1,0:T(8,128)(2,1)S(1)} %get-tuple-element.41), channel_id=1, source_target_pairs={{0,2},{1,3},{2,4},{3,5},{4,6},{5,7},{6,0},{7,1},{8,10},{9,11},{10,... | collective-permute-start | bytes 368648 | tf_op jit(solution)/shard_map/ppermute | solution.py:851
  48.2 8.2 %collective-permute-start.8 = (bf16[96,640]{1,0:T(8,128)(2,1)S(1)}, bf16[96,640]{1,0:T(8,128)(2,1)S(1)}, u32[]{:S(2)}, u32[]{:S(2)}) collective-permute-start(bf16[96,640]{1,0:T(8,128)(2,1)S(1)} %get-tuple-element.36), channel_id=1, source_target_pairs={{0,6},{1,7},{2,0},{3,1},{4,2},{5,3},{6,4},{7,5},{8,14},{9,15},{10,... | collective-permute-start | bytes 368648 | tf_op jit(solution)/shard_map/ppermute | solution.py:851
  50.1 6.8 %collective-permute-start.9 = (bf16[96,640]{1,0:T(8,128)(2,1)S(1)}, bf16[96,640]{1,0:T(8,128)(2,1)S(1)}, u32[]{:S(2)}, u32[]{:S(2)}) collective-permute-start(bf16[96,640]{1,0:T(8,128)(2,1)S(1)} %get-tuple-element.40), channel_id=1, source_target_pairs={{0,4},{1,5},{2,6},{3,7},{4,0},{5,1},{6,2},{7,3},{8,12},{9,13},{10,... | collective-permute-start | bytes 368648 | tf_op jit(solution)/shard_map/ppermute | solution.py:851
  50.9 6.0 %copy-start = (bf16[512,2304]{1,0:T(8,128)(2,1)S(1)}, bf16[512,2304]{1,0:T(8,128)(2,1)}, u32[]{:S(2)}) copy-start(bf16[512,2304]{1,0:T(8,128)(2,1)} %out_hbm.1) | copy-start | bytes 7077892
  50.9 6.0 %copy-start.1 = (bf16[512,512]{1,0:T(8,128)(2,1)S(1)}, bf16[512,512]{1,0:T(8,128)(2,1)}, u32[]{:S(2)}) copy-start(bf16[512,512]{1,0:T(8,128)(2,1)} %ve_ref.1) | copy-start | bytes 1572868
  57.6 1.4 %collective-permute-start.11 = (bf16[24,2304]{1,0:T(8,128)(2,1)S(1)}, bf16[24,2304]{1,0:T(8,128)(2,1)S(1)}, u32[]{:S(2)}, u32[]{:S(2)}) collective-permute-start(bf16[24,2304]{1,0:T(8,128)(2,1)S(1)} %shard_map.229), channel_id=1, source_target_pairs={{0,1},{1,0},{2,3},{3,2},{4,5},{5,4},{6,7},{7,6},{8,9},{9,8},{10,11... | collective-permute-start | bytes 331784 | tf_op jit(solution)/shard_map/ppermute | solution.py:856
  64.4 12.1 %collective-permute-start.14 = (bf16[16,144,512]{2,1,0:T(8,128)(2,1)}, bf16[16,144,512]{2,1,0:T(8,128)(2,1)}, u32[]{:S(2)}, u32[]{:S(2)}) collective-permute-start(bf16[16,144,512]{2,1,0:T(8,128)(2,1)} %all-to-all-done.1.mine_ref), channel_id=1, source_target_pairs={{0,1},{1,0},{2,3},{3,2},{4,5},{5,4},{6,7},{7,6},{8,9},{9,8},{10,11... | collective-permute-start | bytes 7077896 | tf_op jit(solution)/shard_map/ppermute | solution.py:856
  64.4 23.7 %all-to-all-start.3 = ((bf16[128,32,128]{2,1,0:T(8,128)(2,1)}), bf16[128,32,128]{2,1,0:T(8,128)(2,1)S(1)}, u32[]{:S(2)}, u32[]{:S(2)}) async-start(bf16[128,32,128]{2,1,0:T(8,128)(2,1)} %get-tuple-element.48), calls=%async_computation.3 | async-start | bytes 2097152 | tf_op jit(solution)/shard_map/all_to_all | solution.py:885
  68.1 5.5 %collective-permute-start.12 = (bf16[24,2304]{1,0:T(8,128)(2,1)S(1)}, bf16[24,2304]{1,0:T(8,128)(2,1)S(1)}, u32[]{:S(2)}, u32[]{:S(2)}) collective-permute-start(bf16[24,2304]{1,0:T(8,128)(2,1)S(1)} %add_convert_fusion.1), channel_id=1, source_target_pairs={{0,2},{1,3},{2,0},{3,1},{4,6},{5,7},{6,4},{7,5},{8,10},{9,11},{10,... | collective-permute-start | bytes 331784 | tf_op jit(solution)/shard_map/ppermute | solution.py:878
  73.7 11.3 %copy-start.5 = (bf16[24,2304]{1,0:T(8,128)(2,1)}, bf16[24,2304]{1,0:T(8,128)(2,1)S(1)}, u32[]{:S(2)}) copy-start(bf16[24,2304]{1,0:T(8,128)(2,1)S(1)} %add_convert_fusion.one_hbm) | copy-start | bytes 331780
  73.7 11.3 %collective-permute-start.13 = (bf16[24,2304]{1,0:T(8,128)(2,1)S(1)}, bf16[24,2304]{1,0:T(8,128)(2,1)S(1)}, u32[]{:S(2)}, u32[]{:S(2)}) collective-permute-start(bf16[24,2304]{1,0:T(8,128)(2,1)S(1)} %add_convert_fusion.one_hbm), channel_id=1, source_target_pairs={{0,6},{1,7},{2,4},{3,5},{4,2},{5,3},{6,0},{7,1},{8,14},{9,15},{10,... | collective-permute-start | bytes 331784 | tf_op jit(solution)/shard_map/ppermute | solution.py:878
  85.0 7.4 %copy-start.6 = (bf16[24,2304]{1,0:T(8,128)(2,1)}, bf16[24,2304]{1,0:T(8,128)(2,1)S(1)}, u32[]{:S(2)}) copy-start(bf16[24,2304]{1,0:T(8,128)(2,1)S(1)} %collective-permute-done.13.two_hbm) | copy-start | bytes 331780
  88.1 4.3 %copy-start.4 = (bf16[128,32,128]{2,1,0:T(8,128)(2,1)}, bf16[128,32,128]{2,1,0:T(8,128)(2,1)S(1)}, u32[]{:S(2)}) copy-start(bf16[128,32,128]{2,1,0:T(8,128)(2,1)S(1)} %all-to-all-done.3) | copy-start | bytes 3145732
  88.1 22.5 %all-to-all-start.2 = ((bf16[8,576,128]{2,1,0:T(8,128)(2,1)}), bf16[8,576,128]{2,1,0:T(8,128)(2,1)S(1)}, u32[]{:S(2)}, u32[]{:S(2)}) async-start(bf16[8,576,128]{2,1,0:T(8,128)(2,1)} %shard_map.230), calls=%async_computation.2 | async-start | bytes 2359296 | tf_op jit(solution)/shard_map/all_to_all | solution.py:897
  99.2 1.7 %collective-permute-start.15 = (bf16[4,24,288]{2,1,0:T(8,128)(2,1)}, bf16[4,24,288]{2,1,0:T(8,128)(2,1)S(1)}, u32[]{:S(2)}, u32[]{:S(2)}) collective-permute-start(bf16[4,24,288]{2,1,0:T(8,128)(2,1)} %get-tuple-element.50), channel_id=1, source_target_pairs={{0,1},{1,0},{2,3},{3,2},{4,5},{5,4},{6,7},{7,6},{8,9},{9,8},{10,11... | collective-permute-start | bytes 165896 | tf_op jit(solution)/shard_map/ppermute | solution.py:856
  101.7 8.5 %collective-permute-start.16 = (bf16[24,288]{1,0:T(8,128)(2,1)S(1)}, bf16[24,288]{1,0:T(8,128)(2,1)S(1)}, u32[]{:S(2)}, u32[]{:S(2)}) collective-permute-start(bf16[24,288]{1,0:T(8,128)(2,1)S(1)} %get-tuple-element.56), channel_id=1, source_target_pairs={{0,2},{1,3},{2,4},{3,5},{4,6},{5,7},{6,0},{7,1},{8,10},{9,11},{10,... | collective-permute-start | bytes 41480 | tf_op jit(solution)/shard_map/ppermute | solution.py:851
  103.7 6.9 %collective-permute-start.17 = (bf16[24,288]{1,0:T(8,128)(2,1)S(1)}, bf16[24,288]{1,0:T(8,128)(2,1)S(1)}, u32[]{:S(2)}, u32[]{:S(2)}) collective-permute-start(bf16[24,288]{1,0:T(8,128)(2,1)S(1)} %get-tuple-element.55), channel_id=1, source_target_pairs={{0,4},{1,5},{2,6},{3,7},{4,0},{5,1},{6,2},{7,3},{8,12},{9,13},{10,... | collective-permute-start | bytes 41480 | tf_op jit(solution)/shard_map/ppermute | solution.py:851
  106.4 4.2 %collective-permute-start.18 = (bf16[24,288]{1,0:T(8,128)(2,1)S(1)}, bf16[24,288]{1,0:T(8,128)(2,1)S(1)}, u32[]{:S(2)}, u32[]{:S(2)}) collective-permute-start(bf16[24,288]{1,0:T(8,128)(2,1)S(1)} %get-tuple-element.54), channel_id=1, source_target_pairs={{0,6},{1,7},{2,0},{3,1},{4,2},{5,3},{6,4},{7,5},{8,14},{9,15},{10,... | collective-permute-start | bytes 41480 | tf_op jit(solution)/shard_map/ppermute | solution.py:851

commit v6 on v5

--- a/solution.py
+++ b/solution.py
@@ -444,7 +444,7 @@
 def prefill_attend(q, mine, other, key_expand, value_expand, mla_output, shares):
     heads, rows, _ = q.shape
     sources, packed, _ = mine.shape
-    side = max(1, min(sources, 1024 // rows))
+    side = max(1, min(sources, 2048 // rows))
     width = mla_output.shape[1]
     dense = rows * width // shares // 128
     whole = lambda shape: pl.BlockSpec(shape, lambda i: (0,) * len(shape))

time: 113 us -> 113 us (level)
  transfers between devices with their start and end apart: 23 -> 23, of which waited for: 14 -> 14; matrix products, arithmetic and copies ran while one was open for 3% -> 3% of each run, Pallas kernels for 28% -> 29%
where the time goes in v6:
time: 113 us; the launch traced here: 112 us
  starting transfers between devices  42.4 us (38%)
  Pallas kernels  35.7 us (32%)
  waiting for transfers between devices  29 us (26%)
  other arithmetic  2 us (2%)
  local copies, waits for them, and re-layouts  1.46 us (1%)
    ppermute x9, starting transfers between devices, shift(): lax.ppermute(value, 'grp', [(g, (g + 2 * by) % grp_size) for g in range(g...  16 us
    ppermute x9, waiting for transfers between devices, shift(): lax.ppermute(value, 'grp', [(g, (g + 2 * by) % grp_size) for g in range(g...  9.76 us
    pallas_call x1, Pallas kernels, prefill_attend(): pl.pallas_call(functools.partial(flash_kernel, heads), grid=(sources // s...  9.53 us
    all_to_all x1, starting transfers between devices, shards(): lax.all_to_all(own_tokens, 'seq', split_axis=0, concat_axis=0, tiled=True)  8.14 us
    pallas_call x1, Pallas kernels, front(): pl.pallas_call(functools.partial(front_kernel, count), in_specs=[smem] +...  6.95 us
    pallas_call x1, Pallas kernels, kda(): pl.pallas_call(functools.partial(kda_kernel, heads, requests), in_specs=[...  6.82 us
    pallas_call x1, Pallas kernels, prefill_queries(): pl.pallas_call(prefill_query_kernel, in_specs=[pl.BlockSpec(memory_space=...  5.47 us
    all_to_all x1, waiting for transfers between devices, shards(): lax.all_to_all(own_latent, 'seq', split_axis=0, concat_axis=0, tiled=True)  5.4 us
  transfers between devices with their start and end apart: 23, of which 14 were waited for; matrix products, arithmetic and copies ran while one was open for 3% of the time, Pallas kernels for 29%

profile of v6, /device:TPU:0, one launch (start us, length us, event | category | flops | bytes accessed | tf_op | source)
XLA Modules:
  0.0 111.5 jit_solution(13378952834341199014)
XLA Ops:
  0.6 2.1 %shard_map.224 = bf16[16,3,16,576]{3,2,1,0:T(8,128)(2,1)} custom-call(bf16[16,6,64,576]{3,2,1,0:T(8,128)(2,1)} %bitcast.38), custom_call_target="tpu_custom_call" | custom-call | tf_op jit(solution)/shard_map/pallas_call | solution.py:102
  2.7 8.1 %all-to-all-start = ((bf16[16,3,16,576]{3,2,1,0:T(8,128)(2,1)}), bf16[16,3,16,576]{3,2,1,0:T(8,128)(2,1)S(1)}, u32[]{:S(2)}, u32[]{:S(2)}) async-start(bf16[16,3,16,576]{3,2,1,0:T(8,128)(2,1)} %shard_map.224), calls=%async_computation | async-start | bytes 1966080 | tf_op jit(solution)/shard_map/all_to_all | solution.py:858
  10.9 7.0 %shard_map.225 = (bf16[16,144,512]{2,1,0:T(8,128)(2,1)}, bf16[32,576]{1,0:T(8,128)(2,1)}, bf16[96,640]{1,0:T(8,128)(2,1)}) custom-call(s32[8]{0:T(128)} %lengths_ref.1, f32[776,128]{1,0:T(8,128)} %constant.64.clone.fine_hbm, f32[16,128]{1,0:T(8,128)} %constant.65.clone.coarse_hbm, bf16[256,2304]{1,0:T(8,128)(2,1)} %x_hbm.1, bf16[24,2304]{1,0:T(8,128)(2,1)} %bitcast.43, ...), custom_call_target="tpu_custom_call" | custom-call | tf_op jit(solution)/shard_map/pallas_call | solution.py:254
  17.9 1.6 %collective-permute-start = (bf16[96,640]{1,0:T(8,128)(2,1)}, bf16[96,640]{1,0:T(8,128)(2,1)S(1)}, u32[]{:S(2)}, u32[]{:S(2)}) collective-permute-start(bf16[96,640]{1,0:T(8,128)(2,1)} %get-tuple-element.29.refs_0_), channel_id=1, source_target_pairs={{0,2},{1,3},{2,4},{3,5},{4,6},{5,7},{6,0},{7,1},{8,10},{9,11},{10,... | collective-permute-start | bytes 368648 | tf_op jit(solution)/shard_map/ppermute | solution.py:851
  19.5 0.1 copy.32
  19.6 0.1 select_reduce_fusion
  19.7 0.1 copy.31
  19.9 0.1 fusion.1
  20.1 0.1 select_n.61.refs_10_
  20.2 4.1 %collective-permute-done.refs_1_ = bf16[96,640]{1,0:T(8,128)(2,1)S(1)} collective-permute-done((bf16[96,640]{1,0:T(8,128)(2,1)}, bf16[96,640]{1,0:T(8,128)(2,1)S(1)}, u32[]{:S(2)}, u32[]{:S(2)}) %collective-permute-start) | collective-permute-done | bytes 122912 | tf_op jit(solution)/shard_map/ppermute | solution.py:851
  24.2 3.5 %all-to-all-done = bf16[16,3,16,576]{3,2,1,0:T(8,128)(2,1)S(1)} async-done(((bf16[16,3,16,576]{3,2,1,0:T(8,128)(2,1)}), bf16[16,3,16,576]{3,2,1,0:T(8,128)(2,1)S(1)}, u32[]{:S(2)}, u32[]{:S(2)}) %all-to-all-start) | async-done | bytes 884768 | tf_op jit(solution)/shard_map/all_to_all | solution.py:858
  27.7 4.6 %all-to-all-start.1 = ((bf16[16,144,512]{2,1,0:T(8,128)(2,1)}), bf16[16,144,512]{2,1,0:T(8,128)(2,1)}, u32[]{:S(2)}, u32[]{:S(2)}) async-start(bf16[16,144,512]{2,1,0:T(8,128)(2,1)} %get-tuple-element.42), calls=%async_computation.1 | async-start | bytes 4718592 | tf_op jit(solution)/shard_map/all_to_all | solution.py:863
  32.3 3.1 %collective-permute-start.1 = (bf16[96,640]{1,0:T(8,128)(2,1)S(1)}, bf16[96,640]{1,0:T(8,128)(2,1)S(1)}, u32[]{:S(2)}, u32[]{:S(2)}) collective-permute-start(bf16[96,640]{1,0:T(8,128)(2,1)S(1)} %copy-done.2), channel_id=1, source_target_pairs={{0,4},{1,5},{2,6},{3,7},{4,0},{5,1},{6,2},{7,3},{8,12},{9,13},{10,... | collective-permute-start | bytes 368648 | tf_op jit(solution)/shard_map/ppermute | solution.py:851
  35.4 1.1 %collective-permute-start.2 = (bf16[96,640]{1,0:T(8,128)(2,1)S(1)}, bf16[96,640]{1,0:T(8,128)(2,1)S(1)}, u32[]{:S(2)}, u32[]{:S(2)}) collective-permute-start(bf16[96,640]{1,0:T(8,128)(2,1)S(1)} %copy-done.2), channel_id=1, source_target_pairs={{0,6},{1,7},{2,0},{3,1},{4,2},{5,3},{6,4},{7,5},{8,14},{9,15},{10,... | collective-permute-start | bytes 368648 | tf_op jit(solution)/shard_map/ppermute | solution.py:851
  36.6 0.5 collective-permute-start.4
  37.1 1.7 %collective-permute-done.1.refs_2_ = bf16[96,640]{1,0:T(8,128)(2,1)S(1)} collective-permute-done((bf16[96,640]{1,0:T(8,128)(2,1)S(1)}, bf16[96,640]{1,0:T(8,128)(2,1)S(1)}, u32[]{:S(2)}, u32[]{:S(2)}) %collective-permute-start.1) | collective-permute-done | bytes 122912 | tf_op jit(solution)/shard_map/ppermute | solution.py:851
  38.8 1.5 %collective-permute-done.2.refs_3_ = bf16[96,640]{1,0:T(8,128)(2,1)S(1)} collective-permute-done((bf16[96,640]{1,0:T(8,128)(2,1)S(1)}, bf16[96,640]{1,0:T(8,128)(2,1)S(1)}, u32[]{:S(2)}, u32[]{:S(2)}) %collective-permute-start.2) | collective-permute-done | bytes 122912 | tf_op jit(solution)/shard_map/ppermute | solution.py:851
  40.3 1.3 %collective-permute-done.6.refs_7_ = bf16[96,640]{1,0:T(8,128)(2,1)S(1)} collective-permute-done((bf16[96,640]{1,0:T(8,128)(2,1)S(1)}, bf16[96,640]{1,0:T(8,128)(2,1)S(1)}, u32[]{:S(2)}, u32[]{:S(2)}) %collective-permute-start.6) | collective-permute-done | bytes 122912 | tf_op jit(solution)/shard_map/ppermute | solution.py:856
  41.6 2.8 %shard_map.226 = (bf16[4,96,640]{2,1,0:T(8,128)(2,1)S(1)}, bf16[4,96,640]{2,1,0:T(8,128)(2,1)S(1)}) custom-call(bf16[96,640]{1,0:T(8,128)(2,1)S(1)} %copy-done.2, bf16[96,640]{1,0:T(8,128)(2,1)S(1)} %collective-permute-done.refs_1_, bf16[96,640]{1,0:T(8,128)(2,1)S(1)} %collective-permute-done.1.refs_2_, bf16[96,640]{1,0:T(8,128)(2,1)S(1)} %collective-permute-done.2.refs_3_, ...), custom_call_target="tpu_custom_call" | custom-call | tf_op jit(solution)/shard_map/pallas_call | solution.py:576
  44.5 0.2 collective-permute-start.7
  44.7 1.7 %collective-permute-done.7.got_ref = bf16[4,96,640]{2,1,0:T(8,128)(2,1)S(1)} collective-permute-done((bf16[4,96,640]{2,1,0:T(8,128)(2,1)S(1)}, bf16[4,96,640]{2,1,0:T(8,128)(2,1)S(1)}, u32[]{:S(2)}, u32[]{:S(2)}) %collective-permute-start.7) | collective-permute-done | bytes 491552 | tf_op jit(solution)/shard_map/ppermute | solution.py:856
  46.4 0.4 shard_map.227
  46.8 1.4 %collective-permute-start.10 = (bf16[96,640]{1,0:T(8,128)(2,1)S(1)}, bf16[96,640]{1,0:T(8,128)(2,1)S(1)}, u32[]{:S(2)}, u32[]{:S(2)}) collective-permute-start(bf16[96,640]{1,0:T(8,128)(2,1)S(1)} %get-tuple-element.41), channel_id=1, source_target_pairs={{0,2},{1,3},{2,4},{3,5},{4,6},{5,7},{6,0},{7,1},{8,10},{9,11},{10,... | collective-permute-start | bytes 368648 | tf_op jit(solution)/shard_map/ppermute | solution.py:851
  48.2 1.9 %collective-permute-start.8 = (bf16[96,640]{1,0:T(8,128)(2,1)S(1)}, bf16[96,640]{1,0:T(8,128)(2,1)S(1)}, u32[]{:S(2)}, u32[]{:S(2)}) collective-permute-start(bf16[96,640]{1,0:T(8,128)(2,1)S(1)} %get-tuple-element.36), channel_id=1, source_target_pairs={{0,6},{1,7},{2,0},{3,1},{4,2},{5,3},{6,4},{7,5},{8,14},{9,15},{10,... | collective-permute-start | bytes 368648 | tf_op jit(solution)/shard_map/ppermute | solution.py:851
  50.1 0.8 collective-permute-start.9
  50.9 5.5 %shard_map.228 = (bf16[4,256,192]{2,1,0:T(8,128)(2,1)}, bf16[128,32,128]{2,1,0:T(8,128)(2,1)}) custom-call(f32[776,128]{1,0:T(8,128)} %constant.64.clone.fine_hbm, f32[16,128]{1,0:T(8,128)} %constant.65.clone.coarse_hbm, bf16[256,2304]{1,0:T(8,128)(2,1)} %x_hbm.1, bf16[2304,768]{1,0:T(8,128)(2,1)} %query_proj_hbm.3, f32[128,32,128]{2,1,0:T(8,128)} %bitcast.42), custom_call_target="tpu_custom_call" | custom-call | tf_op jit(solution)/shard_map/pallas_call | solution.py:342
  56.4 0.5 collective-permute-done.9.refs_2_
  56.9 0.7 shard_map.229
  57.7 1.3 %collective-permute-done.11 = bf16[24,2304]{1,0:T(8,128)(2,1)S(1)} collective-permute-done((bf16[24,2304]{1,0:T(8,128)(2,1)S(1)}, bf16[24,2304]{1,0:T(8,128)(2,1)S(1)}, u32[]{:S(2)}, u32[]{:S(2)}) %collective-permute-start.11) | collective-permute-done | bytes 110624 | tf_op jit(solution)/shard_map/ppermute | solution.py:856
  59.0 5.4 %all-to-all-done.1.mine_ref = bf16[16,144,512]{2,1,0:T(8,128)(2,1)} async-done(((bf16[16,144,512]{2,1,0:T(8,128)(2,1)}), bf16[16,144,512]{2,1,0:T(8,128)(2,1)}, u32[]{:S(2)}, u32[]{:S(2)}) %all-to-all-start.1) | async-done | bytes 2359328 | tf_op jit(solution)/shard_map/all_to_all | solution.py:863
  64.4 3.7 %all-to-all-start.3 = ((bf16[128,32,128]{2,1,0:T(8,128)(2,1)}), bf16[128,32,128]{2,1,0:T(8,128)(2,1)S(1)}, u32[]{:S(2)}, u32[]{:S(2)}) async-start(bf16[128,32,128]{2,1,0:T(8,128)(2,1)} %get-tuple-element.48), calls=%async_computation.3 | async-start | bytes 2097152 | tf_op jit(solution)/shard_map/all_to_all | solution.py:885
  68.1 1.6 %collective-permute-start.12 = (bf16[24,2304]{1,0:T(8,128)(2,1)S(1)}, bf16[24,2304]{1,0:T(8,128)(2,1)S(1)}, u32[]{:S(2)}, u32[]{:S(2)}) collective-permute-start(bf16[24,2304]{1,0:T(8,128)(2,1)S(1)} %add_convert_fusion.1), channel_id=1, source_target_pairs={{0,2},{1,3},{2,0},{3,1},{4,6},{5,7},{6,4},{7,5},{8,10},{9,11},{10,... | collective-permute-start | bytes 331784 | tf_op jit(solution)/shard_map/ppermute | solution.py:878
  69.7 4.0 %collective-permute-done.12 = bf16[24,2304]{1,0:T(8,128)(2,1)S(1)} collective-permute-done((bf16[24,2304]{1,0:T(8,128)(2,1)S(1)}, bf16[24,2304]{1,0:T(8,128)(2,1)S(1)}, u32[]{:S(2)}, u32[]{:S(2)}) %collective-permute-start.12) | collective-permute-done | bytes 110624 | tf_op jit(solution)/shard_map/ppermute | solution.py:878
  73.7 2.8 %collective-permute-start.13 = (bf16[24,2304]{1,0:T(8,128)(2,1)S(1)}, bf16[24,2304]{1,0:T(8,128)(2,1)S(1)}, u32[]{:S(2)}, u32[]{:S(2)}) collective-permute-start(bf16[24,2304]{1,0:T(8,128)(2,1)S(1)} %add_convert_fusion.one_hbm), channel_id=1, source_target_pairs={{0,6},{1,7},{2,4},{3,5},{4,2},{5,3},{6,0},{7,1},{8,14},{9,15},{10,... | collective-permute-start | bytes 331784 | tf_op jit(solution)/shard_map/ppermute | solution.py:878
  76.5 9.5 %shard_map.230 = bf16[8,576,128]{2,1,0:T(8,128)(2,1)} custom-call(bf16[4,256,192]{2,1,0:T(8,128)(2,1)} %get-tuple-element.38.q_ref, bf16[16,144,512]{2,1,0:T(8,128)(2,1)} %all-to-all-done.1.mine_ref, bf16[16,144,512]{2,1,0:T(8,128)(2,1)} %collective-permute-done.14.other_ref, bf16[512,512]{1,0:T(8,128)(2,1)} %ke_ref.1, bf16[512,512]{1,0:T(8,128)(2,1)} %ve_ref.1, ...), custom_call_target="tpu_custom_call" | custom-call | tf_op jit(solution)/shard_map/pallas_call | solution.py:451
  86.1 2.0 %all-to-all-done.3 = bf16[128,32,128]{2,1,0:T(8,128)(2,1)S(1)} async-done(((bf16[128,32,128]{2,1,0:T(8,128)(2,1)}), bf16[128,32,128]{2,1,0:T(8,128)(2,1)S(1)}, u32[]{:S(2)}, u32[]{:S(2)}) %all-to-all-start.3) | async-done | bytes 1048608 | tf_op jit(solution)/shard_map/all_to_all | solution.py:885
  88.1 4.3 %all-to-all-start.2 = ((bf16[8,576,128]{2,1,0:T(8,128)(2,1)}), bf16[8,576,128]{2,1,0:T(8,128)(2,1)S(1)}, u32[]{:S(2)}, u32[]{:S(2)}) async-start(bf16[8,576,128]{2,1,0:T(8,128)(2,1)} %shard_map.230), calls=%async_computation.2 | async-start | bytes 2359296 | tf_op jit(solution)/shard_map/all_to_all | solution.py:897
  92.4 6.8 %shard_map.231 = (f32[24,288]{1,0:T(8,128)}, f32[4,24,288]{2,1,0:T(8,128)}, bf16[4,24,288]{2,1,0:T(8,128)(2,1)}) custom-call(f32[4]{0:T(128)} %rate_ref.1, bf16[24,2304]{1,0:T(8,128)(2,1)} %copy-done.5, bf16[24,2304]{1,0:T(8,128)(2,1)} %copy-done.6, bf16[24,2304]{1,0:T(8,128)(2,1)} %bitcast.44, bf16[3,2304,512]{2,1,0:T(8,128)(2,1)} %bitcast.39, ...), custom_call_target="tpu_custom_call" | custom-call | tf_op jit(solution)/shard_map/pallas_call | solution.py:773
  99.2 0.6 collective-permute-start.15
  99.8 1.1 constant_dynamic-slice_fusion.x_ref
  100.9 0.8 fusion.4
  101.7 1.9 %collective-permute-start.16 = (bf16[24,288]{1,0:T(8,128)(2,1)S(1)}, bf16[24,288]{1,0:T(8,128)(2,1)S(1)}, u32[]{:S(2)}, u32[]{:S(2)}) collective-permute-start(bf16[24,288]{1,0:T(8,128)(2,1)S(1)} %get-tuple-element.56), channel_id=1, source_target_pairs={{0,2},{1,3},{2,4},{3,5},{4,6},{5,7},{6,0},{7,1},{8,10},{9,11},{10,... | collective-permute-start | bytes 41480 | tf_op jit(solution)/shard_map/ppermute | solution.py:851
  103.7 2.7 %collective-permute-start.17 = (bf16[24,288]{1,0:T(8,128)(2,1)S(1)}, bf16[24,288]{1,0:T(8,128)(2,1)S(1)}, u32[]{:S(2)}, u32[]{:S(2)}) collective-permute-start(bf16[24,288]{1,0:T(8,128)(2,1)S(1)} %get-tuple-element.55), channel_id=1, source_target_pairs={{0,4},{1,5},{2,6},{3,7},{4,0},{5,1},{6,2},{7,3},{8,12},{9,13},{10,... | collective-permute-start | bytes 41480 | tf_op jit(solution)/shard_map/ppermute | solution.py:851
  106.4 1.5 %collective-permute-start.18 = (bf16[24,288]{1,0:T(8,128)(2,1)S(1)}, bf16[24,288]{1,0:T(8,128)(2,1)S(1)}, u32[]{:S(2)}, u32[]{:S(2)}) collective-permute-start(bf16[24,288]{1,0:T(8,128)(2,1)S(1)} %get-tuple-element.54), channel_id=1, source_target_pairs={{0,6},{1,7},{2,0},{3,1},{4,2},{5,3},{6,4},{7,5},{8,14},{9,15},{10,... | collective-permute-start | bytes 41480 | tf_op jit(solution)/shard_map/ppermute | solution.py:851
  107.8 0.8 bitcast_add_fusion.refs_0_
  108.6 1.7 %collective-permute-done.16.refs_1_ = bf16[24,288]{1,0:T(8,128)(2,1)S(1)} collective-permute-done((bf16[24,288]{1,0:T(8,128)(2,1)S(1)}, bf16[24,288]{1,0:T(8,128)(2,1)S(1)}, u32[]{:S(2)}, u32[]{:S(2)}) %collective-permute-start.16) | collective-permute-done | bytes 13856 | tf_op jit(solution)/shard_map/ppermute | solution.py:851
  110.3 0.3 collective-permute-done.17.refs_2_
  110.6 0.9 shard_map.232
  (43 shorter events, 0.4 us)
Async XLA Ops:
  2.7 25.0 %all-to-all-start = ((bf16[16,3,16,576]{3,2,1,0:T(8,128)(2,1)}), bf16[16,3,16,576]{3,2,1,0:T(8,128)(2,1)S(1)}, u32[]{:S(2)}, u32[]{:S(2)}) async-start(bf16[16,3,16,576]{3,2,1,0:T(8,128)(2,1)} %shard_map.224), calls=%async_computation | async-start | bytes 1966080 | tf_op jit(solution)/shard_map/all_to_all | solution.py:858
  10.9 8.6 %copy-start.7 = (s32[16,1,6]{0,1,2:T(1,128)S(1)}, s32[16,1,6]{0,1,2:T(1,128)}, u32[]{:S(2)}) copy-start(s32[16,1,6]{0,1,2:T(1,128)} %param.26) | copy-start | bytes 1156
  10.9 8.7 %copy-start.8 = (s32[8]{0:T(128)S(1)}, s32[8]{0:T(128)}, u32[]{:S(2)}) copy-start(s32[8]{0:T(128)} %lengths_ref.1) | copy-start | bytes 100
  10.9 8.9 %copy-start.9 = (s32[16,1]{0,1:T(1,128)S(1)}, s32[16,1]{0,1:T(1,128)}, u32[]{:S(2)}) copy-start(s32[16,1]{0,1:T(1,128)} %param.27) | copy-start | bytes 196
  17.9 6.4 %collective-permute-start = (bf16[96,640]{1,0:T(8,128)(2,1)}, bf16[96,640]{1,0:T(8,128)(2,1)S(1)}, u32[]{:S(2)}, u32[]{:S(2)}) collective-permute-start(bf16[96,640]{1,0:T(8,128)(2,1)} %get-tuple-element.29.refs_0_), channel_id=1, source_target_pairs={{0,2},{1,3},{2,4},{3,5},{4,6},{5,7},{6,0},{7,1},{8,10},{9,11},{10,... | collective-permute-start | bytes 368648 | tf_op jit(solution)/shard_map/ppermute | solution.py:851
  27.7 4.6 %copy-start.2 = (bf16[96,640]{1,0:T(8,128)(2,1)S(1)}, bf16[96,640]{1,0:T(8,128)(2,1)}, u32[]{:S(2)}) copy-start(bf16[96,640]{1,0:T(8,128)(2,1)} %get-tuple-element.29.refs_0_) | copy-start | bytes 368644
  27.7 13.9 %copy-start.3 = (bf16[32,576]{1,0:T(8,128)(2,1)S(1)}, bf16[32,576]{1,0:T(8,128)(2,1)}, u32[]{:S(2)}) copy-start(bf16[32,576]{1,0:T(8,128)(2,1)} %get-tuple-element.30.refs_9_) | copy-start | bytes 110596
  27.7 36.7 %all-to-all-start.1 = ((bf16[16,144,512]{2,1,0:T(8,128)(2,1)}), bf16[16,144,512]{2,1,0:T(8,128)(2,1)}, u32[]{:S(2)}, u32[]{:S(2)}) async-start(bf16[16,144,512]{2,1,0:T(8,128)(2,1)} %get-tuple-element.42), calls=%async_computation.1 | async-start | bytes 4718592 | tf_op jit(solution)/shard_map/all_to_all | solution.py:863
  32.3 6.5 %collective-permute-start.1 = (bf16[96,640]{1,0:T(8,128)(2,1)S(1)}, bf16[96,640]{1,0:T(8,128)(2,1)S(1)}, u32[]{:S(2)}, u32[]{:S(2)}) collective-permute-start(bf16[96,640]{1,0:T(8,128)(2,1)S(1)} %copy-done.2), channel_id=1, source_target_pairs={{0,4},{1,5},{2,6},{3,7},{4,0},{5,1},{6,2},{7,3},{8,12},{9,13},{10,... | collective-permute-start | bytes 368648 | tf_op jit(solution)/shard_map/ppermute | solution.py:851
  35.4 4.9 %collective-permute-start.2 = (bf16[96,640]{1,0:T(8,128)(2,1)S(1)}, bf16[96,640]{1,0:T(8,128)(2,1)S(1)}, u32[]{:S(2)}, u32[]{:S(2)}) collective-permute-start(bf16[96,640]{1,0:T(8,128)(2,1)S(1)} %copy-done.2), channel_id=1, source_target_pairs={{0,6},{1,7},{2,0},{3,1},{4,2},{5,3},{6,4},{7,5},{8,14},{9,15},{10,... | collective-permute-start | bytes 368648 | tf_op jit(solution)/shard_map/ppermute | solution.py:851
  36.6 3.7 %collective-permute-start.3 = (bf16[96,640]{1,0:T(8,128)(2,1)S(1)}, bf16[96,640]{1,0:T(8,128)(2,1)S(1)}, u32[]{:S(2)}, u32[]{:S(2)}) collective-permute-start(bf16[96,640]{1,0:T(8,128)(2,1)S(1)} %copy-done.2), channel_id=1, source_target_pairs={{0,1},{1,0},{2,3},{3,2},{4,5},{5,4},{6,7},{7,6},{8,9},{9,8},{10,11... | collective-permute-start | bytes 368648 | tf_op jit(solution)/shard_map/ppermute | solution.py:856
  36.6 3.7 %collective-permute-start.4 = (bf16[96,640]{1,0:T(8,128)(2,1)S(1)}, bf16[96,640]{1,0:T(8,128)(2,1)S(1)}, u32[]{:S(2)}, u32[]{:S(2)}) collective-permute-start(bf16[96,640]{1,0:T(8,128)(2,1)S(1)} %collective-permute-done.refs_1_), channel_id=1, source_target_pairs={{0,1},{1,0},{2,3},{3,2},{4,5},{5,4},{6,7},{7,6},{8,9},{9,8},{10,11... | collective-permute-start | bytes 368648 | tf_op jit(solution)/shard_map/ppermute | solution.py:856
  38.8 1.5 %collective-permute-start.5 = (bf16[96,640]{1,0:T(8,128)(2,1)S(1)}, bf16[96,640]{1,0:T(8,128)(2,1)S(1)}, u32[]{:S(2)}, u32[]{:S(2)}) collective-permute-start(bf16[96,640]{1,0:T(8,128)(2,1)S(1)} %collective-permute-done.1.refs_2_), channel_id=1, source_target_pairs={{0,1},{1,0},{2,3},{3,2},{4,5},{5,4},{6,7},{7,6},{8,9},{9,8},{10,11... | collective-permute-start | bytes 368648 | tf_op jit(solution)/shard_map/ppermute | solution.py:856
  40.3 1.3 %collective-permute-start.6 = (bf16[96,640]{1,0:T(8,128)(2,1)S(1)}, bf16[96,640]{1,0:T(8,128)(2,1)S(1)}, u32[]{:S(2)}, u32[]{:S(2)}) collective-permute-start(bf16[96,640]{1,0:T(8,128)(2,1)S(1)} %collective-permute-done.2.refs_3_), channel_id=1, source_target_pairs={{0,1},{1,0},{2,3},{3,2},{4,5},{5,4},{6,7},{7,6},{8,9},{9,8},{10,11... | collective-permute-start | bytes 368648 | tf_op jit(solution)/shard_map/ppermute | solution.py:856
  44.5 1.9 %collective-permute-start.7 = (bf16[4,96,640]{2,1,0:T(8,128)(2,1)S(1)}, bf16[4,96,640]{2,1,0:T(8,128)(2,1)S(1)}, u32[]{:S(2)}, u32[]{:S(2)}) collective-permute-start(bf16[4,96,640]{2,1,0:T(8,128)(2,1)S(1)} %get-tuple-element.34), channel_id=1, source_target_pairs={{0,1},{1,0},{2,3},{3,2},{4,5},{5,4},{6,7},{7,6},{8,9},{9,8},{10,11... | collective-permute-start | bytes 1474568 | tf_op jit(solution)/shard_map/ppermute | solution.py:856
  46.8 9.6 %collective-permute-start.10 = (bf16[96,640]{1,0:T(8,128)(2,1)S(1)}, bf16[96,640]{1,0:T(8,128)(2,1)S(1)}, u32[]{:S(2)}, u32[]{:S(2)}) collective-permute-start(bf16[96,640]{1,0:T(8,128)(2,1)S(1)} %get-tuple-element.41), channel_id=1, source_target_pairs={{0,2},{1,3},{2,4},{3,5},{4,6},{5,7},{6,0},{7,1},{8,10},{9,11},{10,... | collective-permute-start | bytes 368648 | tf_op jit(solution)/shard_map/ppermute | solution.py:851
  48.2 8.2 %collective-permute-start.8 = (bf16[96,640]{1,0:T(8,128)(2,1)S(1)}, bf16[96,640]{1,0:T(8,128)(2,1)S(1)}, u32[]{:S(2)}, u32[]{:S(2)}) collective-permute-start(bf16[96,640]{1,0:T(8,128)(2,1)S(1)} %get-tuple-element.36), channel_id=1, source_target_pairs={{0,6},{1,7},{2,0},{3,1},{4,2},{5,3},{6,4},{7,5},{8,14},{9,15},{10,... | collective-permute-start | bytes 368648 | tf_op jit(solution)/shard_map/ppermute | solution.py:851
  50.1 6.8 %collective-permute-start.9 = (bf16[96,640]{1,0:T(8,128)(2,1)S(1)}, bf16[96,640]{1,0:T(8,128)(2,1)S(1)}, u32[]{:S(2)}, u32[]{:S(2)}) collective-permute-start(bf16[96,640]{1,0:T(8,128)(2,1)S(1)} %get-tuple-element.40), channel_id=1, source_target_pairs={{0,4},{1,5},{2,6},{3,7},{4,0},{5,1},{6,2},{7,3},{8,12},{9,13},{10,... | collective-permute-start | bytes 368648 | tf_op jit(solution)/shard_map/ppermute | solution.py:851
  50.9 6.0 %copy-start = (bf16[512,2304]{1,0:T(8,128)(2,1)S(1)}, bf16[512,2304]{1,0:T(8,128)(2,1)}, u32[]{:S(2)}) copy-start(bf16[512,2304]{1,0:T(8,128)(2,1)} %out_hbm.1) | copy-start | bytes 7077892
  50.9 6.0 %copy-start.1 = (bf16[512,512]{1,0:T(8,128)(2,1)S(1)}, bf16[512,512]{1,0:T(8,128)(2,1)}, u32[]{:S(2)}) copy-start(bf16[512,512]{1,0:T(8,128)(2,1)} %ve_ref.1) | copy-start | bytes 1572868
  57.6 1.4 %collective-permute-start.11 = (bf16[24,2304]{1,0:T(8,128)(2,1)S(1)}, bf16[24,2304]{1,0:T(8,128)(2,1)S(1)}, u32[]{:S(2)}, u32[]{:S(2)}) collective-permute-start(bf16[24,2304]{1,0:T(8,128)(2,1)S(1)} %shard_map.229), channel_id=1, source_target_pairs={{0,1},{1,0},{2,3},{3,2},{4,5},{5,4},{6,7},{7,6},{8,9},{9,8},{10,11... | collective-permute-start | bytes 331784 | tf_op jit(solution)/shard_map/ppermute | solution.py:856
  64.4 12.1 %collective-permute-start.14 = (bf16[16,144,512]{2,1,0:T(8,128)(2,1)}, bf16[16,144,512]{2,1,0:T(8,128)(2,1)}, u32[]{:S(2)}, u32[]{:S(2)}) collective-permute-start(bf16[16,144,512]{2,1,0:T(8,128)(2,1)} %all-to-all-done.1.mine_ref), channel_id=1, source_target_pairs={{0,1},{1,0},{2,3},{3,2},{4,5},{5,4},{6,7},{7,6},{8,9},{9,8},{10,11... | collective-permute-start | bytes 7077896 | tf_op jit(solution)/shard_map/ppermute | solution.py:856
  64.4 23.7 %all-to-all-start.3 = ((bf16[128,32,128]{2,1,0:T(8,128)(2,1)}), bf16[128,32,128]{2,1,0:T(8,128)(2,1)S(1)}, u32[]{:S(2)}, u32[]{:S(2)}) async-start(bf16[128,32,128]{2,1,0:T(8,128)(2,1)} %get-tuple-element.48), calls=%async_computation.3 | async-start | bytes 2097152 | tf_op jit(solution)/shard_map/all_to_all | solution.py:885
  68.1 5.5 %collective-permute-start.12 = (bf16[24,2304]{1,0:T(8,128)(2,1)S(1)}, bf16[24,2304]{1,0:T(8,128)(2,1)S(1)}, u32[]{:S(2)}, u32[]{:S(2)}) collective-permute-start(bf16[24,2304]{1,0:T(8,128)(2,1)S(1)} %add_convert_fusion.1), channel_id=1, source_target_pairs={{0,2},{1,3},{2,0},{3,1},{4,6},{5,7},{6,4},{7,5},{8,10},{9,11},{10,... | collective-permute-start | bytes 331784 | tf_op jit(solution)/shard_map/ppermute | solution.py:878
  73.7 12.4 %copy-start.5 = (bf16[24,2304]{1,0:T(8,128)(2,1)}, bf16[24,2304]{1,0:T(8,128)(2,1)S(1)}, u32[]{:S(2)}) copy-start(bf16[24,2304]{1,0:T(8,128)(2,1)S(1)} %add_convert_fusion.one_hbm) | copy-start | bytes 331780
  73.7 12.4 %collective-permute-start.13 = (bf16[24,2304]{1,0:T(8,128)(2,1)S(1)}, bf16[24,2304]{1,0:T(8,128)(2,1)S(1)}, u32[]{:S(2)}, u32[]{:S(2)}) collective-permute-start(bf16[24,2304]{1,0:T(8,128)(2,1)S(1)} %add_convert_fusion.one_hbm), channel_id=1, source_target_pairs={{0,6},{1,7},{2,4},{3,5},{4,2},{5,3},{6,0},{7,1},{8,14},{9,15},{10,... | collective-permute-start | bytes 331784 | tf_op jit(solution)/shard_map/ppermute | solution.py:878
  86.1 6.3 %copy-start.6 = (bf16[24,2304]{1,0:T(8,128)(2,1)}, bf16[24,2304]{1,0:T(8,128)(2,1)S(1)}, u32[]{:S(2)}) copy-start(bf16[24,2304]{1,0:T(8,128)(2,1)S(1)} %collective-permute-done.13.two_hbm) | copy-start | bytes 331780
  88.1 4.3 %copy-start.4 = (bf16[128,32,128]{2,1,0:T(8,128)(2,1)}, bf16[128,32,128]{2,1,0:T(8,128)(2,1)S(1)}, u32[]{:S(2)}) copy-start(bf16[128,32,128]{2,1,0:T(8,128)(2,1)S(1)} %all-to-all-done.3) | copy-start | bytes 3145732
  88.1 22.5 %all-to-all-start.2 = ((bf16[8,576,128]{2,1,0:T(8,128)(2,1)}), bf16[8,576,128]{2,1,0:T(8,128)(2,1)S(1)}, u32[]{:S(2)}, u32[]{:S(2)}) async-start(bf16[8,576,128]{2,1,0:T(8,128)(2,1)} %shard_map.230), calls=%async_computation.2 | async-start | bytes 2359296 | tf_op jit(solution)/shard_map/all_to_all | solution.py:897
  99.2 1.7 %collective-permute-start.15 = (bf16[4,24,288]{2,1,0:T(8,128)(2,1)}, bf16[4,24,288]{2,1,0:T(8,128)(2,1)S(1)}, u32[]{:S(2)}, u32[]{:S(2)}) collective-permute-start(bf16[4,24,288]{2,1,0:T(8,128)(2,1)} %get-tuple-element.50), channel_id=1, source_target_pairs={{0,1},{1,0},{2,3},{3,2},{4,5},{5,4},{6,7},{7,6},{8,9},{9,8},{10,11... | collective-permute-start | bytes 165896 | tf_op jit(solution)/shard_map/ppermute | solution.py:856
  101.7 8.5 %collective-permute-start.16 = (bf16[24,288]{1,0:T(8,128)(2,1)S(1)}, bf16[24,288]{1,0:T(8,128)(2,1)S(1)}, u32[]{:S(2)}, u32[]{:S(2)}) collective-permute-start(bf16[24,288]{1,0:T(8,128)(2,1)S(1)} %get-tuple-element.56), channel_id=1, source_target_pairs={{0,2},{1,3},{2,4},{3,5},{4,6},{5,7},{6,0},{7,1},{8,10},{9,11},{10,... | collective-permute-start | bytes 41480 | tf_op jit(solution)/shard_map/ppermute | solution.py:851
  103.7 6.9 %collective-permute-start.17 = (bf16[24,288]{1,0:T(8,128)(2,1)S(1)}, bf16[24,288]{1,0:T(8,128)(2,1)S(1)}, u32[]{:S(2)}, u32[]{:S(2)}) collective-permute-start(bf16[24,288]{1,0:T(8,128)(2,1)S(1)} %get-tuple-element.55), channel_id=1, source_target_pairs={{0,4},{1,5},{2,6},{3,7},{4,0},{5,1},{6,2},{7,3},{8,12},{9,13},{10,... | collective-permute-start | bytes 41480 | tf_op jit(solution)/shard_map/ppermute | solution.py:851
  106.4 4.2 %collective-permute-start.18 = (bf16[24,288]{1,0:T(8,128)(2,1)S(1)}, bf16[24,288]{1,0:T(8,128)(2,1)S(1)}, u32[]{:S(2)}, u32[]{:S(2)}) collective-permute-start(bf16[24,288]{1,0:T(8,128)(2,1)S(1)} %get-tuple-element.54), channel_id=1, source_target_pairs={{0,6},{1,7},{2,0},{3,1},{4,2},{5,3},{6,4},{7,5},{8,14},{9,15},{10,... | collective-permute-start | bytes 41480 | tf_op jit(solution)/shard_map/ppermute | solution.py:851

commit v7 on v6

--- a/solution.py
+++ b/solution.py
@@ -408,13 +408,25 @@
             )
             scores.append(dot_nt(whole_keys, q_ref[head]))
         if masked:
-            row = lax.broadcasted_iota(jnp.int32, (block, rows), 0)
-            from_other = row >= side
-            row = jnp.where(from_other, row - side, row)
-            which = jnp.where(from_other, 1 - core, core)
-            key_pos = step * block + (row // half) * rows + which * half + lax.rem(row, half)
-            live = key_pos <= first + lax.broadcasted_iota(jnp.int32, (block, rows), 1)
-            scores = [jnp.where(live, s, masked_score) for s in scores]
+            ahead = lax.broadcasted_iota(jnp.int32, (half, rows), 0) - lax.broadcasted_iota(
+                jnp.int32, (half, rows), 1
+            )
+            count = mine_ref.shape[0]
+            limits = [
+                first - (step * count + i) * rows - which * half
+                for which in (core, 1 - core)
+                for i in range(count)
+            ]
+            scores = [
+                jnp.concatenate(
+                    [
+                        jnp.where(ahead <= limit, s[j * half : (j + 1) * half], masked_score)
+                        for j, limit in enumerate(limits)
+                    ],
+                    axis=0,
+                )
+                for s in scores
+            ]
         for head in range(heads):
             old = peak[head]
             new = jnp.maximum(old, jnp.max(scores[head], axis=0, keepdims=True))

time: 113 us -> 113 us (level)
  no operation moved by 1% of the time
where the time goes in v7:
time: 113 us; the launch traced here: 112 us
  starting transfers between devices  42.4 us (38%)
  Pallas kernels  35.7 us (32%)
  waiting for transfers between devices  29 us (26%)
  other arithmetic  2 us (2%)
  local copies, waits for them, and re-layouts  1.46 us (1%)
    ppermute x9, starting transfers between devices, shift(): lax.ppermute(value, 'grp', [(g, (g + 2 * by) % grp_size) for g in range(g...  16 us
    ppermute x9, waiting for transfers between devices, shift(): lax.ppermute(value, 'grp', [(g, (g + 2 * by) % grp_size) for g in range(g...  9.76 us
    pallas_call x1, Pallas kernels, prefill_attend(): pl.pallas_call(functools.partial(flash_kernel, heads), grid=(sources // s...  9.57 us
    all_to_all x1, starting transfers between devices, shards(): lax.all_to_all(own_tokens, 'seq', split_axis=0, concat_axis=0, tiled=True)  8.14 us
    pallas_call x1, Pallas kernels, front(): pl.pallas_call(functools.partial(front_kernel, count), in_specs=[smem] +...  6.95 us
    pallas_call x1, Pallas kernels, kda(): pl.pallas_call(functools.partial(kda_kernel, heads, requests), in_specs=[...  6.82 us
    pallas_call x1, Pallas kernels, prefill_queries(): pl.pallas_call(prefill_query_kernel, in_specs=[pl.BlockSpec(memory_space=...  5.47 us
    all_to_all x1, waiting for transfers between devices, shards(): lax.all_to_all(own_latent, 'seq', split_axis=0, concat_axis=0, tiled=True)  5.4 us
  transfers between devices with their start and end apart: 23, of which 14 were waited for; matrix products, arithmetic and copies ran while one was open for 3% of the time, Pallas kernels for 29%

profile of v7, /device:TPU:0, one launch (start us, length us, event | category | flops | bytes accessed | tf_op | source)
XLA Modules:
  0.0 111.5 jit_solution(8532945613294795025)
XLA Ops:
  0.6 2.1 %shard_map.224 = bf16[16,3,16,576]{3,2,1,0:T(8,128)(2,1)} custom-call(bf16[16,6,64,576]{3,2,1,0:T(8,128)(2,1)} %bitcast.38), custom_call_target="tpu_custom_call" | custom-call | tf_op jit(solution)/shard_map/pallas_call | solution.py:102
  2.7 8.1 %all-to-all-start = ((bf16[16,3,16,576]{3,2,1,0:T(8,128)(2,1)}), bf16[16,3,16,576]{3,2,1,0:T(8,128)(2,1)S(1)}, u32[]{:S(2)}, u32[]{:S(2)}) async-start(bf16[16,3,16,576]{3,2,1,0:T(8,128)(2,1)} %shard_map.224), calls=%async_computation | async-start | bytes 1966080 | tf_op jit(solution)/shard_map/all_to_all | solution.py:870
  10.9 7.0 %shard_map.225 = (bf16[16,144,512]{2,1,0:T(8,128)(2,1)}, bf16[32,576]{1,0:T(8,128)(2,1)}, bf16[96,640]{1,0:T(8,128)(2,1)}) custom-call(s32[8]{0:T(128)} %lengths_ref.1, f32[776,128]{1,0:T(8,128)} %constant.64.clone.fine_hbm, f32[16,128]{1,0:T(8,128)} %constant.65.clone.coarse_hbm, bf16[256,2304]{1,0:T(8,128)(2,1)} %x_hbm.1, bf16[24,2304]{1,0:T(8,128)(2,1)} %bitcast.43, ...), custom_call_target="tpu_custom_call" | custom-call | tf_op jit(solution)/shard_map/pallas_call | solution.py:254
  17.9 1.6 %collective-permute-start = (bf16[96,640]{1,0:T(8,128)(2,1)}, bf16[96,640]{1,0:T(8,128)(2,1)S(1)}, u32[]{:S(2)}, u32[]{:S(2)}) collective-permute-start(bf16[96,640]{1,0:T(8,128)(2,1)} %get-tuple-element.29.refs_0_), channel_id=1, source_target_pairs={{0,2},{1,3},{2,4},{3,5},{4,6},{5,7},{6,0},{7,1},{8,10},{9,11},{10,... | collective-permute-start | bytes 368648 | tf_op jit(solution)/shard_map/ppermute | solution.py:863
  19.5 0.1 copy.32
  19.6 0.1 select_reduce_fusion
  19.7 0.1 copy.31
  19.9 0.1 fusion.1
  20.1 0.1 select_n.61.refs_10_
  20.2 4.1 %collective-permute-done.refs_1_ = bf16[96,640]{1,0:T(8,128)(2,1)S(1)} collective-permute-done((bf16[96,640]{1,0:T(8,128)(2,1)}, bf16[96,640]{1,0:T(8,128)(2,1)S(1)}, u32[]{:S(2)}, u32[]{:S(2)}) %collective-permute-start) | collective-permute-done | bytes 122912 | tf_op jit(solution)/shard_map/ppermute | solution.py:863
  24.2 3.5 %all-to-all-done = bf16[16,3,16,576]{3,2,1,0:T(8,128)(2,1)S(1)} async-done(((bf16[16,3,16,576]{3,2,1,0:T(8,128)(2,1)}), bf16[16,3,16,576]{3,2,1,0:T(8,128)(2,1)S(1)}, u32[]{:S(2)}, u32[]{:S(2)}) %all-to-all-start) | async-done | bytes 884768 | tf_op jit(solution)/shard_map/all_to_all | solution.py:870
  27.7 4.6 %all-to-all-start.1 = ((bf16[16,144,512]{2,1,0:T(8,128)(2,1)}), bf16[16,144,512]{2,1,0:T(8,128)(2,1)}, u32[]{:S(2)}, u32[]{:S(2)}) async-start(bf16[16,144,512]{2,1,0:T(8,128)(2,1)} %get-tuple-element.42), calls=%async_computation.1 | async-start | bytes 4718592 | tf_op jit(solution)/shard_map/all_to_all | solution.py:875
  32.3 3.1 %collective-permute-start.1 = (bf16[96,640]{1,0:T(8,128)(2,1)S(1)}, bf16[96,640]{1,0:T(8,128)(2,1)S(1)}, u32[]{:S(2)}, u32[]{:S(2)}) collective-permute-start(bf16[96,640]{1,0:T(8,128)(2,1)S(1)} %copy-done.2), channel_id=1, source_target_pairs={{0,4},{1,5},{2,6},{3,7},{4,0},{5,1},{6,2},{7,3},{8,12},{9,13},{10,... | collective-permute-start | bytes 368648 | tf_op jit(solution)/shard_map/ppermute | solution.py:863
  35.4 1.1 %collective-permute-start.2 = (bf16[96,640]{1,0:T(8,128)(2,1)S(1)}, bf16[96,640]{1,0:T(8,128)(2,1)S(1)}, u32[]{:S(2)}, u32[]{:S(2)}) collective-permute-start(bf16[96,640]{1,0:T(8,128)(2,1)S(1)} %copy-done.2), channel_id=1, source_target_pairs={{0,6},{1,7},{2,0},{3,1},{4,2},{5,3},{6,4},{7,5},{8,14},{9,15},{10,... | collective-permute-start | bytes 368648 | tf_op jit(solution)/shard_map/ppermute | solution.py:863
  36.6 0.5 collective-permute-start.4
  37.1 1.7 %collective-permute-done.1.refs_2_ = bf16[96,640]{1,0:T(8,128)(2,1)S(1)} collective-permute-done((bf16[96,640]{1,0:T(8,128)(2,1)S(1)}, bf16[96,640]{1,0:T(8,128)(2,1)S(1)}, u32[]{:S(2)}, u32[]{:S(2)}) %collective-permute-start.1) | collective-permute-done | bytes 122912 | tf_op jit(solution)/shard_map/ppermute | solution.py:863
  38.8 1.5 %collective-permute-done.2.refs_3_ = bf16[96,640]{1,0:T(8,128)(2,1)S(1)} collective-permute-done((bf16[96,640]{1,0:T(8,128)(2,1)S(1)}, bf16[96,640]{1,0:T(8,128)(2,1)S(1)}, u32[]{:S(2)}, u32[]{:S(2)}) %collective-permute-start.2) | collective-permute-done | bytes 122912 | tf_op jit(solution)/shard_map/ppermute | solution.py:863
  40.3 1.3 %collective-permute-done.6.refs_7_ = bf16[96,640]{1,0:T(8,128)(2,1)S(1)} collective-permute-done((bf16[96,640]{1,0:T(8,128)(2,1)S(1)}, bf16[96,640]{1,0:T(8,128)(2,1)S(1)}, u32[]{:S(2)}, u32[]{:S(2)}) %collective-permute-start.6) | collective-permute-done | bytes 122912 | tf_op jit(solution)/shard_map/ppermute | solution.py:868
  41.6 2.8 %shard_map.226 = (bf16[4,96,640]{2,1,0:T(8,128)(2,1)S(1)}, bf16[4,96,640]{2,1,0:T(8,128)(2,1)S(1)}) custom-call(bf16[96,640]{1,0:T(8,128)(2,1)S(1)} %copy-done.2, bf16[96,640]{1,0:T(8,128)(2,1)S(1)} %collective-permute-done.refs_1_, bf16[96,640]{1,0:T(8,128)(2,1)S(1)} %collective-permute-done.1.refs_2_, bf16[96,640]{1,0:T(8,128)(2,1)S(1)} %collective-permute-done.2.refs_3_, ...), custom_call_target="tpu_custom_call" | custom-call | tf_op jit(solution)/shard_map/pallas_call | solution.py:588
  44.5 0.2 collective-permute-start.7
  44.7 1.7 %collective-permute-done.7.got_ref = bf16[4,96,640]{2,1,0:T(8,128)(2,1)S(1)} collective-permute-done((bf16[4,96,640]{2,1,0:T(8,128)(2,1)S(1)}, bf16[4,96,640]{2,1,0:T(8,128)(2,1)S(1)}, u32[]{:S(2)}, u32[]{:S(2)}) %collective-permute-start.7) | collective-permute-done | bytes 491552 | tf_op jit(solution)/shard_map/ppermute | solution.py:868
  46.4 0.4 shard_map.227
  46.8 1.4 %collective-permute-start.10 = (bf16[96,640]{1,0:T(8,128)(2,1)S(1)}, bf16[96,640]{1,0:T(8,128)(2,1)S(1)}, u32[]{:S(2)}, u32[]{:S(2)}) collective-permute-start(bf16[96,640]{1,0:T(8,128)(2,1)S(1)} %get-tuple-element.41), channel_id=1, source_target_pairs={{0,2},{1,3},{2,4},{3,5},{4,6},{5,7},{6,0},{7,1},{8,10},{9,11},{10,... | collective-permute-start | bytes 368648 | tf_op jit(solution)/shard_map/ppermute | solution.py:863
  48.2 1.9 %collective-permute-start.8 = (bf16[96,640]{1,0:T(8,128)(2,1)S(1)}, bf16[96,640]{1,0:T(8,128)(2,1)S(1)}, u32[]{:S(2)}, u32[]{:S(2)}) collective-permute-start(bf16[96,640]{1,0:T(8,128)(2,1)S(1)} %get-tuple-element.36), channel_id=1, source_target_pairs={{0,6},{1,7},{2,0},{3,1},{4,2},{5,3},{6,4},{7,5},{8,14},{9,15},{10,... | collective-permute-start | bytes 368648 | tf_op jit(solution)/shard_map/ppermute | solution.py:863
  50.1 0.8 collective-permute-start.9
  50.9 5.5 %shard_map.228 = (bf16[4,256,192]{2,1,0:T(8,128)(2,1)}, bf16[128,32,128]{2,1,0:T(8,128)(2,1)}) custom-call(f32[776,128]{1,0:T(8,128)} %constant.64.clone.fine_hbm, f32[16,128]{1,0:T(8,128)} %constant.65.clone.coarse_hbm, bf16[256,2304]{1,0:T(8,128)(2,1)} %x_hbm.1, bf16[2304,768]{1,0:T(8,128)(2,1)} %query_proj_hbm.3, f32[128,32,128]{2,1,0:T(8,128)} %bitcast.42), custom_call_target="tpu_custom_call" | custom-call | tf_op jit(solution)/shard_map/pallas_call | solution.py:342
  56.4 0.5 collective-permute-done.9.refs_2_
  56.9 0.7 shard_map.229
  57.7 1.3 %collective-permute-done.11 = bf16[24,2304]{1,0:T(8,128)(2,1)S(1)} collective-permute-done((bf16[24,2304]{1,0:T(8,128)(2,1)S(1)}, bf16[24,2304]{1,0:T(8,128)(2,1)S(1)}, u32[]{:S(2)}, u32[]{:S(2)}) %collective-permute-start.11) | collective-permute-done | bytes 110624 | tf_op jit(solution)/shard_map/ppermute | solution.py:868
  59.0 5.4 %all-to-all-done.1.mine_ref = bf16[16,144,512]{2,1,0:T(8,128)(2,1)} async-done(((bf16[16,144,512]{2,1,0:T(8,128)(2,1)}), bf16[16,144,512]{2,1,0:T(8,128)(2,1)}, u32[]{:S(2)}, u32[]{:S(2)}) %all-to-all-start.1) | async-done | bytes 2359328 | tf_op jit(solution)/shard_map/all_to_all | solution.py:875
  64.4 3.7 %all-to-all-start.3 = ((bf16[128,32,128]{2,1,0:T(8,128)(2,1)}), bf16[128,32,128]{2,1,0:T(8,128)(2,1)S(1)}, u32[]{:S(2)}, u32[]{:S(2)}) async-start(bf16[128,32,128]{2,1,0:T(8,128)(2,1)} %get-tuple-element.48), calls=%async_computation.3 | async-start | bytes 2097152 | tf_op jit(solution)/shard_map/all_to_all | solution.py:897
  68.1 1.6 %collective-permute-start.12 = (bf16[24,2304]{1,0:T(8,128)(2,1)S(1)}, bf16[24,2304]{1,0:T(8,128)(2,1)S(1)}, u32[]{:S(2)}, u32[]{:S(2)}) collective-permute-start(bf16[24,2304]{1,0:T(8,128)(2,1)S(1)} %add_convert_fusion.1), channel_id=1, source_target_pairs={{0,2},{1,3},{2,0},{3,1},{4,6},{5,7},{6,4},{7,5},{8,10},{9,11},{10,... | collective-permute-start | bytes 331784 | tf_op jit(solution)/shard_map/ppermute | solution.py:890
  69.7 4.0 %collective-permute-done.12 = bf16[24,2304]{1,0:T(8,128)(2,1)S(1)} collective-permute-done((bf16[24,2304]{1,0:T(8,128)(2,1)S(1)}, bf16[24,2304]{1,0:T(8,128)(2,1)S(1)}, u32[]{:S(2)}, u32[]{:S(2)}) %collective-permute-start.12) | collective-permute-done | bytes 110624 | tf_op jit(solution)/shard_map/ppermute | solution.py:890
  73.7 2.8 %collective-permute-start.13 = (bf16[24,2304]{1,0:T(8,128)(2,1)S(1)}, bf16[24,2304]{1,0:T(8,128)(2,1)S(1)}, u32[]{:S(2)}, u32[]{:S(2)}) collective-permute-start(bf16[24,2304]{1,0:T(8,128)(2,1)S(1)} %add_convert_fusion.one_hbm), channel_id=1, source_target_pairs={{0,6},{1,7},{2,4},{3,5},{4,2},{5,3},{6,0},{7,1},{8,14},{9,15},{10,... | collective-permute-start | bytes 331784 | tf_op jit(solution)/shard_map/ppermute | solution.py:890
  76.5 9.6 %shard_map.230 = bf16[8,576,128]{2,1,0:T(8,128)(2,1)} custom-call(bf16[4,256,192]{2,1,0:T(8,128)(2,1)} %get-tuple-element.38.q_ref, bf16[16,144,512]{2,1,0:T(8,128)(2,1)} %all-to-all-done.1.mine_ref, bf16[16,144,512]{2,1,0:T(8,128)(2,1)} %collective-permute-done.14.other_ref, bf16[512,512]{1,0:T(8,128)(2,1)} %ke_ref.1, bf16[512,512]{1,0:T(8,128)(2,1)} %ve_ref.1, ...), custom_call_target="tpu_custom_call" | custom-call | tf_op jit(solution)/shard_map/pallas_call | solution.py:463
  86.1 1.9 %all-to-all-done.3 = bf16[128,32,128]{2,1,0:T(8,128)(2,1)S(1)} async-done(((bf16[128,32,128]{2,1,0:T(8,128)(2,1)}), bf16[128,32,128]{2,1,0:T(8,128)(2,1)S(1)}, u32[]{:S(2)}, u32[]{:S(2)}) %all-to-all-start.3) | async-done | bytes 1048608 | tf_op jit(solution)/shard_map/all_to_all | solution.py:897
  88.1 4.3 %all-to-all-start.2 = ((bf16[8,576,128]{2,1,0:T(8,128)(2,1)}), bf16[8,576,128]{2,1,0:T(8,128)(2,1)S(1)}, u32[]{:S(2)}, u32[]{:S(2)}) async-start(bf16[8,576,128]{2,1,0:T(8,128)(2,1)} %shard_map.230), calls=%async_computation.2 | async-start | bytes 2359296 | tf_op jit(solution)/shard_map/all_to_all | solution.py:909
  92.4 6.8 %shard_map.231 = (f32[24,288]{1,0:T(8,128)}, f32[4,24,288]{2,1,0:T(8,128)}, bf16[4,24,288]{2,1,0:T(8,128)(2,1)}) custom-call(f32[4]{0:T(128)} %rate_ref.1, bf16[24,2304]{1,0:T(8,128)(2,1)} %copy-done.5, bf16[24,2304]{1,0:T(8,128)(2,1)} %copy-done.6, bf16[24,2304]{1,0:T(8,128)(2,1)} %bitcast.44, bf16[3,2304,512]{2,1,0:T(8,128)(2,1)} %bitcast.39, ...), custom_call_target="tpu_custom_call" | custom-call | tf_op jit(solution)/shard_map/pallas_call | solution.py:785
  99.2 0.6 collective-permute-start.15
  99.8 1.1 constant_dynamic-slice_fusion.x_ref
  100.9 0.8 fusion.4
  101.7 1.9 %collective-permute-start.16 = (bf16[24,288]{1,0:T(8,128)(2,1)S(1)}, bf16[24,288]{1,0:T(8,128)(2,1)S(1)}, u32[]{:S(2)}, u32[]{:S(2)}) collective-permute-start(bf16[24,288]{1,0:T(8,128)(2,1)S(1)} %get-tuple-element.56), channel_id=1, source_target_pairs={{0,2},{1,3},{2,4},{3,5},{4,6},{5,7},{6,0},{7,1},{8,10},{9,11},{10,... | collective-permute-start | bytes 41480 | tf_op jit(solution)/shard_map/ppermute | solution.py:863
  103.7 2.7 %collective-permute-start.17 = (bf16[24,288]{1,0:T(8,128)(2,1)S(1)}, bf16[24,288]{1,0:T(8,128)(2,1)S(1)}, u32[]{:S(2)}, u32[]{:S(2)}) collective-permute-start(bf16[24,288]{1,0:T(8,128)(2,1)S(1)} %get-tuple-element.55), channel_id=1, source_target_pairs={{0,4},{1,5},{2,6},{3,7},{4,0},{5,1},{6,2},{7,3},{8,12},{9,13},{10,... | collective-permute-start | bytes 41480 | tf_op jit(solution)/shard_map/ppermute | solution.py:863
  106.4 1.5 %collective-permute-start.18 = (bf16[24,288]{1,0:T(8,128)(2,1)S(1)}, bf16[24,288]{1,0:T(8,128)(2,1)S(1)}, u32[]{:S(2)}, u32[]{:S(2)}) collective-permute-start(bf16[24,288]{1,0:T(8,128)(2,1)S(1)} %get-tuple-element.54), channel_id=1, source_target_pairs={{0,6},{1,7},{2,0},{3,1},{4,2},{5,3},{6,4},{7,5},{8,14},{9,15},{10,... | collective-permute-start | bytes 41480 | tf_op jit(solution)/shard_map/ppermute | solution.py:863
  107.8 0.8 bitcast_add_fusion.refs_0_
  108.6 1.7 %collective-permute-done.16.refs_1_ = bf16[24,288]{1,0:T(8,128)(2,1)S(1)} collective-permute-done((bf16[24,288]{1,0:T(8,128)(2,1)S(1)}, bf16[24,288]{1,0:T(8,128)(2,1)S(1)}, u32[]{:S(2)}, u32[]{:S(2)}) %collective-permute-start.16) | collective-permute-done | bytes 13856 | tf_op jit(solution)/shard_map/ppermute | solution.py:863
  110.3 0.3 collective-permute-done.17.refs_2_
  110.6 0.9 shard_map.232
  (43 shorter events, 0.4 us)
Async XLA Ops:
  2.7 25.0 %all-to-all-start = ((bf16[16,3,16,576]{3,2,1,0:T(8,128)(2,1)}), bf16[16,3,16,576]{3,2,1,0:T(8,128)(2,1)S(1)}, u32[]{:S(2)}, u32[]{:S(2)}) async-start(bf16[16,3,16,576]{3,2,1,0:T(8,128)(2,1)} %shard_map.224), calls=%async_computation | async-start | bytes 1966080 | tf_op jit(solution)/shard_map/all_to_all | solution.py:870
  10.9 8.6 %copy-start.7 = (s32[16,1,6]{0,1,2:T(1,128)S(1)}, s32[16,1,6]{0,1,2:T(1,128)}, u32[]{:S(2)}) copy-start(s32[16,1,6]{0,1,2:T(1,128)} %param.26) | copy-start | bytes 1156
  10.9 8.7 %copy-start.8 = (s32[8]{0:T(128)S(1)}, s32[8]{0:T(128)}, u32[]{:S(2)}) copy-start(s32[8]{0:T(128)} %lengths_ref.1) | copy-start | bytes 100
  10.9 8.9 %copy-start.9 = (s32[16,1]{0,1:T(1,128)S(1)}, s32[16,1]{0,1:T(1,128)}, u32[]{:S(2)}) copy-start(s32[16,1]{0,1:T(1,128)} %param.27) | copy-start | bytes 196
  17.9 6.4 %collective-permute-start = (bf16[96,640]{1,0:T(8,128)(2,1)}, bf16[96,640]{1,0:T(8,128)(2,1)S(1)}, u32[]{:S(2)}, u32[]{:S(2)}) collective-permute-start(bf16[96,640]{1,0:T(8,128)(2,1)} %get-tuple-element.29.refs_0_), channel_id=1, source_target_pairs={{0,2},{1,3},{2,4},{3,5},{4,6},{5,7},{6,0},{7,1},{8,10},{9,11},{10,... | collective-permute-start | bytes 368648 | tf_op jit(solution)/shard_map/ppermute | solution.py:863
  27.7 4.6 %copy-start.2 = (bf16[96,640]{1,0:T(8,128)(2,1)S(1)}, bf16[96,640]{1,0:T(8,128)(2,1)}, u32[]{:S(2)}) copy-start(bf16[96,640]{1,0:T(8,128)(2,1)} %get-tuple-element.29.refs_0_) | copy-start | bytes 368644
  27.7 13.9 %copy-start.3 = (bf16[32,576]{1,0:T(8,128)(2,1)S(1)}, bf16[32,576]{1,0:T(8,128)(2,1)}, u32[]{:S(2)}) copy-start(bf16[32,576]{1,0:T(8,128)(2,1)} %get-tuple-element.30.refs_9_) | copy-start | bytes 110596
  27.7 36.7 %all-to-all-start.1 = ((bf16[16,144,512]{2,1,0:T(8,128)(2,1)}), bf16[16,144,512]{2,1,0:T(8,128)(2,1)}, u32[]{:S(2)}, u32[]{:S(2)}) async-start(bf16[16,144,512]{2,1,0:T(8,128)(2,1)} %get-tuple-element.42), calls=%async_computation.1 | async-start | bytes 4718592 | tf_op jit(solution)/shard_map/all_to_all | solution.py:875
  32.3 6.5 %collective-permute-start.1 = (bf16[96,640]{1,0:T(8,128)(2,1)S(1)}, bf16[96,640]{1,0:T(8,128)(2,1)S(1)}, u32[]{:S(2)}, u32[]{:S(2)}) collective-permute-start(bf16[96,640]{1,0:T(8,128)(2,1)S(1)} %copy-done.2), channel_id=1, source_target_pairs={{0,4},{1,5},{2,6},{3,7},{4,0},{5,1},{6,2},{7,3},{8,12},{9,13},{10,... | collective-permute-start | bytes 368648 | tf_op jit(solution)/shard_map/ppermute | solution.py:863
  35.4 4.9 %collective-permute-start.2 = (bf16[96,640]{1,0:T(8,128)(2,1)S(1)}, bf16[96,640]{1,0:T(8,128)(2,1)S(1)}, u32[]{:S(2)}, u32[]{:S(2)}) collective-permute-start(bf16[96,640]{1,0:T(8,128)(2,1)S(1)} %copy-done.2), channel_id=1, source_target_pairs={{0,6},{1,7},{2,0},{3,1},{4,2},{5,3},{6,4},{7,5},{8,14},{9,15},{10,... | collective-permute-start | bytes 368648 | tf_op jit(solution)/shard_map/ppermute | solution.py:863
  36.6 3.7 %collective-permute-start.3 = (bf16[96,640]{1,0:T(8,128)(2,1)S(1)}, bf16[96,640]{1,0:T(8,128)(2,1)S(1)}, u32[]{:S(2)}, u32[]{:S(2)}) collective-permute-start(bf16[96,640]{1,0:T(8,128)(2,1)S(1)} %copy-done.2), channel_id=1, source_target_pairs={{0,1},{1,0},{2,3},{3,2},{4,5},{5,4},{6,7},{7,6},{8,9},{9,8},{10,11... | collective-permute-start | bytes 368648 | tf_op jit(solution)/shard_map/ppermute | solution.py:868
  36.6 3.7 %collective-permute-start.4 = (bf16[96,640]{1,0:T(8,128)(2,1)S(1)}, bf16[96,640]{1,0:T(8,128)(2,1)S(1)}, u32[]{:S(2)}, u32[]{:S(2)}) collective-permute-start(bf16[96,640]{1,0:T(8,128)(2,1)S(1)} %collective-permute-done.refs_1_), channel_id=1, source_target_pairs={{0,1},{1,0},{2,3},{3,2},{4,5},{5,4},{6,7},{7,6},{8,9},{9,8},{10,11... | collective-permute-start | bytes 368648 | tf_op jit(solution)/shard_map/ppermute | solution.py:868
  38.8 1.5 %collective-permute-start.5 = (bf16[96,640]{1,0:T(8,128)(2,1)S(1)}, bf16[96,640]{1,0:T(8,128)(2,1)S(1)}, u32[]{:S(2)}, u32[]{:S(2)}) collective-permute-start(bf16[96,640]{1,0:T(8,128)(2,1)S(1)} %collective-permute-done.1.refs_2_), channel_id=1, source_target_pairs={{0,1},{1,0},{2,3},{3,2},{4,5},{5,4},{6,7},{7,6},{8,9},{9,8},{10,11... | collective-permute-start | bytes 368648 | tf_op jit(solution)/shard_map/ppermute | solution.py:868
  40.3 1.3 %collective-permute-start.6 = (bf16[96,640]{1,0:T(8,128)(2,1)S(1)}, bf16[96,640]{1,0:T(8,128)(2,1)S(1)}, u32[]{:S(2)}, u32[]{:S(2)}) collective-permute-start(bf16[96,640]{1,0:T(8,128)(2,1)S(1)} %collective-permute-done.2.refs_3_), channel_id=1, source_target_pairs={{0,1},{1,0},{2,3},{3,2},{4,5},{5,4},{6,7},{7,6},{8,9},{9,8},{10,11... | collective-permute-start | bytes 368648 | tf_op jit(solution)/shard_map/ppermute | solution.py:868
  44.5 1.9 %collective-permute-start.7 = (bf16[4,96,640]{2,1,0:T(8,128)(2,1)S(1)}, bf16[4,96,640]{2,1,0:T(8,128)(2,1)S(1)}, u32[]{:S(2)}, u32[]{:S(2)}) collective-permute-start(bf16[4,96,640]{2,1,0:T(8,128)(2,1)S(1)} %get-tuple-element.34), channel_id=1, source_target_pairs={{0,1},{1,0},{2,3},{3,2},{4,5},{5,4},{6,7},{7,6},{8,9},{9,8},{10,11... | collective-permute-start | bytes 1474568 | tf_op jit(solution)/shard_map/ppermute | solution.py:868
  46.8 9.6 %collective-permute-start.10 = (bf16[96,640]{1,0:T(8,128)(2,1)S(1)}, bf16[96,640]{1,0:T(8,128)(2,1)S(1)}, u32[]{:S(2)}, u32[]{:S(2)}) collective-permute-start(bf16[96,640]{1,0:T(8,128)(2,1)S(1)} %get-tuple-element.41), channel_id=1, source_target_pairs={{0,2},{1,3},{2,4},{3,5},{4,6},{5,7},{6,0},{7,1},{8,10},{9,11},{10,... | collective-permute-start | bytes 368648 | tf_op jit(solution)/shard_map/ppermute | solution.py:863
  48.2 8.2 %collective-permute-start.8 = (bf16[96,640]{1,0:T(8,128)(2,1)S(1)}, bf16[96,640]{1,0:T(8,128)(2,1)S(1)}, u32[]{:S(2)}, u32[]{:S(2)}) collective-permute-start(bf16[96,640]{1,0:T(8,128)(2,1)S(1)} %get-tuple-element.36), channel_id=1, source_target_pairs={{0,6},{1,7},{2,0},{3,1},{4,2},{5,3},{6,4},{7,5},{8,14},{9,15},{10,... | collective-permute-start | bytes 368648 | tf_op jit(solution)/shard_map/ppermute | solution.py:863
  50.1 6.8 %collective-permute-start.9 = (bf16[96,640]{1,0:T(8,128)(2,1)S(1)}, bf16[96,640]{1,0:T(8,128)(2,1)S(1)}, u32[]{:S(2)}, u32[]{:S(2)}) collective-permute-start(bf16[96,640]{1,0:T(8,128)(2,1)S(1)} %get-tuple-element.40), channel_id=1, source_target_pairs={{0,4},{1,5},{2,6},{3,7},{4,0},{5,1},{6,2},{7,3},{8,12},{9,13},{10,... | collective-permute-start | bytes 368648 | tf_op jit(solution)/shard_map/ppermute | solution.py:863
  50.9 6.0 %copy-start = (bf16[512,2304]{1,0:T(8,128)(2,1)S(1)}, bf16[512,2304]{1,0:T(8,128)(2,1)}, u32[]{:S(2)}) copy-start(bf16[512,2304]{1,0:T(8,128)(2,1)} %out_hbm.1) | copy-start | bytes 7077892
  50.9 6.0 %copy-start.1 = (bf16[512,512]{1,0:T(8,128)(2,1)S(1)}, bf16[512,512]{1,0:T(8,128)(2,1)}, u32[]{:S(2)}) copy-start(bf16[512,512]{1,0:T(8,128)(2,1)} %ve_ref.1) | copy-start | bytes 1572868
  57.6 1.4 %collective-permute-start.11 = (bf16[24,2304]{1,0:T(8,128)(2,1)S(1)}, bf16[24,2304]{1,0:T(8,128)(2,1)S(1)}, u32[]{:S(2)}, u32[]{:S(2)}) collective-permute-start(bf16[24,2304]{1,0:T(8,128)(2,1)S(1)} %shard_map.229), channel_id=1, source_target_pairs={{0,1},{1,0},{2,3},{3,2},{4,5},{5,4},{6,7},{7,6},{8,9},{9,8},{10,11... | collective-permute-start | bytes 331784 | tf_op jit(solution)/shard_map/ppermute | solution.py:868
  64.4 12.1 %collective-permute-start.14 = (bf16[16,144,512]{2,1,0:T(8,128)(2,1)}, bf16[16,144,512]{2,1,0:T(8,128)(2,1)}, u32[]{:S(2)}, u32[]{:S(2)}) collective-permute-start(bf16[16,144,512]{2,1,0:T(8,128)(2,1)} %all-to-all-done.1.mine_ref), channel_id=1, source_target_pairs={{0,1},{1,0},{2,3},{3,2},{4,5},{5,4},{6,7},{7,6},{8,9},{9,8},{10,11... | collective-permute-start | bytes 7077896 | tf_op jit(solution)/shard_map/ppermute | solution.py:868
  64.4 23.7 %all-to-all-start.3 = ((bf16[128,32,128]{2,1,0:T(8,128)(2,1)}), bf16[128,32,128]{2,1,0:T(8,128)(2,1)S(1)}, u32[]{:S(2)}, u32[]{:S(2)}) async-start(bf16[128,32,128]{2,1,0:T(8,128)(2,1)} %get-tuple-element.48), calls=%async_computation.3 | async-start | bytes 2097152 | tf_op jit(solution)/shard_map/all_to_all | solution.py:897
  68.1 5.5 %collective-permute-start.12 = (bf16[24,2304]{1,0:T(8,128)(2,1)S(1)}, bf16[24,2304]{1,0:T(8,128)(2,1)S(1)}, u32[]{:S(2)}, u32[]{:S(2)}) collective-permute-start(bf16[24,2304]{1,0:T(8,128)(2,1)S(1)} %add_convert_fusion.1), channel_id=1, source_target_pairs={{0,2},{1,3},{2,0},{3,1},{4,6},{5,7},{6,4},{7,5},{8,10},{9,11},{10,... | collective-permute-start | bytes 331784 | tf_op jit(solution)/shard_map/ppermute | solution.py:890
  73.7 12.4 %copy-start.5 = (bf16[24,2304]{1,0:T(8,128)(2,1)}, bf16[24,2304]{1,0:T(8,128)(2,1)S(1)}, u32[]{:S(2)}) copy-start(bf16[24,2304]{1,0:T(8,128)(2,1)S(1)} %add_convert_fusion.one_hbm) | copy-start | bytes 331780
  73.7 12.4 %collective-permute-start.13 = (bf16[24,2304]{1,0:T(8,128)(2,1)S(1)}, bf16[24,2304]{1,0:T(8,128)(2,1)S(1)}, u32[]{:S(2)}, u32[]{:S(2)}) collective-permute-start(bf16[24,2304]{1,0:T(8,128)(2,1)S(1)} %add_convert_fusion.one_hbm), channel_id=1, source_target_pairs={{0,6},{1,7},{2,4},{3,5},{4,2},{5,3},{6,0},{7,1},{8,14},{9,15},{10,... | collective-permute-start | bytes 331784 | tf_op jit(solution)/shard_map/ppermute | solution.py:890
  86.1 6.3 %copy-start.6 = (bf16[24,2304]{1,0:T(8,128)(2,1)}, bf16[24,2304]{1,0:T(8,128)(2,1)S(1)}, u32[]{:S(2)}) copy-start(bf16[24,2304]{1,0:T(8,128)(2,1)S(1)} %collective-permute-done.13.two_hbm) | copy-start | bytes 331780
  88.1 4.3 %copy-start.4 = (bf16[128,32,128]{2,1,0:T(8,128)(2,1)}, bf16[128,32,128]{2,1,0:T(8,128)(2,1)S(1)}, u32[]{:S(2)}) copy-start(bf16[128,32,128]{2,1,0:T(8,128)(2,1)S(1)} %all-to-all-done.3) | copy-start | bytes 3145732
  88.1 22.5 %all-to-all-start.2 = ((bf16[8,576,128]{2,1,0:T(8,128)(2,1)}), bf16[8,576,128]{2,1,0:T(8,128)(2,1)S(1)}, u32[]{:S(2)}, u32[]{:S(2)}) async-start(bf16[8,576,128]{2,1,0:T(8,128)(2,1)} %shard_map.230), calls=%async_computation.2 | async-start | bytes 2359296 | tf_op jit(solution)/shard_map/all_to_all | solution.py:909
  99.2 1.7 %collective-permute-start.15 = (bf16[4,24,288]{2,1,0:T(8,128)(2,1)}, bf16[4,24,288]{2,1,0:T(8,128)(2,1)S(1)}, u32[]{:S(2)}, u32[]{:S(2)}) collective-permute-start(bf16[4,24,288]{2,1,0:T(8,128)(2,1)} %get-tuple-element.50), channel_id=1, source_target_pairs={{0,1},{1,0},{2,3},{3,2},{4,5},{5,4},{6,7},{7,6},{8,9},{9,8},{10,11... | collective-permute-start | bytes 165896 | tf_op jit(solution)/shard_map/ppermute | solution.py:868
  101.7 8.5 %collective-permute-start.16 = (bf16[24,288]{1,0:T(8,128)(2,1)S(1)}, bf16[24,288]{1,0:T(8,128)(2,1)S(1)}, u32[]{:S(2)}, u32[]{:S(2)}) collective-permute-start(bf16[24,288]{1,0:T(8,128)(2,1)S(1)} %get-tuple-element.56), channel_id=1, source_target_pairs={{0,2},{1,3},{2,4},{3,5},{4,6},{5,7},{6,0},{7,1},{8,10},{9,11},{10,... | collective-permute-start | bytes 41480 | tf_op jit(solution)/shard_map/ppermute | solution.py:863
  103.7 6.9 %collective-permute-start.17 = (bf16[24,288]{1,0:T(8,128)(2,1)S(1)}, bf16[24,288]{1,0:T(8,128)(2,1)S(1)}, u32[]{:S(2)}, u32[]{:S(2)}) collective-permute-start(bf16[24,288]{1,0:T(8,128)(2,1)S(1)} %get-tuple-element.55), channel_id=1, source_target_pairs={{0,4},{1,5},{2,6},{3,7},{4,0},{5,1},{6,2},{7,3},{8,12},{9,13},{10,... | collective-permute-start | bytes 41480 | tf_op jit(solution)/shard_map/ppermute | solution.py:863
  106.4 4.2 %collective-permute-start.18 = (bf16[24,288]{1,0:T(8,128)(2,1)S(1)}, bf16[24,288]{1,0:T(8,128)(2,1)S(1)}, u32[]{:S(2)}, u32[]{:S(2)}) collective-permute-start(bf16[24,288]{1,0:T(8,128)(2,1)S(1)} %get-tuple-element.54), channel_id=1, source_target_pairs={{0,6},{1,7},{2,0},{3,1},{4,2},{5,3},{6,4},{7,5},{8,14},{9,15},{10,... | collective-permute-start | bytes 41480 | tf_op jit(solution)/shard_map/ppermute | solution.py:863
